TPU v7x, 32 devices: a whole 2x2x4 slice. The times are simulated.
32 devices in a mesh: seq: 8 (over z, x), head: 4 (over y, core).
Axes of the slice: x: 2, y: 2, z: 4, core: 2. Of those that a mesh axis runs over, the one named last changes fastest.
Arguments:
- tokens: bfloat16 [4096, 2048], P('seq'), may hold values from -6 to 6
- gain_attn: float32 [2048], replicated, may hold values from 0.1 to 1.9
- gain_mlp: float32 [2048], replicated, may hold values from 0.1 to 1.9
- w_query: bfloat16 [2048, 2048], P(None, 'head'), may hold values from -0.125 to 0.125
- w_key: bfloat16 [2048, 2048], P(None, 'head'), may hold values from -0.125 to 0.125
- w_value: bfloat16 [2048, 2048], P(None, 'head'), may hold values from -0.125 to 0.125
- w_out: bfloat16 [2048, 2048], P(None, 'head'), may hold values from -1.5 to 1.5
- w_gate: bfloat16 [2048, 5504], P(None, 'head'), may hold values from -0.125 to 0.125
- w_up: bfloat16 [2048, 5504], P(None, 'head'), may hold values from -0.125 to 0.125
- w_down: bfloat16 [2048, 5504], P(None, 'head'), may hold values from -0.078125 to 0.078125
- prev_keys: bfloat16 [2048, 2048], P(None, 'head'), may hold values from -6 to 6
- prev_values: bfloat16 [2048, 2048], P(None, 'head'), may hold values from -6 to 6
- lengths: int32 [4], replicated, may hold values from 1 to 3648, as said below
- out_grad: bfloat16 [4096, 2048], P('seq'), may hold values from -6 to 6
Outputs:
- block_out: bfloat16 [4096, 2048], P('seq')
- tokens_grad: bfloat16 [4096, 2048], P('seq')
- gain_attn_grad: float32 [2048], P('seq')
- gain_mlp_grad: float32 [2048], P('seq')
- w_query_grad: float32 [2048, 2048], P('seq', 'head')
- w_key_grad: float32 [2048, 2048], P('seq', 'head')
- w_value_grad: float32 [2048, 2048], P('seq', 'head')
- w_out_grad: float32 [2048, 2048], P('seq', 'head')
- w_gate_grad: float32 [2048, 5504], P('seq', 'head')
- w_up_grad: float32 [2048, 5504], P('seq', 'head')
- w_down_grad: float32 [2048, 5504], P('seq', 'head')
Inputs may be any that keep to these rules, and one draw needn't show every extreme that they name: The lengths rounded up to multiples of 64 add up to exactly 4096.
All inputs are finite; a program needn't handle non-finite values.
Results may differ from a plain program's by a relative error of at most 0.02.
Values may be sent and summed in bfloat16 or wider, within the bound.
A program may use at most 320 MiB of HBM per device.

v0:
```python
import math

import jax
import jax.numpy as jnp
from jax import lax
from jax.sharding import PartitionSpec as P

HEAD_DIM = 128
WINDOW = 2048
PAD = 64
NSEQ = 4
HALO_DEVS = 4
QB = 512


EPS = 1e-06
MASKED = -1e30


def passed_along(block, axis, distance):
    devices = range(lax.axis_size(axis))
    route = [(i - distance, i) for i in devices if i - distance in devices]
    return lax.ppermute(block, axis, route)


def token_meta(global_rows, lengths):
    padded = (lengths + PAD - 1) // PAD * PAD
    starts = jnp.cumsum(padded) - padded
    member = jnp.sum((global_rows[:, None] >= starts[None, :]).astype(jnp.int32), axis=1) - 1
    member = jnp.maximum(member, 0)
    one_hot = member[:, None] == jnp.arange(NSEQ, dtype=jnp.int32)[None, :]
    start_row = jnp.sum(jnp.where(one_hot, starts[None, :], 0), axis=1)
    length_row = jnp.sum(jnp.where(one_hot, lengths[None, :], 0), axis=1)
    position = global_rows - start_row
    return (member, position, position < length_row)


def rope_tables(position):
    half_dim = HEAD_DIM // 2
    freq = jnp.exp(-math.log(10000.0) * (2.0 * jnp.arange(half_dim, dtype=jnp.float32) / HEAD_DIM))
    angle = position.astype(jnp.float32)[:, None] * freq[None, :]
    return (jnp.cos(angle)[:, None, :], jnp.sin(angle)[:, None, :])


def rotate(values, cosine, sine):
    half_dim = values.shape[-1] // 2
    front_half = values[..., :half_dim]
    back_half = values[..., half_dim:]
    return jnp.concatenate(
        [front_half * cosine - back_half * sine, back_half * cosine + front_half * sine], axis=-1
    )


def rotate_back(grads, cosine, sine):
    half_dim = grads.shape[-1] // 2
    front_half = grads[..., :half_dim]
    back_half = grads[..., half_dim:]
    return jnp.concatenate(
        [front_half * cosine + back_half * sine, back_half * cosine - front_half * sine], axis=-1
    )


def window_mask(query_meta, key_meta):
    member_q, position_q, valid_q = query_meta
    member_k, position_k, valid_k = key_meta
    distance = position_q[:, None] - position_k[None, :]
    same_seq = member_q[:, None] == member_k[None, :]
    return same_seq & (distance >= 0) & (distance < WINDOW) & valid_k[None, :] & valid_q[:, None]


def masked_scores(query_blk, key_blk, key_mask):
    scores = jnp.einsum(
        "qhd,khd->hqk", query_blk, key_blk, preferred_element_type=jnp.float32
    ) * HEAD_DIM ** (-0.5)
    return jnp.where(key_mask[None], scores, MASKED)


def outer_sum(left, right):
    return lax.dot_general(
        left, right, (((0,), (0,)), ((), ())), preferred_element_type=jnp.float32
    )


def times_transpose(left, right):
    return lax.dot_general(
        left, right, (((1,), (1,)), ((), ())), preferred_element_type=jnp.float32
    )


def norm_back(grad_normed, inputs, scale_rows, gain):
    unit = inputs * scale_rows
    grad_unit = grad_normed * gain
    gain_part = jnp.sum(grad_normed * unit, axis=0)
    grad_inputs = scale_rows * (
        grad_unit - unit * jnp.mean(grad_unit * unit, axis=-1, keepdims=True)
    )
    return (grad_inputs, gain_part)


def on_device(
    tokens,
    gain_attn,
    gain_mlp,
    w_query,
    w_key,
    w_value,
    w_out,
    w_gate,
    w_up,
    w_down,
    prev_keys,
    prev_values,
    lengths,
    out_grad,
):
    row_count = tokens.shape[0]
    width_here = w_query.shape[1]
    heads_here = width_here // HEAD_DIM
    head_scale = HEAD_DIM ** (-0.5)
    seq_index = lax.axis_index("seq")
    first_row = seq_index * row_count
    query_meta = token_meta(first_row + jnp.arange(row_count, dtype=jnp.int32), lengths)
    key_meta = token_meta(
        first_row - WINDOW + jnp.arange(WINDOW + row_count, dtype=jnp.int32), lengths
    )
    valid_rows = query_meta[2]
    cosine, sine = rope_tables(query_meta[1])
    inputs = tokens.astype(jnp.float32)
    scale_one = lax.rsqrt(jnp.mean(inputs * inputs, axis=-1, keepdims=True) + EPS)
    normed_one = (inputs * scale_one * gain_attn).astype(jnp.bfloat16)
    query_raw = jnp.dot(normed_one, w_query, preferred_element_type=jnp.float32).reshape(
        row_count, heads_here, HEAD_DIM
    )
    key_raw = jnp.dot(normed_one, w_key, preferred_element_type=jnp.float32).reshape(
        row_count, heads_here, HEAD_DIM
    )
    value_raw = jnp.dot(normed_one, w_value, preferred_element_type=jnp.float32).reshape(
        row_count, heads_here, HEAD_DIM
    )
    queries = rotate(query_raw, cosine, sine).astype(jnp.bfloat16)
    keys_own = rotate(key_raw, cosine, sine).astype(jnp.bfloat16)
    values_own = value_raw.astype(jnp.bfloat16)
    key_parts = []
    value_parts = []
    for distance in range(HALO_DEVS, 0, -1):
        got_keys, got_values = passed_along((keys_own, values_own), "seq", distance)
        source = seq_index - distance
        cache_start = jnp.clip(source * row_count + WINDOW, 0, WINDOW - row_count)
        cached_keys = lax.dynamic_slice_in_dim(prev_keys, cache_start, row_count, 0).reshape(
            row_count, heads_here, HEAD_DIM
        )
        cached_values = lax.dynamic_slice_in_dim(prev_values, cache_start, row_count, 0).reshape(
            row_count, heads_here, HEAD_DIM
        )
        key_parts.append(jnp.where(source >= 0, got_keys, cached_keys))
        value_parts.append(jnp.where(source >= 0, got_values, cached_values))
    keys_ext = jnp.concatenate(key_parts + [keys_own], axis=0)
    values_ext = jnp.concatenate(value_parts + [values_own], axis=0)
    block_start = 0
    key_rows = slice(block_start, block_start + WINDOW + QB)
    key_mask = window_mask(query_meta, key_meta)
    scores = masked_scores(queries, keys_ext, key_mask)
    row_top = jnp.max(scores, axis=-1, keepdims=True)
    exp_scores = jnp.exp(scores - row_top)
    row_total = jnp.sum(exp_scores, axis=-1, keepdims=True)
    attended_parts = jnp.einsum(
        "hqk,khd->qhd",
        (exp_scores / row_total).astype(jnp.bfloat16),
        values_ext,
        preferred_element_type=jnp.float32,
    )
    log_totals = [row_top + jnp.log(row_total)]
    attended = attended_parts
    attended = (
        jnp.where(valid_rows[:, None, None], attended, 0.0)
        .reshape(row_count, width_here)
        .astype(jnp.bfloat16)
    )
    branch_attn = lax.psum(times_transpose(attended, w_out), "head")
    mid = inputs + branch_attn
    scale_two = lax.rsqrt(jnp.mean(mid * mid, axis=-1, keepdims=True) + EPS)
    normed_two = (mid * scale_two * gain_mlp).astype(jnp.bfloat16)
    gate = jnp.dot(normed_two, w_gate, preferred_element_type=jnp.float32)
    up_proj = jnp.dot(normed_two, w_up, preferred_element_type=jnp.float32)
    sigmoid_gate = jax.nn.sigmoid(gate)
    silu_gate = jax.nn.silu(gate)
    act = (silu_gate * up_proj).astype(jnp.bfloat16)
    branch_mlp = lax.psum(times_transpose(act, w_down).astype(jnp.bfloat16), "head").astype(
        jnp.float32
    )
    block_out = (mid + branch_mlp).astype(jnp.bfloat16)
    grad_out = out_grad.astype(jnp.float32)
    grad_branch = grad_out.astype(jnp.bfloat16)
    w_down_grad = outer_sum(grad_branch, act)
    grad_act = jnp.dot(grad_branch, w_down, preferred_element_type=jnp.float32)
    grad_gate = (grad_act * up_proj * sigmoid_gate * (1.0 + gate * (1.0 - sigmoid_gate))).astype(
        jnp.bfloat16
    )
    grad_up = (grad_act * silu_gate).astype(jnp.bfloat16)
    w_gate_grad = outer_sum(normed_two, grad_gate)
    w_up_grad = outer_sum(normed_two, grad_up)
    grad_norm_two = lax.psum(
        times_transpose(grad_gate, w_gate) + times_transpose(grad_up, w_up), "head"
    )
    grad_mid_norm, gain_mlp_part = norm_back(grad_norm_two, mid, scale_two, gain_mlp)
    grad_mid = grad_out + grad_mid_norm
    mlp_sums = (w_gate_grad, w_up_grad, w_down_grad, gain_mlp_part)
    grad_attn_branch = grad_mid.astype(jnp.bfloat16)
    w_out_grad = outer_sum(grad_attn_branch, attended)
    grad_attended = jnp.dot(grad_attn_branch, w_out, preferred_element_type=jnp.float32).astype(
        jnp.bfloat16
    )
    grad_attended = jnp.where(
        valid_rows[:, None, None], grad_attended.reshape(row_count, heads_here, HEAD_DIM), 0.0
    )
    grad_keys_ext = jnp.zeros((WINDOW + row_count, heads_here, HEAD_DIM), jnp.float32)
    grad_values_ext = jnp.zeros((WINDOW + row_count, heads_here, HEAD_DIM), jnp.float32)
    grad_query_parts = []
    for block_num, block_start in enumerate(range(0, row_count, QB)):
        key_rows = slice(block_start, block_start + WINDOW + QB)
        key_mask = window_mask(query_meta, key_meta)
        scores = masked_scores(queries, keys_ext, key_mask)
        probs = jnp.exp(scores - log_totals[block_num])
        grad_probs = jnp.einsum(
            "qhd,khd->hqk", grad_attended, values_ext, preferred_element_type=jnp.float32
        )
        row_inner = jnp.sum(probs * grad_probs, axis=-1, keepdims=True)
        grad_scores = (probs * (grad_probs - row_inner)).astype(jnp.bfloat16)
        grad_query_parts.append(
            jnp.einsum("hqk,khd->qhd", grad_scores, keys_ext, preferred_element_type=jnp.float32)
            * head_scale
        )
        grad_keys_ext = grad_keys_ext.at[key_rows].add(
            jnp.einsum("hqk,qhd->khd", grad_scores, queries, preferred_element_type=jnp.float32)
            * head_scale
        )
        grad_values_ext = grad_values_ext.at[key_rows].add(
            jnp.einsum(
                "hqk,qhd->khd",
                probs.astype(jnp.bfloat16),
                grad_attended,
                preferred_element_type=jnp.float32,
            )
        )
    grad_keys_own = grad_keys_ext[WINDOW:]
    grad_values_own = grad_values_ext[WINDOW:]
    for distance in range(1, HALO_DEVS + 1):
        slot_start = (HALO_DEVS - distance) * row_count
        back_keys, back_values = (
            passed_along(
                grad_keys_ext[slot_start : slot_start + row_count].astype(jnp.bfloat16),
                "seq",
                -distance,
            ).astype(jnp.float32),
            passed_along(
                grad_values_ext[slot_start : slot_start + row_count].astype(jnp.bfloat16),
                "seq",
                -distance,
            ).astype(jnp.float32),
        )
        grad_keys_own = grad_keys_own + back_keys
        grad_values_own = grad_values_own + back_values
    grad_queries = grad_query_parts[0]
    grad_query_raw = (
        rotate_back(grad_queries, cosine, sine).reshape(row_count, width_here).astype(jnp.bfloat16)
    )
    grad_key_raw = (
        rotate_back(grad_keys_own, cosine, sine).reshape(row_count, width_here).astype(jnp.bfloat16)
    )
    grad_value_raw = grad_values_own.reshape(row_count, width_here).astype(jnp.bfloat16)
    w_query_grad = outer_sum(normed_one, grad_query_raw)
    w_key_grad = outer_sum(normed_one, grad_key_raw)
    w_value_grad = outer_sum(normed_one, grad_value_raw)
    grad_norm_part = (
        times_transpose(grad_query_raw, w_query)
        + times_transpose(grad_key_raw, w_key)
        + times_transpose(grad_value_raw, w_value)
    )
    grad_norm_one = lax.psum(grad_norm_part.astype(jnp.bfloat16), "head").astype(jnp.float32)
    grad_in_norm, gain_attn_part = norm_back(grad_norm_one, inputs, scale_one, gain_attn)
    tokens_grad = (grad_mid + grad_in_norm).astype(jnp.bfloat16)
    summed = (
        lax.psum_scatter(
            w_query_grad.astype(jnp.bfloat16), "seq", scatter_dimension=0, tiled=True
        ).astype(jnp.float32),
        lax.psum_scatter(
            w_key_grad.astype(jnp.bfloat16), "seq", scatter_dimension=0, tiled=True
        ).astype(jnp.float32),
        lax.psum_scatter(
            w_value_grad.astype(jnp.bfloat16), "seq", scatter_dimension=0, tiled=True
        ).astype(jnp.float32),
        lax.psum_scatter(
            w_out_grad.astype(jnp.bfloat16), "seq", scatter_dimension=0, tiled=True
        ).astype(jnp.float32),
        lax.psum_scatter(
            gain_attn_part.astype(jnp.bfloat16), "seq", scatter_dimension=0, tiled=True
        ).astype(jnp.float32),
        lax.psum_scatter(
            mlp_sums[0].astype(jnp.bfloat16), "seq", scatter_dimension=0, tiled=True
        ).astype(jnp.float32),
        lax.psum_scatter(
            mlp_sums[1].astype(jnp.bfloat16), "seq", scatter_dimension=0, tiled=True
        ).astype(jnp.float32),
        lax.psum_scatter(
            mlp_sums[2].astype(jnp.bfloat16), "seq", scatter_dimension=0, tiled=True
        ).astype(jnp.float32),
        lax.psum_scatter(
            mlp_sums[3].astype(jnp.bfloat16), "seq", scatter_dimension=0, tiled=True
        ).astype(jnp.float32),
    )
    attn_sums = summed[:5]
    mlp_sums = summed[5:]
    return (
        block_out,
        tokens_grad,
        attn_sums[4],
        mlp_sums[3],
        attn_sums[0],
        attn_sums[1],
        attn_sums[2],
        attn_sums[3],
        mlp_sums[0],
        mlp_sums[1],
        mlp_sums[2],
    )


def solution(mesh):
    placed = (
        P("seq", None),
        P(),
        P(),
        P(None, "head"),
        P(None, "head"),
        P(None, "head"),
        P(None, "head"),
        P(None, "head"),
        P(None, "head"),
        P(None, "head"),
        P(None, "head"),
        P(None, "head"),
        P(),
        P("seq", None),
    )
    return jax.shard_map(
        on_device,
        mesh=mesh,
        in_specs=placed,
        out_specs=(
            P("seq", None),
            P("seq", None),
            P("seq"),
            P("seq"),
            P("seq", "head"),
            P("seq", "head"),
            P("seq", "head"),
            P("seq", "head"),
            P("seq", "head"),
            P("seq", "head"),
            P("seq", "head"),
        ),
        check_vma=False,
    )
```

profile of v0, /device:TPU:0, one launch (start us, length us, event | category | flops | bytes accessed | tf_op | source)
XLA Modules:
  0.0 1326.1 jit_solution(3645130983424933034)
XLA Ops:
  11.9 3.6 fusion.54
  18.0 2.4 copy.150
  20.3 3.6 fusion.52
  25.0 2.4 copy.151
  27.4 2.4 copy.152
  30.7 3.6 subtract_convert_fusion.3
  35.5 6.9 collective-permute-start.4
  42.3 5.2 collective-permute-start.5
  47.6 2.1 collective-permute-start.6
  49.7 3.1 collective-permute-start.7
  55.2 2.2 collective-permute-start
  57.8 2.6 fusion.14
  60.4 4.6 constant_dynamic-slice_fusion.2
  103.1 2.7 collective-permute-start.3
  107.7 4.1 collective-permute-done.1
  112.0 9.3 collective-permute-done.2
  122.8 9.8 fusion.65
  132.7 9.6 fusion
  142.3 9.3 fusion.29
  152.4 3.4 fusion.68
  156.1 141.4 %all-reduce.8.cloned.1.call-done = f32[512,2048]{1,0:T(8,128)} async-done(((f32[512,2048]{1,0:T(8,128)}), f32[512,2048]{1,0:T(8,128)}) %all-reduce.8.cloned.1.call-update) | async-done | bytes 4194320 | tf_op jit(solution)/shard_map/psum | solution.py:179
  297.5 3.5 multiply_reduce_fusion.3
  303.2 6.6 fusion.69
  309.8 3.1 fusion.70
  313.0 5.5 multiply_convert_fusion.2
  318.5 3.6 fusion.71
  322.2 5.0 convolution_add_fusion
  327.7 7.8 convolution_convert_fusion.7
  335.6 77.4 %all-reduce.10.cloned.1.call-done = f32[512,2048]{1,0:T(8,128)} async-done(((f32[512,2048]{1,0:T(8,128)}), f32[512,2048]{1,0:T(8,128)}) %all-reduce.10.cloned.1.call-update) | async-done | bytes 4194320 | tf_op jit(solution)/shard_map/psum | solution.py:202
  413.0 4.6 multiply_reduce_fusion.1
  418.9 2.7 multiply_add_fusion
  424.3 13.1 fusion.67
  437.4 14.9 %multiply_reduce_fusion = (f32[4,512]{1,0:T(4,128)S(1)}, f32[4,512,2560]{2,1,0:T(8,128)}) fusion(f32[4,512,2560]{2,1,0:T(8,128)} %get-tuple-element.107, f32[4,512]{1,0:T(4,128)S(1)} %log_add_fusion, bf16[2560,4,128]{2,0,1:T(8,128)(2,1)} %copy-done.11, bf16[512,4,128]{0,2,1:T(8,128)(2,1)} %bitcast.74, pred[512]{0:T(512)(128)(4,1)S(1)} %lt.34), kind=kOutput, calls=%fused_computation.1 | convolution fusion | flops 1358166016 | bytes 45105664 | tf_op jit(solution)/shard_map/qhd,khd->hqk/dot_general | solution.py:224
  454.9 14.6 %multiply_convert_fusion = bf16[4,512,2560]{2,1,0:T(8,128)(2,1)S(1)} fusion(f32[4,512,2560]{2,1,0:T(8,128)} %get-tuple-element.109, f32[4,512,2560]{2,1,0:T(8,128)} %get-tuple-element.107, f32[4,512]{1,0:T(4,128)S(1)} %get-tuple-element.108, f32[4,512]{1,0:T(4,128)S(1)} %log_add_fusion), kind=kLoop, calls=%fused_computation | loop fusion | flops 20971520 | bytes 52445184 | tf_op jit(solution)/shard_map/convert_element_type | solution.py:228
  469.5 6.6 fusion.66
  483.2 2.9 fusion.27
  486.1 10.8 collective-permute-done.10
  498.2 32.7 %collective-permute-done.11 = bf16[512,4,128]{2,0,1:T(8,128)(2,1)S(1)} collective-permute-done((bf16[512,4,128]{2,0,1:T(8,128)(2,1)S(1)}, bf16[512,4,128]{2,0,1:T(8,128)(2,1)S(1)}, u32[]{:S(2)}, u32[]{:S(2)}) %collective-permute-start.11) | collective-permute-done | bytes 524320 | tf_op jit(solution)/shard_map/ppermute | solution.py:23
  537.4 5.1 fusion.73
  545.8 62.8 %collective-permute-done.15 = bf16[512,4,128]{0,2,1:T(8,128)(2,1)} collective-permute-done((bf16[512,4,128]{0,2,1:T(8,128)(2,1)}, bf16[512,4,128]{0,2,1:T(8,128)(2,1)}, u32[]{:S(2)}, u32[]{:S(2)}) %collective-permute-start.15) | collective-permute-done | bytes 524320 | tf_op jit(solution)/shard_map/ppermute | solution.py:23
  608.6 2.2 fusion.33
  611.6 2.7 add_convert_fusion
  615.3 5.6 convolution_convert_fusion.3
  621.1 3.9 convolution_convert_fusion.4
  625.1 2.9 convolution_convert_fusion.5
  628.3 2.8 convolution_convert_fusion.6
  631.2 7.6 convolution_convert_fusion.1
  640.2 6.4 convolution_convert_fusion
  647.9 6.4 fusion.6
  656.2 40.5 %all-reduce.12.cloned.1.call-done = (bf16[512,2048]{1,0:T(8,128)(2,1)}, bf16[512,2048]{1,0:T(8,128)(2,1)}) async-done(((bf16[512,2048]{1,0:T(8,128)(2,1)}, bf16[512,2048]{1,0:T(8,128)(2,1)}), (bf16[512,2048]{1,0:T(8,128)(2,1)}, bf16[512,2048]{1,0:T(8,128)(2,1)})) %all-reduce.12.cloned.1.call-update) | async-done | bytes 4194320 | tf_op jit(solution)/shard_map/psum | solution.py:188
  696.7 2.9 fusion.24
  699.6 21.7 %all-reduce.2 = (bf16[2048]{0:T(1024)(128)(2,1)S(1)}, bf16[2048]{0:T(1024)(128)(2,1)S(1)}) all-reduce(bf16[2048]{0:T(1024)(128)(2,1)S(1)} %get-tuple-element.53, bf16[2048]{0:T(1024)(128)(2,1)S(1)} %get-tuple-element.51), channel_id=2, replica_groups=mesh['seq'=8,'head'=4] {'seq'}, use_global_device_ids=true, to_apply=%region_19.20.clone | all-reduce | flops 4096 | bytes 16384
  722.6 5.1 add_convert_fusion.1
  727.7 2.7 fusion.21
  730.4 38.4 %reduce-scatter.14.cloned.1.call-done = bf16[256,512]{1,0:T(8,128)(2,1)} async-done(((bf16[2048,512]{1,0:T(8,128)(2,1)}), bf16[256,512]{1,0:T(8,128)(2,1)}) %reduce-scatter.14.cloned.1.call-update) | async-done | bytes 262160 | tf_op jit(solution)/shard_map/reduce_scatter | solution.py:292
  770.6 68.6 %reduce-scatter.12.cloned.1.call-done = bf16[256,512]{1,0:T(8,128)(2,1)} async-done(((bf16[2048,512]{1,0:T(8,128)(2,1)}), bf16[256,512]{1,0:T(8,128)(2,1)}) %reduce-scatter.12.cloned.1.call-update) | async-done | bytes 262160 | tf_op jit(solution)/shard_map/reduce_scatter | solution.py:289
  841.0 68.6 %reduce-scatter.10.cloned.1.call-done = bf16[256,512]{1,0:T(8,128)(2,1)} async-done(((bf16[2048,512]{1,0:T(8,128)(2,1)}), bf16[256,512]{1,0:T(8,128)(2,1)}) %reduce-scatter.10.cloned.1.call-update) | async-done | bytes 262160 | tf_op jit(solution)/shard_map/reduce_scatter | solution.py:286
  911.4 68.8 %reduce-scatter.8.cloned.1.call-done = bf16[256,512]{1,0:T(8,128)(2,1)} async-done(((bf16[2048,512]{1,0:T(8,128)(2,1)}), bf16[256,512]{1,0:T(8,128)(2,1)}) %reduce-scatter.8.cloned.1.call-update) | async-done | bytes 262160 | tf_op jit(solution)/shard_map/reduce_scatter | solution.py:283
  982.1 109.8 %reduce-scatter.16.cloned.1.call-done = bf16[256,1376]{0,1:T(8,128)(2,1)} async-done(((bf16[2048,1376]{0,1:T(8,128)(2,1)}), bf16[256,1376]{0,1:T(8,128)(2,1)}) %reduce-scatter.16.cloned.1.call-update) | async-done | bytes 704528 | tf_op jit(solution)/shard_map/reduce_scatter | solution.py:298
  1091.9 2.3 convert_element_type.241
  1094.2 110.1 %reduce-scatter.18.cloned.1.call-done = bf16[256,1376]{0,1:T(8,128)(2,1)} async-done(((bf16[2048,1376]{0,1:T(8,128)(2,1)}), bf16[256,1376]{0,1:T(8,128)(2,1)}) %reduce-scatter.18.cloned.1.call-update) | async-done | bytes 704528 | tf_op jit(solution)/shard_map/reduce_scatter | solution.py:301
  1204.3 2.3 convert_element_type.243
  1206.6 109.9 %reduce-scatter.20.cloned.1.call-done = bf16[256,1376]{0,1:T(8,128)(2,1)} async-done(((bf16[2048,1376]{0,1:T(8,128)(2,1)}), bf16[256,1376]{0,1:T(8,128)(2,1)}) %reduce-scatter.20.cloned.1.call-update) | async-done | bytes 704528 | tf_op jit(solution)/shard_map/reduce_scatter | solution.py:304
  1316.5 2.3 convert_element_type.246
  (230 shorter events, 97.8 us)
Async XLA Ops:
  7.2 145.2 %copy-start = (bf16[2048,512]{1,0:T(8,128)(2,1)S(1)}, bf16[2048,512]{1,0:T(8,128)(2,1)}, u32[]{:S(2)}) copy-start(bf16[2048,512]{1,0:T(8,128)(2,1)} %param.28) | copy-start | bytes 6291460
  7.2 290.4 %all-reduce.8.cloned.1.call-start = ((), (), s32[]{:S(2)}) async-start(), calls=%async_computation.7 | async-start | bytes 8388608 | tf_op jit(solution)/shard_map/psum | solution.py:179
  11.9 40.9 %copy-start.45 = (f32[512]{0:T(512)}, f32[512]{0:T(512)S(1)}, u32[]{:S(2)}) copy-start(f32[512]{0:T(512)S(1)} %add_rsqrt_fusion.1) | copy-start | bytes 6148
  30.7 22.1 %copy-start.6 = (bf16[512,2048]{1,0:T(8,128)(2,1)S(1)}, bf16[512,2048]{1,0:T(8,128)(2,1)}, u32[]{:S(2)}) copy-start(bf16[512,2048]{1,0:T(8,128)(2,1)} %param.22) | copy-start | bytes 6291460
  30.7 22.0 %copy-start.27 = (bf16[2048,512]{1,0:T(8,128)(2,1)S(1)}, bf16[2048,512]{1,0:T(8,128)(2,1)}, u32[]{:S(2)}) copy-start(bf16[2048,512]{1,0:T(8,128)(2,1)} %param.27) | copy-start | bytes 6291460
  35.4 22.1 %copy-start.47 = (s32[4]{0:T(128)S(1)}, s32[4]{0:T(128)}, u32[]{:S(2)}) copy-start(s32[4]{0:T(128)} %param.34) | copy-start | bytes 52
  35.5 62.2 %collective-permute-start.4 = (bf16[512,4,128]{2,0,1:T(8,128)(2,1)}, bf16[512,4,128]{2,0,1:T(8,128)(2,1)}, u32[]{:S(2)}, u32[]{:S(2)}) collective-permute-start(bf16[512,4,128]{2,0,1:T(8,128)(2,1)} %pad_maximum_fusion.1), channel_id=1, source_target_pairs={{0,16},{4,20},{8,24},{12,28},{1,17},{5,21},{9,25},{13,29},{2,18},{... | collective-permute-start | bytes 1572872 | tf_op jit(solution)/shard_map/ppermute | solution.py:23
  42.3 58.0 %collective-permute-start.5 = (bf16[512,4,128]{2,0,1:T(8,128)(2,1)}, bf16[512,4,128]{2,0,1:T(8,128)(2,1)}, u32[]{:S(2)}, u32[]{:S(2)}) collective-permute-start(bf16[512,4,128]{2,0,1:T(8,128)(2,1)} %pad_maximum_fusion.1), channel_id=1, source_target_pairs={{0,12},{4,16},{8,20},{12,24},{16,28},{1,13},{5,17},{9,21},{13,25},... | collective-permute-start | bytes 1572872 | tf_op jit(solution)/shard_map/ppermute | solution.py:23
  47.6 55.5 %collective-permute-start.6 = (bf16[512,4,128]{2,0,1:T(8,128)(2,1)}, bf16[512,4,128]{2,0,1:T(8,128)(2,1)}, u32[]{:S(2)}, u32[]{:S(2)}) collective-permute-start(bf16[512,4,128]{2,0,1:T(8,128)(2,1)} %pad_maximum_fusion.1), channel_id=1, source_target_pairs={{0,8},{4,12},{8,16},{12,20},{16,24},{20,28},{1,9},{5,13},{9,17},{1... | collective-permute-start | bytes 1572872 | tf_op jit(solution)/shard_map/ppermute | solution.py:23
  49.7 56.4 %collective-permute-start.7 = (bf16[512,4,128]{2,0,1:T(8,128)(2,1)}, bf16[512,4,128]{2,0,1:T(8,128)(2,1)}, u32[]{:S(2)}, u32[]{:S(2)}) collective-permute-start(bf16[512,4,128]{2,0,1:T(8,128)(2,1)} %pad_maximum_fusion.1), channel_id=1, source_target_pairs={{0,4},{4,8},{8,12},{12,16},{16,20},{20,24},{24,28},{1,5},{5,9},{9,... | collective-permute-start | bytes 1572872 | tf_op jit(solution)/shard_map/ppermute | solution.py:23
  55.2 52.3 %collective-permute-start = (bf16[512,4,128]{2,0,1:T(8,128)(2,1)}, bf16[512,4,128]{2,0,1:T(8,128)(2,1)}, u32[]{:S(2)}, u32[]{:S(2)}) collective-permute-start(bf16[512,4,128]{2,0,1:T(8,128)(2,1)} %copy.106), channel_id=1, source_target_pairs={{0,16},{4,20},{8,24},{12,28},{1,17},{5,21},{9,25},{13,29},{2,18},{... | collective-permute-start | bytes 1572872 | tf_op jit(solution)/shard_map/ppermute | solution.py:23
  97.7 8.1 copy-start.36
  97.7 8.4 copy-start.35
  97.7 14.1 %collective-permute-start.1 = (bf16[512,4,128]{2,0,1:T(8,128)(2,1)}, bf16[512,4,128]{2,0,1:T(8,128)(2,1)S(1)}, u32[]{:S(2)}, u32[]{:S(2)}) collective-permute-start(bf16[512,4,128]{2,0,1:T(8,128)(2,1)} %copy.106), channel_id=1, source_target_pairs={{0,12},{4,16},{8,20},{12,24},{16,28},{1,13},{5,17},{9,21},{13,25},... | collective-permute-start | bytes 1572872 | tf_op jit(solution)/shard_map/ppermute | solution.py:23
  100.3 7.1 copy-start.34
  100.4 20.9 %collective-permute-start.2 = (bf16[512,4,128]{2,0,1:T(8,128)(2,1)}, bf16[512,4,128]{2,0,1:T(8,128)(2,1)S(1)}, u32[]{:S(2)}, u32[]{:S(2)}) collective-permute-start(bf16[512,4,128]{2,0,1:T(8,128)(2,1)} %copy.106), channel_id=1, source_target_pairs={{0,8},{4,12},{8,16},{12,20},{16,24},{20,28},{1,9},{5,13},{9,17},{1... | collective-permute-start | bytes 1572872 | tf_op jit(solution)/shard_map/ppermute | solution.py:23
  103.1 8.7 copy-start.33
  103.1 18.4 %collective-permute-start.3 = (bf16[512,4,128]{2,0,1:T(8,128)(2,1)}, bf16[512,4,128]{2,0,1:T(8,128)(2,1)S(1)}, u32[]{:S(2)}, u32[]{:S(2)}) collective-permute-start(bf16[512,4,128]{2,0,1:T(8,128)(2,1)} %copy.106), channel_id=1, source_target_pairs={{0,4},{4,8},{8,12},{12,16},{16,20},{20,24},{24,28},{1,5},{5,9},{9,... | collective-permute-start | bytes 1572872 | tf_op jit(solution)/shard_map/ppermute | solution.py:23
  106.0 15.2 %copy-start.32 = (bf16[512,4,128]{2,0,1:T(8,128)(2,1)S(1)}, bf16[512,4,128]{2,0,1:T(8,128)(2,1)}, u32[]{:S(2)}) copy-start(bf16[512,4,128]{2,0,1:T(8,128)(2,1)} %copy.114) | copy-start | bytes 1572868
  106.3 15.2 %copy-start.31 = (bf16[512,4,128]{2,0,1:T(8,128)(2,1)S(1)}, bf16[512,4,128]{2,0,1:T(8,128)(2,1)}, u32[]{:S(2)}) copy-start(bf16[512,4,128]{2,0,1:T(8,128)(2,1)} %copy.117) | copy-start | bytes 1572868
  107.5 15.3 %copy-start.12 = (bf16[2560,4,128]{2,0,1:T(8,128)(2,1)}, bf16[2560,4,128]{2,0,1:T(8,128)(2,1)S(1)}, u32[]{:S(2)}) copy-start(bf16[2560,4,128]{2,0,1:T(8,128)(2,1)S(1)} %constant_dynamic-update-slice_fusion.1) | copy-start | bytes 7864324
  107.7 15.2 %copy-start.14 = (bf16[512,4,64]{2,0,1:T(8,128)(2,1)S(1)}, bf16[512,4,64]{2,0,1:T(8,128)(2,1)}, u32[]{:S(2)}) copy-start(bf16[512,4,64]{2,0,1:T(8,128)(2,1)} %get-tuple-element.80) | copy-start | bytes 786436
  107.7 15.2 %copy-start.16 = (bf16[512,4,64]{2,0,1:T(8,128)(2,1)S(1)}, bf16[512,4,64]{2,0,1:T(8,128)(2,1)}, u32[]{:S(2)}) copy-start(bf16[512,4,64]{2,0,1:T(8,128)(2,1)} %get-tuple-element.81) | copy-start | bytes 786436
  122.8 19.5 %copy-start.11 = (bf16[2560,4,128]{2,0,1:T(8,128)(2,1)}, bf16[2560,4,128]{2,0,1:T(8,128)(2,1)S(1)}, u32[]{:S(2)}) copy-start(bf16[2560,4,128]{2,0,1:T(8,128)(2,1)S(1)} %constant_dynamic-update-slice_fusion) | copy-start | bytes 7864324
  155.8 145.3 %copy-start.42 = (f32[2048]{0:T(1024)S(1)}, f32[2048]{0:T(1024)}, u32[]{:S(2)}) copy-start(f32[2048]{0:T(1024)} %param.24) | copy-start | bytes 24580
  155.8 257.2 %all-reduce.10.cloned.1.call-start = ((), (), s32[]{:S(2)}) async-start(), calls=%async_computation.8 | async-start | bytes 8388608 | tf_op jit(solution)/shard_map/psum | solution.py:202
  301.1 8.7 slice-start
  303.2 6.6 copy-start.29
  303.2 6.6 slice-start.1
  303.2 9.8 slice-start.4
  309.8 8.7 slice-start.2
  313.0 5.5 slice-start.3
  327.2 369.5 %all-reduce.12.cloned.1.call-start = ((), (), s32[]{:S(2)}) async-start(), calls=%async_computation.16 | async-start | bytes 8388608 | tf_op jit(solution)/shard_map/psum | solution.py:188
  413.0 5.9 copy-start.9
  453.6 91.8 %collective-permute-start.12 = (bf16[512,4,128]{0,2,1:T(8,128)(2,1)}, bf16[512,4,128]{0,2,1:T(8,128)(2,1)}, u32[]{:S(2)}, u32[]{:S(2)}) collective-permute-start(bf16[512,4,128]{0,2,1:T(8,128)(2,1)} %get-tuple-element.72), channel_id=1, source_target_pairs={{4,0},{8,4},{12,8},{16,12},{20,16},{24,20},{28,24},{5,1},{9,5},{13... | collective-permute-start | bytes 1572872 | tf_op jit(solution)/shard_map/ppermute | solution.py:23
  454.9 14.6 %copy-start.15 = (bf16[512,4,64]{2,0,1:T(8,128)(2,1)S(1)}, bf16[512,4,64]{2,0,1:T(8,128)(2,1)}, u32[]{:S(2)}) copy-start(bf16[512,4,64]{2,0,1:T(8,128)(2,1)} %get-tuple-element.80) | copy-start | bytes 786436
  454.9 14.6 %copy-start.17 = (bf16[512,4,64]{2,0,1:T(8,128)(2,1)S(1)}, bf16[512,4,64]{2,0,1:T(8,128)(2,1)}, u32[]{:S(2)}) copy-start(bf16[512,4,64]{2,0,1:T(8,128)(2,1)} %get-tuple-element.81) | copy-start | bytes 786436
  476.2 7.0 copy-start.13
  478.0 18.9 %collective-permute-start.10 = (bf16[512,4,128]{2,0,1:T(8,128)(2,1)S(1)}, bf16[512,4,128]{2,0,1:T(8,128)(2,1)S(1)}, u32[]{:S(2)}, u32[]{:S(2)}) collective-permute-start(bf16[512,4,128]{2,0,1:T(8,128)(2,1)S(1)} %get-tuple-element.78), channel_id=1, source_target_pairs={{12,0},{16,4},{20,8},{24,12},{28,16},{13,1},{17,5},{21,9},{25,13},... | collective-permute-start | bytes 1572872 | tf_op jit(solution)/shard_map/ppermute | solution.py:23
  479.3 51.6 %collective-permute-start.11 = (bf16[512,4,128]{2,0,1:T(8,128)(2,1)S(1)}, bf16[512,4,128]{2,0,1:T(8,128)(2,1)S(1)}, u32[]{:S(2)}, u32[]{:S(2)}) collective-permute-start(bf16[512,4,128]{2,0,1:T(8,128)(2,1)S(1)} %get-tuple-element.77), channel_id=1, source_target_pairs={{16,0},{20,4},{24,8},{28,12},{17,1},{21,5},{25,9},{29,13},{18,2},{... | collective-permute-start | bytes 1572872 | tf_op jit(solution)/shard_map/ppermute | solution.py:23
  480.6 51.6 %collective-permute-start.8 = (bf16[512,4,128]{2,0,1:T(8,128)(2,1)S(1)}, bf16[512,4,128]{2,0,1:T(8,128)(2,1)S(1)}, u32[]{:S(2)}, u32[]{:S(2)}) collective-permute-start(bf16[512,4,128]{2,0,1:T(8,128)(2,1)S(1)} %get-tuple-element.76), channel_id=1, source_target_pairs={{4,0},{8,4},{12,8},{16,12},{20,16},{24,20},{28,24},{5,1},{9,5},{13... | collective-permute-start | bytes 1572872 | tf_op jit(solution)/shard_map/ppermute | solution.py:23
  481.9 51.9 %collective-permute-start.9 = (bf16[512,4,128]{2,0,1:T(8,128)(2,1)S(1)}, bf16[512,4,128]{2,0,1:T(8,128)(2,1)S(1)}, u32[]{:S(2)}, u32[]{:S(2)}) collective-permute-start(bf16[512,4,128]{2,0,1:T(8,128)(2,1)S(1)} %get-tuple-element.79), channel_id=1, source_target_pairs={{8,0},{12,4},{16,8},{20,12},{24,16},{28,20},{9,1},{13,5},{17,9},{2... | collective-permute-start | bytes 1572872 | tf_op jit(solution)/shard_map/ppermute | solution.py:23
  486.1 49.2 %copy-start.24 = (f32[512,64]{1,0:T(8,128)S(1)}, f32[512,64]{1,0:T(8,128)}, u32[]{:S(2)}) copy-start(f32[512,64]{1,0:T(8,128)} %copy-done.23) | copy-start | bytes 393220
  486.1 49.2 %copy-start.26 = (f32[512,64]{1,0:T(8,128)S(1)}, f32[512,64]{1,0:T(8,128)}, u32[]{:S(2)}) copy-start(f32[512,64]{1,0:T(8,128)} %copy-done.25) | copy-start | bytes 393220
  496.9 48.4 %collective-permute-start.13 = (bf16[512,4,128]{0,2,1:T(8,128)(2,1)}, bf16[512,4,128]{0,2,1:T(8,128)(2,1)}, u32[]{:S(2)}, u32[]{:S(2)}) collective-permute-start(bf16[512,4,128]{0,2,1:T(8,128)(2,1)} %get-tuple-element.75), channel_id=1, source_target_pairs={{8,0},{12,4},{16,8},{20,12},{24,16},{28,20},{9,1},{13,5},{17,9},{2... | collective-permute-start | bytes 1572872 | tf_op jit(solution)/shard_map/ppermute | solution.py:23
  530.9 14.9 %collective-permute-start.14 = (bf16[512,4,128]{0,2,1:T(8,128)(2,1)}, bf16[512,4,128]{0,2,1:T(8,128)(2,1)}, u32[]{:S(2)}, u32[]{:S(2)}) collective-permute-start(bf16[512,4,128]{0,2,1:T(8,128)(2,1)} %get-tuple-element.74), channel_id=1, source_target_pairs={{12,0},{16,4},{20,8},{24,12},{28,16},{13,1},{17,5},{21,9},{25,13},... | collective-permute-start | bytes 1572872 | tf_op jit(solution)/shard_map/ppermute | solution.py:23
  532.2 76.4 %collective-permute-start.15 = (bf16[512,4,128]{0,2,1:T(8,128)(2,1)}, bf16[512,4,128]{0,2,1:T(8,128)(2,1)}, u32[]{:S(2)}, u32[]{:S(2)}) collective-permute-start(bf16[512,4,128]{0,2,1:T(8,128)(2,1)} %get-tuple-element.73), channel_id=1, source_target_pairs={{16,0},{20,4},{24,8},{28,12},{17,1},{21,5},{25,9},{29,13},{18,2},{... | collective-permute-start | bytes 1572872 | tf_op jit(solution)/shard_map/ppermute | solution.py:23
  537.3 5.1 copy-start.21
  537.4 5.1 copy-start.38
  544.0 67.6 %copy-start.8 = (f32[512,2048]{1,0:T(8,128)S(1)}, f32[512,2048]{1,0:T(8,128)}, u32[]{:S(2)}) copy-start(f32[512,2048]{1,0:T(8,128)} %fusion.73) | copy-start | bytes 12582916
  545.3 66.3 %copy-start.28 = (bf16[2048,512]{1,0:T(8,128)(2,1)S(1)}, bf16[2048,512]{1,0:T(8,128)(2,1)}, u32[]{:S(2)}) copy-start(bf16[2048,512]{1,0:T(8,128)(2,1)} %param.27) | copy-start | bytes 6291460
  614.3 6.7 copy-start.7
  614.3 6.7 copy-start.44
  614.3 6.7 copy-start.46
  614.3 154.4 %reduce-scatter.14.cloned.1.call-start = ((), (), s32[]{:S(2)}) async-start(), calls=%async_computation.12 | async-start | bytes 2359296 | tf_op jit(solution)/shard_map/reduce_scatter | solution.py:292
  621.0 218.2 %reduce-scatter.12.cloned.1.call-start = ((), (), s32[]{:S(2)}) async-start(), calls=%async_computation.11 | async-start | bytes 2359296 | tf_op jit(solution)/shard_map/reduce_scatter | solution.py:289
  625.0 284.6 %reduce-scatter.10.cloned.1.call-start = ((), (), s32[]{:S(2)}) async-start(), calls=%async_computation.10 | async-start | bytes 2359296 | tf_op jit(solution)/shard_map/reduce_scatter | solution.py:286
  628.0 352.2 %reduce-scatter.8.cloned.1.call-start = ((), (), s32[]{:S(2)}) async-start(), calls=%async_computation.9 | async-start | bytes 2359296 | tf_op jit(solution)/shard_map/reduce_scatter | solution.py:283
  631.1 460.8 %reduce-scatter.16.cloned.1.call-start = ((), (), s32[]{:S(2)}) async-start(), calls=%async_computation.13 | async-start | bytes 6340608 | tf_op jit(solution)/shard_map/reduce_scatter | solution.py:298
  638.8 565.5 %reduce-scatter.18.cloned.1.call-start = ((), (), s32[]{:S(2)}) async-start(), calls=%async_computation.14 | async-start | bytes 6340608 | tf_op jit(solution)/shard_map/reduce_scatter | solution.py:301
  646.6 669.9 %reduce-scatter.20.cloned.1.call-start = ((), (), s32[]{:S(2)}) async-start(), calls=%async_computation.15 | async-start | bytes 6340608 | tf_op jit(solution)/shard_map/reduce_scatter | solution.py:304
  722.6 5.1 copy-start.5
  722.6 5.1 copy-start.10
  980.2 338.6 %copy-start.1 = (bf16[2048,512]{1,0:T(8,128)(2,1)S(1)}, bf16[2048,512]{1,0:T(8,128)(2,1)}, u32[]{:S(2)}) copy-start(bf16[2048,512]{1,0:T(8,128)(2,1)} %param.28) | copy-start | bytes 6291460
  (19 other events, 47.1 us)
Sparse Core Ops, SparseCore 0:
  155.9 141.5 all-reduce.7
  327.3 85.6 all-reduce.9
  614.4 82.2 all-reduce.11
  700.5 68.1 reduce-scatter.13
  772.5 66.5 reduce-scatter.11
  843.0 66.5 reduce-scatter.9
  913.5 66.5 reduce-scatter.7
  984.3 107.6 reduce-scatter.15
  1096.0 108.2 reduce-scatter.17
  1208.3 108.2 reduce-scatter.19
where the time goes:
time: 1340 us; the launch traced here: 1330 us
  waiting for transfers between devices  954 us (71%)
  matrix products  146 us (11%)
  other arithmetic  84 us (6%)
  local copies, waits for them, and re-layouts  66.9 us (5%)
  starting transfers between devices  37.1 us (3%)
  blocking collectives  21.7 us (2%)
  between operations  16.4 us (1%)
    psum x1, waiting for transfers between devices, on_device(): branch_attn = lax.psum(times_transpose(attended, w_out), 'head')  141 us
    ppermute x16, waiting for transfers between devices, passed_along(): return lax.ppermute(block, axis, route)  120 us
    reduce_scatter x1, waiting for transfers between devices, on_device(): lax.psum_scatter(mlp_sums[1].astype(jnp.bfloat16), 'seq', scatter_dimensi...  110 us
    reduce_scatter x1, waiting for transfers between devices, on_device(): lax.psum_scatter(mlp_sums[2].astype(jnp.bfloat16), 'seq', scatter_dimensi...  110 us
    reduce_scatter x1, waiting for transfers between devices, on_device(): lax.psum_scatter(mlp_sums[0].astype(jnp.bfloat16), 'seq', scatter_dimensi...  110 us
    psum x1, waiting for transfers between devices, on_device(): lax.psum(times_transpose(grad_gate, w_gate) + times_transpose(grad_up, w_...  77.4 us
    reduce_scatter x1, waiting for transfers between devices, on_device(): lax.psum_scatter(w_query_grad.astype(jnp.bfloat16), 'seq', scatter_dimens...  68.8 us
    reduce_scatter x1, waiting for transfers between devices, on_device(): lax.psum_scatter(w_key_grad.astype(jnp.bfloat16), 'seq', scatter_dimensio...  68.6 us
  transfers between devices with their start and end apart: 26, of which 16 were waited for; matrix products, arithmetic and copies ran while one was open for 11% of the time, Pallas kernels for 0%

commit v1 on v0

v1 whole, which is shorter than its diff:
```python
import functools
import math

import jax
import jax.numpy as jnp
from jax import lax
from jax.experimental import pallas as pl
from jax.experimental.pallas import tpu as pltpu
from jax.sharding import PartitionSpec as P

HEAD_DIM = 128
WINDOW = 2048
PAD = 64
NSEQ = 4
EPS = 1e-06
MASKED = -1e30
LOG2E = 1.4426950408889634
BIG = 1 << 28
F32 = jnp.float32
BF16 = jnp.bfloat16


def swap(block, axis, bit):
    return lax.ppermute(block, axis, [(i, i ^ bit) for i in range(lax.axis_size(axis))])


def shifted(block, distance):
    n = lax.axis_size("seq")
    return lax.ppermute(
        block, "seq", [(i, i + distance) for i in range(n) if 0 <= i + distance < n]
    )


def head_sum(partial):
    core = lax.axis_index("head") & 1
    rows, width = partial.shape
    halves = partial.reshape(rows, 2, width // 2)
    low, high = halves[:, 0], halves[:, 1]
    keep = jnp.where(core == 0, low, high)
    give = jnp.where(core == 0, high, low).astype(BF16)
    chip = (keep + swap(give, "head", 1).astype(F32)).astype(BF16)
    total = (chip.astype(F32) + swap(chip, "head", 2).astype(F32)).astype(BF16)
    other = swap(total, "head", 1)
    return jnp.concatenate(
        [jnp.where(core == 0, total, other), jnp.where(core == 0, other, total)], axis=1
    ).astype(F32)


def pair_rows(left):
    n = lax.axis_size("seq")
    bit = lax.axis_index("seq") & 1
    rows, width = left.shape
    parts = left.reshape(rows, n // 2, 2, width // n)
    keep = lax.dynamic_index_in_dim(parts, bit, 2, keepdims=False).reshape(rows, width // 2)
    give = lax.dynamic_index_in_dim(parts, 1 - bit, 2, keepdims=False).reshape(rows, width // 2)
    return jnp.concatenate([keep, swap(give, "seq", 1)], axis=0)


def pair_tokens(right):
    return jnp.concatenate([right, swap(right, "seq", 1)], axis=0)


def scatter_sum(grad):
    n = lax.axis_size("seq")
    index = lax.axis_index("seq")
    rows, cols = grad.shape
    shares = n // 2
    part = grad
    bit = 2
    while bit < n:
        shares //= 2
        mine = (index // bit) & 1
        view = part.reshape(shares, 2, rows // (n // 2), cols)
        keep = lax.dynamic_index_in_dim(view, mine, 1, keepdims=False)
        give = lax.dynamic_index_in_dim(view, 1 - mine, 1, keepdims=False)
        total = keep.astype(F32) + swap(give, "seq", bit).astype(F32)
        bit *= 2
        part = total.astype(BF16) if bit < n else total
    return part.reshape(rows // (n // 2), cols).astype(F32)


def gain_sum(part):
    n = lax.axis_size("seq")
    total = part
    bit = 1
    while bit < n:
        total = total + swap(total, "seq", bit)
        bit *= 2
    width = part.shape[0] // n
    return lax.dynamic_slice_in_dim(total, lax.axis_index("seq") * width, width, 0)


def fwd_kernel(lo_ref, valid_ref, q_ref, *refs):
    rows = q_ref.shape[0]
    n_parts = (len(refs) - 3) // 2
    k_refs, v_refs = refs[:n_parts], refs[n_parts : 2 * n_parts]
    out_ref, lse_ref, s_ref = refs[2 * n_parts :]
    sub = s_ref.shape[0]
    scale = HEAD_DIM ** (-0.5) * LOG2E
    for start in range(0, rows, sub):
        q = q_ref[start : start + sub, :]
        lo = lo_ref[start : start + sub, :]
        top = None
        for d in range(n_parts):
            s = lax.dot_general(
                q, k_refs[d][...], (((1,), (1,)), ((), ())), preferred_element_type=F32
            )
            u = lax.broadcasted_iota(jnp.int32, s.shape, 1) - d * rows
            seen = u >= lo
            if d == 0:
                t = lax.broadcasted_iota(jnp.int32, s.shape, 0) + start
                seen = seen & (u <= t)
            s = jnp.where(seen, s * scale, MASKED)
            s_ref[:, d * rows : (d + 1) * rows] = s
            part_top = jnp.max(s, axis=1, keepdims=True)
            top = part_top if top is None else jnp.maximum(top, part_top)
        total = jnp.zeros_like(top)
        acc = jnp.zeros((sub, HEAD_DIM), F32)
        for d in range(n_parts):
            p = jnp.exp2(s_ref[:, d * rows : (d + 1) * rows] - top)
            total = total + jnp.sum(p, axis=1, keepdims=True)
            acc = acc + jnp.dot(p.astype(BF16), v_refs[d][...], preferred_element_type=F32)
        out = jnp.where(valid_ref[start : start + sub, :] > 0, acc / total, 0.0)
        out_ref[start : start + sub, :] = out.astype(BF16)
        lse_ref[0, start : start + sub, :] = top + jnp.log2(total)


def attention_fwd(lo, valid, queries, keys, values):
    rows, width = queries.shape
    heads = width // HEAD_DIM
    n_parts = len(keys)
    column = pl.BlockSpec((rows, HEAD_DIM), lambda h: (0, h))
    whole = pl.BlockSpec((rows, 1), lambda h: (0, 0))
    flops = 4 * rows * rows * n_parts * width
    return pl.pallas_call(
        fwd_kernel,
        grid=(heads,),
        in_specs=[whole, whole] + [column] * (1 + 2 * n_parts),
        out_specs=[column, pl.BlockSpec((1, rows, 1), lambda h: (h, 0, 0))],
        out_shape=[
            jax.ShapeDtypeStruct((rows, width), BF16),
            jax.ShapeDtypeStruct((heads, rows, 1), F32),
        ],
        scratch_shapes=[pltpu.VMEM((rows // 2, n_parts * rows), F32)],
        compiler_params=pltpu.CompilerParams(vmem_limit_bytes=48 << 20),
        cost_estimate=pl.CostEstimate(
            flops=flops, bytes_accessed=12 * rows * width * 2, transcendentals=flops // 512
        ),
        name="attention_fwd",
    )(lo, valid, queries, *keys, *values)


def dq_kernel(lo_ref, q_ref, do_ref, lse_ref, delta_ref, *refs):
    rows = q_ref.shape[0]
    n_parts = (len(refs) - 1) // 2
    k_refs, v_refs = refs[:n_parts], refs[n_parts : 2 * n_parts]
    out_ref = refs[-1]
    scale = HEAD_DIM ** (-0.5) * LOG2E
    sub = rows // 2
    for start in range(0, rows, sub):
        rs = slice(start, start + sub)
        q, do, lo = q_ref[rs, :], do_ref[rs, :], lo_ref[rs, :]
        lse, delta = lse_ref[0, rs, :], delta_ref[0, rs, :]
        acc = jnp.zeros((sub, HEAD_DIM), F32)
        for d in range(n_parts):
            k = k_refs[d][...]
            s = lax.dot_general(q, k, (((1,), (1,)), ((), ())), preferred_element_type=F32)
            u = lax.broadcasted_iota(jnp.int32, s.shape, 1) - d * rows
            seen = u >= lo
            if d == 0:
                t = lax.broadcasted_iota(jnp.int32, s.shape, 0) + start
                seen = seen & (u <= t)
            p = jnp.exp2(jnp.where(seen, s * scale, MASKED) - lse)
            dp = lax.dot_general(
                do, v_refs[d][...], (((1,), (1,)), ((), ())), preferred_element_type=F32
            )
            ds = (p * (dp - delta)).astype(BF16)
            acc = acc + jnp.dot(ds, k, preferred_element_type=F32)
        out_ref[rs, :] = acc * HEAD_DIM ** (-0.5)


def attention_dq(lo, queries, grad_att, lse, delta, keys, values):
    rows, width = queries.shape
    heads = width // HEAD_DIM
    n_parts = len(keys)
    column = pl.BlockSpec((rows, HEAD_DIM), lambda h: (0, h))
    stat = pl.BlockSpec((1, rows, 1), lambda h: (h, 0, 0))
    flops = 6 * rows * rows * n_parts * width
    return pl.pallas_call(
        dq_kernel,
        grid=(heads,),
        in_specs=[pl.BlockSpec((rows, 1), lambda h: (0, 0)), column, column, stat, stat]
        + [column] * (2 * n_parts),
        out_specs=column,
        out_shape=jax.ShapeDtypeStruct((rows, width), F32),
        compiler_params=pltpu.CompilerParams(vmem_limit_bytes=48 << 20),
        cost_estimate=pl.CostEstimate(
            flops=flops, bytes_accessed=14 * rows * width * 2, transcendentals=flops // 768
        ),
        name="attention_dq",
    )(lo, queries, grad_att, lse, delta, *keys, *values)


def dkv_kernel(lo_ref, k_ref, v_ref, *refs):
    rows = k_ref.shape[0]
    n_parts = (len(refs) - 2) // 3
    q_refs, do_refs, st_refs = (
        refs[:n_parts],
        refs[n_parts : 2 * n_parts],
        refs[2 * n_parts : 3 * n_parts],
    )
    dk_ref, dv_ref = refs[-2:]
    scale = HEAD_DIM ** (-0.5) * LOG2E
    sub = rows // 2
    for start in range(0, rows, sub):
        rs = slice(start, start + sub)
        k, v = k_ref[rs, :], v_ref[rs, :]
        dk = jnp.zeros((sub, HEAD_DIM), F32)
        dv = jnp.zeros((sub, HEAD_DIM), F32)
        for d in range(n_parts):
            q, do = q_refs[d][...], do_refs[d][...]
            s = lax.dot_general(k, q, (((1,), (1,)), ((), ())), preferred_element_type=F32)
            u = lax.broadcasted_iota(jnp.int32, s.shape, 0) + start
            seen = u >= lo_ref[:, d * rows : (d + 1) * rows]
            if d == 0:
                seen = seen & (u <= lax.broadcasted_iota(jnp.int32, s.shape, 1))
            lse, delta = st_refs[d][0, 0:1, :], st_refs[d][0, 1:2, :]
            p = jnp.exp2(jnp.where(seen, s * scale - lse, MASKED))
            dv = dv + jnp.dot(p.astype(BF16), do, preferred_element_type=F32)
            dp = lax.dot_general(v, do, (((1,), (1,)), ((), ())), preferred_element_type=F32)
            ds = (p * (dp - delta)).astype(BF16)
            dk = dk + jnp.dot(ds, q, preferred_element_type=F32)
        dk_ref[rs, :] = dk * HEAD_DIM ** (-0.5)
        dv_ref[rs, :] = dv


def attention_dkv(lo_row, keys, values, queries, grad_atts, stats):
    rows, width = keys.shape
    heads = width // HEAD_DIM
    n_parts = len(queries)
    column = pl.BlockSpec((rows, HEAD_DIM), lambda h: (0, h))
    stat = pl.BlockSpec((1, 2, rows), lambda h: (h, 0, 0))
    flops = 8 * rows * rows * n_parts * width
    return pl.pallas_call(
        dkv_kernel,
        grid=(heads,),
        in_specs=[pl.BlockSpec((1, n_parts * rows), lambda h: (0, 0)), column, column]
        + [column] * (2 * n_parts)
        + [stat] * n_parts,
        out_specs=[column, column],
        out_shape=[jax.ShapeDtypeStruct((rows, width), F32)] * 2,
        compiler_params=pltpu.CompilerParams(vmem_limit_bytes=48 << 20),
        cost_estimate=pl.CostEstimate(
            flops=flops, bytes_accessed=16 * rows * width * 2, transcendentals=flops // 1024
        ),
        name="attention_dkv",
    )(lo_row, keys, values, *queries, *grad_atts, *stats)


def first_key(rows, lengths, total):
    padded = (lengths + PAD - 1) // PAD * PAD
    starts = jnp.cumsum(padded) - padded
    start_row = jnp.zeros_like(rows)
    length_row = jnp.full_like(rows, 0) + lengths[0]
    low_row = jnp.full_like(rows, -BIG)
    for r in range(1, NSEQ):
        inside = rows >= starts[r]
        start_row = jnp.where(inside, starts[r], start_row)
        low_row = jnp.where(inside, starts[r], low_row)
        length_row = jnp.where(inside, lengths[r], length_row)
    position = rows - start_row
    valid = position < length_row
    low = jnp.where(valid, jnp.maximum(low_row, rows - (WINDOW - 1)), rows)
    low = jnp.where(rows < total, low, BIG)
    return low, valid, position


def outer_sum(left, right):
    return lax.dot_general(left, right, (((0,), (0,)), ((), ())), preferred_element_type=F32)


def times_transpose(left, right):
    return lax.dot_general(left, right, (((1,), (1,)), ((), ())), preferred_element_type=F32)


def turned(values):
    half = HEAD_DIM // 2
    out = []
    for start in range(0, values.shape[1], HEAD_DIM):
        out += [values[:, start + half : start + HEAD_DIM], values[:, start : start + half]]
    return jnp.concatenate(out, axis=1)


def norm_back(grad_normed, inputs, scale_rows, gain):
    unit = inputs * scale_rows
    grad_unit = grad_normed * gain
    gain_part = jnp.sum(grad_normed * unit, axis=0)
    grad_inputs = scale_rows * (
        grad_unit - unit * jnp.mean(grad_unit * unit, axis=-1, keepdims=True)
    )
    return (grad_inputs, gain_part)


def on_device(
    tokens,
    gain_attn,
    gain_mlp,
    w_query,
    w_key,
    w_value,
    w_out,
    w_gate,
    w_up,
    w_down,
    prev_keys,
    prev_values,
    lengths,
    out_grad,
):
    rows = tokens.shape[0]
    width = w_query.shape[1]
    heads = width // HEAD_DIM
    devices = lax.axis_size("seq")
    index = lax.axis_index("seq")
    odd = (index & 1) == 1
    first_row = index * rows
    far = WINDOW // rows
    low, valid, position = first_key(
        first_row + jnp.arange((far + 1) * rows, dtype=jnp.int32), lengths, devices * rows
    )
    low = low - first_row
    low_col = low[:rows, None]
    low_row = low[None, :]
    valid_col = valid[:rows, None]
    valid_int = valid_col.astype(jnp.int32)
    half = HEAD_DIM // 2
    freq = jnp.exp(-math.log(10000.0) * (2.0 * jnp.arange(half, dtype=F32) / HEAD_DIM))
    angle = position[:rows].astype(F32)[:, None] * freq[None, :]
    cos_one, sin_one = jnp.cos(angle), jnp.sin(angle)
    cosine = jnp.tile(jnp.concatenate([cos_one, cos_one], axis=1), (1, heads))
    sine = jnp.tile(jnp.concatenate([-sin_one, sin_one], axis=1), (1, heads))

    inputs = tokens.astype(F32)
    scale_one = lax.rsqrt(jnp.mean(inputs * inputs, axis=-1, keepdims=True) + EPS)
    normed_one = (inputs * scale_one * gain_attn).astype(BF16)
    key_raw = jnp.dot(normed_one, w_key, preferred_element_type=F32)
    keys_own = (key_raw * cosine + turned(key_raw) * sine).astype(BF16)
    values_own = jnp.dot(normed_one, w_value, preferred_element_type=F32).astype(BF16)

    def borrowed(own, prev):
        def cached(distance):
            at = jnp.clip((index - distance) * rows + WINDOW, 0, WINDOW - rows)
            return lax.dynamic_slice_in_dim(prev, at, rows, 0)

        two = jnp.where(index >= 2, shifted(own, 2), cached(2))
        one = swap(jnp.where(odd, two, own), "seq", 1)
        four = jnp.where(index >= 2, shifted(two, 2), cached(4))
        three = swap(jnp.where(odd, four, two), "seq", 1)
        return [own, one, two, three, four]

    def lent(own):
        two = shifted(own, -2)
        one = swap(jnp.where(odd, own, two), "seq", 1)
        four = shifted(two, -2)
        three = swap(jnp.where(odd, two, four), "seq", 1)
        return [own, one, two, three, four]

    keys = borrowed(keys_own, prev_keys)
    values = borrowed(values_own, prev_values)
    query_raw = jnp.dot(normed_one, w_query, preferred_element_type=F32)
    queries = (query_raw * cosine + turned(query_raw) * sine).astype(BF16)
    queries_lent = lent(queries)
    grad_branch = out_grad
    grad_act = jnp.dot(grad_branch, w_down, preferred_element_type=F32)

    attended, lse = attention_fwd(low_col, valid_int, queries, keys, values)
    mid = inputs + head_sum(times_transpose(attended, w_out))
    scale_two = lax.rsqrt(jnp.mean(mid * mid, axis=-1, keepdims=True) + EPS)
    normed_two = (mid * scale_two * gain_mlp).astype(BF16)
    gate = jnp.dot(normed_two, w_gate, preferred_element_type=F32)
    up_proj = jnp.dot(normed_two, w_up, preferred_element_type=F32)
    sigmoid_gate = jax.nn.sigmoid(gate)
    silu_gate = gate * sigmoid_gate
    act = (silu_gate * up_proj).astype(BF16)
    grad_gate = (grad_act * up_proj * sigmoid_gate * (1.0 + gate * (1.0 - sigmoid_gate))).astype(
        BF16
    )
    grad_up = (grad_act * silu_gate).astype(BF16)

    grad_norm_two = head_sum(times_transpose(grad_gate, w_gate) + times_transpose(grad_up, w_up))

    w_down_grad = scatter_sum(outer_sum(pair_rows(grad_branch), pair_tokens(act)).astype(BF16))
    normed_two_pair = pair_rows(normed_two)
    w_gate_grad = scatter_sum(outer_sum(normed_two_pair, pair_tokens(grad_gate)).astype(BF16))
    w_up_grad = scatter_sum(outer_sum(normed_two_pair, pair_tokens(grad_up)).astype(BF16))

    block_out = (mid + head_sum(times_transpose(act, w_down))).astype(BF16)

    grad_out = out_grad.astype(F32)
    grad_mid_norm, gain_mlp_part = norm_back(grad_norm_two, mid, scale_two, gain_mlp)
    grad_mid = grad_out + grad_mid_norm
    gain_mlp_grad = gain_sum(gain_mlp_part)
    grad_attn_branch = grad_mid.astype(BF16)
    grad_att = jnp.dot(grad_attn_branch, w_out, preferred_element_type=F32).astype(BF16)
    grad_att = jnp.where(valid_col, grad_att, jnp.zeros_like(grad_att))
    grad_atts = lent(grad_att)
    delta = jnp.sum(
        (grad_att.astype(F32) * attended.astype(F32)).reshape(rows, heads, HEAD_DIM), axis=-1
    )
    stats = lent(jnp.stack([lse[:, :, 0], delta.T], axis=1))
    grad_queries = attention_dq(
        low_col, queries, grad_att, lse, delta.T[:, :, None], keys, values
    )
    grad_keys, grad_values = attention_dkv(
        low_row, keys_own, values_own, queries_lent, grad_atts, stats
    )
    grad_query_raw = (grad_queries * cosine - turned(grad_queries) * sine).astype(BF16)
    grad_key_raw = (grad_keys * cosine - turned(grad_keys) * sine).astype(BF16)
    grad_value_raw = grad_values.astype(BF16)

    w_out_grad = scatter_sum(
        outer_sum(pair_rows(grad_attn_branch), pair_tokens(attended)).astype(BF16)
    )
    normed_one_pair = pair_rows(normed_one)
    w_query_grad = scatter_sum(outer_sum(normed_one_pair, pair_tokens(grad_query_raw)).astype(BF16))
    w_key_grad = scatter_sum(outer_sum(normed_one_pair, pair_tokens(grad_key_raw)).astype(BF16))
    w_value_grad = scatter_sum(outer_sum(normed_one_pair, pair_tokens(grad_value_raw)).astype(BF16))
    grad_norm_one = head_sum(
        times_transpose(grad_query_raw, w_query)
        + times_transpose(grad_key_raw, w_key)
        + times_transpose(grad_value_raw, w_value)
    )
    grad_in_norm, gain_attn_part = norm_back(grad_norm_one, inputs, scale_one, gain_attn)
    tokens_grad = (grad_mid + grad_in_norm).astype(BF16)
    gain_attn_grad = gain_sum(gain_attn_part)
    return (
        block_out,
        tokens_grad,
        gain_attn_grad,
        gain_mlp_grad,
        w_query_grad,
        w_key_grad,
        w_value_grad,
        w_out_grad,
        w_gate_grad,
        w_up_grad,
        w_down_grad,
    )


def solution(mesh):
    by_head = P(None, "head")
    both = P("seq", "head")
    placed = (P("seq", None), P(), P()) + (by_head,) * 9 + (P(), P("seq", None))
    return jax.shard_map(
        on_device,
        mesh=mesh,
        in_specs=placed,
        out_specs=(P("seq", None), P("seq", None), P("seq"), P("seq")) + (both,) * 7,
        check_vma=False,
    )
```

time: 1340 us -> 711 us (0.53)
  waiting for transfers between devices: 954 us -> 226 us
  starting transfers between devices: 37.1 us -> 114 us
  matrix products: 146 us -> 74.3 us
  local copies, waits for them, and re-layouts: 66.9 us -> 128 us
  Pallas kernels: 0 us -> 45.5 us
  other arithmetic: 84 us -> 111 us
  blocking collectives: 21.7 us -> 0 us
  between operations: 16.4 us -> 2.56 us
    reduce_scatter x7 -> x0, waiting for transfers between devices: 574 us -> none  [the longest x1 110 us: on_device(): lax.psum_scatter(mlp_sums[1].astype(jnp.bfloat16), 'seq', scatter_dimensi...]
    psum x3 -> x0, waiting for transfers between devices: 259 us -> none  [the longest x1 141 us: on_device(): branch_attn = lax.psum(times_transpose(attended, w_out), 'head')]
    ppermute x16 -> x63, waiting for transfers between devices: 120 us -> 226 us  [the longest x53 208 us: swap(): lax.ppermute(block, axis, [(i, i ^ bit) for i in range(lax.axis_size(axis...]
    ppermute x16 -> x63, starting transfers between devices: 35.7 us -> 114 us  [the longest x53 85.3 us: swap(): lax.ppermute(block, axis, [(i, i ^ bit) for i in range(lax.axis_size(axis...]
    dot_general x13 -> x7, matrix products: 81.7 us -> 20.7 us  [the longest x1 5.42 us: on_device(): gate = jnp.dot(normed_two, w_gate, preferred_element_type=F32)]
    pallas_call x0 -> x3, Pallas kernels: none -> 45.5 us  [the longest x1 19.8 us: attention_dkv(): pl.pallas_call(dkv_kernel, grid=(heads,), in_specs=[pl.BlockSpec((1, n_pa...]
    dynamic_slice x1 -> x10, local copies, waits for them, and re-layouts: 4.62 us -> 37.8 us  [the longest x3 25.3 us: scatter_sum(): keep = lax.dynamic_index_in_dim(view, mine, 1, keepdims=False)]
    unnamed x1 -> x0, blocking collectives: 21.7 us -> none
  transfers between devices with their start and end apart: 26 -> 63, of which waited for: 16 -> 24; matrix products, arithmetic and copies ran while one was open for 11% -> 39% of each run, Pallas kernels for 0% -> 5%
where the time goes in v1:
time: 711 us; the launch traced here: 702 us
  waiting for transfers between devices  226 us (32%)
  local copies, waits for them, and re-layouts  128 us (18%)
  starting transfers between devices  114 us (16%)
  other arithmetic  111 us (16%)
  matrix products  74.3 us (10%)
  Pallas kernels  45.5 us (6%)
    ppermute x53, waiting for transfers between devices, swap(): lax.ppermute(block, axis, [(i, i ^ bit) for i in range(lax.axis_size(axis...  208 us
    ppermute x53, starting transfers between devices, swap(): lax.ppermute(block, axis, [(i, i ^ bit) for i in range(lax.axis_size(axis...  85.3 us
    dot_general x7, matrix products, outer_sum(): lax.dot_general(left, right, (((0,), (0,)), ((), ())), preferred_element_...  29.9 us
    ppermute x10, starting transfers between devices, shifted(): lax.ppermute(block, 'seq', [(i, i + distance) for i in range(n) if 0 <= i...  28.6 us
    unnamed x186, local copies, waits for them, and re-layouts  27.4 us
    dynamic_slice x3, local copies, waits for them, and re-layouts, scatter_sum(): keep = lax.dynamic_index_in_dim(view, mine, 1, keepdims=False)  25.3 us
    reshape x3, local copies, waits for them, and re-layouts, scatter_sum(): view = part.reshape(shares, 2, rows // (n // 2), cols)  23.1 us
    pallas_call x1, Pallas kernels, attention_dkv(): pl.pallas_call(dkv_kernel, grid=(heads,), in_specs=[pl.BlockSpec((1, n_pa...  19.8 us
  transfers between devices with their start and end apart: 63, of which 24 were waited for; matrix products, arithmetic and copies ran while one was open for 39% of the time, Pallas kernels for 5%

profile of v1, /device:TPU:0, one launch (start us, length us, event | category | flops | bytes accessed | tf_op | source)
XLA Modules:
  0.0 702.4 jit_solution(7617614779348834445)
XLA Ops:
  0.7 4.1 copy.152
  30.2 5.7 collective-permute-start
  38.0 3.5 collective-permute-start.4
  41.6 5.9 collective-permute-done
  49.8 5.4 collective-permute-start.2
  55.2 3.6 collective-permute-done.4
  61.3 5.8 collective-permute-start.6
  67.6 4.3 select_compare_fusion
  87.9 11.2 %collective-permute-done.5.refs_6_ = bf16[512,512]{1,0:T(8,128)(2,1)} collective-permute-done((bf16[512,512]{1,0:T(8,128)(2,1)}, bf16[512,512]{1,0:T(8,128)(2,1)}, u32[]{:S(2)}, u32[]{:S(2)}) %collective-permute-start.5) | collective-permute-done | bytes 524320 | tf_op jit(solution)/shard_map/ppermute | solution.py:24
  99.2 11.2 %collective-permute-done.3.refs_3_ = bf16[512,512]{1,0:T(8,128)(2,1)} collective-permute-done((bf16[512,512]{1,0:T(8,128)(2,1)}, bf16[512,512]{1,0:T(8,128)(2,1)}, u32[]{:S(2)}, u32[]{:S(2)}) %collective-permute-start.3) | collective-permute-done | bytes 524320 | tf_op jit(solution)/shard_map/ppermute | solution.py:24
  110.4 7.7 %collective-permute-done.7.refs_8_ = bf16[512,512]{1,0:T(8,128)(2,1)} collective-permute-done((bf16[512,512]{1,0:T(8,128)(2,1)}, bf16[512,512]{1,0:T(8,128)(2,1)}, u32[]{:S(2)}, u32[]{:S(2)}) %collective-permute-start.7) | collective-permute-done | bytes 524320 | tf_op jit(solution)/shard_map/ppermute | solution.py:24
  120.1 11.4 %attention_fwd.1 = (bf16[512,512]{1,0:T(8,128)(2,1)S(1)}, f32[4,512,1]{2,1,0:T(8,128)}) custom-call(s32[512,1]{1,0:T(8,128)S(1)} %copy.171.lo_ref, s32[512,1]{1,0:T(8,128)S(1)} %copy-done.8, bf16[512,512]{1,0:T(8,128)(2,1)S(1)} %get-tuple-element.83.q_ref.refs_0_, bf16[512,512]{1,0:T(8,128)(2,1)S(1)} %get-tuple-element.82.refs_0_.k_ref, ...), custom_call_target="tpu_custom_call" | custom-call | flops 2684354560 | bytes 6291456 | tf_op jit(solution)/shard_map/attention_fwd/pallas_call | solution.py:135
  140.1 3.9 copy.177
  144.0 18.8 %collective-permute-done.9 = bf16[512,1024]{0,1:T(8,128)(2,1)} collective-permute-done((bf16[512,1024]{0,1:T(8,128)(2,1)}, bf16[512,1024]{0,1:T(8,128)(2,1)}, u32[]{:S(2)}, u32[]{:S(2)}) %collective-permute-start.9) | collective-permute-done | bytes 1048608 | tf_op jit(solution)/shard_map/ppermute | solution.py:24
  168.5 3.2 constant_dynamic-slice_fusion.20
  171.7 5.1 fusion.107
  186.4 5.4 multiply_convert_fusion.1
  192.5 6.7 fusion.106
  199.3 3.6 fusion.108
  202.9 5.0 convolution_add_fusion
  207.9 5.5 copy.205
  213.4 3.4 fusion.49
  217.1 3.4 fusion.48
  220.7 4.4 fusion.80.lo_ref
  230.0 3.2 constant_dynamic-slice_fusion.12
  234.2 3.2 fusion.40
  243.3 6.8 convolution_convert_fusion
  250.2 7.6 %reshape.373 = bf16[2,2,256,1376]{2,1,0,3:T(2,128)(2,1)} reshape(bf16[1024,1376]{0,1:T(8,128)(2,1)} %convolution_convert_fusion) | data formatting | bytes 5636096 | tf_op jit(solution)/shard_map/reshape | solution.py:73
  257.8 8.8 %constant_dynamic-slice_fusion.2 = (bf16[2,1,256,1376]{2,1,0,3:T(2,128)(2,1)}, bf16[2,1,256,1376]{2,1,0,3:T(2,128)(2,1)S(1)}) fusion(bf16[2,2,256,1376]{2,1,0,3:T(2,128)(2,1)} %reshape.373, s32[]{:T(128)S(6)} %select_n.446, s32[]{:T(128)S(6)} %select_n.447), kind=kLoop, calls=%fused_computation.190 | loop fusion | bytes 5636104 | tf_op jit(solution)/shard_map/jit(dynamic_index_in_dim)/dynamic_slice | solution.py:74
  267.9 47.1 %collective-permute-done.52 = bf16[512,1024]{0,1:T(8,128)(2,1)} collective-permute-done((bf16[512,1024]{0,1:T(8,128)(2,1)}, bf16[512,1024]{0,1:T(8,128)(2,1)}, u32[]{:S(2)}, u32[]{:S(2)}) %collective-permute-start.52) | collective-permute-done | bytes 1048608 | tf_op jit(solution)/shard_map/ppermute | solution.py:24
  317.5 6.4 convolution_convert_fusion.1
  323.9 8.0 %reshape.368 = bf16[2,2,256,1376]{2,1,0,3:T(2,128)(2,1)} reshape(bf16[1024,1376]{0,1:T(8,128)(2,1)} %convolution_convert_fusion.1) | data formatting | bytes 5636096 | tf_op jit(solution)/shard_map/reshape | solution.py:73
  331.8 8.8 %constant_dynamic-slice_fusion.7 = (bf16[2,1,256,1376]{2,1,0,3:T(2,128)(2,1)}, bf16[2,1,256,1376]{2,1,0,3:T(2,128)(2,1)S(1)}) fusion(bf16[2,2,256,1376]{2,1,0,3:T(2,128)(2,1)} %reshape.368, s32[]{:T(128)S(6)} %select_n.446, s32[]{:T(128)S(6)} %select_n.447), kind=kLoop, calls=%fused_computation.195 | loop fusion | bytes 5636104 | tf_op jit(solution)/shard_map/jit(dynamic_index_in_dim)/dynamic_slice | solution.py:74
  342.8 6.4 convolution_convert_fusion.2
  349.2 7.5 %reshape.366 = bf16[2,2,256,1376]{2,1,0,3:T(2,128)(2,1)} reshape(bf16[1024,1376]{0,1:T(8,128)(2,1)} %convolution_convert_fusion.2) | data formatting | bytes 5636096 | tf_op jit(solution)/shard_map/reshape | solution.py:73
  356.7 7.7 %constant_dynamic-slice_fusion.10 = (bf16[2,1,256,1376]{2,1,0,3:T(2,128)(2,1)S(1)}, bf16[2,1,256,1376]{2,1,0,3:T(2,128)(2,1)S(1)}) fusion(bf16[2,2,256,1376]{2,1,0,3:T(2,128)(2,1)} %reshape.366, s32[]{:T(128)S(6)} %select_n.446, s32[]{:T(128)S(6)} %select_n.447), kind=kLoop, calls=%fused_computation.198 | loop fusion | bytes 5636104 | tf_op jit(solution)/shard_map/jit(dynamic_index_in_dim)/dynamic_slice | solution.py:74
  376.7 18.2 %collective-permute-done.57 = bf16[2,256,1376]{1,2,0:T(8,128)(2,1)} collective-permute-done((bf16[2,256,1376]{1,2,0:T(8,128)(2,1)}, bf16[2,256,1376]{1,2,0:T(8,128)(2,1)}, u32[]{:S(2)}, u32[]{:S(2)}) %collective-permute-start.57) | collective-permute-done | bytes 1409056 | tf_op jit(solution)/shard_map/ppermute | solution.py:24
  397.6 25.7 %collective-permute-done.54 = bf16[2,256,1376]{1,2,0:T(8,128)(2,1)S(1)} collective-permute-done((bf16[2,256,1376]{1,2,0:T(8,128)(2,1)S(1)}, bf16[2,256,1376]{1,2,0:T(8,128)(2,1)S(1)}, u32[]{:S(2)}, u32[]{:S(2)}) %collective-permute-start.54) | collective-permute-done | bytes 1409056 | tf_op jit(solution)/shard_map/ppermute | solution.py:24
  430.7 4.7 fusion.95
  452.3 14.3 %attention_dq.1 = f32[512,512]{1,0:T(8,128)} custom-call(s32[512,1]{1,0:T(8,128)S(1)} %copy.171.lo_ref, bf16[512,512]{1,0:T(8,128)(2,1)S(1)} %get-tuple-element.83.q_ref.refs_0_, bf16[512,512]{1,0:T(8,128)(2,1)S(1)} %copy-done.1, f32[4,512,1]{2,1,0:T(8,128)} %get-tuple-element.16.lse_ref, f32[4,512,1]{2,1,0:T(8,128)} %copy.183.delta_ref, ...), custom_call_target="tpu_custom_call" | custom-call | flops 4026531840 | bytes 7340032 | tf_op jit(solution)/shard_map/attention_dq/pallas_call | solution.py:189
  468.1 3.3 collective-permute-start.36
  483.9 3.7 collective-permute-done.27.refs_14_
  493.7 10.9 %collective-permute-done.49 = bf16[512,512]{1,0:T(8,128)(2,1)S(1)} collective-permute-done((bf16[512,512]{1,0:T(8,128)(2,1)}, bf16[512,512]{1,0:T(8,128)(2,1)S(1)}, u32[]{:S(2)}, u32[]{:S(2)}) %collective-permute-start.49) | collective-permute-done | bytes 524320 | tf_op jit(solution)/shard_map/ppermute | solution.py:24
  508.1 6.6 collective-permute-start.50
  514.7 3.6 collective-permute-done.23.refs_9_
  522.9 4.4 collective-permute-done.50
  531.3 13.3 %collective-permute-done.26.refs_11_ = f32[4,2,512]{2,1,0:T(2,128)S(1)} collective-permute-done((f32[4,2,512]{2,1,0:T(2,128)S(1)}, f32[4,2,512]{2,1,0:T(2,128)S(1)}, u32[]{:S(2)}, u32[]{:S(2)}) %collective-permute-start.26) | collective-permute-done | bytes 16416 | tf_op jit(solution)/shard_map/ppermute | solution.py:24
  544.6 12.2 %collective-permute-start.55 = (bf16[1,256,1376]{1,2,0:T(8,128)(2,1)}, bf16[1,256,1376]{1,2,0:T(8,128)(2,1)}, u32[]{:S(2)}, u32[]{:S(2)}) collective-permute-start(bf16[1,256,1376]{1,2,0:T(8,128)(2,1)} %constant_dynamic-slice_fusion.8), channel_id=1, source_target_pairs={{0,16},{4,20},{8,24},{12,28},{16,0},{20,4},{24,8},{28,12},{1,17},{... | collective-permute-start | bytes 2113544 | tf_op jit(solution)/shard_map/ppermute | solution.py:24
  557.2 19.8 %attention_dkv.1 = (f32[512,512]{1,0:T(8,128)}, f32[512,512]{1,0:T(8,128)}) custom-call(s32[1,2560]{1,0:T(1,128)S(1)} %fusion.80.lo_ref, bf16[512,512]{1,0:T(8,128)(2,1)S(1)} %get-tuple-element.82.refs_0_.k_ref, bf16[512,512]{1,0:T(8,128)(2,1)} %convolution_convert_fusion.7.refs_5_.v_ref, bf16[512,512]{1,0:T(8,128)(2,1)S(1)} %get-tuple-element.83.q_ref.refs_0_, ...), custom_call_target="tpu_custom_call" | custom-call | flops 5368709120 | bytes 8388608 | tf_op jit(solution)/shard_map/attention_dkv/pallas_call | solution.py:244
  584.2 3.5 fusion.58
  591.3 4.5 add_add_fusion
  595.8 5.6 copy.206
  613.4 3.6 collective-permute-start.46
  623.8 3.6 collective-permute-start.43
  627.3 4.7 collective-permute-done.39
  634.6 3.6 collective-permute-start.40
  638.7 3.6 collective-permute-done.30
  642.9 6.4 collective-permute-start.44
  649.3 11.5 %collective-permute-done.40 = bf16[2,256,512]{2,1,0:T(8,128)(2,1)S(1)} collective-permute-done((bf16[2,256,512]{2,1,0:T(8,128)(2,1)S(1)}, bf16[2,256,512]{2,1,0:T(8,128)(2,1)S(1)}, u32[]{:S(2)}, u32[]{:S(2)}) %collective-permute-start.40) | collective-permute-done | bytes 524320 | tf_op jit(solution)/shard_map/ppermute | solution.py:24
  662.0 10.1 %collective-permute-done.44 = bf16[1,256,512]{2,1,0:T(8,128)(2,1)S(1)} collective-permute-done((bf16[1,256,512]{2,1,0:T(8,128)(2,1)S(1)}, bf16[1,256,512]{2,1,0:T(8,128)(2,1)S(1)}, u32[]{:S(2)}, u32[]{:S(2)}) %collective-permute-start.44) | collective-permute-done | bytes 262176 | tf_op jit(solution)/shard_map/ppermute | solution.py:24
  683.2 3.4 collective-permute-start.34
  686.6 6.9 fusion.9
  693.5 3.9 copy.198
  697.4 3.9 copy.199
  (395 shorter events, 210.1 us)
Async XLA Ops:
  0.6 130.9 %copy-start = (bf16[2048,512]{1,0:T(8,128)(2,1)S(1)}, bf16[2048,512]{1,0:T(8,128)(2,1)}, u32[]{:S(2)}) copy-start(bf16[2048,512]{1,0:T(8,128)(2,1)} %param.20) | copy-start | bytes 6291460
  30.2 17.3 %collective-permute-start = (bf16[512,512]{1,0:T(8,128)(2,1)S(1)}, bf16[512,512]{1,0:T(8,128)(2,1)}, u32[]{:S(2)}, u32[]{:S(2)}) collective-permute-start(bf16[512,512]{1,0:T(8,128)(2,1)S(1)} %get-tuple-element.82.refs_0_.k_ref), channel_id=1, source_target_pairs={{0,8},{4,12},{8,16},{12,20},{16,24},{20,28},{1,9},{5,13},{9,17},{1... | collective-permute-start | bytes 1572872 | tf_op jit(solution)/shard_map/ppermute | solution.py:29
  38.0 20.8 %collective-permute-start.4 = (bf16[512,512]{1,0:T(8,128)(2,1)}, bf16[512,512]{1,0:T(8,128)(2,1)}, u32[]{:S(2)}, u32[]{:S(2)}) collective-permute-start(bf16[512,512]{1,0:T(8,128)(2,1)} %convolution_convert_fusion.7.refs_5_.v_ref), channel_id=1, source_target_pairs={{0,8},{4,12},{8,16},{12,20},{16,24},{20,28},{1,9},{5,13},{9,17},{1... | collective-permute-start | bytes 1572872 | tf_op jit(solution)/shard_map/ppermute | solution.py:29
  49.8 25.0 %collective-permute-start.2 = (bf16[512,512]{1,0:T(8,128)(2,1)}, bf16[512,512]{1,0:T(8,128)(2,1)}, u32[]{:S(2)}, u32[]{:S(2)}) collective-permute-start(bf16[512,512]{1,0:T(8,128)(2,1)} %get-tuple-element.52.refs_2_), channel_id=1, source_target_pairs={{0,8},{4,12},{8,16},{12,20},{16,24},{20,28},{1,9},{5,13},{9,17},{1... | collective-permute-start | bytes 1572872 | tf_op jit(solution)/shard_map/ppermute | solution.py:29
  61.3 18.9 %collective-permute-start.6 = (bf16[512,512]{1,0:T(8,128)(2,1)}, bf16[512,512]{1,0:T(8,128)(2,1)}, u32[]{:S(2)}, u32[]{:S(2)}) collective-permute-start(bf16[512,512]{1,0:T(8,128)(2,1)} %get-tuple-element.48.refs_7_), channel_id=1, source_target_pairs={{0,8},{4,12},{8,16},{12,20},{16,24},{20,28},{1,9},{5,13},{9,17},{1... | collective-permute-start | bytes 1572872 | tf_op jit(solution)/shard_map/ppermute | solution.py:29
  72.7 15.2 %collective-permute-start.1 = (bf16[512,512]{1,0:T(8,128)(2,1)}, bf16[512,512]{1,0:T(8,128)(2,1)}, u32[]{:S(2)}, u32[]{:S(2)}) collective-permute-start(bf16[512,512]{1,0:T(8,128)(2,1)} %get-tuple-element.51), channel_id=1, source_target_pairs={{0,4},{4,0},{8,12},{12,8},{16,20},{20,16},{24,28},{28,24},{1,5},{5... | collective-permute-start | bytes 1572872 | tf_op jit(solution)/shard_map/ppermute | solution.py:24
  74.1 25.1 %collective-permute-start.5 = (bf16[512,512]{1,0:T(8,128)(2,1)}, bf16[512,512]{1,0:T(8,128)(2,1)}, u32[]{:S(2)}, u32[]{:S(2)}) collective-permute-start(bf16[512,512]{1,0:T(8,128)(2,1)} %get-tuple-element.47), channel_id=1, source_target_pairs={{0,4},{4,0},{8,12},{12,8},{16,20},{20,16},{24,28},{28,24},{1,5},{5... | collective-permute-start | bytes 1572872 | tf_op jit(solution)/shard_map/ppermute | solution.py:24
  77.2 33.2 %collective-permute-start.3 = (bf16[512,512]{1,0:T(8,128)(2,1)}, bf16[512,512]{1,0:T(8,128)(2,1)}, u32[]{:S(2)}, u32[]{:S(2)}) collective-permute-start(bf16[512,512]{1,0:T(8,128)(2,1)} %get-tuple-element.49), channel_id=1, source_target_pairs={{0,4},{4,0},{8,12},{12,8},{16,20},{20,16},{24,28},{28,24},{1,5},{5... | collective-permute-start | bytes 1572872 | tf_op jit(solution)/shard_map/ppermute | solution.py:24
  82.6 35.6 %collective-permute-start.7 = (bf16[512,512]{1,0:T(8,128)(2,1)}, bf16[512,512]{1,0:T(8,128)(2,1)}, u32[]{:S(2)}, u32[]{:S(2)}) collective-permute-start(bf16[512,512]{1,0:T(8,128)(2,1)} %get-tuple-element.45), channel_id=1, source_target_pairs={{0,4},{4,0},{8,12},{12,8},{16,20},{20,16},{24,28},{28,24},{1,5},{5... | collective-permute-start | bytes 1572872 | tf_op jit(solution)/shard_map/ppermute | solution.py:24
  133.0 2.7 collective-permute-start.8
  137.3 25.5 %collective-permute-start.9 = (bf16[512,1024]{0,1:T(8,128)(2,1)}, bf16[512,1024]{0,1:T(8,128)(2,1)}, u32[]{:S(2)}, u32[]{:S(2)}) collective-permute-start(bf16[512,1024]{0,1:T(8,128)(2,1)} %fusion.42), channel_id=1, source_target_pairs={{0,2},{1,3},{2,0},{3,1},{4,6},{5,7},{6,4},{7,5},{8,10},{9,11},{10,... | collective-permute-start | bytes 3145736 | tf_op jit(solution)/shard_map/ppermute | solution.py:24
  138.8 38.1 %collective-permute-start.17 = (bf16[512,512]{1,0:T(8,128)(2,1)S(1)}, bf16[512,512]{1,0:T(8,128)(2,1)}, u32[]{:S(2)}, u32[]{:S(2)}) collective-permute-start(bf16[512,512]{1,0:T(8,128)(2,1)S(1)} %get-tuple-element.83.q_ref.refs_0_), channel_id=1, source_target_pairs={{8,0},{12,4},{16,8},{20,12},{24,16},{28,20},{9,1},{13,5},{17,9},{2... | collective-permute-start | bytes 1572872 | tf_op jit(solution)/shard_map/ppermute | solution.py:29
  165.6 12.7 %collective-permute-start.10 = (bf16[512,1024]{0,1:T(8,128)(2,1)}, bf16[512,1024]{0,1:T(8,128)(2,1)}, u32[]{:S(2)}, u32[]{:S(2)}) collective-permute-start(bf16[512,1024]{0,1:T(8,128)(2,1)} %add_convert_fusion.4), channel_id=1, source_target_pairs={{0,1},{1,0},{2,3},{3,2},{4,5},{5,4},{6,7},{7,6},{8,9},{9,8},{10,11... | collective-permute-start | bytes 3145736 | tf_op jit(solution)/shard_map/ppermute | solution.py:24
  167.2 74.1 %collective-permute-start.59 = (bf16[512,1024]{0,1:T(8,128)(2,1)}, bf16[512,1024]{0,1:T(8,128)(2,1)}, u32[]{:S(2)}, u32[]{:S(2)}) collective-permute-start(bf16[512,1024]{0,1:T(8,128)(2,1)} %bitcast.54), channel_id=1, source_target_pairs={{0,4},{4,0},{8,12},{12,8},{16,20},{20,16},{24,28},{28,24},{1,5},{5... | collective-permute-start | bytes 3145736 | tf_op jit(solution)/shard_map/ppermute | solution.py:24
  176.9 48.2 %collective-permute-start.19 = (bf16[512,512]{1,0:T(8,128)(2,1)}, bf16[512,512]{1,0:T(8,128)(2,1)}, u32[]{:S(2)}, u32[]{:S(2)}) collective-permute-start(bf16[512,512]{1,0:T(8,128)(2,1)} %collective-permute-done.17.refs_2_), channel_id=1, source_target_pairs={{8,0},{12,4},{16,8},{20,12},{24,16},{28,20},{9,1},{13,5},{17,9},{2... | collective-permute-start | bytes 1572872 | tf_op jit(solution)/shard_map/ppermute | solution.py:29
  191.8 51.0 %collective-permute-start.60 = (bf16[512,1376]{0,1:T(8,128)(2,1)}, bf16[512,1376]{0,1:T(8,128)(2,1)}, u32[]{:S(2)}, u32[]{:S(2)}) collective-permute-start(bf16[512,1376]{0,1:T(8,128)(2,1)} %get-tuple-element.55), channel_id=1, source_target_pairs={{0,4},{4,0},{8,12},{12,8},{16,20},{20,16},{24,28},{28,24},{1,5},{5... | collective-permute-start | bytes 4227080 | tf_op jit(solution)/shard_map/ppermute | solution.py:24
  216.8 16.4 %collective-permute-start.14 = (bf16[512,1024]{0,1:T(8,128)(2,1)}, bf16[512,1024]{0,1:T(8,128)(2,1)}, u32[]{:S(2)}, u32[]{:S(2)}) collective-permute-start(bf16[512,1024]{0,1:T(8,128)(2,1)} %fusion.49), channel_id=1, source_target_pairs={{0,1},{1,0},{2,3},{3,2},{4,5},{5,4},{6,7},{7,6},{8,9},{9,8},{10,11... | collective-permute-start | bytes 3145736 | tf_op jit(solution)/shard_map/ppermute | solution.py:24
  220.5 16.9 %collective-permute-start.11 = (bf16[512,1024]{0,1:T(8,128)(2,1)}, bf16[512,1024]{0,1:T(8,128)(2,1)}, u32[]{:S(2)}, u32[]{:S(2)}) collective-permute-start(bf16[512,1024]{0,1:T(8,128)(2,1)} %fusion.48), channel_id=1, source_target_pairs={{0,1},{1,0},{2,3},{3,2},{4,5},{5,4},{6,7},{7,6},{8,9},{9,8},{10,11... | collective-permute-start | bytes 3145736 | tf_op jit(solution)/shard_map/ppermute | solution.py:24
  229.0 88.5 %collective-permute-start.56 = (bf16[512,1376]{0,1:T(8,128)(2,1)}, bf16[512,1376]{0,1:T(8,128)(2,1)}, u32[]{:S(2)}, u32[]{:S(2)}) collective-permute-start(bf16[512,1376]{0,1:T(8,128)(2,1)} %copy-done.63), channel_id=1, source_target_pairs={{0,4},{4,0},{8,12},{12,8},{16,20},{20,16},{24,28},{28,24},{1,5},{5... | collective-permute-start | bytes 4227080 | tf_op jit(solution)/shard_map/ppermute | solution.py:24
  233.3 108.7 %collective-permute-start.53 = (bf16[512,1376]{0,1:T(8,128)(2,1)}, bf16[512,1376]{0,1:T(8,128)(2,1)}, u32[]{:S(2)}, u32[]{:S(2)}) collective-permute-start(bf16[512,1376]{0,1:T(8,128)(2,1)} %copy-done.83), channel_id=1, source_target_pairs={{0,4},{4,0},{8,12},{12,8},{16,20},{20,16},{24,28},{28,24},{1,5},{5... | collective-permute-start | bytes 4227080 | tf_op jit(solution)/shard_map/ppermute | solution.py:24
  237.4 77.7 %collective-permute-start.52 = (bf16[512,1024]{0,1:T(8,128)(2,1)}, bf16[512,1024]{0,1:T(8,128)(2,1)}, u32[]{:S(2)}, u32[]{:S(2)}) collective-permute-start(bf16[512,1024]{0,1:T(8,128)(2,1)} %bitcast.45), channel_id=1, source_target_pairs={{0,4},{4,0},{8,12},{12,8},{16,20},{20,16},{24,28},{28,24},{1,5},{5... | collective-permute-start | bytes 3145736 | tf_op jit(solution)/shard_map/ppermute | solution.py:24
  241.3 124.7 %collective-permute-start.15 = (bf16[512,1024]{0,1:T(8,128)(2,1)}, bf16[512,1024]{0,1:T(8,128)(2,1)}, u32[]{:S(2)}, u32[]{:S(2)}) collective-permute-start(bf16[512,1024]{0,1:T(8,128)(2,1)} %fusion.40), channel_id=1, source_target_pairs={{0,2},{1,3},{2,0},{3,1},{4,6},{5,7},{6,4},{7,5},{8,10},{9,11},{10,... | collective-permute-start | bytes 3145736 | tf_op jit(solution)/shard_map/ppermute | solution.py:24
  242.8 125.1 %collective-permute-start.12 = (bf16[512,1024]{0,1:T(8,128)(2,1)}, bf16[512,1024]{0,1:T(8,128)(2,1)}, u32[]{:S(2)}, u32[]{:S(2)}) collective-permute-start(bf16[512,1024]{0,1:T(8,128)(2,1)} %fusion.41), channel_id=1, source_target_pairs={{0,2},{1,3},{2,0},{3,1},{4,6},{5,7},{6,4},{7,5},{8,10},{9,11},{10,... | collective-permute-start | bytes 3145736 | tf_op jit(solution)/shard_map/ppermute | solution.py:24
  315.1 56.2 %collective-permute-start.61 = (bf16[2,256,1376]{1,2,0:T(8,128)(2,1)}, bf16[2,256,1376]{1,2,0:T(8,128)(2,1)}, u32[]{:S(2)}, u32[]{:S(2)}) collective-permute-start(bf16[2,256,1376]{1,2,0:T(8,128)(2,1)} %bitcast.193), channel_id=1, source_target_pairs={{0,8},{4,12},{8,0},{12,4},{16,24},{20,28},{24,16},{28,20},{1,9},{5... | collective-permute-start | bytes 4227080 | tf_op jit(solution)/shard_map/ppermute | solution.py:24
  341.9 52.9 %collective-permute-start.57 = (bf16[2,256,1376]{1,2,0:T(8,128)(2,1)}, bf16[2,256,1376]{1,2,0:T(8,128)(2,1)}, u32[]{:S(2)}, u32[]{:S(2)}) collective-permute-start(bf16[2,256,1376]{1,2,0:T(8,128)(2,1)} %bitcast.194), channel_id=1, source_target_pairs={{0,8},{4,12},{8,0},{12,4},{16,24},{20,28},{24,16},{28,20},{1,9},{5... | collective-permute-start | bytes 4227080 | tf_op jit(solution)/shard_map/ppermute | solution.py:24
  364.7 58.7 %collective-permute-start.54 = (bf16[2,256,1376]{1,2,0:T(8,128)(2,1)S(1)}, bf16[2,256,1376]{1,2,0:T(8,128)(2,1)S(1)}, u32[]{:S(2)}, u32[]{:S(2)}) collective-permute-start(bf16[2,256,1376]{1,2,0:T(8,128)(2,1)S(1)} %bitcast.214), channel_id=1, source_target_pairs={{0,8},{4,12},{8,0},{12,4},{16,24},{20,28},{24,16},{28,20},{1,9},{5... | collective-permute-start | bytes 4227080 | tf_op jit(solution)/shard_map/ppermute | solution.py:24
  367.8 56.9 %collective-permute-start.16 = (bf16[512,1024]{0,1:T(8,128)(2,1)S(1)}, bf16[512,1024]{0,1:T(8,128)(2,1)S(1)}, u32[]{:S(2)}, u32[]{:S(2)}) collective-permute-start(bf16[512,1024]{0,1:T(8,128)(2,1)S(1)} %add_convert_fusion.2), channel_id=1, source_target_pairs={{0,1},{1,0},{2,3},{3,2},{4,5},{5,4},{6,7},{7,6},{8,9},{9,8},{10,11... | collective-permute-start | bytes 3145736 | tf_op jit(solution)/shard_map/ppermute | solution.py:24
  370.8 97.3 %collective-permute-start.13 = (bf16[512,1024]{0,1:T(8,128)(2,1)}, bf16[512,1024]{0,1:T(8,128)(2,1)}, u32[]{:S(2)}, u32[]{:S(2)}) collective-permute-start(bf16[512,1024]{0,1:T(8,128)(2,1)} %add_convert_fusion.3), channel_id=1, source_target_pairs={{0,1},{1,0},{2,3},{3,2},{4,5},{5,4},{6,7},{7,6},{8,9},{9,8},{10,11... | collective-permute-start | bytes 3145736 | tf_op jit(solution)/shard_map/ppermute | solution.py:24
  374.1 114.5 %collective-permute-start.62 = (bf16[1,256,1376]{1,2,0:T(8,128)(2,1)}, bf16[1,256,1376]{1,2,0:T(8,128)(2,1)}, u32[]{:S(2)}, u32[]{:S(2)}) collective-permute-start(bf16[1,256,1376]{1,2,0:T(8,128)(2,1)} %constant_dynamic-slice_fusion), channel_id=1, source_target_pairs={{0,16},{4,20},{8,24},{12,28},{16,0},{20,4},{24,8},{28,12},{1,17},{... | collective-permute-start | bytes 2113544 | tf_op jit(solution)/shard_map/ppermute | solution.py:24
  436.9 68.5 %collective-permute-start.48 = (bf16[512,1024]{0,1:T(8,128)(2,1)}, bf16[512,1024]{0,1:T(8,128)(2,1)}, u32[]{:S(2)}, u32[]{:S(2)}) collective-permute-start(bf16[512,1024]{0,1:T(8,128)(2,1)} %bitcast.38), channel_id=1, source_target_pairs={{0,4},{4,0},{8,12},{12,8},{16,20},{20,16},{24,28},{28,24},{1,5},{5... | collective-permute-start | bytes 3145736 | tf_op jit(solution)/shard_map/ppermute | solution.py:24
  446.5 43.1 %collective-permute-start.21 = (bf16[512,512]{1,0:T(8,128)(2,1)}, bf16[512,512]{1,0:T(8,128)(2,1)}, u32[]{:S(2)}, u32[]{:S(2)}) collective-permute-start(bf16[512,512]{1,0:T(8,128)(2,1)} %get-tuple-element.135.do_ref.refs_5_), channel_id=1, source_target_pairs={{8,0},{12,4},{16,8},{20,12},{24,16},{28,20},{9,1},{13,5},{17,9},{2... | collective-permute-start | bytes 1572872 | tf_op jit(solution)/shard_map/ppermute | solution.py:29
  449.1 17.5 %collective-permute-start.35 = (f32[2048]{0:T(1024)S(1)}, f32[2048]{0:T(1024)S(1)}, u32[]{:S(2)}, u32[]{:S(2)}) collective-permute-start(f32[2048]{0:T(1024)S(1)} %get-tuple-element.41), channel_id=1, source_target_pairs={{0,4},{4,0},{8,12},{12,8},{16,20},{20,16},{24,28},{28,24},{1,5},{5... | collective-permute-start | bytes 24584 | tf_op jit(solution)/shard_map/ppermute | solution.py:24
  466.7 14.2 %collective-permute-start.25 = (f32[4,2,512]{2,1,0:T(2,128)S(1)}, f32[4,2,512]{2,1,0:T(2,128)S(1)}, u32[]{:S(2)}, u32[]{:S(2)}) collective-permute-start(f32[4,2,512]{2,1,0:T(2,128)S(1)} %pad_maximum_fusion.12.refs_10_), channel_id=1, source_target_pairs={{8,0},{12,4},{16,8},{20,12},{24,16},{28,20},{9,1},{13,5},{17,9},{2... | collective-permute-start | bytes 49160 | tf_op jit(solution)/shard_map/ppermute | solution.py:29
  468.1 6.4 collective-permute-start.36
  474.5 7.4 %collective-permute-start.37 = (f32[2048]{0:T(1024)S(1)}, f32[2048]{0:T(1024)S(1)}, u32[]{:S(2)}, u32[]{:S(2)}) collective-permute-start(f32[2048]{0:T(1024)S(1)} %add.278), channel_id=1, source_target_pairs={{0,16},{4,20},{8,24},{12,28},{16,0},{20,4},{24,8},{28,12},{1,17},{... | collective-permute-start | bytes 24584 | tf_op jit(solution)/shard_map/ppermute | solution.py:24
  480.9 47.6 %collective-permute-start.18 = (bf16[512,512]{1,0:T(8,128)(2,1)}, bf16[512,512]{1,0:T(8,128)(2,1)S(1)}, u32[]{:S(2)}, u32[]{:S(2)}) collective-permute-start(bf16[512,512]{1,0:T(8,128)(2,1)} %get-tuple-element.119), channel_id=1, source_target_pairs={{0,4},{4,0},{8,12},{12,8},{16,20},{20,16},{24,28},{28,24},{1,5},{5... | collective-permute-start | bytes 1572872 | tf_op jit(solution)/shard_map/ppermute | solution.py:24
  481.9 5.6 collective-permute-start.27
  487.5 17.0 %collective-permute-start.49 = (bf16[512,512]{1,0:T(8,128)(2,1)}, bf16[512,512]{1,0:T(8,128)(2,1)S(1)}, u32[]{:S(2)}, u32[]{:S(2)}) collective-permute-start(bf16[512,512]{1,0:T(8,128)(2,1)} %copy-done.3), channel_id=1, source_target_pairs={{0,4},{4,0},{8,12},{12,8},{16,20},{20,16},{24,28},{28,24},{1,5},{5... | collective-permute-start | bytes 1572872 | tf_op jit(solution)/shard_map/ppermute | solution.py:24
  488.7 31.0 %collective-permute-start.58 = (bf16[1,256,1376]{1,2,0:T(8,128)(2,1)}, bf16[1,256,1376]{1,2,0:T(8,128)(2,1)S(1)}, u32[]{:S(2)}, u32[]{:S(2)}) collective-permute-start(bf16[1,256,1376]{1,2,0:T(8,128)(2,1)} %constant_dynamic-slice_fusion.5), channel_id=1, source_target_pairs={{0,16},{4,20},{8,24},{12,28},{16,0},{20,4},{24,8},{28,12},{1,17},{... | collective-permute-start | bytes 2113544 | tf_op jit(solution)/shard_map/ppermute | solution.py:24
  489.6 28.6 %collective-permute-start.23 = (bf16[512,512]{1,0:T(8,128)(2,1)}, bf16[512,512]{1,0:T(8,128)(2,1)S(1)}, u32[]{:S(2)}, u32[]{:S(2)}) collective-permute-start(bf16[512,512]{1,0:T(8,128)(2,1)} %collective-permute-done.21.refs_7_), channel_id=1, source_target_pairs={{8,0},{12,4},{16,8},{20,12},{24,16},{28,20},{9,1},{13,5},{17,9},{2... | collective-permute-start | bytes 1572872 | tf_op jit(solution)/shard_map/ppermute | solution.py:29
  504.5 25.8 %collective-permute-start.20 = (bf16[512,512]{1,0:T(8,128)(2,1)S(1)}, bf16[512,512]{1,0:T(8,128)(2,1)S(1)}, u32[]{:S(2)}, u32[]{:S(2)}) collective-permute-start(bf16[512,512]{1,0:T(8,128)(2,1)S(1)} %copy-done.75), channel_id=1, source_target_pairs={{0,4},{4,0},{8,12},{12,8},{16,20},{20,16},{24,28},{28,24},{1,5},{5... | collective-permute-start | bytes 1572872 | tf_op jit(solution)/shard_map/ppermute | solution.py:24
  508.1 19.3 %collective-permute-start.50 = (bf16[2,256,512]{2,1,0:T(8,128)(2,1)S(1)}, bf16[2,256,512]{2,1,0:T(8,128)(2,1)S(1)}, u32[]{:S(2)}, u32[]{:S(2)}) collective-permute-start(bf16[2,256,512]{2,1,0:T(8,128)(2,1)S(1)} %dynamic-slice_bitcast_fusion), channel_id=1, source_target_pairs={{0,8},{4,12},{8,0},{12,4},{16,24},{20,28},{24,16},{28,20},{1,9},{5... | collective-permute-start | bytes 1572872 | tf_op jit(solution)/shard_map/ppermute | solution.py:24
  519.6 37.6 %collective-permute-start.22 = (bf16[512,512]{1,0:T(8,128)(2,1)S(1)}, bf16[512,512]{1,0:T(8,128)(2,1)S(1)}, u32[]{:S(2)}, u32[]{:S(2)}) collective-permute-start(bf16[512,512]{1,0:T(8,128)(2,1)S(1)} %get-tuple-element.117), channel_id=1, source_target_pairs={{0,4},{4,0},{8,12},{12,8},{16,20},{20,16},{24,28},{28,24},{1,5},{5... | collective-permute-start | bytes 1572872 | tf_op jit(solution)/shard_map/ppermute | solution.py:24
  519.7 37.5 %collective-permute-start.24 = (bf16[512,512]{1,0:T(8,128)(2,1)S(1)}, bf16[512,512]{1,0:T(8,128)(2,1)S(1)}, u32[]{:S(2)}, u32[]{:S(2)}) collective-permute-start(bf16[512,512]{1,0:T(8,128)(2,1)S(1)} %get-tuple-element.116), channel_id=1, source_target_pairs={{0,4},{4,0},{8,12},{12,8},{16,20},{20,16},{24,28},{28,24},{1,5},{5... | collective-permute-start | bytes 1572872 | tf_op jit(solution)/shard_map/ppermute | solution.py:24
  527.4 17.2 %collective-permute-start.26 = (f32[4,2,512]{2,1,0:T(2,128)S(1)}, f32[4,2,512]{2,1,0:T(2,128)S(1)}, u32[]{:S(2)}, u32[]{:S(2)}) collective-permute-start(f32[4,2,512]{2,1,0:T(2,128)S(1)} %get-tuple-element.121), channel_id=1, source_target_pairs={{0,4},{4,0},{8,12},{12,8},{16,20},{20,16},{24,28},{28,24},{1,5},{5... | collective-permute-start | bytes 49160 | tf_op jit(solution)/shard_map/ppermute | solution.py:24
  528.5 28.4 %collective-permute-start.28 = (f32[4,2,512]{2,1,0:T(2,128)S(1)}, f32[4,2,512]{2,1,0:T(2,128)S(1)}, u32[]{:S(2)}, u32[]{:S(2)}) collective-permute-start(f32[4,2,512]{2,1,0:T(2,128)S(1)} %get-tuple-element.120), channel_id=1, source_target_pairs={{0,4},{4,0},{8,12},{12,8},{16,20},{20,16},{24,28},{28,24},{1,5},{5... | collective-permute-start | bytes 49160 | tf_op jit(solution)/shard_map/ppermute | solution.py:24
  530.3 80.0 %collective-permute-start.38 = (bf16[512,1024]{0,1:T(8,128)(2,1)}, bf16[512,1024]{0,1:T(8,128)(2,1)}, u32[]{:S(2)}, u32[]{:S(2)}) collective-permute-start(bf16[512,1024]{0,1:T(8,128)(2,1)} %bitcast.23), channel_id=1, source_target_pairs={{0,4},{4,0},{8,12},{12,8},{16,20},{20,16},{24,28},{28,24},{1,5},{5... | collective-permute-start | bytes 3145736 | tf_op jit(solution)/shard_map/ppermute | solution.py:24
  544.6 59.5 %collective-permute-start.55 = (bf16[1,256,1376]{1,2,0:T(8,128)(2,1)}, bf16[1,256,1376]{1,2,0:T(8,128)(2,1)}, u32[]{:S(2)}, u32[]{:S(2)}) collective-permute-start(bf16[1,256,1376]{1,2,0:T(8,128)(2,1)} %constant_dynamic-slice_fusion.8), channel_id=1, source_target_pairs={{0,16},{4,20},{8,24},{12,28},{16,0},{20,4},{24,8},{28,12},{1,17},{... | collective-permute-start | bytes 2113544 | tf_op jit(solution)/shard_map/ppermute | solution.py:24
  556.8 50.8 %collective-permute-start.51 = (bf16[1,256,512]{2,1,0:T(8,128)(2,1)}, bf16[1,256,512]{2,1,0:T(8,128)(2,1)}, u32[]{:S(2)}, u32[]{:S(2)}) collective-permute-start(bf16[1,256,512]{2,1,0:T(8,128)(2,1)} %constant_dynamic-slice_fusion.13), channel_id=1, source_target_pairs={{0,16},{4,20},{8,24},{12,28},{16,0},{20,4},{24,8},{28,12},{1,17},{... | collective-permute-start | bytes 786440 | tf_op jit(solution)/shard_map/ppermute | solution.py:24
  579.2 31.2 %collective-permute-start.45 = (bf16[512,512]{1,0:T(8,128)(2,1)}, bf16[512,512]{1,0:T(8,128)(2,1)}, u32[]{:S(2)}, u32[]{:S(2)}) collective-permute-start(bf16[512,512]{1,0:T(8,128)(2,1)} %convert_element_type.366), channel_id=1, source_target_pairs={{0,4},{4,0},{8,12},{12,8},{16,20},{20,16},{24,28},{28,24},{1,5},{5... | collective-permute-start | bytes 1572872 | tf_op jit(solution)/shard_map/ppermute | solution.py:24
  604.0 12.9 %collective-permute-start.29 = (bf16[512,1024]{0,1:T(8,128)(2,1)S(1)}, bf16[512,1024]{0,1:T(8,128)(2,1)S(1)}, u32[]{:S(2)}, u32[]{:S(2)}) collective-permute-start(bf16[512,1024]{0,1:T(8,128)(2,1)S(1)} %fusion.50), channel_id=1, source_target_pairs={{0,1},{1,0},{2,3},{3,2},{4,5},{5,4},{6,7},{7,6},{8,9},{9,8},{10,11... | collective-permute-start | bytes 3145736 | tf_op jit(solution)/shard_map/ppermute | solution.py:24
  606.5 14.7 %collective-permute-start.42 = (bf16[512,512]{1,0:T(8,128)(2,1)S(1)}, bf16[512,512]{1,0:T(8,128)(2,1)S(1)}, u32[]{:S(2)}, u32[]{:S(2)}) collective-permute-start(bf16[512,512]{1,0:T(8,128)(2,1)S(1)} %copy-done.55), channel_id=1, source_target_pairs={{0,4},{4,0},{8,12},{12,8},{16,20},{20,16},{24,28},{28,24},{1,5},{5... | collective-permute-start | bytes 1572872 | tf_op jit(solution)/shard_map/ppermute | solution.py:24
  607.6 24.5 %collective-permute-start.39 = (bf16[512,512]{1,0:T(8,128)(2,1)S(1)}, bf16[512,512]{1,0:T(8,128)(2,1)S(1)}, u32[]{:S(2)}, u32[]{:S(2)}) collective-permute-start(bf16[512,512]{1,0:T(8,128)(2,1)S(1)} %copy-done.53), channel_id=1, source_target_pairs={{0,4},{4,0},{8,12},{12,8},{16,20},{20,16},{24,28},{28,24},{1,5},{5... | collective-permute-start | bytes 1572872 | tf_op jit(solution)/shard_map/ppermute | solution.py:24
  613.4 24.8 %collective-permute-start.46 = (bf16[2,256,512]{2,1,0:T(8,128)(2,1)S(1)}, bf16[2,256,512]{2,1,0:T(8,128)(2,1)S(1)}, u32[]{:S(2)}, u32[]{:S(2)}) collective-permute-start(bf16[2,256,512]{2,1,0:T(8,128)(2,1)S(1)} %dynamic-slice_bitcast_fusion.1), channel_id=1, source_target_pairs={{0,8},{4,12},{8,0},{12,4},{16,24},{20,28},{24,16},{28,20},{1,9},{5... | collective-permute-start | bytes 1572872 | tf_op jit(solution)/shard_map/ppermute | solution.py:24
  617.5 24.8 %collective-permute-start.30 = (bf16[512,1024]{0,1:T(8,128)(2,1)S(1)}, bf16[512,1024]{0,1:T(8,128)(2,1)S(1)}, u32[]{:S(2)}, u32[]{:S(2)}) collective-permute-start(bf16[512,1024]{0,1:T(8,128)(2,1)S(1)} %fusion.39), channel_id=1, source_target_pairs={{0,2},{1,3},{2,0},{3,1},{4,6},{5,7},{6,4},{7,5},{8,10},{9,11},{10,... | collective-permute-start | bytes 3145736 | tf_op jit(solution)/shard_map/ppermute | solution.py:24
  623.8 18.9 %collective-permute-start.43 = (bf16[2,256,512]{2,1,0:T(8,128)(2,1)S(1)}, bf16[2,256,512]{2,1,0:T(8,128)(2,1)S(1)}, u32[]{:S(2)}, u32[]{:S(2)}) collective-permute-start(bf16[2,256,512]{2,1,0:T(8,128)(2,1)S(1)} %dynamic-slice_bitcast_fusion.2), channel_id=1, source_target_pairs={{0,8},{4,12},{8,0},{12,4},{16,24},{20,28},{24,16},{28,20},{1,9},{5... | collective-permute-start | bytes 1572872 | tf_op jit(solution)/shard_map/ppermute | solution.py:24
  634.6 26.2 %collective-permute-start.40 = (bf16[2,256,512]{2,1,0:T(8,128)(2,1)S(1)}, bf16[2,256,512]{2,1,0:T(8,128)(2,1)S(1)}, u32[]{:S(2)}, u32[]{:S(2)}) collective-permute-start(bf16[2,256,512]{2,1,0:T(8,128)(2,1)S(1)} %dynamic-slice_bitcast_fusion.3), channel_id=1, source_target_pairs={{0,8},{4,12},{8,0},{12,4},{16,24},{20,28},{24,16},{28,20},{1,9},{5... | collective-permute-start | bytes 1572872 | tf_op jit(solution)/shard_map/ppermute | solution.py:24
  638.3 22.8 %collective-permute-start.47 = (bf16[1,256,512]{2,1,0:T(8,128)(2,1)S(1)}, bf16[1,256,512]{2,1,0:T(8,128)(2,1)S(1)}, u32[]{:S(2)}, u32[]{:S(2)}) collective-permute-start(bf16[1,256,512]{2,1,0:T(8,128)(2,1)S(1)} %constant_dynamic-slice_fusion.16), channel_id=1, source_target_pairs={{0,16},{4,20},{8,24},{12,28},{16,0},{20,4},{24,8},{28,12},{1,17},{... | collective-permute-start | bytes 786440 | tf_op jit(solution)/shard_map/ppermute | solution.py:24
  642.6 30.4 %collective-permute-start.31 = (bf16[512,1024]{0,1:T(8,128)(2,1)S(1)}, bf16[512,1024]{0,1:T(8,128)(2,1)S(1)}, u32[]{:S(2)}, u32[]{:S(2)}) collective-permute-start(bf16[512,1024]{0,1:T(8,128)(2,1)S(1)} %add_convert_fusion.1), channel_id=1, source_target_pairs={{0,1},{1,0},{2,3},{3,2},{4,5},{5,4},{6,7},{7,6},{8,9},{9,8},{10,11... | collective-permute-start | bytes 3145736 | tf_op jit(solution)/shard_map/ppermute | solution.py:24
  642.9 29.2 %collective-permute-start.44 = (bf16[1,256,512]{2,1,0:T(8,128)(2,1)S(1)}, bf16[1,256,512]{2,1,0:T(8,128)(2,1)S(1)}, u32[]{:S(2)}, u32[]{:S(2)}) collective-permute-start(bf16[1,256,512]{2,1,0:T(8,128)(2,1)S(1)} %constant_dynamic-slice_fusion.17), channel_id=1, source_target_pairs={{0,16},{4,20},{8,24},{12,28},{16,0},{20,4},{24,8},{28,12},{1,17},{... | collective-permute-start | bytes 786440 | tf_op jit(solution)/shard_map/ppermute | solution.py:24
  661.0 15.7 %collective-permute-start.41 = (bf16[1,256,512]{2,1,0:T(8,128)(2,1)S(1)}, bf16[1,256,512]{2,1,0:T(8,128)(2,1)S(1)}, u32[]{:S(2)}, u32[]{:S(2)}) collective-permute-start(bf16[1,256,512]{2,1,0:T(8,128)(2,1)S(1)} %constant_dynamic-slice_fusion.18), channel_id=1, source_target_pairs={{0,16},{4,20},{8,24},{12,28},{16,0},{20,4},{24,8},{28,12},{1,17},{... | collective-permute-start | bytes 786440 | tf_op jit(solution)/shard_map/ppermute | solution.py:24
  675.6 3.7 collective-permute-start.32
  679.3 3.9 collective-permute-start.33
  683.2 18.2 %collective-permute-start.34 = (f32[2048]{0:T(1024)S(1)}, f32[2048]{0:T(1024)S(1)}, u32[]{:S(2)}, u32[]{:S(2)}) collective-permute-start(f32[2048]{0:T(1024)S(1)} %add.274), channel_id=1, source_target_pairs={{0,16},{4,20},{8,24},{12,28},{16,0},{20,4},{24,8},{28,12},{1,17},{... | collective-permute-start | bytes 24584 | tf_op jit(solution)/shard_map/ppermute | solution.py:24
  (90 other events, 744.8 us)

commit v2 on v1

v2 whole, which is shorter than its diff:
```python
import functools
import math

import jax
import jax.numpy as jnp
from jax import lax
from jax.experimental import pallas as pl
from jax.experimental.pallas import tpu as pltpu
from jax.sharding import PartitionSpec as P

HEAD_DIM = 128
WINDOW = 2048
PAD = 64
NSEQ = 4
EPS = 1e-06
MASKED = -1e30
LOG2E = 1.4426950408889634
BIG = 1 << 28
F32 = jnp.float32
BF16 = jnp.bfloat16


def swap(block, axis, bit):
    return lax.ppermute(block, axis, [(i, i ^ bit) for i in range(lax.axis_size(axis))])


def shifted(block, distance):
    n = lax.axis_size("seq")
    return lax.ppermute(
        block, "seq", [(i, i + distance) for i in range(n) if 0 <= i + distance < n]
    )


BIG_VMEM = pltpu.CompilerParams(vmem_limit_bytes=48 << 20)


def cost(flops, moved):
    return pl.CostEstimate(flops=int(flops), bytes_accessed=int(moved), transcendentals=0)


def dot_nt(left, right):
    return lax.dot_general(left, right, (((1,), (1,)), ((), ())), preferred_element_type=F32)


def split_columns(mine, values, keep_ref, give_ref, flip):
    pairs = keep_ref.shape[0]
    depth = values.shape[1] // (2 * pairs)
    if flip:
        values = values.T
    for j in range(pairs):
        even = slice(2 * j * depth, (2 * j + 1) * depth)
        odd = slice((2 * j + 1) * depth, (2 * j + 2) * depth)
        even, odd = (values[even, :], values[odd, :]) if flip else (values[:, even], values[:, odd])
        keep_ref[j] = jnp.where(mine, even, odd)
        give_ref[j] = jnp.where(mine, odd, even)


def row_blocks(width, step):
    return pl.BlockSpec((step, width), lambda i, bits: (i, 0))


def prep_kernel(bits_ref, x_ref, gain_ref, out_ref, keep_ref, give_ref):
    x = x_ref[...].astype(F32)
    scale = lax.rsqrt(jnp.mean(x * x, axis=-1, keepdims=True) + EPS)
    normed = (x * scale * gain_ref[...]).astype(BF16)
    out_ref[...] = normed
    split_columns(bits_ref[0] == 0, normed, keep_ref, give_ref, True)


def split_kernel(bits_ref, x_ref, keep_ref, give_ref):
    split_columns(bits_ref[0] == 0, x_ref[...], keep_ref, give_ref, False)


def joined(bits_ref, own_ref, other_ref):
    low = bits_ref[1] == 0
    own, other = own_ref[...].astype(F32), other_ref[...].astype(F32)
    return jnp.concatenate([jnp.where(low, own, other), jnp.where(low, other, own)], axis=1)


def mid_kernel(
    bits_ref, x_ref, own_ref, other_ref, gain_ref, mid_ref, out_ref, keep_ref, give_ref
):
    mid = x_ref[...].astype(F32) + joined(bits_ref, own_ref, other_ref)
    mid_ref[...] = mid
    scale = lax.rsqrt(jnp.mean(mid * mid, axis=-1, keepdims=True) + EPS)
    normed = (mid * scale * gain_ref[...]).astype(BF16)
    out_ref[...] = normed
    split_columns(bits_ref[0] == 0, normed, keep_ref, give_ref, False)


def back_kernel(
    bits_ref, x_ref, own_ref, other_ref, gain_ref, add_ref, out_ref, part_ref, *more
):
    x = x_ref[...].astype(F32)
    scale = lax.rsqrt(jnp.mean(x * x, axis=-1, keepdims=True) + EPS)
    grad = joined(bits_ref, own_ref, other_ref)
    unit = x * scale
    grad_unit = grad * gain_ref[...]
    total = add_ref[...].astype(F32) + scale * (
        grad_unit - unit * jnp.mean(grad_unit * unit, axis=-1, keepdims=True)
    )
    out_ref[...] = total.astype(out_ref.dtype)
    part = jnp.sum(grad * unit, axis=0, keepdims=True)

    @pl.when(pl.program_id(0) == 0)
    def _():
        part_ref[...] = part

    @pl.when(pl.program_id(0) > 0)
    def _():
        part_ref[...] += part

    if more:
        low_ref, keep_ref, give_ref = more
        low = total.astype(BF16)
        low_ref[...] = low
        split_columns(bits_ref[0] == 0, low, keep_ref, give_ref, True)


def by_rows(kernel, bits, arrays, gains_at, outs, split, name, part=None):
    rows, width = arrays[0].shape
    step = rows // 4
    shards = lax.axis_size("seq")
    in_specs = [
        pl.BlockSpec((1, width), lambda i, bits: (0, 0))
        if k == gains_at
        else row_blocks(a.shape[1], step)
        for k, a in enumerate(arrays)
    ]
    out_specs, out_shape = [], []
    for k, dtype in enumerate(outs):
        if k == part:
            out_specs.append(pl.BlockSpec((1, width), lambda i, bits: (0, 0)))
            out_shape.append(jax.ShapeDtypeStruct((1, width), F32))
        else:
            out_specs.append(row_blocks(width, step))
            out_shape.append(jax.ShapeDtypeStruct((rows, width), dtype))
    depth = width // shards
    for _ in range(2 if split else 0):
        if split == "flip":
            out_specs.append(pl.BlockSpec((shards // 2, depth, step), lambda i, bits: (0, 0, i)))
            out_shape.append(jax.ShapeDtypeStruct((shards // 2, depth, rows), BF16))
        else:
            out_specs.append(pl.BlockSpec((shards // 2, step, depth), lambda i, bits: (0, i, 0)))
            out_shape.append(jax.ShapeDtypeStruct((shards // 2, rows, depth), BF16))
    return pl.pallas_call(
        kernel,
        grid_spec=pltpu.PrefetchScalarGridSpec(
            num_scalar_prefetch=1, grid=(rows // step,), in_specs=in_specs, out_specs=out_specs
        ),
        out_shape=out_shape,
        compiler_params=BIG_VMEM,
        cost_estimate=cost(rows * width * 10, rows * width * 2 * (len(arrays) + len(out_shape))),
        name=name,
    )(bits, *arrays)


def project_kernel(x_ref, w_ref, cos_ref, sin_ref, out_ref):
    raw = jnp.dot(x_ref[...], w_ref[...], preferred_element_type=F32)
    for start in range(0, raw.shape[1], HEAD_DIM):
        u = raw[:, start : start + HEAD_DIM]
        u = u * cos_ref[...] + pltpu.roll(u, HEAD_DIM // 2, 1) * sin_ref[...]
        out_ref[:, start : start + HEAD_DIM] = u.astype(BF16)


def plain_kernel(x_ref, w_ref, out_ref):
    out_ref[...] = jnp.dot(x_ref[...], w_ref[...], preferred_element_type=F32).astype(BF16)


def project(x, weight, tables, name):
    rows, depth = x.shape
    width = weight.shape[1]
    step = 2 * HEAD_DIM
    table = pl.BlockSpec((rows, HEAD_DIM), lambda i: (0, 0))
    return pl.pallas_call(
        project_kernel if tables else plain_kernel,
        grid=(width // step,),
        in_specs=[
            pl.BlockSpec((rows, depth), lambda i: (0, 0)),
            pl.BlockSpec((depth, step), lambda i: (0, i)),
        ]
        + [table] * len(tables),
        out_specs=pl.BlockSpec((rows, step), lambda i: (0, i)),
        out_shape=jax.ShapeDtypeStruct((rows, width), BF16),
        compiler_params=BIG_VMEM,
        cost_estimate=cost(2 * rows * depth * width, 2 * (rows + width) * depth),
        name=name,
    )(x, weight, *tables)


def half_kernel(pairs, flip, added, bits_ref, *refs):
    total = refs[2 * pairs][...].astype(F32) if added else None
    for k in range(pairs):
        term = dot_nt(refs[k][...], refs[pairs + k][...])
        total = term if total is None else total + term
    refs[-1][...] = total.astype(BF16)


def half_product(bits, lefts, rights, flip, added, name):
    rows = lefts[0].shape[0]
    width = rights[0].shape[0] // 2
    step = min(width, 512)
    steps = width // step

    def at(i, bits):
        return ((bits[1] ^ flip) * steps + i, 0)

    specs = [pl.BlockSpec(a.shape, lambda i, bits: (0, 0)) for a in lefts]
    specs += [pl.BlockSpec((step, a.shape[1]), at) for a in rights]
    extra = []
    if added is not None:
        extra = [added]
        specs.append(pl.BlockSpec((rows, step), lambda i, bits: (0, i)))
    depth = sum(a.shape[1] for a in lefts)
    return pl.pallas_call(
        functools.partial(half_kernel, len(lefts), flip, added is not None),
        grid_spec=pltpu.PrefetchScalarGridSpec(
            num_scalar_prefetch=1,
            grid=(steps,),
            in_specs=specs,
            out_specs=pl.BlockSpec((rows, step), lambda i, bits: (0, i)),
        ),
        out_shape=jax.ShapeDtypeStruct((rows, width), BF16),
        compiler_params=BIG_VMEM,
        cost_estimate=cost(2 * rows * depth * width, 2 * (rows + width) * depth),
        name=name,
    )(bits, *lefts, *rights, *extra)


def head_sum(bits, lefts, rights, name):
    give = half_product(bits, lefts, rights, 1, None, name + "_give")
    chip = half_product(bits, lefts, rights, 0, swap(give, "head", 1), name + "_keep")
    total = (chip.astype(F32) + swap(chip, "head", 2).astype(F32)).astype(BF16)
    return total, swap(total, "head", 1)


def head_sum_of(give, keep):
    chip = (keep.astype(F32) + swap(give, "head", 1).astype(F32)).astype(BF16)
    total = (chip.astype(F32) + swap(chip, "head", 2).astype(F32)).astype(BF16)
    return total, swap(total, "head", 1)


def dot_tn(left, right):
    return lax.dot_general(left, right, (((0,), (0,)), ((), ())), preferred_element_type=F32)


def mlp_kernel(
    bits_ref,
    x_ref,
    g_ref,
    wg_ref,
    wu_ref,
    wd_ref,
    act_ref,
    gg_ref,
    gu_ref,
    norm_keep_ref,
    norm_give_ref,
    out_keep_ref,
    out_give_ref,
    norm_ref,
    branch_ref,
):
    step = pl.program_id(0)
    x, g = x_ref[...], g_ref[...]
    gate = dot_nt(wg_ref[...], x)
    up = dot_nt(wu_ref[...], x)
    grad = dot_nt(wd_ref[...], g)
    sig = 1.0 / (1.0 + jnp.exp(-gate))
    silu = gate * sig
    act = (silu * up).astype(BF16)
    grad_gate = (grad * up * sig * (1.0 + gate * (1.0 - sig))).astype(BF16)
    grad_up = (grad * silu).astype(BF16)
    act_ref[...] = act
    gg_ref[...] = grad_gate
    gu_ref[...] = grad_up

    @pl.when(step == 0)
    def _():
        norm_ref[...] = jnp.zeros_like(norm_ref)
        branch_ref[...] = jnp.zeros_like(branch_ref)

    norm_ref[...] += jnp.dot(grad_gate.T, wg_ref[...], preferred_element_type=F32)
    norm_ref[...] += jnp.dot(grad_up.T, wu_ref[...], preferred_element_type=F32)
    branch_ref[...] += jnp.dot(act.T, wd_ref[...], preferred_element_type=F32)

    @pl.when(step == pl.num_programs(0) - 1)
    def _():
        half = norm_ref.shape[1] // 2
        low = bits_ref[1] == 0
        for total, keep_ref, give_ref in (
            (norm_ref, norm_keep_ref, norm_give_ref),
            (branch_ref, out_keep_ref, out_give_ref),
        ):
            first, second = total[:, :half], total[:, half:]
            keep_ref[...] = jnp.where(low, first, second).astype(BF16)
            give_ref[...] = jnp.where(low, second, first).astype(BF16)


def mlp(bits, x, grad, w_gate, w_up, w_down):
    rows, depth = x.shape
    width = w_gate.shape[0]
    step = width // 2
    whole = pl.BlockSpec((rows, depth), lambda i, bits: (0, 0))
    half = pl.BlockSpec((rows, depth // 2), lambda i, bits: (0, 0))
    block = pl.BlockSpec((step, depth), lambda i, bits: (i, 0))
    return pl.pallas_call(
        mlp_kernel,
        grid_spec=pltpu.PrefetchScalarGridSpec(
            num_scalar_prefetch=1,
            grid=(width // step,),
            in_specs=[whole, whole, block, block, block],
            out_specs=[pl.BlockSpec((step, rows), lambda i, bits: (i, 0))] * 3 + [half] * 4,
            scratch_shapes=[pltpu.VMEM((rows, depth), F32)] * 2,
        ),
        out_shape=[jax.ShapeDtypeStruct((width, rows), BF16)] * 3
        + [jax.ShapeDtypeStruct((rows, depth // 2), BF16)] * 4,
        compiler_params=pltpu.CompilerParams(vmem_limit_bytes=56 << 20),
        cost_estimate=cost(12 * rows * depth * width, 6 * depth * width),
        name="mlp",
    )(bits, x, grad, w_gate, w_up, w_down)


def blocks_kernel(order_ref, flip, xa_ref, xb_ref, ga_ref, gb_ref, *refs):
    if flip:
        total = jnp.dot(ga_ref[...], xa_ref[0], preferred_element_type=F32)
        total = total + jnp.dot(gb_ref[...], xb_ref[0], preferred_element_type=F32)
    else:
        total = jnp.dot(xa_ref[0], ga_ref[...], preferred_element_type=F32)
        total = total + jnp.dot(xb_ref[0], gb_ref[...], preferred_element_type=F32)
    if len(refs) == 2:
        total = total + refs[0][0].astype(F32)
    refs[-1][0] = total.astype(BF16)


def grad_blocks(order, x_own, x_got, g_own, g_got, added, flip, name):
    count = order.shape[0]
    if flip:
        _, rows, depth = x_own.shape
        cols = g_own.shape[0]
        shape = (cols, depth)
    else:
        _, depth, rows = x_own.shape
        cols = g_own.shape[1]
        shape = (depth, cols)
    x_spec = pl.BlockSpec((1,) + x_own.shape[1:], lambda i, order: (order[i], 0, 0))
    g_spec = pl.BlockSpec(g_own.shape, lambda i, order: (0, 0))
    out_spec = pl.BlockSpec((1,) + shape, lambda i, order: (i, 0, 0))
    extra = [] if added is None else [added]

    def kernel(order_ref, *refs):
        blocks_kernel(order_ref, flip, *refs)

    return pl.pallas_call(
        kernel,
        grid_spec=pltpu.PrefetchScalarGridSpec(
            num_scalar_prefetch=1,
            grid=(count,),
            in_specs=[x_spec, x_spec, g_spec, g_spec] + [out_spec] * len(extra),
            out_specs=out_spec,
        ),
        out_shape=jax.ShapeDtypeStruct((count,) + shape, BF16),
        compiler_params=BIG_VMEM,
        cost_estimate=cost(
            4 * count * depth * rows * cols, 2 * count * depth * cols + 4 * rows * cols
        ),
        name=name,
    )(order, x_own, x_got, g_own, g_got, *extra)


def weight_grad(x_pair, g_own, name, flip=False):
    n = lax.axis_size("seq")
    x_own, x_got = x_pair
    g_got = swap(g_own, "seq", 1)
    mine = lax.axis_index("seq") // 2
    bits = (n // 2).bit_length() - 1
    relative = [
        sum(((p >> k) & 1) << (bits - 1 - k) for k in range(bits)) for p in range(n // 2)
    ]
    order = mine ^ jnp.array(relative, jnp.int32)
    count = n // 4
    give = grad_blocks(order[count:], x_own, x_got, g_own, g_got, None, flip, name + "_give")
    part = grad_blocks(
        order[:count], x_own, x_got, g_own, g_got, swap(give, "seq", 2), flip, name + "_keep"
    )
    bit = 4
    while bit < n:
        count //= 2
        total = part[:count].astype(F32) + swap(part[count:], "seq", bit).astype(F32)
        bit *= 2
        part = total.astype(BF16) if bit < n else total
    return part[0].astype(F32).T if flip else part[0].astype(F32)


def gain_sum(part):
    n = lax.axis_size("seq")
    total = part
    bit = 1
    while bit < n:
        total = total + swap(total, "seq", bit)
        bit *= 2
    width = part.shape[-1] // n
    return lax.dynamic_slice_in_dim(total, lax.axis_index("seq") * width, width, total.ndim - 1)


def out_back_kernel(valid_ref, g_ref, w_ref, att_ref, do_ref, delta_ref, row_ref):
    rows = g_ref.shape[0]
    do = jnp.dot(g_ref[...], w_ref[...], preferred_element_type=F32).astype(BF16)
    do = jnp.where(valid_ref[...] > 0, do.astype(F32), 0.0)
    do_ref[...] = do.astype(BF16)
    product = do * att_ref[...].astype(F32)
    for k in range(do.shape[1] // HEAD_DIM):
        delta = jnp.sum(product[:, k * HEAD_DIM : (k + 1) * HEAD_DIM], axis=1, keepdims=True)
        delta_ref[k] = delta
        row_ref[k] = jnp.broadcast_to(delta, (rows, HEAD_DIM)).T[0:1, :]


def out_back(valid, grad, w_out, attended):
    rows, depth = grad.shape
    width = w_out.shape[1]
    heads = width // HEAD_DIM
    step = 2 * HEAD_DIM
    column = pl.BlockSpec((rows, step), lambda i: (0, i))
    return pl.pallas_call(
        out_back_kernel,
        grid=(width // step,),
        in_specs=[
            pl.BlockSpec((rows, 1), lambda i: (0, 0)),
            pl.BlockSpec((rows, depth), lambda i: (0, 0)),
            pl.BlockSpec((depth, step), lambda i: (0, i)),
            column,
        ],
        out_specs=[
            column,
            pl.BlockSpec((2, rows, 1), lambda i: (i, 0, 0)),
            pl.BlockSpec((2, 1, rows), lambda i: (i, 0, 0)),
        ],
        out_shape=[
            jax.ShapeDtypeStruct((rows, width), BF16),
            jax.ShapeDtypeStruct((heads, rows, 1), F32),
            jax.ShapeDtypeStruct((heads, 1, rows), F32),
        ],
        compiler_params=BIG_VMEM,
        cost_estimate=cost(2 * rows * depth * width, 2 * (rows + width) * depth),
        name="out_back",
    )(valid, grad, w_out, attended)


def turned_back(grad, cosine, sine):
    return (grad * cosine - pltpu.roll(grad, HEAD_DIM // 2, 1) * sine).astype(BF16)


def dq_kernel(lo_ref, cos_ref, sin_ref, q_ref, do_ref, lse_ref, delta_ref, k_refs, v_refs, out_ref):
    rows = q_ref.shape[1]
    n_parts = k_refs.shape[0]
    scale = HEAD_DIM ** (-0.5) * LOG2E
    sub = rows // 2
    for start in range(0, rows, sub):
        rs = slice(start, start + sub)
        q, do, lo = q_ref[0, rs, :], do_ref[rs, :], lo_ref[rs, :]
        lse, delta = lse_ref[0, rs, :], delta_ref[0, rs, :]
        acc = jnp.zeros((sub, HEAD_DIM), F32)
        for d in range(n_parts):
            k = k_refs[d]
            s = lax.dot_general(q, k, (((1,), (1,)), ((), ())), preferred_element_type=F32)
            u = lax.broadcasted_iota(jnp.int32, s.shape, 1) - d * rows
            seen = u >= lo
            if d == 0:
                t = lax.broadcasted_iota(jnp.int32, s.shape, 0) + start
                seen = seen & (u <= t)
            p = jnp.exp2(jnp.where(seen, s * scale, MASKED) - lse)
            dp = lax.dot_general(
                do, v_refs[d], (((1,), (1,)), ((), ())), preferred_element_type=F32
            )
            ds = (p * (dp - delta)).astype(BF16)
            acc = acc + jnp.dot(ds, k, preferred_element_type=F32)
        out_ref[rs, :] = turned_back(acc * HEAD_DIM ** (-0.5), cos_ref[rs, :], sin_ref[rs, :])


def attention_dq(lo, tables, queries, grad_att, lse, delta, keys, values):
    n_parts, rows, width = queries.shape
    heads = width // HEAD_DIM
    stack = pl.BlockSpec((n_parts, rows, HEAD_DIM), lambda h: (0, 0, h))
    first = pl.BlockSpec((1, rows, HEAD_DIM), lambda h: (0, 0, h))
    column = pl.BlockSpec((rows, HEAD_DIM), lambda h: (0, h))
    stat = pl.BlockSpec((1, rows, 1), lambda h: (h, 0, 0))
    table = pl.BlockSpec((rows, HEAD_DIM), lambda h: (0, 0))
    flops = 6 * rows * rows * n_parts * width
    return pl.pallas_call(
        dq_kernel,
        grid=(heads,),
        in_specs=[pl.BlockSpec((rows, 1), lambda h: (0, 0)), table, table]
        + [first, column, stat, stat, stack, stack],
        out_specs=column,
        out_shape=jax.ShapeDtypeStruct((rows, width), BF16),
        compiler_params=pltpu.CompilerParams(vmem_limit_bytes=48 << 20),
        cost_estimate=pl.CostEstimate(
            flops=flops, bytes_accessed=14 * rows * width * 2, transcendentals=flops // 768
        ),
        name="attention_dq",
    )(lo, *tables, queries, grad_att, lse, delta, keys, values)


def dkv_kernel(lo_ref, cos_ref, sin_ref, k_ref, v_ref, *refs):
    rows = k_ref.shape[1]
    q_refs, refs = refs[0], refs[1:]
    n_parts = q_refs.shape[0]
    do_refs, lse_refs, delta_refs = (refs[k * n_parts : (k + 1) * n_parts] for k in range(3))
    dk_ref, dv_ref = refs[-2:]
    scale = HEAD_DIM ** (-0.5) * LOG2E
    sub = rows // 2
    for start in range(0, rows, sub):
        rs = slice(start, start + sub)
        k, v = k_ref[0, rs, :], v_ref[0, rs, :]
        dk = jnp.zeros((sub, HEAD_DIM), F32)
        dv = jnp.zeros((sub, HEAD_DIM), F32)
        for d in range(n_parts):
            q, do = q_refs[d], do_refs[d][...]
            s = lax.dot_general(k, q, (((1,), (1,)), ((), ())), preferred_element_type=F32)
            u = lax.broadcasted_iota(jnp.int32, s.shape, 0) + start
            seen = u >= lo_ref[:, d * rows : (d + 1) * rows]
            if d == 0:
                seen = seen & (u <= lax.broadcasted_iota(jnp.int32, s.shape, 1))
            lse, delta = lse_refs[d][0], delta_refs[d][0]
            p = jnp.exp2(jnp.where(seen, s * scale - lse, MASKED))
            dv = dv + jnp.dot(p.astype(BF16), do, preferred_element_type=F32)
            dp = lax.dot_general(v, do, (((1,), (1,)), ((), ())), preferred_element_type=F32)
            ds = (p * (dp - delta)).astype(BF16)
            dk = dk + jnp.dot(ds, q, preferred_element_type=F32)
        dk_ref[rs, :] = turned_back(dk * HEAD_DIM ** (-0.5), cos_ref[rs, :], sin_ref[rs, :])
        dv_ref[rs, :] = dv.astype(BF16)


def attention_dkv(lo_row, tables, keys, values, queries, grad_atts, lses, deltas):
    n_parts, rows, width = keys.shape
    heads = width // HEAD_DIM
    stack = pl.BlockSpec((n_parts, rows, HEAD_DIM), lambda h: (0, 0, h))
    first = pl.BlockSpec((1, rows, HEAD_DIM), lambda h: (0, 0, h))
    column = pl.BlockSpec((rows, HEAD_DIM), lambda h: (0, h))
    stat = pl.BlockSpec((1, 1, rows), lambda h: (h, 0, 0))
    table = pl.BlockSpec((rows, HEAD_DIM), lambda h: (0, 0))
    flops = 8 * rows * rows * n_parts * width
    return pl.pallas_call(
        dkv_kernel,
        grid=(heads,),
        in_specs=[pl.BlockSpec((1, n_parts * rows), lambda h: (0, 0)), table, table]
        + [first, first, stack]
        + [column] * n_parts
        + [stat] * (2 * n_parts),
        out_specs=[column, column],
        out_shape=[jax.ShapeDtypeStruct((rows, width), BF16)] * 2,
        compiler_params=pltpu.CompilerParams(vmem_limit_bytes=48 << 20),
        cost_estimate=pl.CostEstimate(
            flops=flops, bytes_accessed=16 * rows * width * 2, transcendentals=flops // 1024
        ),
        name="attention_dkv",
    )(lo_row, *tables, keys, values, queries, *grad_atts, *lses, *deltas)


def forward_kernel(
    devices,
    cores,
    x_ref,
    gain_one_ref,
    gain_two_ref,
    cos_ref,
    sin_ref,
    lo_ref,
    valid_ref,
    wk_hbm,
    wv_hbm,
    wq_hbm,
    wo_hbm,
    prev_k_hbm,
    prev_v_hbm,
    k_out,
    v_out,
    q_out,
    one_keep_out,
    one_give_out,
    mid_out,
    two_out,
    two_keep_out,
    two_give_out,
    att_out,
    lse_out,
    row_out,
    kx,
    vx,
    qx,
    wk,
    wv,
    wq,
    wo,
    normed,
    flipped,
    tops,
    totals,
    acc,
    core_send,
    core_got,
    chip,
    y_got,
    own_half,
    other_half,
    mid,
    two_blocks,
    load_sem,
    store_sem,
    k_send,
    k_recv,
    v_send,
    v_recv,
    q_send,
    q_recv,
    sum_send,
    sum_recv,
):
    rows, width = x_ref.shape
    heads = kx.shape[2] // HEAD_DIM
    s, h = lax.axis_index("seq"), lax.axis_index("head")
    odd, core = lax.rem(s, 2), lax.rem(h, 2)
    pair = s + 1 - 2 * odd
    mate = h + 1 - 2 * core
    across = lax.rem(h + cores // 2, cores)
    has_left, has_right = s >= 2, s < devices - 2
    scale = HEAD_DIM ** (-0.5) * LOG2E

    def remote(src, dst, send, recv, seq, head):
        return pltpu.make_async_remote_copy(
            src_ref=src,
            dst_ref=dst,
            send_sem=send,
            recv_sem=recv,
            device_id=(seq, head),
            device_id_type=pl.DeviceIdType.MESH,
        )

    loads = [
        pltpu.make_async_copy(src, dst, load_sem.at[i])
        for i, (src, dst) in enumerate(((wk_hbm, wk), (wv_hbm, wv), (wq_hbm, wq), (wo_hbm, wo)))
    ]
    for load in loads:
        load.start()

    barrier = pltpu.get_barrier_semaphore()

    def greet(seq, head):
        pl.semaphore_signal(
            barrier, inc=1, device_id=(seq, head), device_id_type=pl.DeviceIdType.MESH
        )

    greet(pair, h)
    greet(s, mate)
    greet(s, across)

    @pl.when(has_left)
    def _():
        greet(s - 2, h)

    @pl.when(has_right)
    def _():
        greet(s + 2, h)

    step = rows // 4

    def normalize(i, _):
        at = pl.ds(pl.multiple_of(i * step, step), step)
        x = x_ref[at, :].astype(F32)
        root = lax.rsqrt(jnp.mean(x * x, axis=-1, keepdims=True) + EPS)
        normed[at, :] = (x * root * gain_one_ref[...]).astype(BF16)
        return 0

    lax.fori_loop(0, 4, normalize, 0)

    def turn_into(weight, out):
        raw = jnp.dot(normed[...], weight[...], preferred_element_type=F32)
        for k in range(heads):
            u = raw[:, k * HEAD_DIM : (k + 1) * HEAD_DIM]
            u = u * cos_ref[...] + pltpu.roll(u, HEAD_DIM // 2, 1) * sin_ref[...]
            out[0, :, k * HEAD_DIM : (k + 1) * HEAD_DIM] = u.astype(BF16)

    loads[0].wait()
    turn_into(wk, kx)

    inner = has_left & has_right

    @pl.when(inner)
    def _():
        pl.semaphore_wait(barrier, 5)

    @pl.when(jnp.logical_not(inner))
    def _():
        pl.semaphore_wait(barrier, 4)

    def hop(buf, send, recv, slot, seq, src, dst):
        return remote(buf.at[src], buf.at[dst], send.at[slot], recv.at[slot], seq, h)

    chains = {
        "k": (kx, k_send, k_recv, s + 2, has_right, has_left, 0),
        "v": (vx, v_send, v_recv, s + 2, has_right, has_left, 0),
        "q": (qx, q_send, q_recv, s - 2, has_left, has_right, 1),
    }

    def first_hops(name):
        buf, send, recv, seq, sends, gets, early = chains[name]

        @pl.when(sends)
        def _():
            hop(buf, send, recv, 0, seq, 0, 2).start()

        @pl.when(odd == early)
        def _():
            hop(buf, send, recv, 2, pair, 0, 1).start()

    def second_hops(name):
        buf, send, recv, seq, sends, gets, early = chains[name]

        @pl.when(gets)
        def _():
            hop(buf, send, recv, 0, seq, 0, 2).wait_recv()

        @pl.when(sends)
        def _():
            hop(buf, send, recv, 1, seq, 2, 4).start()

        @pl.when(odd == early)
        def _():
            hop(buf, send, recv, 3, pair, 2, 3).start()

        @pl.when(odd != early)
        def _():
            hop(buf, send, recv, 2, pair, 2, 1).start()

    def third_hops(name):
        buf, send, recv, seq, sends, gets, early = chains[name]

        @pl.when(gets)
        def _():
            hop(buf, send, recv, 1, seq, 2, 4).wait_recv()

        @pl.when(odd != early)
        def _():
            hop(buf, send, recv, 3, pair, 4, 3).start()

    def pair_arrived(name, slot):
        buf, send, recv, seq, sends, gets, early = chains[name]
        hop(buf, send, recv, slot, pair, 0, 1 if slot == 2 else 3).wait_recv()

    def all_sent(name):
        buf, send, recv, seq, sends, gets, early = chains[name]

        @pl.when(sends)
        def _():
            hop(buf, send, recv, 0, seq, 0, 2).wait_send()
            hop(buf, send, recv, 1, seq, 2, 4).wait_send()

        hop(buf, send, recv, 2, pair, 0, 1).wait_send()
        hop(buf, send, recv, 3, pair, 0, 3).wait_send()

    first_hops("k")
    loads[1].wait()
    vx[0] = jnp.dot(normed[...], wv[...], preferred_element_type=F32).astype(BF16)
    first_hops("v")

    @pl.when(jnp.logical_not(has_left))
    def _():
        copies = []
        for i, (src, dst) in enumerate(((prev_k_hbm, kx), (prev_v_hbm, vx))):
            for j, d in enumerate((2, 4)):
                at = pl.multiple_of((s - d) * rows + WINDOW, rows)
                copies.append(
                    pltpu.make_async_copy(
                        src.at[pl.ds(at, rows), :], dst.at[d], load_sem.at[4 + 2 * i + j]
                    )
                )
        for copy in copies:
            copy.start()
        for copy in copies:
            copy.wait()

    @pl.when(jnp.logical_not(has_right))
    def _():
        qx[2] = jnp.zeros_like(qx[2])
        qx[4] = jnp.zeros_like(qx[4])

    loads[2].wait()
    turn_into(wq, qx)
    first_hops("q")

    for i in range(4):
        flip_at = slice(i * step, (i + 1) * step)
        flipped[:, :, flip_at] = normed[flip_at, :].T.reshape(devices, width // devices, step)
    split = flipped.reshape(devices // 2, 2, width // devices, rows)
    stores = [
        pltpu.make_async_copy(split.at[:, odd], one_keep_out, store_sem.at[0]),
        pltpu.make_async_copy(split.at[:, 1 - odd], one_give_out, store_sem.at[1]),
    ]
    stores[0].start()
    stores[1].start()

    sub = rows // 2

    def attend(d):
        def body(i, _):
            k = i // 2
            at = pl.ds(pl.multiple_of((i % 2) * sub, sub), sub)
            lanes = pl.ds(pl.multiple_of(k * HEAD_DIM, HEAD_DIM), HEAD_DIM)
            scores = dot_nt(qx[0, at, lanes], kx[d, :, lanes])
            u = lax.broadcasted_iota(jnp.int32, scores.shape, 1) - d * rows
            seen = u >= lo_ref[at, :]
            if d == 0:
                t = lax.broadcasted_iota(jnp.int32, scores.shape, 0) + (i % 2) * sub
                seen = seen & (u <= t)
            scores = jnp.where(seen, scores * scale, MASKED)
            top = jnp.max(scores, axis=1, keepdims=True)
            if d > 0:
                old = tops[k, at, :]
                top = jnp.maximum(top, old)
            p = jnp.exp2(scores - top)
            total = jnp.sum(p, axis=1, keepdims=True)
            mixed = jnp.dot(p.astype(BF16), vx[d, :, lanes], preferred_element_type=F32)
            if d > 0:
                fade = jnp.exp2(old - top)
                total = total + totals[k, at, :] * fade
                mixed = mixed + acc[at, lanes] * fade
            tops[k, at, :] = top
            totals[k, at, :] = total
            acc[at, lanes] = mixed
            return 0

        lax.fori_loop(0, 2 * heads, body, 0)

    attend(0)
    second_hops("k")
    second_hops("v")
    attend(2)
    pair_arrived("k", 2)
    pair_arrived("v", 2)
    attend(1)
    third_hops("k")
    third_hops("v")
    attend(4)
    second_hops("q")
    pair_arrived("k", 3)
    pair_arrived("v", 3)
    attend(3)
    stores.append(pltpu.make_async_copy(kx, k_out, store_sem.at[2]))
    stores.append(pltpu.make_async_copy(vx, v_out, store_sem.at[3]))
    stores[2].start()
    stores[3].start()

    for k in range(heads):
        lanes = slice(k * HEAD_DIM, (k + 1) * HEAD_DIM)
        out = jnp.where(valid_ref[...] > 0, acc[:, lanes] / totals[k], 0.0)
        att_out[:, lanes] = out.astype(BF16)
        lse = tops[k] + jnp.log2(totals[k])
        lse_out[k] = lse
        row_out[k] = jnp.broadcast_to(lse, (rows, HEAD_DIM)).T[0:1, :]

    half = width // 2
    loads[3].wait()
    mine = pl.ds(pl.multiple_of(core * half, half), half)
    theirs = pl.ds(pl.multiple_of((1 - core) * half, half), half)

    def to_mate(i):
        return remote(core_send.at[i], core_got.at[i], sum_send.at[i], sum_recv.at[i], s, mate)

    def over(i):
        return remote(chip.at[i], y_got.at[i], sum_send.at[4 + i], sum_recv.at[4 + i], s, across)

    def back(i):
        return remote(
            own_half.at[i], other_half.at[i], sum_send.at[8 + i], sum_recv.at[8 + i], s, mate
        )

    for i in range(4):
        part = dot_nt(att_out[i * step : (i + 1) * step, :], wo[theirs, :])
        core_send[i] = part.astype(BF16)
        to_mate(i).start()
    for i in range(4):
        part = dot_nt(att_out[i * step : (i + 1) * step, :], wo[mine, :])
        to_mate(i).wait_recv()
        chip[i] = (part + core_got[i].astype(F32)).astype(BF16)
        over(i).start()
    third_hops("q")

    def finish(i):
        at = slice(i * step, (i + 1) * step)
        back(i).wait_recv()
        own, other = own_half[i].astype(F32), other_half[i].astype(F32)
        low = core == 0
        branch = jnp.concatenate([jnp.where(low, own, other), jnp.where(low, other, own)], axis=1)
        total = x_ref[at, :].astype(F32) + branch
        mid[at, :] = total
        root = lax.rsqrt(jnp.mean(total * total, axis=-1, keepdims=True) + EPS)
        two = (total * root * gain_two_ref[...]).astype(BF16)
        normed[at, :] = two
        depth = width // devices
        for j in range(devices):
            two_blocks[j, at, :] = two[:, j * depth : (j + 1) * depth]

    for i in range(4):
        over(i).wait_recv()
        own_half[i] = (chip[i].astype(F32) + y_got[i].astype(F32)).astype(BF16)
        back(i).start()
        if i > 0:
            finish(i - 1)
    finish(3)
    blocks = two_blocks.reshape(devices // 2, 2, rows, width // devices)
    for src, dst in (
        (mid, mid_out),
        (normed, two_out),
        (blocks.at[:, odd], two_keep_out),
        (blocks.at[:, 1 - odd], two_give_out),
    ):
        stores.append(pltpu.make_async_copy(src, dst, store_sem.at[len(stores)]))
        stores[-1].start()
    pair_arrived("q", 2)
    pair_arrived("q", 3)
    stores.append(pltpu.make_async_copy(qx, q_out, store_sem.at[len(stores)]))
    stores[-1].start()
    for name in chains:
        all_sent(name)
    for i in range(4):
        to_mate(i).wait_send()
        over(i).wait_send()
        back(i).wait_send()
    for store in stores:
        store.wait()


def forward(devices, cores, x, gains, tables, low, valid, weights, w_out, prevs):
    rows, width = x.shape
    cols = weights[0].shape[1]
    heads = cols // HEAD_DIM
    depth = width // devices
    parts = WINDOW // rows + 1
    step = rows // 4
    vmem = pl.BlockSpec(memory_space=pltpu.VMEM)
    hbm = pl.BlockSpec(memory_space=pl.ANY)

    def shape(*dims, dtype=BF16):
        return jax.ShapeDtypeStruct(dims, dtype)

    blocks = pltpu.VMEM((4, step, width // 2), BF16)
    dma = pltpu.SemaphoreType.DMA
    return pl.pallas_call(
        functools.partial(forward_kernel, devices, cores),
        in_specs=[vmem] * 7 + [hbm] * 6,
        out_specs=[hbm] * 9 + [vmem] * 3,
        out_shape=[
            shape(parts, rows, cols),
            shape(parts, rows, cols),
            shape(parts, rows, cols),
            shape(devices // 2, depth, rows),
            shape(devices // 2, depth, rows),
            shape(rows, width, dtype=F32),
            shape(rows, width),
            shape(devices // 2, rows, depth),
            shape(devices // 2, rows, depth),
            shape(rows, cols),
            shape(heads, rows, 1, dtype=F32),
            shape(heads, 1, rows, dtype=F32),
        ],
        scratch_shapes=[pltpu.VMEM((parts, rows, cols), BF16)] * 3
        + [pltpu.VMEM((width, cols), BF16)] * 4
        + [
            pltpu.VMEM((rows, width), BF16),
            pltpu.VMEM((devices, depth, rows), BF16),
            pltpu.VMEM((heads, rows, 1), F32),
            pltpu.VMEM((heads, rows, 1), F32),
            pltpu.VMEM((rows, cols), F32),
        ]
        + [blocks] * 6
        + [
            pltpu.VMEM((rows, width), F32),
            pltpu.VMEM((devices, rows, depth), BF16),
            dma((8,)),
            dma((9,)),
        ]
        + [dma((4,))] * 6
        + [dma((12,))] * 2,
        compiler_params=pltpu.CompilerParams(
            collective_id=0, has_side_effects=True, vmem_limit_bytes=56 << 20
        ),
        cost_estimate=cost(10 * rows * width * cols, 40 << 20),
        name="forward",
    )(x, *gains, *tables, low, valid, *weights, w_out, *prevs)


def first_key(rows, lengths, total):
    padded = (lengths + PAD - 1) // PAD * PAD
    starts = jnp.cumsum(padded) - padded
    start_row = jnp.zeros_like(rows)
    length_row = jnp.full_like(rows, 0) + lengths[0]
    low_row = jnp.full_like(rows, -BIG)
    for r in range(1, NSEQ):
        inside = rows >= starts[r]
        start_row = jnp.where(inside, starts[r], start_row)
        low_row = jnp.where(inside, starts[r], low_row)
        length_row = jnp.where(inside, lengths[r], length_row)
    position = rows - start_row
    valid = position < length_row
    low = jnp.where(valid, jnp.maximum(low_row, rows - (WINDOW - 1)), rows)
    low = jnp.where(rows < total, low, BIG)
    return low, valid, position


def on_device(
    tokens,
    gain_attn,
    gain_mlp,
    w_query,
    w_key,
    w_value,
    w_out,
    w_gate,
    w_up,
    w_down,
    prev_keys,
    prev_values,
    lengths,
    out_grad,
):
    rows = tokens.shape[0]
    width = w_query.shape[1]
    heads = width // HEAD_DIM
    devices = lax.axis_size("seq")
    index = lax.axis_index("seq")
    odd = (index & 1) == 1
    first_row = index * rows
    far = WINDOW // rows
    low, valid, position = first_key(
        first_row + jnp.arange((far + 1) * rows, dtype=jnp.int32), lengths, devices * rows
    )
    low = low - first_row
    low_col = low[:rows, None]
    low_row = low[None, :]
    valid_col = valid[:rows, None]
    valid_int = valid_col.astype(jnp.int32)
    half = HEAD_DIM // 2
    freq = jnp.exp(-math.log(10000.0) * (2.0 * jnp.arange(half, dtype=F32) / HEAD_DIM))
    angle = position[:rows].astype(F32)[:, None] * freq[None, :]
    cos_one, sin_one = jnp.cos(angle), jnp.sin(angle)
    tables = (
        jnp.concatenate([cos_one, cos_one], axis=1),
        jnp.concatenate([-sin_one, sin_one], axis=1),
    )
    bits = jnp.stack([index & 1, lax.axis_index("head") & 1]).astype(jnp.int32)
    gain_one, gain_two = gain_attn[None, :], gain_mlp[None, :]

    (
        keys,
        values,
        queries,
        one_keep,
        one_give,
        mid,
        normed_two,
        two_keep,
        two_give,
        attended,
        lse,
        lse_row,
    ) = forward(
        devices,
        lax.axis_size("head"),
        tokens,
        (gain_one, gain_two),
        tables,
        low_col,
        valid_int,
        (w_key, w_value, w_query),
        w_out,
        (prev_keys, prev_values),
    )

    def lent(own):
        two = shifted(own, -2)
        one = swap(jnp.where(odd, own, two), "seq", 1)
        four = shifted(two, -2)
        three = swap(jnp.where(odd, two, four), "seq", 1)
        return [own, one, two, three, four]

    one_pair = (one_keep, swap(one_give, "seq", 1))
    out_keep, out_give = by_rows(split_kernel, bits, (out_grad,), -1, (), "split", "split")
    out_pair = (out_keep, swap(out_give, "seq", 1))

    lses_lent = lent(lse_row)
    two_pair = (two_keep, swap(two_give, "seq", 1))
    act, grad_gate, grad_up, norm_keep, norm_give, branch_keep, branch_give = mlp(
        bits, normed_two, out_grad, w_gate.T, w_up.T, w_down.T
    )
    own, other = head_sum_of(norm_give, norm_keep)
    w_down_grad = weight_grad(out_pair, act, "down", True)
    w_gate_grad = weight_grad(two_pair, grad_gate, "gate", True)
    w_up_grad = weight_grad(two_pair, grad_up, "up", True)

    grad_mid, gain_mlp_part, grad_attn_branch, mid_keep, mid_give = by_rows(
        back_kernel,
        bits,
        (mid, own, other, gain_two, out_grad),
        3,
        (F32, F32, BF16),
        "flip",
        "mid_back",
        part=1,
    )
    mid_pair = (mid_keep, swap(mid_give, "seq", 1))
    own, other = head_sum_of(branch_give, branch_keep)
    low_half = bits[1] == 0
    branch = jnp.concatenate(
        [jnp.where(low_half, own, other), jnp.where(low_half, other, own)], axis=1
    )
    block_out = (mid + branch.astype(F32)).astype(BF16)

    grad_att, delta, delta_row = out_back(valid_int, grad_attn_branch, w_out, attended)
    grad_atts = lent(grad_att)
    deltas_lent = lent(delta_row)
    grad_query_raw = attention_dq(low_col, tables, queries, grad_att, lse, delta, keys, values)
    grad_key_raw, grad_value_raw = attention_dkv(
        low_row, tables, keys, values, queries, grad_atts, lses_lent, deltas_lent
    )

    w_out_grad = weight_grad(mid_pair, attended, "wout")
    w_query_grad = weight_grad(one_pair, grad_query_raw, "query")
    w_key_grad = weight_grad(one_pair, grad_key_raw, "key")
    w_value_grad = weight_grad(one_pair, grad_value_raw, "value")
    own, other = head_sum(
        bits,
        (grad_query_raw, grad_key_raw, grad_value_raw),
        (w_query, w_key, w_value),
        "norm_one",
    )
    tokens_grad, gain_attn_part = by_rows(
        back_kernel,
        bits,
        (tokens, own, other, gain_one, grad_mid),
        3,
        (BF16, F32),
        False,
        "tokens_back",
        part=1,
    )
    gains = gain_sum(jnp.concatenate([gain_attn_part, gain_mlp_part], axis=0))
    gain_attn_grad, gain_mlp_grad = gains[0], gains[1]
    return (
        block_out,
        tokens_grad,
        gain_attn_grad,
        gain_mlp_grad,
        w_query_grad,
        w_key_grad,
        w_value_grad,
        w_out_grad,
        w_gate_grad,
        w_up_grad,
        w_down_grad,
    )


def solution(mesh):
    by_head = P(None, "head")
    both = P("seq", "head")
    placed = (P("seq", None), P(), P()) + (by_head,) * 9 + (P(), P("seq", None))
    return jax.shard_map(
        on_device,
        mesh=mesh,
        in_specs=placed,
        out_specs=(P("seq", None), P("seq", None), P("seq"), P("seq")) + (both,) * 7,
        check_vma=False,
    )
```

time: 711 us -> 596 us (0.84)
  Pallas kernels: 45.5 us -> 242 us
  local copies, waits for them, and re-layouts: 128 us -> 12.8 us
  matrix products: 74.3 us -> 0 us
  other arithmetic: 111 us -> 42 us
  starting transfers between devices: 114 us -> 49.9 us
  waiting for transfers between devices: 226 us -> 244 us
    pallas_call x1 -> x22, Pallas kernels: 11.4 us -> 208 us  [the longest x1 110 us: forward(): pl.pallas_call(functools.partial(forward_kernel, devices, cores), in_spec...]
    dot_general x19 -> x0, matrix products: 66.3 us -> none  [the longest x7 29.9 us: outer_sum(): lax.dot_general(left, right, (((0,), (0,)), ((), ())), preferred_element_...]
    ppermute x53 -> x43, starting transfers between devices: 85.3 us -> 42.2 us  [swap(): lax.ppermute(block, axis, [(i, i ^ bit) for i in range(lax.axis_size(axis...]
    dynamic_slice x10 -> x0, local copies, waits for them, and re-layouts: 37.8 us -> none  [the longest x3 25.3 us: scatter_sum(): keep = lax.dynamic_index_in_dim(view, mine, 1, keepdims=False)]
    reshape x6 -> x0, local copies, waits for them, and re-layouts: 36.8 us -> none  [the longest x3 23.1 us: scatter_sum(): view = part.reshape(shares, 2, rows // (n // 2), cols)]
    convert_element_type x22 -> x6, other arithmetic: 45.1 us -> 11.2 us  [the longest x2 5.26 us: head_sum_of(): chip = (keep.astype(F32) + swap(give, 'head', 1).astype(F32)).astype(BF16)]
    ppermute x10 -> x6, waiting for transfers between devices: 18.5 us -> 49.7 us  [shifted(): lax.ppermute(block, 'seq', [(i, i + distance) for i in range(n) if 0 <= i...]
    ppermute x10 -> x6, starting transfers between devices: 28.6 us -> 7.7 us  [shifted(): lax.ppermute(block, 'seq', [(i, i + distance) for i in range(n) if 0 <= i...]
  transfers between devices with their start and end apart: 63 -> 49, of which waited for: 24 -> 20; matrix products, arithmetic and copies ran while one was open for 39% -> 5% of each run, Pallas kernels for 5% -> 17%
where the time goes in v2:
time: 596 us; the launch traced here: 592 us
  waiting for transfers between devices  244 us (41%)
  Pallas kernels  242 us (41%)
  starting transfers between devices  49.9 us (8%)
  other arithmetic  42 us (7%)
  local copies, waits for them, and re-layouts  12.8 us (2%)
    ppermute x43, waiting for transfers between devices, swap(): lax.ppermute(block, axis, [(i, i ^ bit) for i in range(lax.axis_size(axis...  194 us
    pallas_call x1, Pallas kernels, forward(): pl.pallas_call(functools.partial(forward_kernel, devices, cores), in_spec...  110 us
    ppermute x6, waiting for transfers between devices, shifted(): lax.ppermute(block, 'seq', [(i, i + distance) for i in range(n) if 0 <= i...  49.7 us
    ppermute x43, starting transfers between devices, swap(): lax.ppermute(block, axis, [(i, i ^ bit) for i in range(lax.axis_size(axis...  42.2 us
    pallas_call x14, Pallas kernels, grad_blocks(): pl.pallas_call(kernel, grid_spec=pltpu.PrefetchScalarGridSpec(num_scalar_...  39.1 us
    pallas_call x1, Pallas kernels, mlp(): pl.pallas_call(mlp_kernel, grid_spec=pltpu.PrefetchScalarGridSpec(num_sca...  31.2 us
    pallas_call x1, Pallas kernels, attention_dkv(): pl.pallas_call(dkv_kernel, grid=(heads,), in_specs=[pl.BlockSpec((1, n_pa...  19.4 us
    pallas_call x3, Pallas kernels, by_rows(): pl.pallas_call(kernel, grid_spec=pltpu.PrefetchScalarGridSpec(num_scalar_...  16.8 us
  transfers between devices with their start and end apart: 49, of which 20 were waited for; matrix products, arithmetic and copies ran while one was open for 5% of the time, Pallas kernels for 17%

profile of v2, /device:TPU:0, one launch (start us, length us, event | category | flops | bytes accessed | tf_op | source)
XLA Modules:
  0.0 591.6 jit_solution(3438590825846976644)
XLA Ops:
  1.3 1.5 fusion.16
  4.9 1.9 select_subtract_fusion
  6.8 4.4 select_compare_fusion
  17.6 109.8 %forward.1 = (bf16[5,512,512]{2,1,0:T(8,128)(2,1)}, bf16[5,512,512]{2,1,0:T(8,128)(2,1)}, bf16[5,512,512]{2,1,0:T(8,128)(2,1)}, bf16[4,256,512]{2,1,0:T(8,128)(2...) custom-call(bf16[512,2048]{1,0:T(8,128)(2,1)} %x_ref.4, ...), custom_call_target="tpu_custom_call" | custom-call | flops 5368709120 | bytes 41943040 | tf_op jit(solution)/shard_map/forward/pallas_call | solution.py:948
  127.5 31.2 %mlp.1 = (bf16[1376,512]{1,0:T(8,128)(2,1)}, bf16[1376,512]{1,0:T(8,128)(2,1)}, bf16[1376,512]{1,0:T(8,128)(2,1)}, bf16[512,1024]{1,0:T(8,128)(2,1)}, bf16[512,1...) custom-call(s32[2]{0:T(128)} %pad_add_fusion.bits_ref, ...), custom_call_target="tpu_custom_call" | custom-call | flops 17314086912 | bytes 16908288 | tf_op jit(solution)/shard_map/mlp/pallas_call | solution.py:307
  159.8 2.5 collective-permute-done.3
  162.3 2.6 add_convert_fusion.3
  165.4 2.2 split.1
  167.6 2.0 collective-permute-start.45
  170.9 4.2 collective-permute-done.10.refs_8_
  175.4 15.2 %collective-permute-done.4 = bf16[512,1024]{1,0:T(8,128)(2,1)} collective-permute-done((bf16[512,1024]{1,0:T(8,128)(2,1)}, bf16[512,1024]{1,0:T(8,128)(2,1)}, u32[]{:S(2)}, u32[]{:S(2)}) %collective-permute-start.4) | collective-permute-done | bytes 1048608 | tf_op jit(solution)/shard_map/ppermute | solution.py:24
  190.6 1.9 add_convert_fusion.2.own_ref
  192.6 29.3 %collective-permute-done.45.refs_1_ = bf16[4,512,256]{2,1,0:T(8,128)(2,1)} collective-permute-done((bf16[4,512,256]{2,1,0:T(8,128)(2,1)}, bf16[4,512,256]{2,1,0:T(8,128)(2,1)}, u32[]{:S(2)}, u32[]{:S(2)}) %collective-permute-start.45) | collective-permute-done | bytes 1048608 | tf_op jit(solution)/shard_map/ppermute | solution.py:24
  223.5 5.2 down_give.1
  228.8 2.7 add_convert_fusion.5
  231.4 43.1 %collective-permute-done.38.refs_1_ = bf16[4,512,256]{2,1,0:T(8,128)(2,1)S(1)} collective-permute-done((bf16[4,512,256]{2,1,0:T(8,128)(2,1)}, bf16[4,512,256]{2,1,0:T(8,128)(2,1)S(1)}, u32[]{:S(2)}, u32[]{:S(2)}) %collective-permute-start.38) | collective-permute-done | bytes 1048608 | tf_op jit(solution)/shard_map/ppermute | solution.py:24
  274.5 1.5 collective-permute-start.1
  277.3 5.0 up_give.1
  282.3 2.6 collective-permute-start.43
  285.0 8.0 %mid_back.1 = (f32[512,2048]{1,0:T(8,128)}, f32[1,2048]{1,0:T(1,128)S(1)}, bf16[512,2048]{1,0:T(8,128)(2,1)}, bf16[4,256,512]{2,1,0:T(8,128)(2,1)S(1)}, bf16[4,256,512]{2,1,0:T(8,128)(2,1)S(1)}) custom-call(s32[2]{0:T(128)S(1)} %copy-done.23, f32[512,2048]{1,0:T(8,128)} %get-tuple-element.44.x_ref, bf16[512,1024]{1,0:T(8,128)(2,1)S(1)} %add_convert_fusion.2.own_ref, ...), custom_call_target="tpu_custom_call" | custom-call | flops 10485760 | bytes 20971520 | tf_op jit(solution)/shard_map/mid_back/pallas_call | solution.py:146
  294.9 1.6 copy-done.18
  296.5 3.7 out_back.1
  303.7 4.5 fusion.5.lo_ref
  309.0 16.4 %collective-permute-done.6.refs_3_ = bf16[512,512]{1,0:T(8,128)(2,1)} collective-permute-done((bf16[512,512]{1,0:T(8,128)(2,1)}, bf16[512,512]{1,0:T(8,128)(2,1)}, u32[]{:S(2)}, u32[]{:S(2)}) %collective-permute-start.6) | collective-permute-done | bytes 524320 | tf_op jit(solution)/shard_map/ppermute | solution.py:29
  326.7 4.6 gate_give.1
  331.3 2.7 collective-permute-start.40
  334.0 1.9 add_convert_fusion.4
  337.3 4.1 down_keep.1
  341.4 27.5 %collective-permute-done.14.refs_13_ = f32[4,1,512]{2,1,0:T(1,128)S(1)} collective-permute-done((f32[4,1,512]{2,1,0:T(1,128)S(1)}, f32[4,1,512]{2,1,0:T(1,128)S(1)}, u32[]{:S(2)}, u32[]{:S(2)}) %collective-permute-start.14) | collective-permute-done | bytes 8224 | tf_op jit(solution)/shard_map/ppermute | solution.py:29
  371.3 1.5 collective-permute-start.7
  372.8 1.6 collective-permute-done.16.refs_15_
  377.8 4.6 up_keep.1
  383.4 9.9 %collective-permute-done.13.refs_9_ = f32[4,1,512]{2,1,0:T(1,128)S(1)} collective-permute-done((f32[4,1,512]{2,1,0:T(1,128)S(1)}, f32[4,1,512]{2,1,0:T(1,128)S(1)}, u32[]{:S(2)}, u32[]{:S(2)}) %collective-permute-start.13) | collective-permute-done | bytes 8224 | tf_op jit(solution)/shard_map/ppermute | solution.py:24
  393.4 1.7 collective-permute-start.17
  395.2 13.7 %attention_dq.1.refs_0_.refs_2_ = bf16[512,512]{1,0:T(8,128)(2,1)S(1)} custom-call(s32[512,1]{1,0:T(8,128)S(1)} %copy-done.22, f32[512,128]{1,0:T(8,128)S(1)} %copy-done.21, f32[512,128]{1,0:T(8,128)S(1)} %copy-done.20, bf16[5,512,512]{2,1,0:T(8,128)(2,1)} %get-tuple-element.48.q_ref.refs_0_, bf16[512,512]{1,0:T(8,128)(2,1)} %get-tuple-element.53.do_ref.refs_1_, ...), custom_call_target="tpu_custom_call" | custom-call | flops 4026531840 | bytes 7340032 | tf_op jit(solution)/shard_map/attention_dq/pallas_call | solution.py:489
  410.6 1.6 collective-permute-start.44
  412.2 19.4 %attention_dkv.1 = (bf16[512,512]{1,0:T(8,128)(2,1)S(1)}, bf16[512,512]{1,0:T(8,128)(2,1)S(1)}) custom-call(s32[1,2560]{1,0:T(1,128)S(1)} %fusion.5.lo_ref, f32[512,128]{1,0:T(8,128)S(1)} %copy-done.21, f32[512,128]{1,0:T(8,128)S(1)} %copy-done.20, bf16[5,512,512]{2,1,0:T(8,128)(2,1)} %get-tuple-element.56.k_refs.k_ref, ...), custom_call_target="tpu_custom_call" | custom-call | flops 5368709120 | bytes 8388608 | tf_op jit(solution)/shard_map/attention_dkv/pallas_call | solution.py:543
  431.6 3.9 norm_one_give.1
  435.6 4.0 gate_keep.1
  439.7 1.8 collective-permute-start.25
  442.9 2.0 add_convert_fusion
  444.9 1.5 collective-permute-start.34
  446.4 3.9 norm_one_keep.1
  450.3 8.8 %collective-permute-done.48 = bf16[1,1376,256]{2,1,0:T(8,128)(2,1)} collective-permute-done((bf16[1,1376,256]{2,1,0:T(8,128)(2,1)S(1)}, bf16[1,1376,256]{2,1,0:T(8,128)(2,1)}, u32[]{:S(2)}, u32[]{:S(2)}) %collective-permute-start.48) | collective-permute-done | bytes 704544 | tf_op jit(solution)/shard_map/ppermute | solution.py:24
  459.6 2.3 add_bitcast_fusion
  462.0 1.8 collective-permute-start.35
  463.8 1.6 query_give.1
  465.5 23.8 %collective-permute-done.44 = bf16[1,1376,256]{2,1,0:T(8,128)(2,1)} collective-permute-done((bf16[1,1376,256]{2,1,0:T(8,128)(2,1)}, bf16[1,1376,256]{2,1,0:T(8,128)(2,1)}, u32[]{:S(2)}, u32[]{:S(2)}) %collective-permute-start.44) | collective-permute-done | bytes 704544 | tf_op jit(solution)/shard_map/ppermute | solution.py:24
  489.3 2.4 add_bitcast_fusion.1
  491.7 22.8 %collective-permute-done.26.refs_4_ = bf16[2,256,512]{2,1,0:T(8,128)(2,1)S(1)} collective-permute-done((bf16[2,256,512]{2,1,0:T(8,128)(2,1)S(1)}, bf16[2,256,512]{2,1,0:T(8,128)(2,1)S(1)}, u32[]{:S(2)}, u32[]{:S(2)}) %collective-permute-start.26) | collective-permute-done | bytes 524320 | tf_op jit(solution)/shard_map/ppermute | solution.py:24
  517.9 2.5 collective-permute-start.36
  520.4 1.7 collective-permute-start.31
  524.2 13.5 %collective-permute-done.36.refs_4_ = bf16[2,256,512]{2,1,0:T(8,128)(2,1)S(1)} collective-permute-done((bf16[2,256,512]{2,1,0:T(8,128)(2,1)S(1)}, bf16[2,256,512]{2,1,0:T(8,128)(2,1)S(1)}, u32[]{:S(2)}, u32[]{:S(2)}) %collective-permute-start.36) | collective-permute-done | bytes 524320 | tf_op jit(solution)/shard_map/ppermute | solution.py:24
  540.8 2.2 collective-permute-start.32
  546.8 5.5 collective-permute-done.37
  553.2 8.2 %collective-permute-done.32.refs_4_ = bf16[2,256,512]{2,1,0:T(8,128)(2,1)S(1)} collective-permute-done((bf16[2,256,512]{2,1,0:T(8,128)(2,1)S(1)}, bf16[2,256,512]{2,1,0:T(8,128)(2,1)S(1)}, u32[]{:S(2)}, u32[]{:S(2)}) %collective-permute-start.32) | collective-permute-done | bytes 524320 | tf_op jit(solution)/shard_map/ppermute | solution.py:24
  561.3 1.4 value_keep.1
  563.2 6.6 %tokens_back.1 = (bf16[512,2048]{1,0:T(8,128)(2,1)}, f32[1,2048]{1,0:T(1,128)S(1)}) custom-call(s32[2]{0:T(128)S(1)} %copy-done.23, bf16[512,2048]{1,0:T(8,128)(2,1)S(1)} %copy-done.17, bf16[512,1024]{1,0:T(8,128)(2,1)S(1)} %add_convert_fusion.1.own_ref, bf16[512,1024]{1,0:T(8,128)(2,1)S(1)} %collective-permute-done.20.other_ref, f32[1,2048]{1,0:T(1,128)S(1)} %bitcast.45, ...), custom_call_target="tpu_custom_call" | custom-call | flops 10485760 | bytes 14680064 | tf_op jit(solution)/shard_map/tokens_back/pallas_call | solution.py:146
  569.8 1.7 collective-permute-start.21
  571.6 4.8 collective-permute-done.29.refs_4_
  576.4 1.4 key_keep.1
  578.2 2.5 collective-permute-start.22
  582.5 3.0 collective-permute-start.23
  585.5 4.5 collective-permute-done.30
  (187 shorter events, 51.7 us)
Async XLA Ops:
  158.7 3.6 collective-permute-start.3
  164.9 25.8 %collective-permute-start.4 = (bf16[512,1024]{1,0:T(8,128)(2,1)}, bf16[512,1024]{1,0:T(8,128)(2,1)}, u32[]{:S(2)}, u32[]{:S(2)}) collective-permute-start(bf16[512,1024]{1,0:T(8,128)(2,1)} %add_convert_fusion.3), channel_id=1, source_target_pairs={{0,2},{1,3},{2,0},{3,1},{4,6},{5,7},{6,4},{7,5},{8,10},{9,11},{10,... | collective-permute-start | bytes 3145736 | tf_op jit(solution)/shard_map/ppermute | solution.py:24
  165.4 56.5 %collective-permute-start.46 = (bf16[1376,512]{1,0:T(8,128)(2,1)}, bf16[1376,512]{1,0:T(8,128)(2,1)}, u32[]{:S(2)}, u32[]{:S(2)}) collective-permute-start(bf16[1376,512]{1,0:T(8,128)(2,1)} %get-tuple-element.76.refs_2_), channel_id=1, source_target_pairs={{0,4},{4,0},{8,12},{12,8},{16,20},{20,16},{24,28},{28,24},{1,5},{5... | collective-permute-start | bytes 4227080 | tf_op jit(solution)/shard_map/ppermute | solution.py:24
  167.6 54.5 %copy-start.15 = (bf16[4,512,256]{2,1,0:T(8,128)(2,1)}, bf16[4,512,256]{2,1,0:T(8,128)(2,1)S(1)}, u32[]{:S(2)}) copy-start(bf16[4,512,256]{2,1,0:T(8,128)(2,1)S(1)} %get-tuple-element.74.refs_0_) | copy-start | bytes 3145732
  167.6 54.3 %copy-start.38 = (s32[4]{0:T(128)S(1)}, s32[4]{0:T(128)}, u32[]{:S(2)}) copy-start(s32[4]{0:T(128)} %constant.83.clone) | copy-start | bytes 52
  167.6 54.4 %copy-start.4 = (bf16[1376,512]{1,0:T(8,128)(2,1)S(1)}, bf16[1376,512]{1,0:T(8,128)(2,1)}, u32[]{:S(2)}) copy-start(bf16[1376,512]{1,0:T(8,128)(2,1)} %get-tuple-element.72.refs_2_) | copy-start | bytes 4227076
  167.6 54.3 %collective-permute-start.45 = (bf16[4,512,256]{2,1,0:T(8,128)(2,1)}, bf16[4,512,256]{2,1,0:T(8,128)(2,1)}, u32[]{:S(2)}, u32[]{:S(2)}) collective-permute-start(bf16[4,512,256]{2,1,0:T(8,128)(2,1)} %get-tuple-element.75), channel_id=1, source_target_pairs={{0,4},{4,0},{8,12},{12,8},{16,20},{20,16},{24,28},{28,24},{1,5},{5... | collective-permute-start | bytes 3145736 | tf_op jit(solution)/shard_map/ppermute | solution.py:24
  169.6 59.0 %collective-permute-start = (bf16[512,1024]{1,0:T(8,128)(2,1)}, bf16[512,1024]{1,0:T(8,128)(2,1)}, u32[]{:S(2)}, u32[]{:S(2)}) collective-permute-start(bf16[512,1024]{1,0:T(8,128)(2,1)} %get-tuple-element.47), channel_id=1, source_target_pairs={{0,1},{1,0},{2,3},{3,2},{4,5},{5,4},{6,7},{7,6},{8,9},{9,8},{10,11... | collective-permute-start | bytes 3145736 | tf_op jit(solution)/shard_map/ppermute | solution.py:24
  169.6 5.5 collective-permute-start.10
  175.2 100.8 %collective-permute-start.42 = (bf16[1376,512]{1,0:T(8,128)(2,1)}, bf16[1376,512]{1,0:T(8,128)(2,1)}, u32[]{:S(2)}, u32[]{:S(2)}) collective-permute-start(bf16[1376,512]{1,0:T(8,128)(2,1)} %get-tuple-element.73.refs_2_), channel_id=1, source_target_pairs={{0,4},{4,0},{8,12},{12,8},{16,20},{20,16},{24,28},{28,24},{1,5},{5... | collective-permute-start | bytes 4227080 | tf_op jit(solution)/shard_map/ppermute | solution.py:24
  190.6 83.9 %collective-permute-start.38 = (bf16[4,512,256]{2,1,0:T(8,128)(2,1)}, bf16[4,512,256]{2,1,0:T(8,128)(2,1)S(1)}, u32[]{:S(2)}, u32[]{:S(2)}) collective-permute-start(bf16[4,512,256]{2,1,0:T(8,128)(2,1)} %get-tuple-element.71), channel_id=1, source_target_pairs={{0,4},{4,0},{8,12},{12,8},{16,20},{20,16},{24,28},{28,24},{1,5},{5... | collective-permute-start | bytes 3145736 | tf_op jit(solution)/shard_map/ppermute | solution.py:24
  221.9 60.4 %collective-permute-start.5 = (bf16[512,1024]{1,0:T(8,128)(2,1)S(1)}, bf16[512,1024]{1,0:T(8,128)(2,1)S(1)}, u32[]{:S(2)}, u32[]{:S(2)}) collective-permute-start(bf16[512,1024]{1,0:T(8,128)(2,1)S(1)} %add_convert_fusion.2.own_ref), channel_id=1, source_target_pairs={{0,1},{1,0},{2,3},{3,2},{4,5},{5,4},{6,7},{7,6},{8,9},{9,8},{10,11... | collective-permute-start | bytes 3145736 | tf_op jit(solution)/shard_map/ppermute | solution.py:24
  222.0 87.0 %collective-permute-start.39 = (bf16[1376,512]{1,0:T(8,128)(2,1)S(1)}, bf16[1376,512]{1,0:T(8,128)(2,1)}, u32[]{:S(2)}, u32[]{:S(2)}) collective-permute-start(bf16[1376,512]{1,0:T(8,128)(2,1)S(1)} %copy-done.4), channel_id=1, source_target_pairs={{0,4},{4,0},{8,12},{12,8},{16,20},{20,16},{24,28},{28,24},{1,5},{5... | collective-permute-start | bytes 4227080 | tf_op jit(solution)/shard_map/ppermute | solution.py:24
  228.6 48.7 %copy-start.1 = (bf16[4,512,256]{2,1,0:T(8,128)(2,1)S(1)}, bf16[4,512,256]{2,1,0:T(8,128)(2,1)}, u32[]{:S(2)}) copy-start(bf16[4,512,256]{2,1,0:T(8,128)(2,1)} %get-tuple-element.70.refs_0_) | copy-start | bytes 3145732
  228.7 107.3 %collective-permute-start.47 = (bf16[2,1376,256]{2,1,0:T(8,128)(2,1)}, bf16[2,1376,256]{2,1,0:T(8,128)(2,1)}, u32[]{:S(2)}, u32[]{:S(2)}) collective-permute-start(bf16[2,1376,256]{2,1,0:T(8,128)(2,1)} %down_give.1), channel_id=1, source_target_pairs={{0,8},{4,12},{8,0},{12,4},{16,24},{20,28},{24,16},{28,20},{1,9},{5... | collective-permute-start | bytes 4227080 | tf_op jit(solution)/shard_map/ppermute | solution.py:24
  274.5 56.8 %collective-permute-start.1 = (bf16[512,1024]{1,0:T(8,128)(2,1)}, bf16[512,1024]{1,0:T(8,128)(2,1)}, u32[]{:S(2)}, u32[]{:S(2)}) collective-permute-start(bf16[512,1024]{1,0:T(8,128)(2,1)} %add_convert_fusion.5), channel_id=1, source_target_pairs={{0,2},{1,3},{2,0},{3,1},{4,6},{5,7},{6,4},{7,5},{8,10},{9,11},{10,... | collective-permute-start | bytes 3145736 | tf_op jit(solution)/shard_map/ppermute | solution.py:24
  276.0 25.8 %collective-permute-start.12 = (f32[4,1,512]{2,1,0:T(1,128)S(1)}, f32[4,1,512]{2,1,0:T(1,128)S(1)}, u32[]{:S(2)}, u32[]{:S(2)}) collective-permute-start(f32[4,1,512]{2,1,0:T(1,128)S(1)} %collective-permute-done.10.refs_8_), channel_id=1, source_target_pairs={{8,0},{12,4},{16,8},{20,12},{24,16},{28,20},{9,1},{13,5},{17,9},{2... | collective-permute-start | bytes 24584 | tf_op jit(solution)/shard_map/ppermute | solution.py:29
  282.3 94.2 %collective-permute-start.43 = (bf16[2,1376,256]{2,1,0:T(8,128)(2,1)}, bf16[2,1376,256]{2,1,0:T(8,128)(2,1)}, u32[]{:S(2)}, u32[]{:S(2)}) collective-permute-start(bf16[2,1376,256]{2,1,0:T(8,128)(2,1)} %up_give.1), channel_id=1, source_target_pairs={{0,8},{4,12},{8,0},{12,4},{16,24},{20,28},{24,16},{28,20},{1,9},{5... | collective-permute-start | bytes 4227080 | tf_op jit(solution)/shard_map/ppermute | solution.py:24
  302.4 23.0 %collective-permute-start.6 = (bf16[512,512]{1,0:T(8,128)(2,1)}, bf16[512,512]{1,0:T(8,128)(2,1)}, u32[]{:S(2)}, u32[]{:S(2)}) collective-permute-start(bf16[512,512]{1,0:T(8,128)(2,1)} %get-tuple-element.53.do_ref.refs_1_), channel_id=1, source_target_pairs={{8,0},{12,4},{16,8},{20,12},{24,16},{28,20},{9,1},{13,5},{17,9},{2... | collective-permute-start | bytes 1572872 | tf_op jit(solution)/shard_map/ppermute | solution.py:29
  308.9 66.7 %collective-permute-start.11 = (f32[4,1,512]{2,1,0:T(1,128)S(1)}, f32[4,1,512]{2,1,0:T(1,128)S(1)}, u32[]{:S(2)}, u32[]{:S(2)}) collective-permute-start(f32[4,1,512]{2,1,0:T(1,128)S(1)} %get-tuple-element.84), channel_id=1, source_target_pairs={{0,4},{4,0},{8,12},{12,8},{16,20},{20,16},{24,28},{28,24},{1,5},{5... | collective-permute-start | bytes 24584 | tf_op jit(solution)/shard_map/ppermute | solution.py:24
  325.4 44.8 %collective-permute-start.8 = (bf16[512,512]{1,0:T(8,128)(2,1)}, bf16[512,512]{1,0:T(8,128)(2,1)S(1)}, u32[]{:S(2)}, u32[]{:S(2)}) collective-permute-start(bf16[512,512]{1,0:T(8,128)(2,1)} %collective-permute-done.6.refs_3_), channel_id=1, source_target_pairs={{8,0},{12,4},{16,8},{20,12},{24,16},{28,20},{9,1},{13,5},{17,9},{2... | collective-permute-start | bytes 1572872 | tf_op jit(solution)/shard_map/ppermute | solution.py:29
  331.3 104.2 %collective-permute-start.40 = (bf16[2,1376,256]{2,1,0:T(8,128)(2,1)}, bf16[2,1376,256]{2,1,0:T(8,128)(2,1)}, u32[]{:S(2)}, u32[]{:S(2)}) collective-permute-start(bf16[2,1376,256]{2,1,0:T(8,128)(2,1)} %gate_give.1), channel_id=1, source_target_pairs={{0,8},{4,12},{8,0},{12,4},{16,24},{20,28},{24,16},{28,20},{1,9},{5... | collective-permute-start | bytes 4227080 | tf_op jit(solution)/shard_map/ppermute | solution.py:24
  336.0 32.9 %collective-permute-start.14 = (f32[4,1,512]{2,1,0:T(1,128)S(1)}, f32[4,1,512]{2,1,0:T(1,128)S(1)}, u32[]{:S(2)}, u32[]{:S(2)}) collective-permute-start(f32[4,1,512]{2,1,0:T(1,128)S(1)} %copy-done.30), channel_id=1, source_target_pairs={{8,0},{12,4},{16,8},{20,12},{24,16},{28,20},{9,1},{13,5},{17,9},{2... | collective-permute-start | bytes 24584 | tf_op jit(solution)/shard_map/ppermute | solution.py:29
  368.9 5.5 collective-permute-start.16
  371.3 38.0 %collective-permute-start.7 = (bf16[512,512]{1,0:T(8,128)(2,1)S(1)}, bf16[512,512]{1,0:T(8,128)(2,1)S(1)}, u32[]{:S(2)}, u32[]{:S(2)}) collective-permute-start(bf16[512,512]{1,0:T(8,128)(2,1)S(1)} %get-tuple-element.80), channel_id=1, source_target_pairs={{0,4},{4,0},{8,12},{12,8},{16,20},{20,16},{24,28},{28,24},{1,5},{5... | collective-permute-start | bytes 1572872 | tf_op jit(solution)/shard_map/ppermute | solution.py:24
  374.4 36.2 %collective-permute-start.9 = (bf16[512,512]{1,0:T(8,128)(2,1)S(1)}, bf16[512,512]{1,0:T(8,128)(2,1)S(1)}, u32[]{:S(2)}, u32[]{:S(2)}) collective-permute-start(bf16[512,512]{1,0:T(8,128)(2,1)S(1)} %get-tuple-element.79), channel_id=1, source_target_pairs={{0,4},{4,0},{8,12},{12,8},{16,20},{20,16},{24,28},{28,24},{1,5},{5... | collective-permute-start | bytes 1572872 | tf_op jit(solution)/shard_map/ppermute | solution.py:24
  375.7 17.7 %collective-permute-start.13 = (f32[4,1,512]{2,1,0:T(1,128)S(1)}, f32[4,1,512]{2,1,0:T(1,128)S(1)}, u32[]{:S(2)}, u32[]{:S(2)}) collective-permute-start(f32[4,1,512]{2,1,0:T(1,128)S(1)} %get-tuple-element.83), channel_id=1, source_target_pairs={{0,4},{4,0},{8,12},{12,8},{16,20},{20,16},{24,28},{28,24},{1,5},{5... | collective-permute-start | bytes 24584 | tf_op jit(solution)/shard_map/ppermute | solution.py:24
  376.5 16.9 %collective-permute-start.15 = (f32[4,1,512]{2,1,0:T(1,128)S(1)}, f32[4,1,512]{2,1,0:T(1,128)S(1)}, u32[]{:S(2)}, u32[]{:S(2)}) collective-permute-start(f32[4,1,512]{2,1,0:T(1,128)S(1)} %get-tuple-element.82), channel_id=1, source_target_pairs={{0,4},{4,0},{8,12},{12,8},{16,20},{20,16},{24,28},{28,24},{1,5},{5... | collective-permute-start | bytes 24584 | tf_op jit(solution)/shard_map/ppermute | solution.py:24
  377.8 17.4 %copy-start.35 = (f32[4,512,1]{2,1,0:T(8,128)S(1)}, f32[4,512,1]{2,1,0:T(8,128)}, u32[]{:S(2)}) copy-start(f32[4,512,1]{2,1,0:T(8,128)} %get-tuple-element.54.lse_ref) | copy-start | bytes 24580
  382.3 12.8 %copy-start.7 = (bf16[2,1376,256]{2,1,0:T(8,128)(2,1)}, bf16[2,1376,256]{2,1,0:T(8,128)(2,1)S(1)}, u32[]{:S(2)}) copy-start(bf16[2,1376,256]{2,1,0:T(8,128)(2,1)S(1)} %up_keep.1) | copy-start | bytes 4227076
  382.3 12.8 %copy-start.20 = (f32[512,128]{1,0:T(8,128)S(1)}, f32[512,128]{1,0:T(8,128)}, u32[]{:S(2)}) copy-start(f32[512,128]{1,0:T(8,128)} %pad_maximum_fusion.1.sin_ref) | copy-start | bytes 786436
  382.4 12.8 %copy-start.21 = (f32[512,128]{1,0:T(8,128)S(1)}, f32[512,128]{1,0:T(8,128)}, u32[]{:S(2)}) copy-start(f32[512,128]{1,0:T(8,128)} %pad_maximum_fusion.cos_ref) | copy-start | bytes 786436
  382.4 12.8 %copy-start.22 = (s32[512,1]{1,0:T(8,128)S(1)}, s32[512,1]{1,0:T(8,128)}, u32[]{:S(2)}) copy-start(s32[512,1]{1,0:T(8,128)} %copy.32.lo_ref) | copy-start | bytes 6148
  382.4 12.8 %copy-start.34 = (f32[4,512,1]{2,1,0:T(8,128)S(1)}, f32[4,512,1]{2,1,0:T(8,128)}, u32[]{:S(2)}) copy-start(f32[4,512,1]{2,1,0:T(8,128)} %copy-done.33) | copy-start | bytes 24580
  393.3 46.3 %collective-permute-start.2 = (bf16[512,1024]{1,0:T(8,128)(2,1)S(1)}, bf16[512,1024]{1,0:T(8,128)(2,1)}, u32[]{:S(2)}, u32[]{:S(2)}) collective-permute-start(bf16[512,1024]{1,0:T(8,128)(2,1)S(1)} %add_convert_fusion.4), channel_id=1, source_target_pairs={{0,1},{1,0},{2,3},{3,2},{4,5},{5,4},{6,7},{7,6},{8,9},{9,8},{10,11... | collective-permute-start | bytes 3145736 | tf_op jit(solution)/shard_map/ppermute | solution.py:24
  393.4 15.5 %collective-permute-start.17 = (f32[4,1,512]{2,1,0:T(1,128)S(1)}, f32[4,1,512]{2,1,0:T(1,128)S(1)}, u32[]{:S(2)}, u32[]{:S(2)}) collective-permute-start(f32[4,1,512]{2,1,0:T(1,128)S(1)} %get-tuple-element.81), channel_id=1, source_target_pairs={{0,4},{4,0},{8,12},{12,8},{16,20},{20,16},{24,28},{28,24},{1,5},{5... | collective-permute-start | bytes 24584 | tf_op jit(solution)/shard_map/ppermute | solution.py:24
  395.2 17.0 %copy-start.28 = (f32[4,1,512]{2,1,0:T(1,128)S(1)}, f32[4,1,512]{2,1,0:T(1,128)}, u32[]{:S(2)}) copy-start(f32[4,1,512]{2,1,0:T(1,128)} %copy-done.27) | copy-start | bytes 24580
  408.9 22.7 %copy-start.2 = (bf16[2048,512]{1,0:T(8,128)(2,1)S(1)}, bf16[2048,512]{1,0:T(8,128)(2,1)}, u32[]{:S(2)}) copy-start(bf16[2048,512]{1,0:T(8,128)(2,1)} %refs_3_.3) | copy-start | bytes 6291460
  408.9 53.1 %collective-permute-start.24 = (bf16[4,256,512]{2,1,0:T(8,128)(2,1)}, bf16[4,256,512]{2,1,0:T(8,128)(2,1)S(1)}, u32[]{:S(2)}, u32[]{:S(2)}) collective-permute-start(bf16[4,256,512]{2,1,0:T(8,128)(2,1)} %get-tuple-element.67), channel_id=1, source_target_pairs={{0,4},{4,0},{8,12},{12,8},{16,20},{20,16},{24,28},{28,24},{1,5},{5... | collective-permute-start | bytes 3145736 | tf_op jit(solution)/shard_map/ppermute | solution.py:24
  409.3 49.9 %collective-permute-start.48 = (bf16[1,1376,256]{2,1,0:T(8,128)(2,1)S(1)}, bf16[1,1376,256]{2,1,0:T(8,128)(2,1)}, u32[]{:S(2)}, u32[]{:S(2)}) collective-permute-start(bf16[1,1376,256]{2,1,0:T(8,128)(2,1)S(1)} %slice.188), channel_id=1, source_target_pairs={{0,16},{4,20},{8,24},{12,28},{16,0},{20,4},{24,8},{28,12},{1,17},{... | collective-permute-start | bytes 2113544 | tf_op jit(solution)/shard_map/ppermute | solution.py:24
  410.6 78.7 %collective-permute-start.44 = (bf16[1,1376,256]{2,1,0:T(8,128)(2,1)}, bf16[1,1376,256]{2,1,0:T(8,128)(2,1)}, u32[]{:S(2)}, u32[]{:S(2)}) collective-permute-start(bf16[1,1376,256]{2,1,0:T(8,128)(2,1)} %slice.186), channel_id=1, source_target_pairs={{0,16},{4,20},{8,24},{12,28},{16,0},{20,4},{24,8},{28,12},{1,17},{... | collective-permute-start | bytes 2113544 | tf_op jit(solution)/shard_map/ppermute | solution.py:24
  435.5 9.4 %collective-permute-start.18 = (bf16[512,1024]{1,0:T(8,128)(2,1)S(1)}, bf16[512,1024]{1,0:T(8,128)(2,1)S(1)}, u32[]{:S(2)}, u32[]{:S(2)}) collective-permute-start(bf16[512,1024]{1,0:T(8,128)(2,1)S(1)} %norm_one_give.1), channel_id=1, source_target_pairs={{0,1},{1,0},{2,3},{3,2},{4,5},{5,4},{6,7},{7,6},{8,9},{9,8},{10,11... | collective-permute-start | bytes 3145736 | tf_op jit(solution)/shard_map/ppermute | solution.py:24
  439.7 24.1 %collective-permute-start.25 = (bf16[512,512]{1,0:T(8,128)(2,1)S(1)}, bf16[512,512]{1,0:T(8,128)(2,1)S(1)}, u32[]{:S(2)}, u32[]{:S(2)}) collective-permute-start(bf16[512,512]{1,0:T(8,128)(2,1)S(1)} %attention_dq.1.refs_0_.refs_2_), channel_id=1, source_target_pairs={{0,4},{4,0},{8,12},{12,8},{16,20},{20,16},{24,28},{28,24},{1,5},{5... | collective-permute-start | bytes 1572872 | tf_op jit(solution)/shard_map/ppermute | solution.py:24
  444.9 71.5 %collective-permute-start.34 = (bf16[4,256,512]{2,1,0:T(8,128)(2,1)S(1)}, bf16[4,256,512]{2,1,0:T(8,128)(2,1)S(1)}, u32[]{:S(2)}, u32[]{:S(2)}) collective-permute-start(bf16[4,256,512]{2,1,0:T(8,128)(2,1)S(1)} %copy-done.32), channel_id=1, source_target_pairs={{0,4},{4,0},{8,12},{12,8},{16,20},{20,16},{24,28},{28,24},{1,5},{5... | collective-permute-start | bytes 3145736 | tf_op jit(solution)/shard_map/ppermute | solution.py:24
  450.3 13.5 %copy-start = (bf16[4,256,512]{2,1,0:T(8,128)(2,1)S(1)}, bf16[4,256,512]{2,1,0:T(8,128)(2,1)}, u32[]{:S(2)}) copy-start(bf16[4,256,512]{2,1,0:T(8,128)(2,1)} %get-tuple-element.66.refs_0_) | copy-start | bytes 3145732
  459.1 62.9 %collective-permute-start.19 = (bf16[512,1024]{1,0:T(8,128)(2,1)S(1)}, bf16[512,1024]{1,0:T(8,128)(2,1)S(1)}, u32[]{:S(2)}, u32[]{:S(2)}) collective-permute-start(bf16[512,1024]{1,0:T(8,128)(2,1)S(1)} %norm_one_keep.1), channel_id=1, source_target_pairs={{0,2},{1,3},{2,0},{3,1},{4,6},{5,7},{6,4},{7,5},{8,10},{9,11},{10,... | collective-permute-start | bytes 3145736 | tf_op jit(solution)/shard_map/ppermute | solution.py:24
  462.0 27.3 %copy-start.8 = (bf16[2,1376,256]{2,1,0:T(8,128)(2,1)S(1)}, bf16[2,1376,256]{2,1,0:T(8,128)(2,1)}, u32[]{:S(2)}) copy-start(bf16[2,1376,256]{2,1,0:T(8,128)(2,1)} %copy-done.7) | copy-start | bytes 4227076
  462.0 54.4 %collective-permute-start.35 = (bf16[512,512]{1,0:T(8,128)(2,1)S(1)}, bf16[512,512]{1,0:T(8,128)(2,1)S(1)}, u32[]{:S(2)}, u32[]{:S(2)}) collective-permute-start(bf16[512,512]{1,0:T(8,128)(2,1)S(1)} %copy-done.12), channel_id=1, source_target_pairs={{0,4},{4,0},{8,12},{12,8},{16,20},{20,16},{24,28},{28,24},{1,5},{5... | collective-permute-start | bytes 1572872 | tf_op jit(solution)/shard_map/ppermute | solution.py:24
  463.8 59.1 %collective-permute-start.41 = (bf16[1,1376,256]{2,1,0:T(8,128)(2,1)S(1)}, bf16[1,1376,256]{2,1,0:T(8,128)(2,1)S(1)}, u32[]{:S(2)}, u32[]{:S(2)}) collective-permute-start(bf16[1,1376,256]{2,1,0:T(8,128)(2,1)S(1)} %slice.184), channel_id=1, source_target_pairs={{0,16},{4,20},{8,24},{12,28},{16,0},{20,4},{24,8},{28,12},{1,17},{... | collective-permute-start | bytes 2113544 | tf_op jit(solution)/shard_map/ppermute | solution.py:24
  489.3 25.2 %collective-permute-start.26 = (bf16[2,256,512]{2,1,0:T(8,128)(2,1)S(1)}, bf16[2,256,512]{2,1,0:T(8,128)(2,1)S(1)}, u32[]{:S(2)}, u32[]{:S(2)}) collective-permute-start(bf16[2,256,512]{2,1,0:T(8,128)(2,1)S(1)} %query_give.1), channel_id=1, source_target_pairs={{0,8},{4,12},{8,0},{12,4},{16,24},{20,28},{24,16},{28,20},{1,9},{5... | collective-permute-start | bytes 1572872 | tf_op jit(solution)/shard_map/ppermute | solution.py:24
  491.7 24.7 %copy-start.14 = (bf16[4,256,512]{2,1,0:T(8,128)(2,1)S(1)}, bf16[4,256,512]{2,1,0:T(8,128)(2,1)}, u32[]{:S(2)}) copy-start(bf16[4,256,512]{2,1,0:T(8,128)(2,1)} %copy-done.13) | copy-start | bytes 3145732
  516.0 27.0 %collective-permute-start.27 = (bf16[1,256,512]{2,1,0:T(8,128)(2,1)S(1)}, bf16[1,256,512]{2,1,0:T(8,128)(2,1)S(1)}, u32[]{:S(2)}, u32[]{:S(2)}) collective-permute-start(bf16[1,256,512]{2,1,0:T(8,128)(2,1)S(1)} %slice.176), channel_id=1, source_target_pairs={{0,16},{4,20},{8,24},{12,28},{16,0},{20,4},{24,8},{28,12},{1,17},{... | collective-permute-start | bytes 786440 | tf_op jit(solution)/shard_map/ppermute | solution.py:24
  517.9 19.9 %collective-permute-start.36 = (bf16[2,256,512]{2,1,0:T(8,128)(2,1)S(1)}, bf16[2,256,512]{2,1,0:T(8,128)(2,1)S(1)}, u32[]{:S(2)}, u32[]{:S(2)}) collective-permute-start(bf16[2,256,512]{2,1,0:T(8,128)(2,1)S(1)} %wout_give.1), channel_id=1, source_target_pairs={{0,8},{4,12},{8,0},{12,4},{16,24},{20,28},{24,16},{28,20},{1,9},{5... | collective-permute-start | bytes 1572872 | tf_op jit(solution)/shard_map/ppermute | solution.py:24
  520.4 18.9 %collective-permute-start.31 = (bf16[512,512]{1,0:T(8,128)(2,1)S(1)}, bf16[512,512]{1,0:T(8,128)(2,1)S(1)}, u32[]{:S(2)}, u32[]{:S(2)}) collective-permute-start(bf16[512,512]{1,0:T(8,128)(2,1)S(1)} %get-tuple-element.61.refs_2_), channel_id=1, source_target_pairs={{0,4},{4,0},{8,12},{12,8},{16,20},{20,16},{24,28},{28,24},{1,5},{5... | collective-permute-start | bytes 1572872 | tf_op jit(solution)/shard_map/ppermute | solution.py:24
  522.1 22.9 %collective-permute-start.28 = (bf16[512,512]{1,0:T(8,128)(2,1)S(1)}, bf16[512,512]{1,0:T(8,128)(2,1)S(1)}, u32[]{:S(2)}, u32[]{:S(2)}) collective-permute-start(bf16[512,512]{1,0:T(8,128)(2,1)S(1)} %get-tuple-element.60.refs_1_.refs_2_), channel_id=1, source_target_pairs={{0,4},{4,0},{8,12},{12,8},{16,20},{20,16},{24,28},{28,24},{1,5},{5... | collective-permute-start | bytes 1572872 | tf_op jit(solution)/shard_map/ppermute | solution.py:24
  522.9 40.3 %collective-permute-start.20 = (bf16[512,1024]{1,0:T(8,128)(2,1)S(1)}, bf16[512,1024]{1,0:T(8,128)(2,1)S(1)}, u32[]{:S(2)}, u32[]{:S(2)}) collective-permute-start(bf16[512,1024]{1,0:T(8,128)(2,1)S(1)} %add_convert_fusion.1.own_ref), channel_id=1, source_target_pairs={{0,1},{1,0},{2,3},{3,2},{4,5},{5,4},{6,7},{7,6},{8,9},{9,8},{10,11... | collective-permute-start | bytes 3145736 | tf_op jit(solution)/shard_map/ppermute | solution.py:24
  539.2 13.1 %collective-permute-start.37 = (bf16[1,256,512]{2,1,0:T(8,128)(2,1)S(1)}, bf16[1,256,512]{2,1,0:T(8,128)(2,1)S(1)}, u32[]{:S(2)}, u32[]{:S(2)}) collective-permute-start(bf16[1,256,512]{2,1,0:T(8,128)(2,1)S(1)} %slice.182), channel_id=1, source_target_pairs={{0,16},{4,20},{8,24},{12,28},{16,0},{20,4},{24,8},{28,12},{1,17},{... | collective-permute-start | bytes 786440 | tf_op jit(solution)/shard_map/ppermute | solution.py:24
  540.8 20.6 %collective-permute-start.32 = (bf16[2,256,512]{2,1,0:T(8,128)(2,1)S(1)}, bf16[2,256,512]{2,1,0:T(8,128)(2,1)S(1)}, u32[]{:S(2)}, u32[]{:S(2)}) collective-permute-start(bf16[2,256,512]{2,1,0:T(8,128)(2,1)S(1)} %value_give.1), channel_id=1, source_target_pairs={{0,8},{4,12},{8,0},{12,4},{16,24},{20,28},{24,16},{28,20},{1,9},{5... | collective-permute-start | bytes 1572872 | tf_op jit(solution)/shard_map/ppermute | solution.py:24
  546.4 30.0 %collective-permute-start.29 = (bf16[2,256,512]{2,1,0:T(8,128)(2,1)S(1)}, bf16[2,256,512]{2,1,0:T(8,128)(2,1)S(1)}, u32[]{:S(2)}, u32[]{:S(2)}) collective-permute-start(bf16[2,256,512]{2,1,0:T(8,128)(2,1)S(1)} %key_give.1), channel_id=1, source_target_pairs={{0,8},{4,12},{8,0},{12,4},{16,24},{20,28},{24,16},{28,20},{1,9},{5... | collective-permute-start | bytes 1572872 | tf_op jit(solution)/shard_map/ppermute | solution.py:24
  562.8 17.9 %collective-permute-start.33 = (bf16[1,256,512]{2,1,0:T(8,128)(2,1)S(1)}, bf16[1,256,512]{2,1,0:T(8,128)(2,1)S(1)}, u32[]{:S(2)}, u32[]{:S(2)}) collective-permute-start(bf16[1,256,512]{2,1,0:T(8,128)(2,1)S(1)} %slice.180), channel_id=1, source_target_pairs={{0,16},{4,20},{8,24},{12,28},{16,0},{20,4},{24,8},{28,12},{1,17},{... | collective-permute-start | bytes 786440 | tf_op jit(solution)/shard_map/ppermute | solution.py:24
  569.8 8.4 %collective-permute-start.21 = (f32[2,2048]{1,0:T(2,128)S(1)}, f32[2,2048]{1,0:T(2,128)S(1)}, u32[]{:S(2)}, u32[]{:S(2)}) collective-permute-start(f32[2,2048]{1,0:T(2,128)S(1)} %pad_maximum_fusion.2), channel_id=1, source_target_pairs={{0,4},{4,0},{8,12},{12,8},{16,20},{20,16},{24,28},{28,24},{1,5},{5... | collective-permute-start | bytes 49160 | tf_op jit(solution)/shard_map/ppermute | solution.py:24
  577.8 12.1 %collective-permute-start.30 = (bf16[1,256,512]{2,1,0:T(8,128)(2,1)S(1)}, bf16[1,256,512]{2,1,0:T(8,128)(2,1)S(1)}, u32[]{:S(2)}, u32[]{:S(2)}) collective-permute-start(bf16[1,256,512]{2,1,0:T(8,128)(2,1)S(1)} %slice.178), channel_id=1, source_target_pairs={{0,16},{4,20},{8,24},{12,28},{16,0},{20,4},{24,8},{28,12},{1,17},{... | collective-permute-start | bytes 786440 | tf_op jit(solution)/shard_map/ppermute | solution.py:24
  578.2 4.3 collective-permute-start.22
  582.5 8.3 %collective-permute-start.23 = (f32[2,2048]{1,0:T(2,128)S(1)}, f32[2,2048]{1,0:T(2,128)S(1)}, u32[]{:S(2)}, u32[]{:S(2)}) collective-permute-start(f32[2,2048]{1,0:T(2,128)S(1)} %fusion.18), channel_id=1, source_target_pairs={{0,16},{4,20},{8,24},{12,28},{16,0},{20,4},{24,8},{28,12},{1,17},{... | collective-permute-start | bytes 49160 | tf_op jit(solution)/shard_map/ppermute | solution.py:24
  (24 other events, 122.7 us)

commit v3 on v2

v3 whole, which is shorter than its diff:
```python
import functools
import math

import jax
import jax.numpy as jnp
from jax import lax
from jax.experimental import pallas as pl
from jax.experimental.pallas import tpu as pltpu
from jax.sharding import PartitionSpec as P

HEAD_DIM = 128
WINDOW = 2048
PAD = 64
NSEQ = 4
EPS = 1e-06
MASKED = -1e30
LOG2E = 1.4426950408889634
BIG = 1 << 28
F32 = jnp.float32
BF16 = jnp.bfloat16


def swap(block, axis, bit):
    return lax.ppermute(block, axis, [(i, i ^ bit) for i in range(lax.axis_size(axis))])


def shifted(block, distance):
    n = lax.axis_size("seq")
    return lax.ppermute(
        block, "seq", [(i, i + distance) for i in range(n) if 0 <= i + distance < n]
    )


BIG_VMEM = pltpu.CompilerParams(vmem_limit_bytes=48 << 20)


def cost(flops, moved):
    return pl.CostEstimate(flops=int(flops), bytes_accessed=int(moved), transcendentals=0)


def dot_nt(left, right):
    return lax.dot_general(left, right, (((1,), (1,)), ((), ())), preferred_element_type=F32)


def row_blocks(width, step):
    return pl.BlockSpec((step, width), lambda i, bits: (i, 0))


def joined(bits_ref, own_ref, other_ref):
    low = bits_ref[1] == 0
    own, other = own_ref[...].astype(F32), other_ref[...].astype(F32)
    return jnp.concatenate([jnp.where(low, own, other), jnp.where(low, other, own)], axis=1)


def back_kernel(
    bits_ref, x_ref, own_ref, other_ref, gain_ref, add_ref, out_ref, part_ref
):
    x = x_ref[...].astype(F32)
    scale = lax.rsqrt(jnp.mean(x * x, axis=-1, keepdims=True) + EPS)
    grad = joined(bits_ref, own_ref, other_ref)
    unit = x * scale
    grad_unit = grad * gain_ref[...]
    total = add_ref[...].astype(F32) + scale * (
        grad_unit - unit * jnp.mean(grad_unit * unit, axis=-1, keepdims=True)
    )
    out_ref[...] = total.astype(out_ref.dtype)
    part = jnp.sum(grad * unit, axis=0, keepdims=True)

    @pl.when(pl.program_id(0) == 0)
    def _():
        part_ref[...] = part

    @pl.when(pl.program_id(0) > 0)
    def _():
        part_ref[...] += part


def by_rows(kernel, bits, arrays, gains_at, outs, name, part=None):
    rows, width = arrays[0].shape
    step = rows // 4
    in_specs = [
        pl.BlockSpec((1, width), lambda i, bits: (0, 0))
        if k == gains_at
        else row_blocks(a.shape[1], step)
        for k, a in enumerate(arrays)
    ]
    out_specs, out_shape = [], []
    for k, dtype in enumerate(outs):
        if k == part:
            out_specs.append(pl.BlockSpec((1, width), lambda i, bits: (0, 0)))
            out_shape.append(jax.ShapeDtypeStruct((1, width), F32))
        else:
            out_specs.append(row_blocks(width, step))
            out_shape.append(jax.ShapeDtypeStruct((rows, width), dtype))
    return pl.pallas_call(
        kernel,
        grid_spec=pltpu.PrefetchScalarGridSpec(
            num_scalar_prefetch=1, grid=(rows // step,), in_specs=in_specs, out_specs=out_specs
        ),
        out_shape=out_shape,
        compiler_params=BIG_VMEM,
        cost_estimate=cost(rows * width * 10, rows * width * 2 * (len(arrays) + len(out_shape))),
        name=name,
    )(bits, *arrays)


def half_kernel(pairs, flip, added, bits_ref, *refs):
    total = refs[2 * pairs][...].astype(F32) if added else None
    for k in range(pairs):
        term = dot_nt(refs[k][...], refs[pairs + k][...])
        total = term if total is None else total + term
    refs[-1][...] = total.astype(BF16)


def half_product(bits, lefts, rights, flip, added, name):
    rows = lefts[0].shape[0]
    width = rights[0].shape[0] // 2
    step = min(width, 512)
    steps = width // step

    def at(i, bits):
        return ((bits[1] ^ flip) * steps + i, 0)

    specs = [pl.BlockSpec(a.shape, lambda i, bits: (0, 0)) for a in lefts]
    specs += [pl.BlockSpec((step, a.shape[1]), at) for a in rights]
    extra = []
    if added is not None:
        extra = [added]
        specs.append(pl.BlockSpec((rows, step), lambda i, bits: (0, i)))
    depth = sum(a.shape[1] for a in lefts)
    return pl.pallas_call(
        functools.partial(half_kernel, len(lefts), flip, added is not None),
        grid_spec=pltpu.PrefetchScalarGridSpec(
            num_scalar_prefetch=1,
            grid=(steps,),
            in_specs=specs,
            out_specs=pl.BlockSpec((rows, step), lambda i, bits: (0, i)),
        ),
        out_shape=jax.ShapeDtypeStruct((rows, width), BF16),
        compiler_params=BIG_VMEM,
        cost_estimate=cost(2 * rows * depth * width, 2 * (rows + width) * depth),
        name=name,
    )(bits, *lefts, *rights, *extra)


def mlp_kernel(x_ref, g_ref, wg_ref, wu_ref, wd_ref, act_ref, gg_ref, gu_ref):
    x, g = x_ref[...], g_ref[...]
    gate = dot_nt(wg_ref[...], x)
    up = dot_nt(wu_ref[...], x)
    grad = dot_nt(wd_ref[...], g)
    sig = 1.0 / (1.0 + jnp.exp(-gate))
    silu = gate * sig
    act_ref[...] = (silu * up).astype(BF16)
    gg_ref[...] = (grad * up * sig * (1.0 + gate * (1.0 - sig))).astype(BF16)
    gu_ref[...] = (grad * silu).astype(BF16)


def mlp(x, grad, w_gate, w_up, w_down):
    rows, depth = x.shape
    width = w_gate.shape[0]
    step = -(-width // (4 * 32)) * 32
    whole = pl.BlockSpec((rows, depth), lambda i: (0, 0))
    block = pl.BlockSpec((step, depth), lambda i: (i, 0))
    return pl.pallas_call(
        mlp_kernel,
        grid=(pl.cdiv(width, step),),
        in_specs=[whole, whole, block, block, block],
        out_specs=[pl.BlockSpec((step, rows), lambda i: (i, 0))] * 3,
        out_shape=[jax.ShapeDtypeStruct((width, rows), BF16)] * 3,
        compiler_params=BIG_VMEM,
        cost_estimate=cost(6 * rows * depth * width, 6 * depth * width),
        name="mlp",
    )(x, grad, w_gate, w_up, w_down)


def back_products_kernel(bits_ref, gg_ref, gu_ref, wg_ref, wu_ref, out_ref, gg, gu):
    @pl.when(pl.program_id(0) == 0)
    def _():
        gg[...] = gg_ref[...].T
        gu[...] = gu_ref[...].T

    total = jnp.dot(gg[...], wg_ref[...], preferred_element_type=F32)
    total = total + jnp.dot(gu[...], wu_ref[...], preferred_element_type=F32)
    out_ref[0] = total.astype(BF16)


def back_products(bits, grad_gate, grad_up, w_gate, w_up):
    cols, rows = grad_gate.shape
    width = w_gate.shape[1]
    step = width // 4
    whole = pl.BlockSpec((cols, rows), lambda i, bits: (0, 0))
    column = pl.BlockSpec(
        (cols, step), lambda i, bits: (0, 2 * (bits[1] ^ 1 ^ (i // 2)) + i % 2)
    )
    return pl.pallas_call(
        back_products_kernel,
        grid_spec=pltpu.PrefetchScalarGridSpec(
            num_scalar_prefetch=1,
            grid=(4,),
            in_specs=[whole, whole, column, column],
            out_specs=pl.BlockSpec((1, rows, step), lambda i, bits: (i // 2, 0, i % 2)),
            scratch_shapes=[pltpu.VMEM((rows, cols), BF16)] * 2,
        ),
        out_shape=jax.ShapeDtypeStruct((2, rows, width // 2), BF16),
        compiler_params=BIG_VMEM,
        cost_estimate=cost(4 * rows * cols * width, 4 * cols * width),
        name="back_products",
    )(bits, grad_gate, grad_up, w_gate, w_up)


def blocks_kernel(order_ref, flip, xa_ref, xb_ref, ga_ref, gb_ref, *refs):
    if flip:
        total = jnp.dot(ga_ref[...], xa_ref[0], preferred_element_type=F32)
        total = total + jnp.dot(gb_ref[...], xb_ref[0], preferred_element_type=F32)
    else:
        total = jnp.dot(xa_ref[0], ga_ref[...], preferred_element_type=F32)
        total = total + jnp.dot(xb_ref[0], gb_ref[...], preferred_element_type=F32)
    if len(refs) == 2:
        total = total + refs[0][0].astype(F32)
    refs[-1][0] = total.astype(BF16)


def grad_blocks(order, x_own, x_got, g_own, g_got, added, flip, name):
    count = order.shape[0]
    if flip:
        _, rows, depth = x_own.shape
        cols = g_own.shape[0]
        shape = (cols, depth)
    else:
        _, depth, rows = x_own.shape
        cols = g_own.shape[1]
        shape = (depth, cols)
    x_spec = pl.BlockSpec((1,) + x_own.shape[1:], lambda i, order: (order[i], 0, 0))
    g_spec = pl.BlockSpec(g_own.shape, lambda i, order: (0, 0))
    out_spec = pl.BlockSpec((1,) + shape, lambda i, order: (i, 0, 0))
    extra = [] if added is None else [added]

    def kernel(order_ref, *refs):
        blocks_kernel(order_ref, flip, *refs)

    return pl.pallas_call(
        kernel,
        grid_spec=pltpu.PrefetchScalarGridSpec(
            num_scalar_prefetch=1,
            grid=(count,),
            in_specs=[x_spec, x_spec, g_spec, g_spec] + [out_spec] * len(extra),
            out_specs=out_spec,
        ),
        out_shape=jax.ShapeDtypeStruct((count,) + shape, BF16),
        compiler_params=BIG_VMEM,
        cost_estimate=cost(
            4 * count * depth * rows * cols, 2 * count * depth * cols + 4 * rows * cols
        ),
        name=name,
    )(order, x_own, x_got, g_own, g_got, *extra)


def shard_orders(first, n):
    bits = [1 << k for k in range(n.bit_length() - 1)]
    return [first] + [b for b in bits if b != first]


class Order:
    def __init__(self):
        self.last = None

    def after(self, operand):
        if self.last is None:
            return operand
        return lax.optimization_barrier((operand, self.last))[0]

    def ran(self, result):
        self.last = result
        return result


class WeightGrad:
    def __init__(self, order, x_pair, g_own, g_got, first, name, flip=False):
        n = lax.axis_size("seq")
        self.order, self.flip, self.name = order, flip, name
        self.operands = (*x_pair, g_own, g_got)
        self.bits = shard_orders(first, n)
        index = lax.axis_index("seq")
        shards = []
        for p in range(n // 2):
            apart = sum(
                b for k, b in enumerate(self.bits[1:]) if (p >> (len(self.bits) - 2 - k)) & 1
            )
            shard = index ^ apart
            shards.append(shard // (2 * first) * first + shard % first)
        self.shards = jnp.stack(shards).astype(jnp.int32)
        self.count = n // 4

    def blocks(self, shards, added, name):
        return self.order.ran(
            grad_blocks(
                self.order.after(shards), *self.operands, added, self.flip, self.name + name
            )
        )

    def give(self):
        give = self.blocks(self.shards[self.count :], None, "_give")
        self.got = swap(give, "seq", self.bits[1])

    def keep(self):
        self.part = self.blocks(self.shards[: self.count], self.got, "_keep")
        left = self.count // 2
        self.got = swap(self.part[left:], "seq", self.bits[2])

    def finish(self):
        left, part = self.count // 2, self.part
        total = part[:left].astype(F32) + self.got.astype(F32)
        for bit in self.bits[3:]:
            left //= 2
            part = total.astype(BF16)
            total = part[:left].astype(F32) + swap(part[left:], "seq", bit).astype(F32)
        return total[0].T if self.flip else total[0]


def gain_sum(part):
    n = lax.axis_size("seq")
    total = part
    bit = 1
    while bit < n:
        total = total + swap(total, "seq", bit)
        bit *= 2
    width = part.shape[-1] // n
    return lax.dynamic_slice_in_dim(total, lax.axis_index("seq") * width, width, total.ndim - 1)


def turned_back(grad, cosine, sine):
    return (grad * cosine - pltpu.roll(grad, HEAD_DIM // 2, 1) * sine).astype(BF16)


def place(devices, cores):
    s, h = lax.axis_index("seq"), lax.axis_index("head")
    odd, core = lax.rem(s, 2), lax.rem(h, 2)
    pair = s + 1 - 2 * odd
    mate = h + 1 - 2 * core
    across = lax.rem(h + cores // 2, cores)
    return s, h, odd, core, pair, mate, across


def remote(src, dst, send, recv, seq, head):
    return pltpu.make_async_remote_copy(
        src_ref=src,
        dst_ref=dst,
        send_sem=send,
        recv_sem=recv,
        device_id=(seq, head),
        device_id_type=pl.DeviceIdType.MESH,
    )


def greet(seq, head):
    pl.semaphore_signal(
        pltpu.get_barrier_semaphore(),
        inc=1,
        device_id=(seq, head),
        device_id_type=pl.DeviceIdType.MESH,
    )


def greet_all(devices, cores):
    s, h, odd, core, pair, mate, across = place(devices, cores)
    greet(pair, h)
    greet(s, mate)
    greet(s, across)

    @pl.when(s >= 2)
    def _():
        greet(s - 2, h)

    @pl.when(s < devices - 2)
    def _():
        greet(s + 2, h)


def all_greeted(devices):
    s = lax.axis_index("seq")
    inner = (s >= 2) & (s < devices - 2)

    @pl.when(inner)
    def _():
        pl.semaphore_wait(pltpu.get_barrier_semaphore(), 5)

    @pl.when(jnp.logical_not(inner))
    def _():
        pl.semaphore_wait(pltpu.get_barrier_semaphore(), 4)


class Chain:
    def __init__(self, devices, buf, send, recv, side):
        self.s, self.h = lax.axis_index("seq"), lax.axis_index("head")
        odd = lax.rem(self.s, 2)
        self.pair = self.s + 1 - 2 * odd
        self.buf, self.send, self.recv = buf, send, recv
        self.next = self.s + 2 * side
        left, right = self.s >= 2, self.s < devices - 2
        self.sends, self.gets = (right, left) if side > 0 else (left, right)
        self.early = odd == (0 if side > 0 else 1)
        self.late = odd == (1 if side > 0 else 0)

    def hop(self, slot, seq, src, dst):
        return remote(
            self.buf.at[src], self.buf.at[dst], self.send.at[slot], self.recv.at[slot], seq, self.h
        )

    def first(self):
        @pl.when(self.sends)
        def _():
            self.hop(0, self.next, 0, 2).start()

        @pl.when(self.early)
        def _():
            self.hop(2, self.pair, 0, 1).start()

    def second(self):
        @pl.when(self.gets)
        def _():
            self.hop(0, self.next, 0, 2).wait_recv()

        @pl.when(self.sends)
        def _():
            self.hop(1, self.next, 2, 4).start()

        @pl.when(self.early)
        def _():
            self.hop(3, self.pair, 2, 3).start()

        @pl.when(self.late)
        def _():
            self.hop(2, self.pair, 2, 1).start()

    def third(self):
        @pl.when(self.gets)
        def _():
            self.hop(1, self.next, 2, 4).wait_recv()

        @pl.when(self.late)
        def _():
            self.hop(3, self.pair, 4, 3).start()

    def arrived(self, slot):
        self.hop(slot, self.pair, 0, 1 if slot == 2 else 3).wait_recv()

    def all_sent(self):
        @pl.when(self.sends)
        def _():
            self.hop(0, self.next, 0, 2).wait_send()
            self.hop(1, self.next, 2, 4).wait_send()

        self.hop(2, self.pair, 0, 1).wait_send()
        self.hop(3, self.pair, 0, 3).wait_send()


def differing(s, bit):
    return s + bit - 2 * bit * lax.rem(s // bit, 2)


class Give:
    def __init__(self, devices, first, operands, bufs, send, recv):
        self.s, self.h = lax.axis_index("seq"), lax.axis_index("head")
        g_own, g_got, x_own, x_got = operands
        self.g, self.x, self.slot, self.got, sem = bufs
        self.send, self.recv = send, recv
        bits = shard_orders(first, devices)
        self.partner = differing(self.s, bits[1])
        self.count = devices // 4
        self.loads = [
            pltpu.make_async_copy(g_own, self.g.at[0], sem.at[0]),
            pltpu.make_async_copy(g_got, self.g.at[1], sem.at[1]),
        ]
        for j in range(self.count):
            shard = self.s
            for k, b in enumerate(bits[1:]):
                if ((j + self.count) >> (len(bits) - 2 - k)) & 1:
                    shard = differing(shard, b)
            at = shard // (2 * first) * first + lax.rem(shard, first)
            for k, x in enumerate((x_own, x_got)):
                self.loads.append(
                    pltpu.make_async_copy(x.at[at], self.x.at[k, j], sem.at[2 + 2 * j + k])
                )

    def load(self):
        for copy in self.loads:
            copy.start()

    def loaded(self):
        for copy in self.loads:
            copy.wait()

    def make(self, j):
        total = jnp.dot(self.g[0], self.x[0, j], preferred_element_type=F32)
        total = total + jnp.dot(self.g[1], self.x[1, j], preferred_element_type=F32)
        self.slot[j] = total.astype(BF16)

    def half(self, j, k):
        step = self.slot.shape[1] // 2
        at = pl.ds(k * step, step)
        return remote(
            self.slot.at[j, at, :],
            self.got.at[j, at, :],
            self.send.at[2 * j + k],
            self.recv.at[2 * j + k],
            self.partner,
            self.h,
        )

    def finish(self):
        for j in range(self.count):
            for k in range(2):
                self.half(j, k).wait()


class HeadSum:
    def __init__(self, devices, cores, core_got, chip, y_got, own, other, send, recv):
        self.s, self.h, _, self.core, _, self.mate, self.across = place(devices, cores)
        self.core_got, self.chip, self.y_got = core_got, chip, y_got
        self.own, self.other, self.send, self.recv = own, other, send, recv

    def to_mate(self, i, src=None):
        return remote(
            self.chip.at[i] if src is None else src,
            self.core_got.at[i],
            self.send.at[i],
            self.recv.at[i],
            self.s,
            self.mate,
        )

    def over(self, i):
        return remote(
            self.chip.at[i],
            self.y_got.at[i],
            self.send.at[4 + i],
            self.recv.at[4 + i],
            self.s,
            self.across,
        )

    def back(self, i):
        return remote(
            self.own.at[i],
            self.other.at[i],
            self.send.at[8 + i],
            self.recv.at[8 + i],
            self.s,
            self.mate,
        )

    def chip_sum(self, i, part):
        self.to_mate(i).wait_recv()
        self.chip[i] = (part + self.core_got[i].astype(F32)).astype(BF16)
        self.over(i).start()

    def total(self, i):
        self.over(i).wait_recv()
        self.own[i] = (self.chip[i].astype(F32) + self.y_got[i].astype(F32)).astype(BF16)
        self.back(i).start()

    def joined(self, i):
        self.back(i).wait_recv()
        own, other = self.own[i].astype(F32), self.other[i].astype(F32)
        low = self.core == 0
        return jnp.concatenate([jnp.where(low, own, other), jnp.where(low, other, own)], axis=1)

    def all_sent(self):
        for i in range(4):
            self.to_mate(i).wait_send()
            self.over(i).wait_send()
            self.back(i).wait_send()


def forward_kernel(
    devices,
    cores,
    lengths_ref,
    x_ref,
    gain_one_ref,
    gain_two_ref,
    og_hbm,
    wk_hbm,
    wv_hbm,
    wq_hbm,
    wo_hbm,
    prev_k_hbm,
    prev_v_hbm,
    k_out,
    v_out,
    q_out,
    one_keep_out,
    one_give_out,
    mid_out,
    two_out,
    two_keep_out,
    two_got_out,
    og_keep_out,
    og_give_out,
    att_got,
    att_out,
    lse_out,
    row_out,
    cos_ref,
    sin_ref,
    lo_ref,
    lo_row_ref,
    valid_ref,
    kx,
    vx,
    qx,
    wk,
    wv,
    wq,
    wo,
    normed,
    flipped,
    tops,
    totals,
    acc,
    core_send,
    core_got,
    chip,
    y_got,
    own_half,
    other_half,
    mid,
    two_blocks,
    two_got,
    og,
    load_sem,
    store_sem,
    k_send,
    k_recv,
    v_send,
    v_recv,
    q_send,
    q_recv,
    sum_send,
    sum_recv,
    two_send,
    two_recv,
):
    rows, width = x_ref.shape
    heads = kx.shape[2] // HEAD_DIM
    s, h, odd, core, pair, mate, across = place(devices, cores)
    has_left, has_right = s >= 2, s < devices - 2
    scale = HEAD_DIM ** (-0.5) * LOG2E
    k_chain = Chain(devices, kx, k_send, k_recv, 1)
    v_chain = Chain(devices, vx, v_send, v_recv, 1)
    q_chain = Chain(devices, qx, q_send, q_recv, -1)
    head_sum = HeadSum(
        devices, cores, core_got, chip, y_got, own_half, other_half, sum_send, sum_recv
    )

    loads = [
        pltpu.make_async_copy(src, dst, load_sem.at[i])
        for i, (src, dst) in enumerate(
            ((wk_hbm, wk), (wv_hbm, wv), (wq_hbm, wq), (wo_hbm, wo), (og_hbm, og))
        )
    ]
    for load in loads:
        load.start()

    greet_all(devices, cores)
    step = rows // 4

    def normalize(i, _):
        at = pl.ds(pl.multiple_of(i * step, step), step)
        x = x_ref[at, :].astype(F32)
        root = lax.rsqrt(jnp.mean(x * x, axis=-1, keepdims=True) + EPS)
        normed[at, :] = (x * root * gain_one_ref[...]).astype(BF16)
        return 0

    lax.fori_loop(0, 4, normalize, 0)

    starts, padded = [0], 0
    for r in range(NSEQ - 1):
        padded = padded + (lengths_ref[r] + PAD - 1) // PAD * PAD
        starts.append(padded)

    def sequence_of(at):
        start = jnp.zeros_like(at)
        low = jnp.full_like(at, -BIG)
        length = jnp.zeros_like(at) + lengths_ref[0]
        for r in range(1, NSEQ):
            inside = at >= starts[r]
            start = jnp.where(inside, starts[r], start)
            low = jnp.where(inside, starts[r], low)
            length = jnp.where(inside, lengths_ref[r], length)
        valid = at - start < length
        low = jnp.where(valid, jnp.maximum(low, at - (WINDOW - 1)), at)
        return at - start, valid, jnp.where(at < devices * rows, low, BIG) - s * rows

    at = lax.broadcasted_iota(jnp.int32, (rows, HEAD_DIM), 0) + s * rows
    position, valid, low = sequence_of(at)
    valid_ref[...] = valid[:, 0:1].astype(jnp.int32)
    lo_ref[...] = low[:, 0:1]
    lane = lax.broadcasted_iota(jnp.int32, (1, HEAD_DIM), 1)
    half_dim = HEAD_DIM // 2
    pair_of = lax.rem(lane, half_dim).astype(F32)
    freq = jnp.exp(-math.log(10000.0) * (2.0 * pair_of / HEAD_DIM))
    angle = position.astype(F32) * freq
    cos_ref[...] = jnp.cos(angle)
    sin_ref[...] = jnp.sin(angle) * jnp.where(lane < half_dim, -1.0, 1.0)
    lo_row_ref[...] = sequence_of(lax.broadcasted_iota(jnp.int32, lo_row_ref.shape, 1) + s * rows)[2]

    def turn_into(weight, out):
        raw = jnp.dot(normed[...], weight[...], preferred_element_type=F32)
        for k in range(heads):
            u = raw[:, k * HEAD_DIM : (k + 1) * HEAD_DIM]
            u = u * cos_ref[...] + pltpu.roll(u, HEAD_DIM // 2, 1) * sin_ref[...]
            out[0, :, k * HEAD_DIM : (k + 1) * HEAD_DIM] = u.astype(BF16)

    loads[0].wait()
    turn_into(wk, kx)

    all_greeted(devices)
    k_chain.first()
    loads[1].wait()
    vx[0] = jnp.dot(normed[...], wv[...], preferred_element_type=F32).astype(BF16)
    v_chain.first()

    @pl.when(jnp.logical_not(has_left))
    def _():
        copies = []
        for i, (src, dst) in enumerate(((prev_k_hbm, kx), (prev_v_hbm, vx))):
            for j, d in enumerate((2, 4)):
                at = pl.multiple_of((s - d) * rows + WINDOW, rows)
                copies.append(
                    pltpu.make_async_copy(
                        src.at[pl.ds(at, rows), :], dst.at[d], load_sem.at[5 + 2 * i + j]
                    )
                )
        for copy in copies:
            copy.start()
        for copy in copies:
            copy.wait()

    @pl.when(jnp.logical_not(has_right))
    def _():
        qx[2] = jnp.zeros_like(qx[2])
        qx[4] = jnp.zeros_like(qx[4])

    loads[2].wait()
    turn_into(wq, qx)
    q_chain.first()

    for i in range(4):
        flip_at = slice(i * step, (i + 1) * step)
        flipped[:, :, flip_at] = normed[flip_at, :].T.reshape(devices, width // devices, step)
    split = flipped.reshape(devices // 2, 2, width // devices, rows)
    stores = [
        pltpu.make_async_copy(split.at[:, odd], one_keep_out, store_sem.at[0]),
        pltpu.make_async_copy(split.at[:, 1 - odd], one_give_out, store_sem.at[1]),
    ]
    stores[0].start()
    stores[1].start()

    depth = width // devices
    loads[4].wait()
    for j in range(devices):
        two_blocks[j] = og[:, j * depth : (j + 1) * depth]
    near = lax.rem(s // 2, 2)
    split = two_blocks.reshape(devices // 4, 2, 2, rows, depth)
    og_stores = [
        pltpu.make_async_copy(split.at[:, near], og_keep_out, store_sem.at[4]),
        pltpu.make_async_copy(split.at[:, 1 - near], og_give_out, store_sem.at[5]),
    ]
    og_stores[0].start()
    og_stores[1].start()
    sub = rows // 2

    def attend(d):
        def body(i, _):
            k = i // 2
            at = pl.ds(pl.multiple_of((i % 2) * sub, sub), sub)
            lanes = pl.ds(pl.multiple_of(k * HEAD_DIM, HEAD_DIM), HEAD_DIM)
            scores = dot_nt(qx[0, at, lanes], kx[d, :, lanes])
            u = lax.broadcasted_iota(jnp.int32, scores.shape, 1) - d * rows
            seen = u >= lo_ref[at, :]
            if d == 0:
                t = lax.broadcasted_iota(jnp.int32, scores.shape, 0) + (i % 2) * sub
                seen = seen & (u <= t)
            scores = jnp.where(seen, scores * scale, MASKED)
            top = jnp.max(scores, axis=1, keepdims=True)
            if d > 0:
                old = tops[k, at, :]
                top = jnp.maximum(top, old)
            p = jnp.exp2(scores - top)
            total = jnp.sum(p, axis=1, keepdims=True)
            mixed = jnp.dot(p.astype(BF16), vx[d, :, lanes], preferred_element_type=F32)
            if d > 0:
                fade = jnp.exp2(old - top)
                total = total + totals[k, at, :] * fade
                mixed = mixed + acc[at, lanes] * fade
            tops[k, at, :] = top
            totals[k, at, :] = total
            acc[at, lanes] = mixed
            return 0

        lax.fori_loop(0, 2 * heads, body, 0)

    attend(0)
    k_chain.second()
    v_chain.second()
    attend(2)
    k_chain.arrived(2)
    v_chain.arrived(2)
    attend(1)
    k_chain.third()
    v_chain.third()
    attend(4)
    q_chain.second()
    k_chain.arrived(3)
    v_chain.arrived(3)
    attend(3)
    stores.append(pltpu.make_async_copy(kx, k_out, store_sem.at[2]))
    stores.append(pltpu.make_async_copy(vx, v_out, store_sem.at[3]))
    stores[2].start()
    stores[3].start()

    for k in range(heads):
        lanes = slice(k * HEAD_DIM, (k + 1) * HEAD_DIM)
        out = jnp.where(valid_ref[...] > 0, acc[:, lanes] / totals[k], 0.0)
        att_out[:, lanes] = out.astype(BF16)
        lse = tops[k] + jnp.log2(totals[k])
        lse_out[k] = lse
        row_out[k] = jnp.broadcast_to(lse, (rows, HEAD_DIM)).T[0:1, :]

    att_swap = remote(att_out, att_got, two_send.at[4], two_recv.at[4], pair, h)
    att_swap.start()

    og_stores[0].wait()
    og_stores[1].wait()
    blocks = two_blocks.reshape(devices // 2, 2, rows, depth)

    def to_pair(i):
        at = pl.ds(i * step, step)
        return remote(
            blocks.at[:, 1 - odd, at, :], two_got.at[:, at, :], two_send.at[i], two_recv.at[i], pair, h
        )

    half = width // 2
    loads[3].wait()
    mine = pl.ds(pl.multiple_of(core * half, half), half)
    theirs = pl.ds(pl.multiple_of((1 - core) * half, half), half)

    for i in range(4):
        part = dot_nt(att_out[i * step : (i + 1) * step, :], wo[theirs, :])
        core_send[i] = part.astype(BF16)
        head_sum.to_mate(i, core_send.at[i]).start()
    for i in range(4):
        part = dot_nt(att_out[i * step : (i + 1) * step, :], wo[mine, :])
        head_sum.chip_sum(i, part)
    q_chain.third()

    def finish(i):
        at = slice(i * step, (i + 1) * step)
        total = x_ref[at, :].astype(F32) + head_sum.joined(i)
        mid[at, :] = total
        root = lax.rsqrt(jnp.mean(total * total, axis=-1, keepdims=True) + EPS)
        two = (total * root * gain_two_ref[...]).astype(BF16)
        normed[at, :] = two
        for j in range(devices):
            two_blocks[j, at, :] = two[:, j * depth : (j + 1) * depth]
        to_pair(i).start()

    for i in range(4):
        head_sum.total(i)
        if i > 0:
            finish(i - 1)
    finish(3)
    for src, dst in (
        (mid, mid_out),
        (normed, two_out),
        (blocks.at[:, odd], two_keep_out),
    ):
        stores.append(pltpu.make_async_copy(src, dst, store_sem.at[2 + len(stores)]))
        stores[-1].start()
    q_chain.arrived(2)
    q_chain.arrived(3)
    stores.append(pltpu.make_async_copy(qx, q_out, store_sem.at[2 + len(stores)]))
    stores[-1].start()
    for i in range(4):
        to_pair(i).wait_recv()
    stores.append(pltpu.make_async_copy(two_got, two_got_out, store_sem.at[2 + len(stores)]))
    stores[-1].start()
    att_swap.wait()
    for i in range(4):
        to_pair(i).wait_send()
    for chain in (k_chain, v_chain, q_chain):
        chain.all_sent()
    head_sum.all_sent()
    for store in stores:
        store.wait()


def forward(devices, cores, lengths, x, gains, grad, weights, w_out, prevs):
    rows, width = x.shape
    cols = weights[0].shape[1]
    heads = cols // HEAD_DIM
    depth = width // devices
    parts = WINDOW // rows + 1
    step = rows // 4
    vmem = pl.BlockSpec(memory_space=pltpu.VMEM)
    hbm = pl.BlockSpec(memory_space=pl.ANY)

    def shape(*dims, dtype=BF16):
        return jax.ShapeDtypeStruct(dims, dtype)

    blocks = pltpu.VMEM((4, step, width // 2), BF16)
    dma = pltpu.SemaphoreType.DMA
    return pl.pallas_call(
        functools.partial(forward_kernel, devices, cores),
        in_specs=[pl.BlockSpec(memory_space=pltpu.SMEM)] + [vmem] * 3 + [hbm] * 7,
        out_specs=[hbm] * 11 + [vmem] * 9,
        out_shape=[
            shape(parts, rows, cols),
            shape(parts, rows, cols),
            shape(parts, rows, cols),
            shape(devices // 2, depth, rows),
            shape(devices // 2, depth, rows),
            shape(rows, width, dtype=F32),
            shape(rows, width),
            shape(devices // 2, rows, depth),
            shape(devices // 2, rows, depth),
            shape(devices // 4, 2, rows, depth),
            shape(devices // 4, 2, rows, depth),
            shape(rows, cols),
            shape(rows, cols),
            shape(heads, rows, 1, dtype=F32),
            shape(heads, 1, rows, dtype=F32),
            shape(rows, HEAD_DIM, dtype=F32),
            shape(rows, HEAD_DIM, dtype=F32),
            shape(rows, 1, dtype=jnp.int32),
            shape(1, parts * rows, dtype=jnp.int32),
            shape(rows, 1, dtype=jnp.int32),
        ],
        scratch_shapes=[pltpu.VMEM((parts, rows, cols), BF16)] * 3
        + [pltpu.VMEM((width, cols), BF16)] * 4
        + [
            pltpu.VMEM((rows, width), BF16),
            pltpu.VMEM((devices, depth, rows), BF16),
            pltpu.VMEM((heads, rows, 1), F32),
            pltpu.VMEM((heads, rows, 1), F32),
            pltpu.VMEM((rows, cols), F32),
        ]
        + [blocks] * 6
        + [
            pltpu.VMEM((rows, width), F32),
            pltpu.VMEM((devices, rows, depth), BF16),
            pltpu.VMEM((devices // 2, rows, depth), BF16),
            pltpu.VMEM((rows, width), BF16),
            dma((9,)),
            dma((12,)),
        ]
        + [dma((4,))] * 6
        + [dma((12,))] * 2
        + [dma((5,))] * 2,
        compiler_params=pltpu.CompilerParams(
            collective_id=0, has_side_effects=True, vmem_limit_bytes=56 << 20
        ),
        cost_estimate=cost(10 * rows * width * cols, 40 << 20),
        name="forward",
    )(lengths, x, *gains, grad, *weights, w_out, *prevs)


def norm_two_kernel(
    devices,
    cores,
    parts_ref,
    mid_ref,
    gain_ref,
    og_ref,
    wo_ref,
    att_ref,
    valid_ref,
    lse_row_ref,
    act_ref,
    wd_hbm,
    branch_out,
    gm_out,
    keep_out,
    give_out,
    part_out,
    do_out,
    delta_out,
    stat_out,
    core_got,
    chip,
    y_got,
    own_half,
    other_half,
    flipped,
    wd,
    act,
    store_sem,
    sum_send,
    sum_recv,
):
    rows, width = mid_ref.shape
    heads = att_ref.shape[1] // HEAD_DIM
    step = rows // 4
    s, h, odd, core, pair, mate, across = place(devices, cores)
    head_sum = HeadSum(
        devices, cores, core_got, chip, y_got, own_half, other_half, sum_send, sum_recv
    )
    load = pltpu.make_async_copy(wd_hbm, wd, store_sem.at[2])
    load.start()
    greet(s, mate)
    greet(s, across)
    pl.semaphore_wait(pltpu.get_barrier_semaphore(), 2)
    for i in range(4):
        head_sum.to_mate(i, parts_ref.at[0, pl.ds(i * step, step), :]).start()
    for i in range(4):
        head_sum.chip_sum(i, parts_ref[1, i * step : (i + 1) * step, :].astype(F32))

    half = width // 2
    act[...] = act_ref[...].T
    load.wait()

    def product(i, _):
        start = lax.rem(i // 2 + 1 + core, 2) * half + lax.rem(i, 2) * (half // 2)
        lanes = pl.ds(pl.multiple_of(start, half // 2), half // 2)
        to = pl.ds(pl.multiple_of(lax.rem(i, 2) * (half // 2), half // 2), half // 2)
        branch_out[i // 2, :, to] = jnp.dot(
            act[...], wd[:, lanes], preferred_element_type=F32
        ).astype(BF16)
        return 0

    lax.fori_loop(0, 4, product, 0)

    def finish(i):
        at = slice(i * step, (i + 1) * step)
        x = mid_ref[at, :]
        root = lax.rsqrt(jnp.mean(x * x, axis=-1, keepdims=True) + EPS)
        grad = head_sum.joined(i)
        unit = x * root
        part = jnp.sum(grad * unit, axis=0, keepdims=True)
        part_out[...] = part if i == 0 else part_out[...] + part
        grad = grad * gain_ref[...]
        total = og_ref[at, :].astype(F32) + root * (
            grad - unit * jnp.mean(grad * unit, axis=-1, keepdims=True)
        )
        gm_out[at, :] = total
        low = total.astype(BF16)
        flipped[:, :, at] = low.T.reshape(devices, width // devices, step)
        do = jnp.dot(low, wo_ref[...], preferred_element_type=F32).astype(BF16).astype(F32)
        do = jnp.where(valid_ref[at, :] > 0, do, 0.0)
        do_out[at, :] = do.astype(BF16)
        product = do * att_ref[at, :].astype(F32)
        for k in range(heads):
            delta = jnp.sum(product[:, k * HEAD_DIM : (k + 1) * HEAD_DIM], axis=1, keepdims=True)
            delta_out[k, at, :] = delta
            stat_out[k, 0:1, at] = lse_row_ref[k, :, at]
            stat_out[k, 1:2, at] = jnp.broadcast_to(delta, (step, HEAD_DIM)).T[0:1, :]

    for i in range(4):
        head_sum.total(i)
        if i > 0:
            finish(i - 1)
    finish(3)
    split = flipped.reshape(devices // 2, 2, width // devices, rows)
    stores = [
        pltpu.make_async_copy(split.at[:, odd], keep_out, store_sem.at[0]),
        pltpu.make_async_copy(split.at[:, 1 - odd], give_out, store_sem.at[1]),
    ]
    stores[0].start()
    stores[1].start()
    head_sum.all_sent()
    stores[0].wait()
    stores[1].wait()


def sum_scratch(rows, width):
    return [pltpu.VMEM((4, rows // 4, width // 2), BF16)] * 5


def norm_two_back(
    devices, cores, parts, mid, gain, grad, w_out, attended, valid, lse_row, act, w_down
):
    rows, width = mid.shape
    cols = attended.shape[1]
    heads = cols // HEAD_DIM
    depth = width // devices
    vmem = pl.BlockSpec(memory_space=pltpu.VMEM)
    hbm = pl.BlockSpec(memory_space=pl.ANY)
    dma = pltpu.SemaphoreType.DMA
    return pl.pallas_call(
        functools.partial(norm_two_kernel, devices, cores),
        in_specs=[vmem] * 9 + [hbm],
        out_specs=[vmem, vmem, hbm, hbm] + [vmem] * 4,
        out_shape=[
            jax.ShapeDtypeStruct((2, rows, width // 2), BF16),
            jax.ShapeDtypeStruct((rows, width), F32),
            jax.ShapeDtypeStruct((devices // 2, depth, rows), BF16),
            jax.ShapeDtypeStruct((devices // 2, depth, rows), BF16),
            jax.ShapeDtypeStruct((1, width), F32),
            jax.ShapeDtypeStruct((rows, cols), BF16),
            jax.ShapeDtypeStruct((heads, rows, 1), F32),
            jax.ShapeDtypeStruct((heads, 2, rows), F32),
        ],
        scratch_shapes=sum_scratch(rows, width)
        + [
            pltpu.VMEM((devices, depth, rows), BF16),
            pltpu.VMEM(w_down.shape, BF16),
            pltpu.VMEM(act.shape[::-1], BF16),
            dma((3,)),
            dma((12,)),
            dma((12,)),
        ],
        compiler_params=pltpu.CompilerParams(
            collective_id=1, has_side_effects=True, vmem_limit_bytes=52 << 20
        ),
        cost_estimate=cost(4 * rows * width * cols, 60 << 20),
        name="norm_two_back",
    )(parts, mid, gain, grad, w_out, attended, valid, lse_row, act, w_down)


def attention_back_kernel(
    devices,
    cores,
    do_hbm,
    stat_hbm,
    gg_hbm,
    gg_got_hbm,
    two_hbm,
    two_got_hbm,
    act_hbm,
    act_got_hbm,
    og_hbm,
    og_got_hbm,
    parts_ref,
    mid_ref,
    lo_ref,
    lo_row_ref,
    cos_ref,
    sin_ref,
    kx,
    vx,
    qx,
    lse_ref,
    delta_ref,
    block_out,
    gq_out,
    gk_out,
    gv_out,
    gate_got,
    down_got,
    dx,
    sx,
    dk_acc,
    dv_acc,
    core_got,
    chip,
    y_got,
    own_half,
    other_half,
    gate_g,
    gate_x,
    gate_slot,
    gate_sem,
    gate_send,
    gate_recv,
    down_g,
    down_x,
    down_slot,
    down_sem,
    down_send,
    down_recv,
    load_sem,
    d_send,
    d_recv,
    s_send,
    s_recv,
    sum_send,
    sum_recv,
):
    parts, rows, cols = kx.shape
    heads = cols // HEAD_DIM
    step = rows // 4
    sub = rows // 2
    s, h, odd, core, pair, mate, across = place(devices, cores)
    scale = HEAD_DIM ** (-0.5) * LOG2E
    d_chain = Chain(devices, dx, d_send, d_recv, -1)
    s_chain = Chain(devices, sx, s_send, s_recv, -1)
    head_sum = HeadSum(
        devices, cores, core_got, chip, y_got, own_half, other_half, sum_send, sum_recv
    )
    gate = Give(
        devices,
        1,
        (gg_hbm, gg_got_hbm, two_hbm, two_got_hbm),
        (gate_g, gate_x, gate_slot, gate_got, gate_sem),
        gate_send,
        gate_recv,
    )
    down = Give(
        devices,
        2,
        (act_hbm, act_got_hbm, og_hbm, og_got_hbm),
        (down_g, down_x, down_slot, down_got, down_sem),
        down_send,
        down_recv,
    )
    greet_all(devices, cores)
    loads = [
        pltpu.make_async_copy(do_hbm, dx.at[0], load_sem.at[0]),
        pltpu.make_async_copy(stat_hbm, sx.at[0], load_sem.at[1]),
    ]
    loads[0].start()
    loads[1].start()
    gate.load()
    down.load()

    @pl.when(s >= devices - 2)
    def _():
        for d in (2, 4):
            dx[d] = jnp.zeros_like(dx[d])
            sx[d] = jnp.zeros_like(sx[d])

    loads[0].wait()
    loads[1].wait()
    all_greeted(devices)
    d_chain.first()
    s_chain.first()
    for i in range(4):
        head_sum.to_mate(i, parts_ref.at[0, pl.ds(i * step, step), :]).start()

    def queries_back(start, count):
        def body(i, _):
            k = start + i // 2
            at = pl.ds(pl.multiple_of((i % 2) * sub, sub), sub)
            lanes = pl.ds(pl.multiple_of(k * HEAD_DIM, HEAD_DIM), HEAD_DIM)
            q, do, lo = qx[0, at, lanes], dx[0, at, lanes], lo_ref[at, :]
            lse, delta = lse_ref[k, at, :], delta_ref[k, at, :]
            total = jnp.zeros((sub, HEAD_DIM), F32)
            for d in range(parts):
                key = kx[d, :, lanes]
                scores = dot_nt(q, key)
                u = lax.broadcasted_iota(jnp.int32, scores.shape, 1) - d * rows
                seen = u >= lo
                if d == 0:
                    t = lax.broadcasted_iota(jnp.int32, scores.shape, 0) + (i % 2) * sub
                    seen = seen & (u <= t)
                p = jnp.exp2(jnp.where(seen, scores * scale, MASKED) - lse)
                ds = (p * (dot_nt(do, vx[d, :, lanes]) - delta)).astype(BF16)
                total = total + jnp.dot(ds, key, preferred_element_type=F32)
            gq_out[at, lanes] = turned_back(
                total * HEAD_DIM ** (-0.5), cos_ref[at, :], sin_ref[at, :]
            )
            return 0

        lax.fori_loop(0, 2 * count, body, 0)

    def keys_back(d):
        def body(i, _):
            k = i // 2
            at = pl.ds(pl.multiple_of((i % 2) * sub, sub), sub)
            lanes = pl.ds(pl.multiple_of(k * HEAD_DIM, HEAD_DIM), HEAD_DIM)
            key, value = kx[0, at, lanes], vx[0, at, lanes]
            q, do = qx[d, :, lanes], dx[d, :, lanes]
            scores = dot_nt(key, q)
            u = lax.broadcasted_iota(jnp.int32, scores.shape, 0) + (i % 2) * sub
            seen = u >= lo_row_ref[:, d * rows : (d + 1) * rows]
            if d == 0:
                seen = seen & (u <= lax.broadcasted_iota(jnp.int32, scores.shape, 1))
            lse, delta = sx[d, k, 0:1, :], sx[d, k, 1:2, :]
            p = jnp.exp2(jnp.where(seen, scores * scale - lse, MASKED))
            dv = jnp.dot(p.astype(BF16), do, preferred_element_type=F32)
            ds = (p * (dot_nt(value, do) - delta)).astype(BF16)
            dk = jnp.dot(ds, q, preferred_element_type=F32)
            if d > 0:
                dv = dv + dv_acc[at, lanes]
                dk = dk + dk_acc[at, lanes]
            dv_acc[at, lanes] = dv
            dk_acc[at, lanes] = dk
            return 0

        lax.fori_loop(0, 2 * heads, body, 0)

    gate.loaded()
    gate.make(0)
    gate.half(0, 0).start()
    down.loaded()
    down.make(0)
    down.half(0, 0).start()
    queries_back(0, heads // 4)
    for i in range(4):
        head_sum.chip_sum(i, parts_ref[1, i * step : (i + 1) * step, :].astype(F32))
    s_chain.second()
    d_chain.second()
    gate.half(0, 1).start()
    for j in range(1, gate.count):
        gate.make(j)
        gate.half(j, 0).start()
        gate.half(j, 1).start()
    queries_back(heads // 4, heads // 2)
    down.half(0, 1).start()
    keys_back(0)
    keys_back(2)
    s_chain.third()
    d_chain.third()
    for j in range(1, down.count):
        down.make(j)
        down.half(j, 0).start()
        down.half(j, 1).start()
    queries_back(heads // 4 + heads // 2, heads - heads // 4 - heads // 2)
    for i in range(4):
        head_sum.total(i)
    s_chain.arrived(2)
    d_chain.arrived(2)
    keys_back(1)
    keys_back(4)
    for i in range(4):
        at = slice(i * step, (i + 1) * step)
        block_out[at, :] = (mid_ref[at, :] + head_sum.joined(i)).astype(BF16)
    s_chain.arrived(3)
    d_chain.arrived(3)
    keys_back(3)
    for k in range(heads):
        lanes = slice(k * HEAD_DIM, (k + 1) * HEAD_DIM)
        gk_out[:, lanes] = turned_back(
            dk_acc[:, lanes] * HEAD_DIM ** (-0.5), cos_ref[...], sin_ref[...]
        )
        gv_out[:, lanes] = dv_acc[:, lanes].astype(BF16)
    d_chain.all_sent()
    s_chain.all_sent()
    head_sum.all_sent()
    gate.finish()
    down.finish()


def attention_back(
    devices, cores, do, stat, gate, down, branch, mid, low_col, low_row, tables, keys, values, queries, lse, delta
):
    rows, width = mid.shape
    parts, _, cols = keys.shape
    heads = cols // HEAD_DIM
    units = gate[0].shape[0]
    count, depth = devices // 4, width // devices
    vmem = pl.BlockSpec(memory_space=pltpu.VMEM)
    hbm = pl.BlockSpec(memory_space=pl.ANY)
    dma = pltpu.SemaphoreType.DMA
    give = [
        pltpu.VMEM((2, units, rows), BF16),
        pltpu.VMEM((2, count, rows, depth), BF16),
        pltpu.VMEM((count, units, depth), BF16),
        dma((2 + 2 * count,)),
        dma((2 * count,)),
        dma((2 * count,)),
    ]
    flops = 14 * rows * rows * parts * cols
    return pl.pallas_call(
        functools.partial(attention_back_kernel, devices, cores),
        in_specs=[hbm] * 10 + [vmem] * 11,
        out_specs=[vmem] * 6,
        out_shape=[jax.ShapeDtypeStruct((rows, width), BF16)]
        + [jax.ShapeDtypeStruct((rows, cols), BF16)] * 3
        + [jax.ShapeDtypeStruct((count, units, depth), BF16)] * 2,
        scratch_shapes=[
            pltpu.VMEM((parts, rows, cols), BF16),
            pltpu.VMEM((parts, heads, 2, rows), F32),
            pltpu.VMEM((rows, cols), F32),
            pltpu.VMEM((rows, cols), F32),
        ]
        + sum_scratch(rows, width)
        + give
        + give
        + [dma((2,))]
        + [dma((4,))] * 4
        + [dma((12,))] * 2,
        compiler_params=pltpu.CompilerParams(
            collective_id=2, has_side_effects=True, vmem_limit_bytes=58 << 20
        ),
        cost_estimate=cost(flops, 80 << 20),
        name="attention_back",
    )(do, stat, *gate, *down, branch, mid, low_col, low_row, *tables, keys, values, queries, lse, delta)


def on_device(
    tokens,
    gain_attn,
    gain_mlp,
    w_query,
    w_key,
    w_value,
    w_out,
    w_gate,
    w_up,
    w_down,
    prev_keys,
    prev_values,
    lengths,
    out_grad,
):
    rows = tokens.shape[0]
    width = w_query.shape[1]
    devices, cores = lax.axis_size("seq"), lax.axis_size("head")
    index = lax.axis_index("seq")
    bits = jnp.stack([index & 1, lax.axis_index("head") & 1]).astype(jnp.int32)
    gain_one, gain_two = gain_attn[None, :], gain_mlp[None, :]

    (
        keys,
        values,
        queries,
        one_keep,
        one_give,
        mid,
        normed_two,
        two_keep,
        two_got,
        out_keep,
        out_give,
        attended_got,
        attended,
        lse,
        lse_row,
        cosine,
        sine,
        low_col,
        low_row,
        valid,
    ) = forward(
        devices,
        cores,
        lengths,
        tokens,
        (gain_one, gain_two),
        out_grad,
        (w_key, w_value, w_query),
        w_out,
        (prev_keys, prev_values),
    )
    order = Order()
    out_keep, out_give = (a.reshape(devices // 2, rows, -1) for a in (out_keep, out_give))
    out_pair = (out_keep, swap(out_give, "seq", 2))
    one_pair = (one_keep, swap(one_give, "seq", 1))
    two_pair = (two_keep, two_got)
    w_gate, w_up, w_down = w_gate.T, w_up.T, w_down.T
    act, grad_gate, grad_up = mlp(normed_two, out_grad, w_gate, w_up, w_down)
    act_got = swap(act, "seq", 2)
    gate_got = swap(grad_gate, "seq", 1)
    up_got = swap(grad_up, "seq", 1)
    norm_parts = back_products(bits, grad_gate, grad_up, w_gate, w_up)
    (
        branch_parts,
        grad_mid,
        mid_keep,
        mid_give,
        gain_mlp_part,
        grad_att,
        delta,
        stat,
    ) = norm_two_back(
        devices,
        cores,
        norm_parts,
        mid,
        gain_two,
        out_grad,
        w_out,
        attended,
        valid,
        lse_row,
        act,
        w_down,
    )
    order.ran(delta)
    gate = WeightGrad(order, two_pair, grad_gate, gate_got, 1, "gate", True)
    up = WeightGrad(order, two_pair, grad_up, up_got, 1, "up", True)
    down = WeightGrad(order, out_pair, act, act_got, 2, "down", True)
    block_out, grad_query_raw, grad_key_raw, grad_value_raw, gate.got, down.got = attention_back(
        devices,
        cores,
        order.after(grad_att),
        stat,
        (grad_gate, gate_got, *two_pair),
        (act, act_got, *out_pair),
        branch_parts,
        mid,
        low_col,
        low_row,
        (cosine, sine),
        keys,
        values,
        queries,
        lse,
        delta,
    )
    order.ran(grad_query_raw)
    query_got = swap(grad_query_raw, "seq", 1)
    key_got = swap(grad_key_raw, "seq", 1)
    value_got = swap(grad_value_raw, "seq", 1)
    mid_pair = (mid_keep, swap(order.after(mid_give), "seq", 1))
    gate.keep()
    up.give()
    down.keep()
    lefts = (grad_query_raw, grad_key_raw, grad_value_raw)
    rights = (w_query, w_key, w_value)
    give = order.ran(half_product(order.after(bits), lefts, rights, 1, None, "norm_one_give"))
    give = swap(give, "head", 1)
    query = WeightGrad(order, one_pair, grad_query_raw, query_got, 1, "query")
    key = WeightGrad(order, one_pair, grad_key_raw, key_got, 1, "key")
    value = WeightGrad(order, one_pair, grad_value_raw, value_got, 1, "value")
    wout = WeightGrad(order, mid_pair, attended, attended_got, 1, "wout")
    query.give()
    chip = order.ran(half_product(order.after(bits), lefts, rights, 0, give, "norm_one_keep"))
    chip_got = swap(chip, "head", 2)
    key.give()
    value.give()
    up.keep()
    wout.give()
    own = (chip.astype(F32) + chip_got.astype(F32)).astype(BF16)
    other = swap(own, "head", 1)
    query.keep()
    key.keep()
    tokens_grad, gain_attn_part = by_rows(
        back_kernel,
        order.after(bits),
        (tokens, own, other, gain_one, grad_mid),
        3,
        (BF16, F32),
        "tokens_back",
        part=1,
    )
    order.ran(gain_attn_part)
    value.keep()
    wout.keep()
    gains = gain_sum(jnp.concatenate([gain_attn_part, gain_mlp_part], axis=0))
    gain_attn_grad, gain_mlp_grad = gains[0], gains[1]
    w_gate_grad, w_up_grad, w_down_grad = gate.finish(), up.finish(), down.finish()
    w_out_grad = wout.finish()
    w_query_grad, w_key_grad, w_value_grad = query.finish(), key.finish(), value.finish()
    return (
        block_out,
        tokens_grad,
        gain_attn_grad,
        gain_mlp_grad,
        w_query_grad,
        w_key_grad,
        w_value_grad,
        w_out_grad,
        w_gate_grad,
        w_up_grad,
        w_down_grad,
    )


def solution(mesh):
    by_head = P(None, "head")
    both = P("seq", "head")
    placed = (P("seq", None), P(), P()) + (by_head,) * 9 + (P(), P("seq", None))
    return jax.shard_map(
        on_device,
        mesh=mesh,
        in_specs=placed,
        out_specs=(P("seq", None), P("seq", None), P("seq"), P("seq")) + (both,) * 7,
        check_vma=False,
    )
```

time: 596 us -> 472 us (0.79)
  waiting for transfers between devices: 244 us -> 89.2 us
  Pallas kernels: 242 us -> 318 us
  other arithmetic: 42 us -> 11.8 us
  starting transfers between devices: 49.9 us -> 37.9 us
    ppermute x43 -> x27, waiting for transfers between devices: 194 us -> 89.2 us  [swap(): lax.ppermute(block, axis, [(i, i ^ bit) for i in range(lax.axis_size(axis...]
    pallas_call x4, Pallas kernels: 68 us -> 146 us  [the longest x1 79.9 us: attention_back(): pl.pallas_call(functools.partial(attention_back_kernel, devices, cores),...]
    ppermute x6 -> x0, waiting for transfers between devices: 49.7 us -> none  [shifted(): lax.ppermute(block, 'seq', [(i, i + distance) for i in range(n) if 0 <= i...]
    pallas_call x1, Pallas kernels: 110 us -> 122 us  [forward(): pl.pallas_call(functools.partial(forward_kernel, devices, cores), in_spec...]
    pallas_call x3 -> x1, Pallas kernels: 16.8 us -> 6.64 us  [by_rows(): pl.pallas_call(kernel, grid_spec=pltpu.PrefetchScalarGridSpec(num_scalar_...]
    convert_element_type x8 -> x1, other arithmetic: 11.6 us -> 1.94 us  [on_device(): own = (chip.astype(F32) + chip_got.astype(F32)).astype(BF16)]
    sub x4 -> x0, other arithmetic: 8.39 us -> none  [the longest x2 5.79 us: on_device(): low = low - first_row]
    ppermute x6 -> x0, starting transfers between devices: 7.7 us -> none  [shifted(): lax.ppermute(block, 'seq', [(i, i + distance) for i in range(n) if 0 <= i...]
  transfers between devices with their start and end apart: 49 -> 27, of which waited for: 20 -> 10; matrix products, arithmetic and copies ran while one was open for 5% -> 3% of each run, Pallas kernels for 17% -> 39%
where the time goes in v3:
time: 472 us; the launch traced here: 468 us
  Pallas kernels  318 us (67%)
  waiting for transfers between devices  89.2 us (19%)
  starting transfers between devices  37.9 us (8%)
  other arithmetic  11.8 us (2%)
  local copies, waits for them, and re-layouts  9.97 us (2%)
    pallas_call x1, Pallas kernels, forward(): pl.pallas_call(functools.partial(forward_kernel, devices, cores), in_spec...  122 us
    ppermute x27, waiting for transfers between devices, swap(): lax.ppermute(block, axis, [(i, i ^ bit) for i in range(lax.axis_size(axis...  89.2 us
    pallas_call x1, Pallas kernels, attention_back(): pl.pallas_call(functools.partial(attention_back_kernel, devices, cores),...  79.9 us
    pallas_call x1, Pallas kernels, norm_two_back(): pl.pallas_call(functools.partial(norm_two_kernel, devices, cores), in_spe...  38.4 us
    ppermute x27, starting transfers between devices, swap(): lax.ppermute(block, axis, [(i, i ^ bit) for i in range(lax.axis_size(axis...  37.9 us
    pallas_call x12, Pallas kernels, grad_blocks(): pl.pallas_call(kernel, grid_spec=pltpu.PrefetchScalarGridSpec(num_scalar_...  34.3 us
    pallas_call x1, Pallas kernels, mlp(): pl.pallas_call(mlp_kernel, grid=(pl.cdiv(width, step),), in_specs=[whole,...  15.2 us
    pallas_call x1, Pallas kernels, back_products(): pl.pallas_call(back_products_kernel, grid_spec=pltpu.PrefetchScalarGridSp...  12 us
  transfers between devices with their start and end apart: 27, of which 10 were waited for; matrix products, arithmetic and copies ran while one was open for 3% of the time, Pallas kernels for 39%

profile of v3, /device:TPU:0, one launch (start us, length us, event | category | flops | bytes accessed | tf_op | source)
XLA Modules:
  0.0 467.9 jit_solution(15739451477655538013)
XLA Ops:
  0.6 122.4 %forward.1 = (bf16[5,512,512]{2,1,0:T(8,128)(2,1)}, bf16[5,512,512]{2,1,0:T(8,128)(2,1)}, bf16[5,512,512]{2,1,0:T(8,128)(2,1)}, bf16[4,256,512]{2,1,0:T(8,128)(2...) custom-call(s32[4]{0:T(128)} %lengths_ref.1, ...), custom_call_target="tpu_custom_call" | custom-call | flops 5368709120 | bytes 41943040 | tf_op jit(solution)/shard_map/forward/pallas_call | solution.py:914
  123.0 15.2 %mlp.1 = (bf16[1376,512]{1,0:T(8,128)(2,1)S(1)}, bf16[1376,512]{1,0:T(8,128)(2,1)}, bf16[1376,512]{1,0:T(8,128)(2,1)}) custom-call(bf16[512,2048]{1,0:T(8,128)(2,1)} %get-tuple-element.67.x_ref, bf16[512,2048]{1,0:T(8,128)(2,1)} %og_ref.1, bf16[1376,2048]{1,0:T(8,128)(2,1)} %bitcast.47, bf16[1376,2048]{1,0:T(8,128)(2,1)} %bitcast.49, bf16[1376,2048]{1,0:T(8,128)(2,1)} %bitcast.43), custom_call_target="tpu_custom_call" | custom-call | flops 8657043456 | bytes 16908288 | tf_op jit(solution)/shard_map/mlp/pallas_call | solution.py:164
  138.2 3.4 collective-permute-start
  141.7 1.9 collective-permute-start.2
  143.7 1.9 collective-permute-start.4
  145.8 12.0 %back_products.1.parts_ref = bf16[2,512,1024]{2,1,0:T(8,128)(2,1)S(1)} custom-call(s32[2]{0:T(128)S(1)} %pad_add_fusion.bits_ref, bf16[1376,512]{1,0:T(8,128)(2,1)} %get-tuple-element.68.gg_ref.gg_hbm.refs_2_, bf16[1376,512]{1,0:T(8,128)(2,1)} %get-tuple-element.69.gu_ref.refs_2_, bf16[1376,2048]{1,0:T(8,128)(2,1)} %bitcast.48, bf16[1376,2048]{1,0:T(8,128)(2,1)} %bitcast.50), custom_call_target="tpu_custom_call" | custom-call | flops 5771362304 | bytes 11272192 | tf_op jit(solution)/shard_map/back_products/pallas_call | solution.py:195
  157.8 1.3 copy-done.24
  159.2 38.4 %norm_two_back.1 = (bf16[2,512,1024]{2,1,0:T(8,128)(2,1)}, f32[512,2048]{1,0:T(8,128)}, bf16[4,256,512]{2,1,0:T(8,128)(2,1)}, bf16[4,256,512]{2,1,0:T(8,128)(2,1...) custom-call(bf16[2,512,1024]{2,1,0:T(8,128)(2,1)} %copy-done.24, ...), custom_call_target="tpu_custom_call" | custom-call | flops 2147483648 | bytes 62914560 | tf_op jit(solution)/shard_map/norm_two_back/pallas_call | solution.py:1090
  197.6 0.8 copy-done.34
  199.2 1.0 copy-done.26
  200.2 79.9 %attention_back.1 = (bf16[512,2048]{1,0:T(8,128)(2,1)}, bf16[512,512]{1,0:T(8,128)(2,1)}, bf16[512,512]{1,0:T(8,128)(2,1)}, bf16[512,512]{1,0:T(8,128)(2,1)}, bf...) custom-call(bf16[512,512]{1,0:T(8,128)(2,1)} %copy-done.34, f32[4,2,512]{2,1,0:T(2,128)} %copy-done.35, ...), custom_call_target="tpu_custom_call" | custom-call | flops 9395240960 | bytes 83886080 | tf_op jit(solution)/shard_map/attention_back/pallas_call | solution.py:1355
  280.1 4.4 gate_keep.1
  284.5 1.1 copy-done.9
  285.6 5.3 %up_give.1 = bf16[2,1376,256]{2,1,0:T(8,128)(2,1)} custom-call(s32[2]{0:T(128)S(1)} %pad_add_fusion.2.order_ref, bf16[4,512,256]{2,1,0:T(8,128)(2,1)S(1)} %copy-done.1, bf16[4,512,256]{2,1,0:T(8,128)(2,1)S(1)} %copy-done.2, bf16[1376,512]{1,0:T(8,128)(2,1)} %get-tuple-element.69.gu_ref.refs_2_, bf16[1376,512]{1,0:T(8,128)(2,1)} %collective-permute-done.3.refs_3_), custom_call_target="tpu_custom_call" | custom-call | flops 1442840576 | bytes 4227072 | tf_op jit(solution)/shard_map/up_give/pallas_call | solution.py:241
  291.0 4.3 down_keep.1
  295.4 4.1 norm_one_give.1
  299.6 1.8 collective-permute-start.5
  301.4 0.9 slice.91
  302.3 2.6 collective-permute-start.26
  305.2 9.2 %collective-permute-done.5.refs_3_ = bf16[512,512]{1,0:T(8,128)(2,1)S(1)} collective-permute-done((bf16[512,512]{1,0:T(8,128)(2,1)S(1)}, bf16[512,512]{1,0:T(8,128)(2,1)S(1)}, u32[]{:S(2)}, u32[]{:S(2)}) %collective-permute-start.5) | collective-permute-done | bytes 524320 | tf_op jit(solution)/shard_map/ppermute | solution.py:24
  314.4 1.7 collective-permute-start.8
  316.4 1.4 query_give.1
  317.9 4.8 %norm_one_keep.1 = bf16[512,1024]{1,0:T(8,128)(2,1)} custom-call(s32[2]{0:T(128)S(1)} %pad_add_fusion.bits_ref, bf16[512,512]{1,0:T(8,128)(2,1)S(1)} %copy-done.7, bf16[512,512]{1,0:T(8,128)(2,1)S(1)} %copy-done.5, bf16[512,512]{1,0:T(8,128)(2,1)} %get-tuple-element.101.refs_2_, bf16[2048,512]{1,0:T(8,128)(2,1)S(1)} %copy-done.4, bf16[2048,512]{1,0:T(8,128)(2,1)} %refs_4_.3, ...), custom_call_target="tpu_custom_call" | custom-call | flops 1610612736 | bytes 4718592 | tf_op jit(solution)/shard_map/norm_one_keep/pallas_call | solution.py:131
  322.7 2.9 collective-permute-done.7.refs_3_
  325.6 0.8 copy-done.22
  326.4 1.5 collective-permute-start.13
  327.9 1.2 slice.87
  329.3 1.4 key_give.1
  330.8 6.2 %collective-permute-done.8.refs_3_ = bf16[512,512]{1,0:T(8,128)(2,1)} collective-permute-done((bf16[512,512]{1,0:T(8,128)(2,1)}, bf16[512,512]{1,0:T(8,128)(2,1)}, u32[]{:S(2)}, u32[]{:S(2)}) %collective-permute-start.8) | collective-permute-done | bytes 524320 | tf_op jit(solution)/shard_map/ppermute | solution.py:24
  336.9 2.6 collective-permute-start.24
  340.0 1.6 collective-permute-start.12
  341.6 2.4 add_bitcast_fusion
  344.0 2.6 value_give.1
  346.7 4.4 up_keep.1
  351.1 7.8 %collective-permute-done.10.refs_1_ = bf16[4,256,512]{2,1,0:T(8,128)(2,1)} collective-permute-done((bf16[4,256,512]{2,1,0:T(8,128)(2,1)}, bf16[4,256,512]{2,1,0:T(8,128)(2,1)}, u32[]{:S(2)}, u32[]{:S(2)}) %collective-permute-start.10) | collective-permute-done | bytes 1048608 | tf_op jit(solution)/shard_map/ppermute | solution.py:24
  359.0 2.4 wout_give.1
  361.4 5.6 %collective-permute-done.11.refs_4_ = bf16[2,256,512]{2,1,0:T(8,128)(2,1)S(1)} collective-permute-done((bf16[2,256,512]{2,1,0:T(8,128)(2,1)S(1)}, bf16[2,256,512]{2,1,0:T(8,128)(2,1)S(1)}, u32[]{:S(2)}, u32[]{:S(2)}) %collective-permute-start.11) | collective-permute-done | bytes 524320 | tf_op jit(solution)/shard_map/ppermute | solution.py:24
  367.0 1.4 query_keep.1
  368.5 2.7 collective-permute-start.18
  371.3 11.6 %collective-permute-done.12.refs_4_ = bf16[2,256,512]{2,1,0:T(8,128)(2,1)S(1)} collective-permute-done((bf16[2,256,512]{2,1,0:T(8,128)(2,1)S(1)}, bf16[2,256,512]{2,1,0:T(8,128)(2,1)S(1)}, u32[]{:S(2)}, u32[]{:S(2)}) %collective-permute-start.12) | collective-permute-done | bytes 524320 | tf_op jit(solution)/shard_map/ppermute | solution.py:24
  382.8 1.4 key_keep.1
  384.3 0.6 collective-permute-start.19
  384.9 1.9 add_convert_fusion.own_ref
  387.0 2.4 add_bitcast_fusion.2
  389.4 2.5 collective-permute-start.20
  392.0 1.9 collective-permute-start.25
  393.9 0.9 add_bitcast_fusion.6
  394.7 3.0 collective-permute-done.19
  397.7 0.9 add_bitcast_fusion.5
  398.6 6.6 %tokens_back.1 = (bf16[512,2048]{1,0:T(8,128)(2,1)}, f32[1,2048]{1,0:T(1,128)S(1)}) custom-call(s32[2]{0:T(128)S(1)} %pad_add_fusion.bits_ref, bf16[512,2048]{1,0:T(8,128)(2,1)S(1)} %copy-done.18, bf16[512,1024]{1,0:T(8,128)(2,1)S(1)} %add_convert_fusion.own_ref, bf16[512,1024]{1,0:T(8,128)(2,1)S(1)} %collective-permute-done.14.other_ref, ...), custom_call_target="tpu_custom_call" | custom-call | flops 10485760 | bytes 14680064 | tf_op jit(solution)/shard_map/tokens_back/pallas_call | solution.py:95
  405.3 1.8 collective-permute-start.15
  407.1 22.9 %collective-permute-done.25 = bf16[1,1376,256]{2,1,0:T(8,128)(2,1)S(1)} collective-permute-done((bf16[1,1376,256]{2,1,0:T(8,128)(2,1)S(1)}, bf16[1,1376,256]{2,1,0:T(8,128)(2,1)S(1)}, u32[]{:S(2)}, u32[]{:S(2)}) %collective-permute-start.25) | collective-permute-done | bytes 704544 | tf_op jit(solution)/shard_map/ppermute | solution.py:24
  430.0 1.3 add_bitcast_fusion.1
  431.3 2.4 collective-permute-start.16
  433.7 2.6 value_keep.1
  436.4 2.1 collective-permute-start.17
  438.6 2.4 wout_keep.1
  441.1 0.9 collective-permute-start.23
  442.0 2.1 collective-permute-start.21
  444.6 16.5 %collective-permute-done.23 = bf16[1,256,512]{2,1,0:T(8,128)(2,1)S(1)} collective-permute-done((bf16[1,256,512]{2,1,0:T(8,128)(2,1)S(1)}, bf16[1,256,512]{2,1,0:T(8,128)(2,1)S(1)}, u32[]{:S(2)}, u32[]{:S(2)}) %collective-permute-start.23) | collective-permute-done | bytes 262176 | tf_op jit(solution)/shard_map/ppermute | solution.py:24
  461.2 0.9 add_bitcast_fusion.3
  462.0 3.4 collective-permute-done.21
  465.5 0.9 add_bitcast_fusion.4
  466.3 1.3 copy.26
  (109 shorter events, 3.5 us)
Async XLA Ops:
  138.2 19.6 %copy-start.13 = (bf16[1376,512]{1,0:T(8,128)(2,1)}, bf16[1376,512]{1,0:T(8,128)(2,1)S(1)}, u32[]{:S(2)}) copy-start(bf16[1376,512]{1,0:T(8,128)(2,1)S(1)} %get-tuple-element.74.act_ref.act_hbm.refs_2_) | copy-start | bytes 4227076
  138.2 61.0 %collective-permute-start = (bf16[1376,512]{1,0:T(8,128)(2,1)}, bf16[1376,512]{1,0:T(8,128)(2,1)}, u32[]{:S(2)}, u32[]{:S(2)}) collective-permute-start(bf16[1376,512]{1,0:T(8,128)(2,1)} %get-tuple-element.68.gg_ref.gg_hbm.refs_2_), channel_id=1, source_target_pairs={{0,4},{4,0},{8,12},{12,8},{16,20},{20,16},{24,28},{28,24},{1,5},{5... | collective-permute-start | bytes 4227080 | tf_op jit(solution)/shard_map/ppermute | solution.py:24
  141.6 57.6 %collective-permute-start.1 = (bf16[1376,512]{1,0:T(8,128)(2,1)S(1)}, bf16[1376,512]{1,0:T(8,128)(2,1)}, u32[]{:S(2)}, u32[]{:S(2)}) collective-permute-start(bf16[1376,512]{1,0:T(8,128)(2,1)S(1)} %get-tuple-element.74.act_ref.act_hbm.refs_2_), channel_id=1, source_target_pairs={{0,8},{4,12},{8,0},{12,4},{16,24},{20,28},{24,16},{28,20},{1,9},{5... | collective-permute-start | bytes 4227080 | tf_op jit(solution)/shard_map/ppermute | solution.py:24
  141.7 57.5 %collective-permute-start.2 = (bf16[4,512,256]{2,1,0:T(8,128)(2,1)}, bf16[4,512,256]{2,1,0:T(8,128)(2,1)S(1)}, u32[]{:S(2)}, u32[]{:S(2)}) collective-permute-start(bf16[4,512,256]{2,1,0:T(8,128)(2,1)} %bitcast.8), channel_id=1, source_target_pairs={{0,8},{4,12},{8,0},{12,4},{16,24},{20,28},{24,16},{28,20},{1,9},{5... | collective-permute-start | bytes 3145736 | tf_op jit(solution)/shard_map/ppermute | solution.py:24
  143.7 142.0 %collective-permute-start.3 = (bf16[1376,512]{1,0:T(8,128)(2,1)}, bf16[1376,512]{1,0:T(8,128)(2,1)}, u32[]{:S(2)}, u32[]{:S(2)}) collective-permute-start(bf16[1376,512]{1,0:T(8,128)(2,1)} %get-tuple-element.69.gu_ref.refs_2_), channel_id=1, source_target_pairs={{0,4},{4,0},{8,12},{12,8},{16,20},{20,16},{24,28},{28,24},{1,5},{5... | collective-permute-start | bytes 4227080 | tf_op jit(solution)/shard_map/ppermute | solution.py:24
  143.7 161.2 %collective-permute-start.4 = (bf16[4,256,512]{2,1,0:T(8,128)(2,1)}, bf16[4,256,512]{2,1,0:T(8,128)(2,1)S(1)}, u32[]{:S(2)}, u32[]{:S(2)}) collective-permute-start(bf16[4,256,512]{2,1,0:T(8,128)(2,1)} %get-tuple-element.104), channel_id=1, source_target_pairs={{0,4},{4,0},{8,12},{12,8},{16,20},{20,16},{24,28},{28,24},{1,5},{5... | collective-permute-start | bytes 3145736 | tf_op jit(solution)/shard_map/ppermute | solution.py:24
  145.8 13.4 %copy-start.15 = (bf16[512,512]{1,0:T(8,128)(2,1)S(1)}, bf16[512,512]{1,0:T(8,128)(2,1)}, u32[]{:S(2)}) copy-start(bf16[512,512]{1,0:T(8,128)(2,1)} %get-tuple-element.71.att_ref.refs_2_) | copy-start | bytes 1572868
  145.8 13.4 %copy-start.30 = (s32[512,1]{1,0:T(8,128)S(1)}, s32[512,1]{1,0:T(8,128)}, u32[]{:S(2)}) copy-start(s32[512,1]{1,0:T(8,128)} %get-tuple-element.72.valid_ref) | copy-start | bytes 6148
  145.8 13.4 %copy-start.31 = (f32[2048]{0:T(1024)S(1)}, f32[2048]{0:T(1024)}, u32[]{:S(2)}) copy-start(f32[2048]{0:T(1024)} %param.16) | copy-start | bytes 24580
  145.8 13.4 %copy-start.33 = (f32[4,1,512]{2,1,0:T(1,128)S(1)}, f32[4,1,512]{2,1,0:T(1,128)}, u32[]{:S(2)}) copy-start(f32[4,1,512]{2,1,0:T(1,128)} %get-tuple-element.73.lse_row_ref) | copy-start | bytes 24580
  157.8 1.3 copy-start.24
  197.6 0.8 copy-start.34
  198.4 0.6 copy-start.35
  199.2 1.0 copy-start.26
  200.2 79.9 %copy-start.1 = (bf16[4,512,256]{2,1,0:T(8,128)(2,1)S(1)}, bf16[4,512,256]{2,1,0:T(8,128)(2,1)}, u32[]{:S(2)}) copy-start(bf16[4,512,256]{2,1,0:T(8,128)(2,1)} %get-tuple-element.79.two_hbm.refs_0_) | copy-start | bytes 3145732
  200.2 79.9 %copy-start.2 = (bf16[4,512,256]{2,1,0:T(8,128)(2,1)S(1)}, bf16[4,512,256]{2,1,0:T(8,128)(2,1)}, u32[]{:S(2)}) copy-start(bf16[4,512,256]{2,1,0:T(8,128)(2,1)} %get-tuple-element.80.two_got_hbm.refs_1_) | copy-start | bytes 3145732
  284.5 1.1 copy-start.9
  285.6 5.4 %copy-start.14 = (bf16[1376,512]{1,0:T(8,128)(2,1)S(1)}, bf16[1376,512]{1,0:T(8,128)(2,1)}, u32[]{:S(2)}) copy-start(bf16[1376,512]{1,0:T(8,128)(2,1)} %copy-done.13) | copy-start | bytes 4227076
  285.6 5.4 %copy-start.25 = (bf16[2,2,512,256]{3,2,1,0:T(8,128)(2,1)S(1)}, bf16[2,2,512,256]{3,2,1,0:T(8,128)(2,1)}, u32[]{:S(2)}) copy-start(bf16[2,2,512,256]{3,2,1,0:T(8,128)(2,1)} %get-tuple-element.81) | copy-start | bytes 3145732
  285.6 5.4 %copy-start.27 = (bf16[4,512,256]{2,1,0:T(8,128)(2,1)S(1)}, bf16[4,512,256]{2,1,0:T(8,128)(2,1)}, u32[]{:S(2)}) copy-start(bf16[4,512,256]{2,1,0:T(8,128)(2,1)} %copy-done.26) | copy-start | bytes 3145732
  290.9 49.1 %collective-permute-start.9 = (bf16[2,1376,256]{2,1,0:T(8,128)(2,1)}, bf16[2,1376,256]{2,1,0:T(8,128)(2,1)}, u32[]{:S(2)}, u32[]{:S(2)}) collective-permute-start(bf16[2,1376,256]{2,1,0:T(8,128)(2,1)} %up_give.1), channel_id=1, source_target_pairs={{0,8},{4,12},{8,0},{12,4},{16,24},{20,28},{24,16},{28,20},{1,9},{5... | collective-permute-start | bytes 4227080 | tf_op jit(solution)/shard_map/ppermute | solution.py:24
  291.0 4.4 copy-start.4
  291.0 4.4 copy-start.5
  291.0 4.4 copy-start.7
  295.4 6.0 %copy-start.11 = (bf16[2,1376,256]{2,1,0:T(8,128)(2,1)}, bf16[2,1376,256]{2,1,0:T(8,128)(2,1)S(1)}, u32[]{:S(2)}) copy-start(bf16[2,1376,256]{2,1,0:T(8,128)(2,1)S(1)} %down_keep.1) | copy-start | bytes 4227076
  299.5 16.9 %copy-start = (bf16[4,256,512]{2,1,0:T(8,128)(2,1)S(1)}, bf16[4,256,512]{2,1,0:T(8,128)(2,1)}, u32[]{:S(2)}) copy-start(bf16[4,256,512]{2,1,0:T(8,128)(2,1)} %get-tuple-element.103.refs_0_) | copy-start | bytes 3145732
  299.5 16.6 %collective-permute-start.6 = (bf16[512,1024]{1,0:T(8,128)(2,1)S(1)}, bf16[512,1024]{1,0:T(8,128)(2,1)S(1)}, u32[]{:S(2)}, u32[]{:S(2)}) collective-permute-start(bf16[512,1024]{1,0:T(8,128)(2,1)S(1)} %norm_one_give.1), channel_id=1, source_target_pairs={{0,1},{1,0},{2,3},{3,2},{4,5},{5,4},{6,7},{7,6},{8,9},{9,8},{10,11... | collective-permute-start | bytes 3145736 | tf_op jit(solution)/shard_map/ppermute | solution.py:24
  299.6 14.8 %collective-permute-start.5 = (bf16[512,512]{1,0:T(8,128)(2,1)S(1)}, bf16[512,512]{1,0:T(8,128)(2,1)S(1)}, u32[]{:S(2)}, u32[]{:S(2)}) collective-permute-start(bf16[512,512]{1,0:T(8,128)(2,1)S(1)} %copy-done.7), channel_id=1, source_target_pairs={{0,4},{4,0},{8,12},{12,8},{16,20},{20,16},{24,28},{28,24},{1,5},{5... | collective-permute-start | bytes 1572872 | tf_op jit(solution)/shard_map/ppermute | solution.py:24
  302.3 37.3 %collective-permute-start.26 = (bf16[1,1376,256]{2,1,0:T(8,128)(2,1)}, bf16[1,1376,256]{2,1,0:T(8,128)(2,1)}, u32[]{:S(2)}, u32[]{:S(2)}) collective-permute-start(bf16[1,1376,256]{2,1,0:T(8,128)(2,1)} %slice.91), channel_id=1, source_target_pairs={{0,16},{4,20},{8,24},{12,28},{16,0},{20,4},{24,8},{28,12},{1,17},{... | collective-permute-start | bytes 2113544 | tf_op jit(solution)/shard_map/ppermute | solution.py:24
  304.9 20.7 %collective-permute-start.7 = (bf16[512,512]{1,0:T(8,128)(2,1)S(1)}, bf16[512,512]{1,0:T(8,128)(2,1)S(1)}, u32[]{:S(2)}, u32[]{:S(2)}) collective-permute-start(bf16[512,512]{1,0:T(8,128)(2,1)S(1)} %copy-done.5), channel_id=1, source_target_pairs={{0,4},{4,0},{8,12},{12,8},{16,20},{20,16},{24,28},{28,24},{1,5},{5... | collective-permute-start | bytes 1572872 | tf_op jit(solution)/shard_map/ppermute | solution.py:24
  314.3 3.5 copy-start.20
  314.4 22.6 %collective-permute-start.8 = (bf16[512,512]{1,0:T(8,128)(2,1)}, bf16[512,512]{1,0:T(8,128)(2,1)}, u32[]{:S(2)}, u32[]{:S(2)}) collective-permute-start(bf16[512,512]{1,0:T(8,128)(2,1)} %get-tuple-element.101.refs_2_), channel_id=1, source_target_pairs={{0,4},{4,0},{8,12},{12,8},{16,20},{20,16},{24,28},{28,24},{1,5},{5... | collective-permute-start | bytes 1572872 | tf_op jit(solution)/shard_map/ppermute | solution.py:24
  316.1 42.8 %collective-permute-start.10 = (bf16[4,256,512]{2,1,0:T(8,128)(2,1)}, bf16[4,256,512]{2,1,0:T(8,128)(2,1)}, u32[]{:S(2)}, u32[]{:S(2)}) collective-permute-start(bf16[4,256,512]{2,1,0:T(8,128)(2,1)} %get-tuple-element.112), channel_id=1, source_target_pairs={{0,4},{4,0},{8,12},{12,8},{16,20},{20,16},{24,28},{28,24},{1,5},{5... | collective-permute-start | bytes 3145736 | tf_op jit(solution)/shard_map/ppermute | solution.py:24
  317.8 4.8 %copy-start.28 = (bf16[2,256,512]{2,1,0:T(8,128)(2,1)}, bf16[2,256,512]{2,1,0:T(8,128)(2,1)S(1)}, u32[]{:S(2)}) copy-start(bf16[2,256,512]{2,1,0:T(8,128)(2,1)S(1)} %query_give.1) | copy-start | bytes 1572868
  325.6 0.8 copy-start.22
  326.4 58.6 %collective-permute-start.13 = (bf16[512,1024]{1,0:T(8,128)(2,1)}, bf16[512,1024]{1,0:T(8,128)(2,1)}, u32[]{:S(2)}, u32[]{:S(2)}) collective-permute-start(bf16[512,1024]{1,0:T(8,128)(2,1)} %norm_one_keep.1), channel_id=1, source_target_pairs={{0,2},{1,3},{2,0},{3,1},{4,6},{5,7},{6,4},{7,5},{8,10},{9,11},{10,... | collective-permute-start | bytes 3145736 | tf_op jit(solution)/shard_map/ppermute | solution.py:24
  327.9 1.3 copy-start.6
  327.9 1.4 copy-start.23
  329.3 10.3 %copy-start.29 = (bf16[2,256,512]{2,1,0:T(8,128)(2,1)S(1)}, bf16[2,256,512]{2,1,0:T(8,128)(2,1)}, u32[]{:S(2)}) copy-start(bf16[2,256,512]{2,1,0:T(8,128)(2,1)} %copy-done.28) | copy-start | bytes 1572868
  329.3 12.3 %copy-start.12 = (bf16[2,1376,256]{2,1,0:T(8,128)(2,1)S(1)}, bf16[2,1376,256]{2,1,0:T(8,128)(2,1)}, u32[]{:S(2)}) copy-start(bf16[2,1376,256]{2,1,0:T(8,128)(2,1)} %copy-done.11) | copy-start | bytes 4227076
  336.9 50.0 %collective-permute-start.24 = (bf16[1,1376,256]{2,1,0:T(8,128)(2,1)S(1)}, bf16[1,1376,256]{2,1,0:T(8,128)(2,1)}, u32[]{:S(2)}, u32[]{:S(2)}) collective-permute-start(bf16[1,1376,256]{2,1,0:T(8,128)(2,1)S(1)} %slice.87), channel_id=1, source_target_pairs={{0,16},{4,20},{8,24},{12,28},{16,0},{20,4},{24,8},{28,12},{1,17},{... | collective-permute-start | bytes 2113544 | tf_op jit(solution)/shard_map/ppermute | solution.py:24
  339.6 27.5 %collective-permute-start.11 = (bf16[2,256,512]{2,1,0:T(8,128)(2,1)S(1)}, bf16[2,256,512]{2,1,0:T(8,128)(2,1)S(1)}, u32[]{:S(2)}, u32[]{:S(2)}) collective-permute-start(bf16[2,256,512]{2,1,0:T(8,128)(2,1)S(1)} %copy-done.29), channel_id=1, source_target_pairs={{0,8},{4,12},{8,0},{12,4},{16,24},{20,28},{24,16},{28,20},{1,9},{5... | collective-permute-start | bytes 1572872 | tf_op jit(solution)/shard_map/ppermute | solution.py:24
  340.0 42.8 %collective-permute-start.12 = (bf16[2,256,512]{2,1,0:T(8,128)(2,1)S(1)}, bf16[2,256,512]{2,1,0:T(8,128)(2,1)S(1)}, u32[]{:S(2)}, u32[]{:S(2)}) collective-permute-start(bf16[2,256,512]{2,1,0:T(8,128)(2,1)S(1)} %key_give.1), channel_id=1, source_target_pairs={{0,8},{4,12},{8,0},{12,4},{16,24},{20,28},{24,16},{28,20},{1,9},{5... | collective-permute-start | bytes 1572872 | tf_op jit(solution)/shard_map/ppermute | solution.py:24
  344.0 2.7 copy-start.3
  346.6 12.3 %copy-start.16 = (bf16[512,512]{1,0:T(8,128)(2,1)S(1)}, bf16[512,512]{1,0:T(8,128)(2,1)}, u32[]{:S(2)}) copy-start(bf16[512,512]{1,0:T(8,128)(2,1)} %get-tuple-element.71.att_ref.refs_2_) | copy-start | bytes 1572868
  346.7 12.3 %copy-start.17 = (bf16[4,256,512]{2,1,0:T(8,128)(2,1)S(1)}, bf16[4,256,512]{2,1,0:T(8,128)(2,1)}, u32[]{:S(2)}) copy-start(bf16[4,256,512]{2,1,0:T(8,128)(2,1)} %get-tuple-element.110.refs_0_) | copy-start | bytes 3145732
  346.7 12.3 %copy-start.19 = (bf16[512,512]{1,0:T(8,128)(2,1)S(1)}, bf16[512,512]{1,0:T(8,128)(2,1)}, u32[]{:S(2)}) copy-start(bf16[512,512]{1,0:T(8,128)(2,1)} %get-tuple-element.113.refs_3_) | copy-start | bytes 1572868
  359.0 8.1 %copy-start.8 = (bf16[512,512]{1,0:T(8,128)(2,1)S(1)}, bf16[512,512]{1,0:T(8,128)(2,1)}, u32[]{:S(2)}) copy-start(bf16[512,512]{1,0:T(8,128)(2,1)} %get-tuple-element.93.refs_0_.refs_2_) | copy-start | bytes 1572868
  359.0 8.1 %copy-start.21 = (bf16[512,512]{1,0:T(8,128)(2,1)S(1)}, bf16[512,512]{1,0:T(8,128)(2,1)}, u32[]{:S(2)}) copy-start(bf16[512,512]{1,0:T(8,128)(2,1)} %copy-done.20) | copy-start | bytes 1572868
  368.5 23.5 %collective-permute-start.18 = (bf16[1,256,512]{2,1,0:T(8,128)(2,1)S(1)}, bf16[1,256,512]{2,1,0:T(8,128)(2,1)S(1)}, u32[]{:S(2)}, u32[]{:S(2)}) collective-permute-start(bf16[1,256,512]{2,1,0:T(8,128)(2,1)S(1)} %slice.79), channel_id=1, source_target_pairs={{0,16},{4,20},{8,24},{12,28},{16,0},{20,4},{24,8},{28,12},{1,17},{... | collective-permute-start | bytes 786440 | tf_op jit(solution)/shard_map/ppermute | solution.py:24
  384.3 2.7 copy-start.10
  384.3 13.4 %collective-permute-start.19 = (bf16[1,256,512]{2,1,0:T(8,128)(2,1)S(1)}, bf16[1,256,512]{2,1,0:T(8,128)(2,1)S(1)}, u32[]{:S(2)}, u32[]{:S(2)}) collective-permute-start(bf16[1,256,512]{2,1,0:T(8,128)(2,1)S(1)} %slice.81), channel_id=1, source_target_pairs={{0,16},{4,20},{8,24},{12,28},{16,0},{20,4},{24,8},{28,12},{1,17},{... | collective-permute-start | bytes 786440 | tf_op jit(solution)/shard_map/ppermute | solution.py:24
  386.9 11.7 %collective-permute-start.14 = (bf16[512,1024]{1,0:T(8,128)(2,1)S(1)}, bf16[512,1024]{1,0:T(8,128)(2,1)S(1)}, u32[]{:S(2)}, u32[]{:S(2)}) collective-permute-start(bf16[512,1024]{1,0:T(8,128)(2,1)S(1)} %add_convert_fusion.own_ref), channel_id=1, source_target_pairs={{0,1},{1,0},{2,3},{3,2},{4,5},{5,4},{6,7},{7,6},{8,9},{9,8},{10,11... | collective-permute-start | bytes 3145736 | tf_op jit(solution)/shard_map/ppermute | solution.py:24
  389.4 9.2 %copy-start.18 = (bf16[512,2048]{1,0:T(8,128)(2,1)S(1)}, bf16[512,2048]{1,0:T(8,128)(2,1)}, u32[]{:S(2)}) copy-start(bf16[512,2048]{1,0:T(8,128)(2,1)} %x_ref.3) | copy-start | bytes 6291460
  389.4 9.2 %copy-start.32 = (f32[2048]{0:T(1024)S(1)}, f32[2048]{0:T(1024)}, u32[]{:S(2)}) copy-start(f32[2048]{0:T(1024)} %param.15) | copy-start | bytes 24580
  389.4 44.4 %collective-permute-start.20 = (bf16[2,256,512]{2,1,0:T(8,128)(2,1)S(1)}, bf16[2,256,512]{2,1,0:T(8,128)(2,1)S(1)}, u32[]{:S(2)}, u32[]{:S(2)}) collective-permute-start(bf16[2,256,512]{2,1,0:T(8,128)(2,1)S(1)} %value_give.1), channel_id=1, source_target_pairs={{0,8},{4,12},{8,0},{12,4},{16,24},{20,28},{24,16},{28,20},{1,9},{5... | collective-permute-start | bytes 1572872 | tf_op jit(solution)/shard_map/ppermute | solution.py:24
  391.9 46.7 %collective-permute-start.22 = (bf16[2,256,512]{2,1,0:T(8,128)(2,1)S(1)}, bf16[2,256,512]{2,1,0:T(8,128)(2,1)S(1)}, u32[]{:S(2)}, u32[]{:S(2)}) collective-permute-start(bf16[2,256,512]{2,1,0:T(8,128)(2,1)S(1)} %wout_give.1), channel_id=1, source_target_pairs={{0,8},{4,12},{8,0},{12,4},{16,24},{20,28},{24,16},{28,20},{1,9},{5... | collective-permute-start | bytes 1572872 | tf_op jit(solution)/shard_map/ppermute | solution.py:24
  392.0 38.0 %collective-permute-start.25 = (bf16[1,1376,256]{2,1,0:T(8,128)(2,1)S(1)}, bf16[1,1376,256]{2,1,0:T(8,128)(2,1)S(1)}, u32[]{:S(2)}, u32[]{:S(2)}) collective-permute-start(bf16[1,1376,256]{2,1,0:T(8,128)(2,1)S(1)} %slice.89), channel_id=1, source_target_pairs={{0,16},{4,20},{8,24},{12,28},{16,0},{20,4},{24,8},{28,12},{1,17},{... | collective-permute-start | bytes 2113544 | tf_op jit(solution)/shard_map/ppermute | solution.py:24
  405.3 26.0 %collective-permute-start.15 = (f32[2,2048]{1,0:T(2,128)S(1)}, f32[2,2048]{1,0:T(2,128)S(1)}, u32[]{:S(2)}, u32[]{:S(2)}) collective-permute-start(f32[2,2048]{1,0:T(2,128)S(1)} %pad_maximum_fusion), channel_id=1, source_target_pairs={{0,4},{4,0},{8,12},{12,8},{16,20},{20,16},{24,28},{28,24},{1,5},{5... | collective-permute-start | bytes 49160 | tf_op jit(solution)/shard_map/ppermute | solution.py:24
  431.3 5.1 %collective-permute-start.16 = (f32[2,2048]{1,0:T(2,128)S(1)}, f32[2,2048]{1,0:T(2,128)S(1)}, u32[]{:S(2)}, u32[]{:S(2)}) collective-permute-start(f32[2,2048]{1,0:T(2,128)S(1)} %fusion), channel_id=1, source_target_pairs={{0,8},{4,12},{8,0},{12,4},{16,24},{20,28},{24,16},{28,20},{1,9},{5... | collective-permute-start | bytes 49160 | tf_op jit(solution)/shard_map/ppermute | solution.py:24
  436.4 7.6 %collective-permute-start.17 = (f32[2,2048]{1,0:T(2,128)S(1)}, f32[2,2048]{1,0:T(2,128)S(1)}, u32[]{:S(2)}, u32[]{:S(2)}) collective-permute-start(f32[2,2048]{1,0:T(2,128)S(1)} %fusion.2), channel_id=1, source_target_pairs={{0,16},{4,20},{8,24},{12,28},{16,0},{20,4},{24,8},{28,12},{1,17},{... | collective-permute-start | bytes 49160 | tf_op jit(solution)/shard_map/ppermute | solution.py:24
  441.0 25.3 %copy-start.36 = (bf16[512,2048]{1,0:T(8,128)(2,1)S(1)}, bf16[512,2048]{1,0:T(8,128)(2,1)}, u32[]{:S(2)}) copy-start(bf16[512,2048]{1,0:T(8,128)(2,1)} %get-tuple-element.136) | copy-start | bytes 6291460
  441.1 20.1 %collective-permute-start.23 = (bf16[1,256,512]{2,1,0:T(8,128)(2,1)S(1)}, bf16[1,256,512]{2,1,0:T(8,128)(2,1)S(1)}, u32[]{:S(2)}, u32[]{:S(2)}) collective-permute-start(bf16[1,256,512]{2,1,0:T(8,128)(2,1)S(1)} %slice.85), channel_id=1, source_target_pairs={{0,16},{4,20},{8,24},{12,28},{16,0},{20,4},{24,8},{28,12},{1,17},{... | collective-permute-start | bytes 786440 | tf_op jit(solution)/shard_map/ppermute | solution.py:24
  442.0 23.5 %collective-permute-start.21 = (bf16[1,256,512]{2,1,0:T(8,128)(2,1)S(1)}, bf16[1,256,512]{2,1,0:T(8,128)(2,1)S(1)}, u32[]{:S(2)}, u32[]{:S(2)}) collective-permute-start(bf16[1,256,512]{2,1,0:T(8,128)(2,1)S(1)} %slice.83), channel_id=1, source_target_pairs={{0,16},{4,20},{8,24},{12,28},{16,0},{20,4},{24,8},{28,12},{1,17},{... | collective-permute-start | bytes 786440 | tf_op jit(solution)/shard_map/ppermute | solution.py:24

commit v4 on v3

--- a/solution.py
+++ b/solution.py
@@ -590,7 +590,7 @@
     v_out,
     q_out,
     one_keep_out,
-    one_give_out,
+    one_got_out,
     mid_out,
     two_out,
     two_keep_out,
@@ -627,6 +627,7 @@
     mid,
     two_blocks,
     two_got,
+    one_got,
     og,
     load_sem,
     store_sem,
@@ -749,13 +750,9 @@
     for i in range(4):
         flip_at = slice(i * step, (i + 1) * step)
         flipped[:, :, flip_at] = normed[flip_at, :].T.reshape(devices, width // devices, step)
-    split = flipped.reshape(devices // 2, 2, width // devices, rows)
-    stores = [
-        pltpu.make_async_copy(split.at[:, odd], one_keep_out, store_sem.at[0]),
-        pltpu.make_async_copy(split.at[:, 1 - odd], one_give_out, store_sem.at[1]),
-    ]
+    turned = flipped.reshape(devices // 2, 2, width // devices, rows)
+    stores = [pltpu.make_async_copy(turned.at[:, odd], one_keep_out, store_sem.at[0])]
     stores[0].start()
-    stores[1].start()
 
     depth = width // devices
     loads[4].wait()
@@ -817,8 +814,8 @@
     attend(3)
     stores.append(pltpu.make_async_copy(kx, k_out, store_sem.at[2]))
     stores.append(pltpu.make_async_copy(vx, v_out, store_sem.at[3]))
+    stores[1].start()
     stores[2].start()
-    stores[3].start()
 
     for k in range(heads):
         lanes = slice(k * HEAD_DIM, (k + 1) * HEAD_DIM)
@@ -830,6 +827,18 @@
 
     att_swap = remote(att_out, att_got, two_send.at[4], two_recv.at[4], pair, h)
     att_swap.start()
+    share = devices // 4
+    here = pl.ds(core * share, share)
+    one_swap = remote(
+        turned.at[here, 1 - odd], one_got.at[here], two_send.at[5], two_recv.at[5], pair, h
+    )
+    one_pass = remote(
+        one_got.at[here], one_got.at[here], two_send.at[6], two_recv.at[6], s, mate
+    )
+    two_pass = remote(
+        two_got.at[here], two_got.at[here], two_send.at[7], two_recv.at[7], s, mate
+    )
+    one_swap.start()
 
     og_stores[0].wait()
     og_stores[1].wait()
@@ -838,7 +847,12 @@
     def to_pair(i):
         at = pl.ds(i * step, step)
         return remote(
-            blocks.at[:, 1 - odd, at, :], two_got.at[:, at, :], two_send.at[i], two_recv.at[i], pair, h
+            blocks.at[here, 1 - odd, at, :],
+            two_got.at[here, at, :],
+            two_send.at[i],
+            two_recv.at[i],
+            pair,
+            h,
         )
 
     half = width // 2
@@ -882,11 +896,21 @@
     q_chain.arrived(3)
     stores.append(pltpu.make_async_copy(qx, q_out, store_sem.at[2 + len(stores)]))
     stores[-1].start()
+    one_swap.wait_recv()
+    one_pass.start()
     for i in range(4):
         to_pair(i).wait_recv()
+    two_pass.start()
+    one_pass.wait_recv()
+    stores.append(pltpu.make_async_copy(one_got, one_got_out, store_sem.at[2 + len(stores)]))
+    stores[-1].start()
+    two_pass.wait_recv()
     stores.append(pltpu.make_async_copy(two_got, two_got_out, store_sem.at[2 + len(stores)]))
     stores[-1].start()
     att_swap.wait()
+    one_swap.wait_send()
+    one_pass.wait_send()
+    two_pass.wait_send()
     for i in range(4):
         to_pair(i).wait_send()
     for chain in (k_chain, v_chain, q_chain):
@@ -951,13 +975,14 @@
             pltpu.VMEM((rows, width), F32),
             pltpu.VMEM((devices, rows, depth), BF16),
             pltpu.VMEM((devices // 2, rows, depth), BF16),
+            pltpu.VMEM((devices // 2, depth, rows), BF16),
             pltpu.VMEM((rows, width), BF16),
             dma((9,)),
             dma((12,)),
         ]
         + [dma((4,))] * 6
         + [dma((12,))] * 2
-        + [dma((5,))] * 2,
+        + [dma((8,))] * 2,
         compiler_params=pltpu.CompilerParams(
             collective_id=0, has_side_effects=True, vmem_limit_bytes=56 << 20
         ),
@@ -1127,10 +1152,6 @@
     gg_got_hbm,
     two_hbm,
     two_got_hbm,
-    act_hbm,
-    act_got_hbm,
-    og_hbm,
-    og_got_hbm,
     parts_ref,
     mid_ref,
     lo_ref,
@@ -1147,7 +1168,6 @@
     gk_out,
     gv_out,
     gate_got,
-    down_got,
     dx,
     sx,
     dk_acc,
@@ -1163,12 +1183,6 @@
     gate_sem,
     gate_send,
     gate_recv,
-    down_g,
-    down_x,
-    down_slot,
-    down_sem,
-    down_send,
-    down_recv,
     load_sem,
     d_send,
     d_recv,
@@ -1196,14 +1210,6 @@
         gate_send,
         gate_recv,
     )
-    down = Give(
-        devices,
-        2,
-        (act_hbm, act_got_hbm, og_hbm, og_got_hbm),
-        (down_g, down_x, down_slot, down_got, down_sem),
-        down_send,
-        down_recv,
-    )
     greet_all(devices, cores)
     loads = [
         pltpu.make_async_copy(do_hbm, dx.at[0], load_sem.at[0]),
@@ -1212,7 +1218,6 @@
     loads[0].start()
     loads[1].start()
     gate.load()
-    down.load()
 
     @pl.when(s >= devices - 2)
     def _():
@@ -1283,9 +1288,6 @@
     gate.loaded()
     gate.make(0)
     gate.half(0, 0).start()
-    down.loaded()
-    down.make(0)
-    down.half(0, 0).start()
     queries_back(0, heads // 4)
     for i in range(4):
         head_sum.chip_sum(i, parts_ref[1, i * step : (i + 1) * step, :].astype(F32))
@@ -1297,15 +1299,10 @@
         gate.half(j, 0).start()
         gate.half(j, 1).start()
     queries_back(heads // 4, heads // 2)
-    down.half(0, 1).start()
     keys_back(0)
     keys_back(2)
     s_chain.third()
     d_chain.third()
-    for j in range(1, down.count):
-        down.make(j)
-        down.half(j, 0).start()
-        down.half(j, 1).start()
     queries_back(heads // 4 + heads // 2, heads - heads // 4 - heads // 2)
     for i in range(4):
         head_sum.total(i)
@@ -1329,11 +1326,10 @@
     s_chain.all_sent()
     head_sum.all_sent()
     gate.finish()
-    down.finish()
 
 
 def attention_back(
-    devices, cores, do, stat, gate, down, branch, mid, low_col, low_row, tables, keys, values, queries, lse, delta
+    devices, cores, do, stat, gate, branch, mid, low_col, low_row, tables, keys, values, queries, lse, delta
 ):
     rows, width = mid.shape
     parts, _, cols = keys.shape
@@ -1354,11 +1350,11 @@
     flops = 14 * rows * rows * parts * cols
     return pl.pallas_call(
         functools.partial(attention_back_kernel, devices, cores),
-        in_specs=[hbm] * 10 + [vmem] * 11,
-        out_specs=[vmem] * 6,
+        in_specs=[hbm] * 6 + [vmem] * 11,
+        out_specs=[vmem] * 5,
         out_shape=[jax.ShapeDtypeStruct((rows, width), BF16)]
         + [jax.ShapeDtypeStruct((rows, cols), BF16)] * 3
-        + [jax.ShapeDtypeStruct((count, units, depth), BF16)] * 2,
+        + [jax.ShapeDtypeStruct((count, units, depth), BF16)],
         scratch_shapes=[
             pltpu.VMEM((parts, rows, cols), BF16),
             pltpu.VMEM((parts, heads, 2, rows), F32),
@@ -1366,7 +1362,6 @@
             pltpu.VMEM((rows, cols), F32),
         ]
         + sum_scratch(rows, width)
-        + give
         + give
         + [dma((2,))]
         + [dma((4,))] * 4
@@ -1376,7 +1371,373 @@
         ),
         cost_estimate=cost(flops, 80 << 20),
         name="attention_back",
-    )(do, stat, *gate, *down, branch, mid, low_col, low_row, *tables, keys, values, queries, lse, delta)
+    )(do, stat, *gate, branch, mid, low_col, low_row, *tables, keys, values, queries, lse, delta)
+
+
+class Reduce:
+    def __init__(self, block, near, far, slot, got, keep, last, send, recv):
+        self.h = lax.axis_index("head")
+        self.block, self.near_seq, self.far_seq = block, near, far
+        self.slot, self.got, self.keep, self.last = slot, got, keep, last
+        self.send, self.recv = send, recv
+
+    def near(self, j):
+        return remote(
+            self.slot.at[j], self.got.at[j], self.send.at[j], self.recv.at[j], self.near_seq, self.h
+        )
+
+    def far(self):
+        return remote(
+            self.keep.at[1], self.last, self.send.at[2], self.recv.at[2], self.far_seq, self.h
+        )
+
+    def give(self):
+        for j in range(2):
+            self.slot[j] = self.block(2 + j).astype(BF16)
+            self.near(j).start()
+
+    def combine(self, received=None):
+        for j in (1, 0):
+            total = self.block(j)
+            if received is None:
+                self.near(j).wait_recv()
+            total = total + self.got[j].astype(F32)
+            self.keep[j] = total.astype(BF16)
+            if j == 1:
+                self.far().start()
+
+    def result(self):
+        self.far().wait_recv()
+        return (self.keep[0].astype(F32) + self.last[...].astype(F32)).astype(BF16)
+
+    def all_sent(self, gave):
+        if gave:
+            self.near(0).wait_send()
+            self.near(1).wait_send()
+        self.far().wait_send()
+
+
+def weights_kernel(
+    devices,
+    cores,
+    gate_hbm,
+    gate_other_hbm,
+    up_hbm,
+    up_other_hbm,
+    down_hbm,
+    down_other_hbm,
+    two_hbm,
+    two_other_hbm,
+    og_hbm,
+    og_other_hbm,
+    gate_got_hbm,
+    mid_give_hbm,
+    wq_hbm,
+    wk_hbm,
+    wv_hbm,
+    gm_hbm,
+    x_ref,
+    gain_ref,
+    mlp_part_ref,
+    gq,
+    gk,
+    gv,
+    att,
+    att_other,
+    one,
+    one_other,
+    mid_x,
+    gate_out,
+    up_out,
+    down_out,
+    wq_out,
+    wk_out,
+    wv_out,
+    wo_out,
+    tokens_out,
+    gains_out,
+    g_a,
+    g_b,
+    x_a,
+    x_b,
+    up_slot,
+    down_slot,
+    got_mlp,
+    keep_mlp,
+    last_mlp,
+    gq_other,
+    gk_other,
+    gv_other,
+    mid_other,
+    slot_att,
+    got_att,
+    keep_att,
+    last_att,
+    wq,
+    wk,
+    wv,
+    gm,
+    core_send,
+    core_got,
+    chip,
+    y_got,
+    own_half,
+    other_half,
+    gains_got,
+    load_sem,
+    gm_sem,
+    x_send,
+    x_recv,
+    job_send,
+    job_recv,
+    sum_send,
+    sum_recv,
+    gain_send,
+    gain_recv,
+):
+    rows, width = x_ref.shape
+    half = width // 2
+    step = rows // 4
+    s, h, odd, core, pair, mate, across = place(devices, cores)
+    near, far = differing(s, 2), differing(s, 4)
+    head_sum = HeadSum(
+        devices, cores, core_got, chip, y_got, own_half, other_half, sum_send, sum_recv
+    )
+    greet(pair, h)
+    greet(near, h)
+    greet(far, h)
+    greet(s, mate)
+    greet(s, across)
+
+    def position(first, p):
+        bits = shard_orders(first, devices)
+        shard = s
+        for k, b in enumerate(bits[1:]):
+            if (p >> (len(bits) - 2 - k)) & 1:
+                shard = differing(shard, b)
+        return shard // (2 * first) * first + lax.rem(shard, first)
+
+    count = [0]
+
+    def load(src, dst):
+        copy = pltpu.make_async_copy(src, dst, load_sem.at[count[0]])
+        count[0] += 1
+        copy.start()
+        return copy
+
+    def load_job(g_own, g_other, x_own, x_other, g, x, first, blocks):
+        copies = [load(g_own, g.at[0]), load(g_other, g.at[1])]
+        for p in blocks:
+            at = position(first, p)
+            copies += [load(x_own.at[at], x.at[0, p]), load(x_other.at[at], x.at[1, p])]
+        return copies
+
+    def wait(copies):
+        for copy in copies:
+            copy.wait()
+
+    gate_loads = load_job(gate_hbm, gate_other_hbm, two_hbm, two_other_hbm, g_a, x_a, 1, (0, 1))
+    gate_loads.append(load(gate_got_hbm, got_mlp.at[0]))
+    up_loads = load_job(up_hbm, up_other_hbm, two_hbm, two_other_hbm, g_b, x_b, 1, (0, 1, 2, 3))
+    w_loads = [load(wq_hbm, wq), load(wk_hbm, wk), load(wv_hbm, wv)]
+
+    def gm_load(i):
+        return pltpu.make_async_copy(
+            gm_hbm.at[pl.ds(i * step, step), :], gm.at[i % 2], gm_sem.at[i % 2]
+        )
+
+    gm_load(0).start()
+    gm_load(1).start()
+
+    def mlp_block(g, x):
+        def block(p):
+            total = jnp.dot(g[0], x[0, p], preferred_element_type=F32)
+            return total + jnp.dot(g[1], x[1, p], preferred_element_type=F32)
+
+        return block
+
+    def att_block(x_own, x_other, g_own, g_other):
+        def block(p):
+            at = position(1, p)
+            total = jnp.dot(x_own[at], g_own[...], preferred_element_type=F32)
+            return total + jnp.dot(x_other[at], g_other[...], preferred_element_type=F32)
+
+        return block
+
+    def job(k, block, first_seq, slot, got, keep, last):
+        return Reduce(block, first_seq, far, slot, got, keep, last, job_send.at[k], job_recv.at[k])
+
+    gate = job(0, mlp_block(g_a, x_a), near, None, got_mlp.at[0], keep_mlp.at[0], last_mlp.at[0])
+    up = job(1, mlp_block(g_b, x_b), near, up_slot, got_mlp.at[1], keep_mlp.at[1], last_mlp.at[1])
+    down = job(2, mlp_block(g_a, x_a), pair, down_slot, got_mlp.at[2], keep_mlp.at[2], last_mlp.at[2])
+    attention = []
+    for k, operands in enumerate(
+        (
+            (one, one_other, gq, gq_other),
+            (one, one_other, gk, gk_other),
+            (one, one_other, gv, gv_other),
+            (mid_x, mid_other, att, att_other),
+        )
+    ):
+        attention.append(
+            job(
+                3 + k,
+                att_block(*operands),
+                near,
+                slot_att.at[k],
+                got_att.at[k],
+                keep_att.at[k],
+                last_att.at[k],
+            )
+        )
+
+    pl.semaphore_wait(pltpu.get_barrier_semaphore(), 5)
+    swaps = [
+        remote(src, dst, x_send.at[i], x_recv.at[i], pair, h)
+        for i, (src, dst) in enumerate(
+            ((gq, gq_other), (gk, gk_other), (gv, gv_other), (mid_give_hbm, mid_other))
+        )
+    ]
+    for copy in swaps[:3]:
+        copy.start()
+
+    wait(gate_loads)
+    gate.combine(True)
+    down_loads = load_job(down_hbm, down_other_hbm, og_hbm, og_other_hbm, g_a, x_a, 2, (0, 1, 2, 3))
+    wait(up_loads)
+    up.give()
+    wait(down_loads)
+    down.give()
+    swaps[3].start()
+
+    wait(w_loads)
+    mine, theirs = (pl.multiple_of(c * half, half) for c in (core, 1 - core))
+
+    def product(i, start):
+        at = slice(i * step, (i + 1) * step)
+        total = None
+        for g, w in ((gq, wq), (gk, wk), (gv, wv)):
+            term = dot_nt(g[at, :], w[pl.ds(start, half), :])
+            total = term if total is None else total + term
+        return total
+
+    for i in range(4):
+        core_send[i] = product(i, theirs).astype(BF16)
+        head_sum.to_mate(i, core_send.at[i]).start()
+    for i in range(4):
+        head_sum.chip_sum(i, product(i, mine))
+    for k in range(3):
+        swaps[k].wait_recv()
+        attention[k].give()
+
+    def finish(i):
+        at = slice(i * step, (i + 1) * step)
+        gm_load(i).wait()
+        x = x_ref[at, :].astype(F32)
+        root = lax.rsqrt(jnp.mean(x * x, axis=-1, keepdims=True) + EPS)
+        grad = head_sum.joined(i)
+        unit = x * root
+        part = jnp.sum(grad * unit, axis=0, keepdims=True)
+        gains_out[0:1, :] = part if i == 0 else gains_out[0:1, :] + part
+        grad = grad * gain_ref[...]
+        total = gm[i % 2] + root * (grad - unit * jnp.mean(grad * unit, axis=-1, keepdims=True))
+        tokens_out[at, :] = total.astype(BF16)
+        if i < 2:
+            gm_load(i + 2).start()
+
+    up.combine()
+    for i in range(4):
+        head_sum.total(i)
+        if i > 0:
+            finish(i - 1)
+    finish(3)
+    gains_out[1:2, :] = mlp_part_ref[...]
+
+    def gain_swap(k, seq):
+        return remote(gains_out, gains_got.at[k], gain_send.at[k], gain_recv.at[k], seq, h)
+
+    def gain_step(k, seq):
+        gain_swap(k, seq).wait()
+        gains_out[...] = gains_out[...] + gains_got[k]
+
+    gain_swap(0, pair).start()
+    attention[0].combine()
+    attention[1].combine()
+    gain_step(0, pair)
+    gain_swap(1, near).start()
+    down.combine()
+    swaps[3].wait_recv()
+    attention[3].give()
+    attention[2].combine()
+    gain_step(1, near)
+    gain_swap(2, far).start()
+    attention[3].combine()
+    gate_out[...] = gate.result()
+    down_out[...] = down.result()
+    up_out[...] = up.result()
+    gain_step(2, far)
+    for k, out in enumerate((wq_out, wk_out, wv_out, wo_out)):
+        out[...] = attention[k].result()
+    gate.all_sent(False)
+    down.all_sent(True)
+    up.all_sent(True)
+    for k in range(4):
+        attention[k].all_sent(True)
+        swaps[k].wait_send()
+    head_sum.all_sent()
+
+
+def weight_gradients(
+    devices, cores, mlp_operands, others, weights, grad_mid, x, gain, mlp_part, attention_operands
+):
+    rows, width = x.shape
+    units = mlp_operands[0].shape[0]
+    cols = weights[0].shape[1]
+    depth = width // devices
+    vmem = pl.BlockSpec(memory_space=pltpu.VMEM)
+    hbm = pl.BlockSpec(memory_space=pl.ANY)
+    dma = pltpu.SemaphoreType.DMA
+    operands = (*mlp_operands, *others, *weights, grad_mid)
+    kept = (x, gain, mlp_part, *attention_operands)
+    return pl.pallas_call(
+        functools.partial(weights_kernel, devices, cores),
+        in_specs=[hbm] * len(operands) + [vmem] * len(kept),
+        out_specs=[vmem] * 9,
+        out_shape=[jax.ShapeDtypeStruct((units, depth), BF16)] * 3
+        + [jax.ShapeDtypeStruct((depth, cols), BF16)] * 4
+        + [jax.ShapeDtypeStruct((rows, width), BF16), jax.ShapeDtypeStruct((2, width), F32)],
+        scratch_shapes=[
+            pltpu.VMEM((2, units, rows), BF16),
+            pltpu.VMEM((2, units, rows), BF16),
+            pltpu.VMEM((2, 4, rows, depth), BF16),
+            pltpu.VMEM((2, 4, rows, depth), BF16),
+            pltpu.VMEM((2, units, depth), BF16),
+            pltpu.VMEM((2, units, depth), BF16),
+            pltpu.VMEM((3, 2, units, depth), BF16),
+            pltpu.VMEM((3, 2, units, depth), BF16),
+            pltpu.VMEM((3, units, depth), BF16),
+        ]
+        + [pltpu.VMEM((rows, cols), BF16)] * 3
+        + [
+            pltpu.VMEM((devices // 2, depth, rows), BF16),
+            pltpu.VMEM((4, 2, depth, cols), BF16),
+            pltpu.VMEM((4, 2, depth, cols), BF16),
+            pltpu.VMEM((4, 2, depth, cols), BF16),
+            pltpu.VMEM((4, depth, cols), BF16),
+        ]
+        + [pltpu.VMEM((width, cols), BF16)] * 3
+        + [pltpu.VMEM((2, rows // 4, width), F32)]
+        + [pltpu.VMEM((4, rows // 4, width // 2), BF16)]
+        + sum_scratch(rows, width)
+        + [pltpu.VMEM((3, 2, width), F32)]
+        + [dma((32,)), dma((2,)), dma((4,)), dma((4,)), dma((7, 3)), dma((7, 3))]
+        + [dma((12,)), dma((12,)), dma((3,)), dma((3,))],
+        compiler_params=pltpu.CompilerParams(
+            collective_id=3, has_side_effects=True, vmem_limit_bytes=62 << 20
+        ),
+        cost_estimate=cost(20 * rows * width * cols, 60 << 20),
+        name="weight_gradients",
+    )(*operands, *kept)
 
 
 def on_device(
@@ -1407,7 +1768,7 @@
         values,
         queries,
         one_keep,
-        one_give,
+        one_got,
         mid,
         normed_two,
         two_keep,
@@ -1437,7 +1798,7 @@
     order = Order()
     out_keep, out_give = (a.reshape(devices // 2, rows, -1) for a in (out_keep, out_give))
     out_pair = (out_keep, swap(out_give, "seq", 2))
-    one_pair = (one_keep, swap(one_give, "seq", 1))
+    one_pair = (one_keep, one_got)
     two_pair = (two_keep, two_got)
     w_gate, w_up, w_down = w_gate.T, w_up.T, w_down.T
     act, grad_gate, grad_up = mlp(normed_two, out_grad, w_gate, w_up, w_down)
@@ -1472,13 +1833,12 @@
     gate = WeightGrad(order, two_pair, grad_gate, gate_got, 1, "gate", True)
     up = WeightGrad(order, two_pair, grad_up, up_got, 1, "up", True)
     down = WeightGrad(order, out_pair, act, act_got, 2, "down", True)
-    block_out, grad_query_raw, grad_key_raw, grad_value_raw, gate.got, down.got = attention_back(
+    block_out, grad_query_raw, grad_key_raw, grad_value_raw, gate.got = attention_back(
         devices,
         cores,
         order.after(grad_att),
         stat,
         (grad_gate, gate_got, *two_pair),
-        (act, act_got, *out_pair),
         branch_parts,
         mid,
         low_col,
@@ -1490,6 +1850,39 @@
         lse,
         delta,
     )
+    if devices == 8:
+        sums = weight_gradients(
+            devices,
+            cores,
+            (grad_gate, gate_got, grad_up, up_got, act, act_got),
+            (*two_pair, *out_pair, gate.got, mid_give),
+            (w_query, w_key, w_value),
+            grad_mid,
+            tokens,
+            gain_one,
+            gain_mlp_part,
+            (
+                grad_query_raw,
+                grad_key_raw,
+                grad_value_raw,
+                attended,
+                attended_got,
+                *one_pair,
+                mid_keep,
+            ),
+        )
+        gate_grad, up_grad, down_grad = (a.astype(F32).T for a in sums[:3])
+        gains = lax.dynamic_slice_in_dim(sums[8], index * sums[8].shape[1] // devices, sums[8].shape[1] // devices, 1)
+        return (
+            block_out,
+            sums[7],
+            gains[0],
+            gains[1],
+            *(a.astype(F32) for a in sums[3:7]),
+            gate_grad,
+            up_grad,
+            down_grad,
+        )
     order.ran(grad_query_raw)
     query_got = swap(grad_query_raw, "seq", 1)
     key_got = swap(grad_key_raw, "seq", 1)
@@ -1497,7 +1890,7 @@
     mid_pair = (mid_keep, swap(order.after(mid_give), "seq", 1))
     gate.keep()
     up.give()
-    down.keep()
+    down.give()
     lefts = (grad_query_raw, grad_key_raw, grad_value_raw)
     rights = (w_query, w_key, w_value)
     give = order.ran(half_product(order.after(bits), lefts, rights, 1, None, "norm_one_give"))
@@ -1512,6 +1905,7 @@
     key.give()
     value.give()
     up.keep()
+    down.keep()
     wout.give()
     own = (chip.astype(F32) + chip_got.astype(F32)).astype(BF16)
     other = swap(own, "head", 1)

time: 472 us -> 452 us (0.958)
  Pallas kernels: 318 us -> 425 us
  waiting for transfers between devices: 89.2 us -> 0.01 us
  starting transfers between devices: 37.9 us -> 6.18 us
    pallas_call x15 -> x1, Pallas kernels: 49.8 us -> 172 us  [weight_gradients(): pl.pallas_call(functools.partial(weights_kernel, devices, cores), in_spec...]
    ppermute x27 -> x4, waiting for transfers between devices: 89.2 us -> 0.01 us  [swap(): lax.ppermute(block, axis, [(i, i ^ bit) for i in range(lax.axis_size(axis...]
    ppermute x27 -> x4, starting transfers between devices: 37.9 us -> 6.18 us  [swap(): lax.ppermute(block, axis, [(i, i ^ bit) for i in range(lax.axis_size(axis...]
    pallas_call x1, Pallas kernels: 79.9 us -> 65.4 us  [attention_back(): pl.pallas_call(functools.partial(attention_back_kernel, devices, cores),...]
  transfers between devices with their start and end apart: 27 -> 4, of which waited for: 10 -> 0; matrix products, arithmetic and copies ran while one was open for 3% -> 0% of each run, Pallas kernels for 39% -> 26%
where the time goes in v4:
time: 452 us; the launch traced here: 448 us
  Pallas kernels  425 us (94%)
  local copies, waits for them, and re-layouts  8.42 us (2%)
  other arithmetic  7.64 us (2%)
  starting transfers between devices  6.18 us (1%)
    pallas_call x1, Pallas kernels, weight_gradients(): pl.pallas_call(functools.partial(weights_kernel, devices, cores), in_spec...  172 us
    pallas_call x1, Pallas kernels, forward(): pl.pallas_call(functools.partial(forward_kernel, devices, cores), in_spec...  122 us
    pallas_call x1, Pallas kernels, attention_back(): pl.pallas_call(functools.partial(attention_back_kernel, devices, cores),...  65.4 us
    pallas_call x1, Pallas kernels, norm_two_back(): pl.pallas_call(functools.partial(norm_two_kernel, devices, cores), in_spe...  38.4 us
    pallas_call x1, Pallas kernels, mlp(): pl.pallas_call(mlp_kernel, grid=(pl.cdiv(width, step),), in_specs=[whole,...  15.4 us
    pallas_call x1, Pallas kernels, back_products(): pl.pallas_call(back_products_kernel, grid_spec=pltpu.PrefetchScalarGridSp...  11.3 us
  transfers between devices with their start and end apart: 4, of which 0 were waited for; matrix products, arithmetic and copies ran while one was open for 0% of the time, Pallas kernels for 26%

profile of v4, /device:TPU:0, one launch (start us, length us, event | category | flops | bytes accessed | tf_op | source)
XLA Modules:
  0.0 448.2 jit_solution(10630740230436293142)
XLA Ops:
  0.6 122.4 %forward.1 = (bf16[5,512,512]{2,1,0:T(8,128)(2,1)}, bf16[5,512,512]{2,1,0:T(8,128)(2,1)}, bf16[5,512,512]{2,1,0:T(8,128)(2,1)}, bf16[4,256,512]{2,1,0:T(8,128)(2...) custom-call(s32[4]{0:T(128)} %lengths_ref.1, ...), custom_call_target="tpu_custom_call" | custom-call | flops 5368709120 | bytes 41943040 | tf_op jit(solution)/shard_map/forward/pallas_call | solution.py:938
  123.1 15.4 %mlp.1 = (bf16[1376,512]{1,0:T(8,128)(2,1)S(1)}, bf16[1376,512]{1,0:T(8,128)(2,1)S(1)}, bf16[1376,512]{1,0:T(8,128)(2,1)}) custom-call(bf16[512,2048]{1,0:T(8,128)(2,1)} %get-tuple-element.57.x_ref, bf16[512,2048]{1,0:T(8,128)(2,1)} %og_ref.1, bf16[1376,2048]{1,0:T(8,128)(2,1)} %bitcast.23, bf16[1376,2048]{1,0:T(8,128)(2,1)} %bitcast.25, ...), custom_call_target="tpu_custom_call" | custom-call | flops 8657043456 | bytes 16908288 | tf_op jit(solution)/shard_map/mlp/pallas_call | solution.py:164
  138.5 0.0 copy-start.1
  138.5 0.0 copy-start.6
  138.5 4.1 collective-permute-start
  142.5 0.1 collective-permute-start.1
  142.6 0.1 collective-permute-start.2
  142.7 1.9 collective-permute-start.3
  144.6 0.1 pad_add_fusion.bits_ref
  144.7 0.0 copy-start.2
  144.7 0.0 copy-start.3
  144.7 0.0 copy-start.4
  144.7 0.0 copy-start.5
  144.7 11.3 %back_products.1.parts_ref = bf16[2,512,1024]{2,1,0:T(8,128)(2,1)S(1)} custom-call(s32[2]{0:T(128)S(1)} %pad_add_fusion.bits_ref, bf16[1376,512]{1,0:T(8,128)(2,1)S(1)} %get-tuple-element.58.gg_ref.gg_hbm.gate_hbm, bf16[1376,512]{1,0:T(8,128)(2,1)} %get-tuple-element.59.gu_ref.up_hbm, bf16[1376,2048]{1,0:T(8,128)(2,1)} %bitcast.24, bf16[1376,2048]{1,0:T(8,128)(2,1)} %bitcast.26), custom_call_target="tpu_custom_call" | custom-call | flops 5771362304 | bytes 11272192 | tf_op jit(solution)/shard_map/back_products/pallas_call | solution.py:195
  156.0 0.0 copy-done.1
  156.1 0.0 copy-done.6
  156.1 0.0 copy-start
  156.1 1.3 copy-done
  157.4 0.0 copy-done.2
  157.4 0.0 copy-done.3
  157.4 0.0 copy-done.4
  157.4 0.0 copy-done.5
  157.4 38.4 %norm_two_back.1 = (bf16[2,512,1024]{2,1,0:T(8,128)(2,1)}, f32[512,2048]{1,0:T(8,128)}, bf16[4,256,512]{2,1,0:T(8,128)(2,1)}, bf16[4,256,512]{2,1,0:T(8,128)(2,1...) custom-call(bf16[2,512,1024]{2,1,0:T(8,128)(2,1)} %copy-done, ...), custom_call_target="tpu_custom_call" | custom-call | flops 2147483648 | bytes 62914560 | tf_op jit(solution)/shard_map/norm_two_back/pallas_call | solution.py:1115
  195.8 0.0 copy-start.7
  195.8 0.8 copy-done.7
  196.6 0.0 copy-start.8
  196.6 0.6 copy-done.8
  197.2 0.0 copy-start.9
  197.2 0.6 copy-done.9
  197.8 0.0 collective-permute-done.gg_got_hbm.gate_other_hbm
  197.8 65.4 %attention_back.1 = (bf16[512,2048]{1,0:T(8,128)(2,1)}, bf16[512,512]{1,0:T(8,128)(2,1)}, bf16[512,512]{1,0:T(8,128)(2,1)}, bf16[512,512]{1,0:T(8,128)(2,1)}, bf16[2,1376,256]{2,1,0:T(8,128)(2,1)}) custom-call(bf16[512,512]{1,0:T(8,128)(2,1)} %copy-done.7, f32[4,2,512]{2,1,0:T(2,128)} %copy-done.8, bf16[1376,512]{1,0:T(8,128)(2,1)} %copy-done.6, ...), custom_call_target="tpu_custom_call" | custom-call | flops 9395240960 | bytes 83886080 | tf_op jit(solution)/shard_map/attention_back/pallas_call | solution.py:1351
  263.2 0.0 collective-permute-done.3.og_other_hbm
  263.3 0.0 collective-permute-done.1.up_other_hbm
  263.3 0.0 collective-permute-done.2.down_other_hbm
  263.3 172.0 %weight_gradients.1 = (bf16[1376,256]{1,0:T(8,128)(2,1)}, bf16[1376,256]{1,0:T(8,128)(2,1)}, bf16[1376,256]{1,0:T(8,128)(2,1)}, bf16[256,512]{1,0:T(8,128)(2,1)}...) custom-call(bf16[1376,512]{1,0:T(8,128)(2,1)} %copy-done.6, ...), custom_call_target="tpu_custom_call" | custom-call | flops 10737418240 | bytes 62914560 | tf_op jit(solution)/shard_map/weight_gradients/pallas_call | solution.py:1702
  435.3 0.0 copy-start.17
  435.3 0.0 copy-start.16
  435.3 0.0 copy-start.15
  435.3 0.0 copy-start.14
  435.3 2.4 convert_bitcast_fusion.2
  437.7 0.0 copy-start.12
  437.7 0.0 copy-start.13
  437.7 0.0 copy-done.17
  437.7 0.9 convert_element_type.15
  438.6 0.0 copy-done.16
  438.6 0.9 convert_element_type.16
  439.4 0.0 copy-done.15
  439.4 0.9 convert_element_type.17
  440.3 0.0 copy-done.14
  440.3 0.9 convert_element_type.18
  441.2 0.0 copy-done.12
  441.2 0.0 copy-done.13
  441.2 0.0 copy-start.10
  441.2 1.8 convert_bitcast_fusion
  442.9 1.4 fusion
  444.3 0.0 copy-done.10
  444.3 0.0 copy-start.11
  444.3 1.3 copy.27
  445.7 1.0 copy-done.11
  446.7 1.3 copy.28
Async XLA Ops:
  138.5 17.6 %copy-start.1 = (bf16[1376,512]{1,0:T(8,128)(2,1)}, bf16[1376,512]{1,0:T(8,128)(2,1)S(1)}, u32[]{:S(2)}) copy-start(bf16[1376,512]{1,0:T(8,128)(2,1)S(1)} %get-tuple-element.64.act_ref.down_hbm) | copy-start | bytes 4227076
  138.5 17.6 %copy-start.6 = (bf16[1376,512]{1,0:T(8,128)(2,1)}, bf16[1376,512]{1,0:T(8,128)(2,1)S(1)}, u32[]{:S(2)}) copy-start(bf16[1376,512]{1,0:T(8,128)(2,1)S(1)} %get-tuple-element.58.gg_ref.gg_hbm.gate_hbm) | copy-start | bytes 4227076
  138.5 59.3 %collective-permute-start = (bf16[1376,512]{1,0:T(8,128)(2,1)S(1)}, bf16[1376,512]{1,0:T(8,128)(2,1)}, u32[]{:S(2)}, u32[]{:S(2)}) collective-permute-start(bf16[1376,512]{1,0:T(8,128)(2,1)S(1)} %get-tuple-element.58.gg_ref.gg_hbm.gate_hbm), channel_id=1, source_target_pairs={{0,4},{4,0},{8,12},{12,8},{16,20},{20,16},{24,28},{28,24},{1,5},{5... | collective-permute-start | bytes 4227080 | tf_op jit(solution)/shard_map/ppermute | solution.py:24
  142.5 120.7 %collective-permute-start.1 = (bf16[1376,512]{1,0:T(8,128)(2,1)}, bf16[1376,512]{1,0:T(8,128)(2,1)}, u32[]{:S(2)}, u32[]{:S(2)}) collective-permute-start(bf16[1376,512]{1,0:T(8,128)(2,1)} %get-tuple-element.59.gu_ref.up_hbm), channel_id=1, source_target_pairs={{0,4},{4,0},{8,12},{12,8},{16,20},{20,16},{24,28},{28,24},{1,5},{5... | collective-permute-start | bytes 4227080 | tf_op jit(solution)/shard_map/ppermute | solution.py:24
  142.6 120.7 %collective-permute-start.2 = (bf16[1376,512]{1,0:T(8,128)(2,1)S(1)}, bf16[1376,512]{1,0:T(8,128)(2,1)}, u32[]{:S(2)}, u32[]{:S(2)}) collective-permute-start(bf16[1376,512]{1,0:T(8,128)(2,1)S(1)} %get-tuple-element.64.act_ref.down_hbm), channel_id=1, source_target_pairs={{0,8},{4,12},{8,0},{12,4},{16,24},{20,28},{24,16},{28,20},{1,9},{5... | collective-permute-start | bytes 4227080 | tf_op jit(solution)/shard_map/ppermute | solution.py:24
  142.7 120.5 %collective-permute-start.3 = (bf16[4,512,256]{2,1,0:T(8,128)(2,1)}, bf16[4,512,256]{2,1,0:T(8,128)(2,1)}, u32[]{:S(2)}, u32[]{:S(2)}) collective-permute-start(bf16[4,512,256]{2,1,0:T(8,128)(2,1)} %bitcast.8), channel_id=1, source_target_pairs={{0,8},{4,12},{8,0},{12,4},{16,24},{20,28},{24,16},{28,20},{1,9},{5... | collective-permute-start | bytes 3145736 | tf_op jit(solution)/shard_map/ppermute | solution.py:24
  144.7 12.7 %copy-start.2 = (bf16[512,512]{1,0:T(8,128)(2,1)S(1)}, bf16[512,512]{1,0:T(8,128)(2,1)}, u32[]{:S(2)}) copy-start(bf16[512,512]{1,0:T(8,128)(2,1)} %get-tuple-element.61.att_ref.att) | copy-start | bytes 1572868
  144.7 12.7 %copy-start.3 = (s32[512,1]{1,0:T(8,128)S(1)}, s32[512,1]{1,0:T(8,128)}, u32[]{:S(2)}) copy-start(s32[512,1]{1,0:T(8,128)} %get-tuple-element.62.valid_ref) | copy-start | bytes 6148
  144.7 12.7 %copy-start.4 = (f32[2048]{0:T(1024)S(1)}, f32[2048]{0:T(1024)}, u32[]{:S(2)}) copy-start(f32[2048]{0:T(1024)} %param.16) | copy-start | bytes 24580
  144.7 12.7 %copy-start.5 = (f32[4,1,512]{2,1,0:T(1,128)S(1)}, f32[4,1,512]{2,1,0:T(1,128)}, u32[]{:S(2)}) copy-start(f32[4,1,512]{2,1,0:T(1,128)} %get-tuple-element.63.lse_row_ref) | copy-start | bytes 24580
  156.1 1.3 copy-start
  195.8 0.8 copy-start.7
  196.6 0.6 copy-start.8
  197.2 0.6 copy-start.9
  435.3 2.4 copy-start.17
  435.3 3.3 copy-start.16
  435.3 4.1 copy-start.15
  435.3 5.0 %copy-start.14 = (bf16[256,512]{1,0:T(8,128)(2,1)S(1)}, bf16[256,512]{1,0:T(8,128)(2,1)}, u32[]{:S(2)}) copy-start(bf16[256,512]{1,0:T(8,128)(2,1)} %get-tuple-element.99) | copy-start | bytes 786436
  437.7 3.4 copy-start.12
  437.7 3.4 copy-start.13
  441.2 3.2 copy-start.10
  444.3 2.3 copy-start.11

commit v5 on v4

--- a/solution.py
+++ b/solution.py
@@ -143,71 +143,6 @@
     )(bits, *lefts, *rights, *extra)
 
 
-def mlp_kernel(x_ref, g_ref, wg_ref, wu_ref, wd_ref, act_ref, gg_ref, gu_ref):
-    x, g = x_ref[...], g_ref[...]
-    gate = dot_nt(wg_ref[...], x)
-    up = dot_nt(wu_ref[...], x)
-    grad = dot_nt(wd_ref[...], g)
-    sig = 1.0 / (1.0 + jnp.exp(-gate))
-    silu = gate * sig
-    act_ref[...] = (silu * up).astype(BF16)
-    gg_ref[...] = (grad * up * sig * (1.0 + gate * (1.0 - sig))).astype(BF16)
-    gu_ref[...] = (grad * silu).astype(BF16)
-
-
-def mlp(x, grad, w_gate, w_up, w_down):
-    rows, depth = x.shape
-    width = w_gate.shape[0]
-    step = -(-width // (4 * 32)) * 32
-    whole = pl.BlockSpec((rows, depth), lambda i: (0, 0))
-    block = pl.BlockSpec((step, depth), lambda i: (i, 0))
-    return pl.pallas_call(
-        mlp_kernel,
-        grid=(pl.cdiv(width, step),),
-        in_specs=[whole, whole, block, block, block],
-        out_specs=[pl.BlockSpec((step, rows), lambda i: (i, 0))] * 3,
-        out_shape=[jax.ShapeDtypeStruct((width, rows), BF16)] * 3,
-        compiler_params=BIG_VMEM,
-        cost_estimate=cost(6 * rows * depth * width, 6 * depth * width),
-        name="mlp",
-    )(x, grad, w_gate, w_up, w_down)
-
-
-def back_products_kernel(bits_ref, gg_ref, gu_ref, wg_ref, wu_ref, out_ref, gg, gu):
-    @pl.when(pl.program_id(0) == 0)
-    def _():
-        gg[...] = gg_ref[...].T
-        gu[...] = gu_ref[...].T
-
-    total = jnp.dot(gg[...], wg_ref[...], preferred_element_type=F32)
-    total = total + jnp.dot(gu[...], wu_ref[...], preferred_element_type=F32)
-    out_ref[0] = total.astype(BF16)
-
-
-def back_products(bits, grad_gate, grad_up, w_gate, w_up):
-    cols, rows = grad_gate.shape
-    width = w_gate.shape[1]
-    step = width // 4
-    whole = pl.BlockSpec((cols, rows), lambda i, bits: (0, 0))
-    column = pl.BlockSpec(
-        (cols, step), lambda i, bits: (0, 2 * (bits[1] ^ 1 ^ (i // 2)) + i % 2)
-    )
-    return pl.pallas_call(
-        back_products_kernel,
-        grid_spec=pltpu.PrefetchScalarGridSpec(
-            num_scalar_prefetch=1,
-            grid=(4,),
-            in_specs=[whole, whole, column, column],
-            out_specs=pl.BlockSpec((1, rows, step), lambda i, bits: (i // 2, 0, i % 2)),
-            scratch_shapes=[pltpu.VMEM((rows, cols), BF16)] * 2,
-        ),
-        out_shape=jax.ShapeDtypeStruct((2, rows, width // 2), BF16),
-        compiler_params=BIG_VMEM,
-        cost_estimate=cost(4 * rows * cols * width, 4 * cols * width),
-        name="back_products",
-    )(bits, grad_gate, grad_up, w_gate, w_up)
-
-
 def blocks_kernel(order_ref, flip, xa_ref, xb_ref, ga_ref, gb_ref, *refs):
     if flip:
         total = jnp.dot(ga_ref[...], xa_ref[0], preferred_element_type=F32)
@@ -590,14 +525,14 @@
     v_out,
     q_out,
     one_keep_out,
-    one_got_out,
+    one_give_out,
     mid_out,
     two_out,
     two_keep_out,
     two_got_out,
     og_keep_out,
     og_give_out,
-    att_got,
+    og_got_out,
     att_out,
     lse_out,
     row_out,
@@ -627,7 +562,6 @@
     mid,
     two_blocks,
     two_got,
-    one_got,
     og,
     load_sem,
     store_sem,
@@ -649,6 +583,7 @@
     scale = HEAD_DIM ** (-0.5) * LOG2E
     k_chain = Chain(devices, kx, k_send, k_recv, 1)
     v_chain = Chain(devices, vx, v_send, v_recv, 1)
+    chains = [v_chain, k_chain]
     q_chain = Chain(devices, qx, q_send, q_recv, -1)
     head_sum = HeadSum(
         devices, cores, core_got, chip, y_got, own_half, other_half, sum_send, sum_recv
@@ -693,6 +628,17 @@
         low = jnp.where(valid, jnp.maximum(low, at - (WINDOW - 1)), at)
         return at - start, valid, jnp.where(at < devices * rows, low, BIG) - s * rows
 
+    def turn_into(weight, out):
+        raw = jnp.dot(normed[...], weight[...], preferred_element_type=F32)
+        for k in range(heads):
+            u = raw[:, k * HEAD_DIM : (k + 1) * HEAD_DIM]
+            u = u * cos_ref[...] + pltpu.roll(u, HEAD_DIM // 2, 1) * sin_ref[...]
+            out[0, :, k * HEAD_DIM : (k + 1) * HEAD_DIM] = u.astype(BF16)
+
+    loads[1].wait()
+    vx[0] = jnp.dot(normed[...], wv[...], preferred_element_type=F32).astype(BF16)
+    all_greeted(devices)
+    v_chain.first()
     at = lax.broadcasted_iota(jnp.int32, (rows, HEAD_DIM), 0) + s * rows
     position, valid, low = sequence_of(at)
     valid_ref[...] = valid[:, 0:1].astype(jnp.int32)
@@ -705,22 +651,9 @@
     cos_ref[...] = jnp.cos(angle)
     sin_ref[...] = jnp.sin(angle) * jnp.where(lane < half_dim, -1.0, 1.0)
     lo_row_ref[...] = sequence_of(lax.broadcasted_iota(jnp.int32, lo_row_ref.shape, 1) + s * rows)[2]
-
-    def turn_into(weight, out):
-        raw = jnp.dot(normed[...], weight[...], preferred_element_type=F32)
-        for k in range(heads):
-            u = raw[:, k * HEAD_DIM : (k + 1) * HEAD_DIM]
-            u = u * cos_ref[...] + pltpu.roll(u, HEAD_DIM // 2, 1) * sin_ref[...]
-            out[0, :, k * HEAD_DIM : (k + 1) * HEAD_DIM] = u.astype(BF16)
-
     loads[0].wait()
     turn_into(wk, kx)
-
-    all_greeted(devices)
     k_chain.first()
-    loads[1].wait()
-    vx[0] = jnp.dot(normed[...], wv[...], preferred_element_type=F32).astype(BF16)
-    v_chain.first()
 
     @pl.when(jnp.logical_not(has_left))
     def _():
@@ -751,8 +684,12 @@
         flip_at = slice(i * step, (i + 1) * step)
         flipped[:, :, flip_at] = normed[flip_at, :].T.reshape(devices, width // devices, step)
     turned = flipped.reshape(devices // 2, 2, width // devices, rows)
-    stores = [pltpu.make_async_copy(turned.at[:, odd], one_keep_out, store_sem.at[0])]
+    stores = [
+        pltpu.make_async_copy(turned.at[:, odd], one_keep_out, store_sem.at[0]),
+        pltpu.make_async_copy(turned.at[:, 1 - odd], one_give_out, store_sem.at[1]),
+    ]
     stores[0].start()
+    stores[1].start()
 
     depth = width // devices
     loads[4].wait()
@@ -768,16 +705,19 @@
     og_stores[1].start()
     sub = rows // 2
 
-    def attend(d):
+    def attend(d, only=None):
         def body(i, _):
-            k = i // 2
-            at = pl.ds(pl.multiple_of((i % 2) * sub, sub), sub)
+            if only is None:
+                k, part = i // 2, lax.rem(i, 2)
+            else:
+                k, part = i, only
+            at = pl.ds(pl.multiple_of(part * sub, sub), sub)
             lanes = pl.ds(pl.multiple_of(k * HEAD_DIM, HEAD_DIM), HEAD_DIM)
             scores = dot_nt(qx[0, at, lanes], kx[d, :, lanes])
             u = lax.broadcasted_iota(jnp.int32, scores.shape, 1) - d * rows
             seen = u >= lo_ref[at, :]
             if d == 0:
-                t = lax.broadcasted_iota(jnp.int32, scores.shape, 0) + (i % 2) * sub
+                t = lax.broadcasted_iota(jnp.int32, scores.shape, 0) + part * sub
                 seen = seen & (u <= t)
             scores = jnp.where(seen, scores * scale, MASKED)
             top = jnp.max(scores, axis=1, keepdims=True)
@@ -796,49 +736,25 @@
             acc[at, lanes] = mixed
             return 0
 
-        lax.fori_loop(0, 2 * heads, body, 0)
+        lax.fori_loop(0, 2 * heads if only is None else heads, body, 0)
 
     attend(0)
-    k_chain.second()
-    v_chain.second()
+    for chain in chains:
+        chain.second()
     attend(2)
-    k_chain.arrived(2)
-    v_chain.arrived(2)
+    for chain in chains:
+        chain.arrived(2)
     attend(1)
-    k_chain.third()
-    v_chain.third()
+    for chain in chains:
+        chain.third()
     attend(4)
     q_chain.second()
-    k_chain.arrived(3)
-    v_chain.arrived(3)
-    attend(3)
+    for chain in chains:
+        chain.arrived(3)
     stores.append(pltpu.make_async_copy(kx, k_out, store_sem.at[2]))
     stores.append(pltpu.make_async_copy(vx, v_out, store_sem.at[3]))
-    stores[1].start()
     stores[2].start()
-
-    for k in range(heads):
-        lanes = slice(k * HEAD_DIM, (k + 1) * HEAD_DIM)
-        out = jnp.where(valid_ref[...] > 0, acc[:, lanes] / totals[k], 0.0)
-        att_out[:, lanes] = out.astype(BF16)
-        lse = tops[k] + jnp.log2(totals[k])
-        lse_out[k] = lse
-        row_out[k] = jnp.broadcast_to(lse, (rows, HEAD_DIM)).T[0:1, :]
-
-    att_swap = remote(att_out, att_got, two_send.at[4], two_recv.at[4], pair, h)
-    att_swap.start()
-    share = devices // 4
-    here = pl.ds(core * share, share)
-    one_swap = remote(
-        turned.at[here, 1 - odd], one_got.at[here], two_send.at[5], two_recv.at[5], pair, h
-    )
-    one_pass = remote(
-        one_got.at[here], one_got.at[here], two_send.at[6], two_recv.at[6], s, mate
-    )
-    two_pass = remote(
-        two_got.at[here], two_got.at[here], two_send.at[7], two_recv.at[7], s, mate
-    )
-    one_swap.start()
+    stores[3].start()
 
     og_stores[0].wait()
     og_stores[1].wait()
@@ -860,13 +776,43 @@
     mine = pl.ds(pl.multiple_of(core * half, half), half)
     theirs = pl.ds(pl.multiple_of((1 - core) * half, half), half)
 
-    for i in range(4):
-        part = dot_nt(att_out[i * step : (i + 1) * step, :], wo[theirs, :])
-        core_send[i] = part.astype(BF16)
-        head_sum.to_mate(i, core_send.at[i]).start()
-    for i in range(4):
-        part = dot_nt(att_out[i * step : (i + 1) * step, :], wo[mine, :])
-        head_sum.chip_sum(i, part)
+    for t in range(2):
+        attend(3, t)
+        at = slice(t * sub, (t + 1) * sub)
+        for k in range(heads):
+            columns = slice(k * HEAD_DIM, (k + 1) * HEAD_DIM)
+            out = jnp.where(valid_ref[at, :] > 0, acc[at, columns] / totals[k, at, :], 0.0)
+            att_out[at, columns] = out.astype(BF16)
+        total = dot_nt(att_out[at, :], wo[theirs, :]).astype(BF16)
+        for j in range(2):
+            core_send[2 * t + j] = total[j * step : (j + 1) * step, :]
+            head_sum.to_mate(2 * t + j, core_send.at[2 * t + j]).start()
+        total = dot_nt(att_out[at, :], wo[mine, :])
+        for j in range(2):
+            head_sum.chip_sum(2 * t + j, total[j * step : (j + 1) * step, :])
+    for k in range(heads):
+        lse = tops[k] + jnp.log2(totals[k])
+        lse_out[k] = lse
+        row_out[k] = jnp.broadcast_to(lse, (rows, HEAD_DIM)).T[0:1, :]
+    share = devices // 4
+    here = pl.ds(core * share, share)
+    two_pass = remote(
+        two_got.at[here], two_got.at[here], two_send.at[7], two_recv.at[7], s, mate
+    )
+    og_here = pl.ds(core * (devices // 8), devices // 8)
+    og_swap = remote(
+        og_give_out.at[og_here],
+        og_got_out.at[og_here],
+        two_send.at[8],
+        two_recv.at[8],
+        differing(s, 2),
+        h,
+    )
+    og_pass = remote(
+        og_got_out.at[og_here], og_got_out.at[og_here], two_send.at[9], two_recv.at[9], s, mate
+    )
+    og_swap.start()
+
     q_chain.third()
 
     def finish(i):
@@ -896,24 +842,20 @@
     q_chain.arrived(3)
     stores.append(pltpu.make_async_copy(qx, q_out, store_sem.at[2 + len(stores)]))
     stores[-1].start()
-    one_swap.wait_recv()
-    one_pass.start()
+    og_swap.wait_recv()
+    og_pass.start()
     for i in range(4):
         to_pair(i).wait_recv()
     two_pass.start()
-    one_pass.wait_recv()
-    stores.append(pltpu.make_async_copy(one_got, one_got_out, store_sem.at[2 + len(stores)]))
-    stores[-1].start()
     two_pass.wait_recv()
     stores.append(pltpu.make_async_copy(two_got, two_got_out, store_sem.at[2 + len(stores)]))
     stores[-1].start()
-    att_swap.wait()
-    one_swap.wait_send()
-    one_pass.wait_send()
+    og_swap.wait_send()
+    og_pass.wait()
     two_pass.wait_send()
     for i in range(4):
         to_pair(i).wait_send()
-    for chain in (k_chain, v_chain, q_chain):
+    for chain in (*chains, q_chain):
         chain.all_sent()
     head_sum.all_sent()
     for store in stores:
@@ -938,7 +880,7 @@
     return pl.pallas_call(
         functools.partial(forward_kernel, devices, cores),
         in_specs=[pl.BlockSpec(memory_space=pltpu.SMEM)] + [vmem] * 3 + [hbm] * 7,
-        out_specs=[hbm] * 11 + [vmem] * 9,
+        out_specs=[hbm] * 12 + [vmem] * 8,
         out_shape=[
             shape(parts, rows, cols),
             shape(parts, rows, cols),
@@ -951,7 +893,7 @@
             shape(devices // 2, rows, depth),
             shape(devices // 4, 2, rows, depth),
             shape(devices // 4, 2, rows, depth),
-            shape(rows, cols),
+            shape(devices // 4, 2, rows, depth),
             shape(rows, cols),
             shape(heads, rows, 1, dtype=F32),
             shape(heads, 1, rows, dtype=F32),
@@ -975,14 +917,13 @@
             pltpu.VMEM((rows, width), F32),
             pltpu.VMEM((devices, rows, depth), BF16),
             pltpu.VMEM((devices // 2, rows, depth), BF16),
-            pltpu.VMEM((devices // 2, depth, rows), BF16),
             pltpu.VMEM((rows, width), BF16),
             dma((9,)),
             dma((12,)),
         ]
         + [dma((4,))] * 6
         + [dma((12,))] * 2
-        + [dma((8,))] * 2,
+        + [dma((10,))] * 2,
         compiler_params=pltpu.CompilerParams(
             collective_id=0, has_side_effects=True, vmem_limit_bytes=56 << 20
         ),
@@ -991,74 +932,155 @@
     )(lengths, x, *gains, grad, *weights, w_out, *prevs)
 
 
-def norm_two_kernel(
+def pieces_of(extent, step):
+    return [(start, min(step, extent - start)) for start in range(0, extent, step)]
+
+
+def middle_kernel(
     devices,
     cores,
-    parts_ref,
-    mid_ref,
+    two_ref,
+    og_ref,
     gain_ref,
-    og_ref,
-    wo_ref,
-    att_ref,
     valid_ref,
     lse_row_ref,
-    act_ref,
+    wg_hbm,
+    wu_hbm,
     wd_hbm,
+    mid_hbm,
+    wo_hbm,
+    att_hbm,
     branch_out,
     gm_out,
-    keep_out,
-    give_out,
     part_out,
     do_out,
     delta_out,
     stat_out,
+    act_out,
+    gg_out,
+    gu_out,
+    act_got,
+    gg_got,
+    keep_out,
+    give_out,
+    wg,
+    wu,
+    wd,
+    act_t,
+    gg_t,
+    gu_t,
+    act,
+    gg,
+    gu,
+    mid,
+    wo,
+    att,
+    core_send,
     core_got,
     chip,
     y_got,
     own_half,
     other_half,
     flipped,
-    wd,
-    act,
+    load_sem,
     store_sem,
+    far_send,
+    far_recv,
     sum_send,
     sum_recv,
 ):
-    rows, width = mid_ref.shape
-    heads = att_ref.shape[1] // HEAD_DIM
+    rows, width = mid.shape
+    units = wg.shape[0]
+    heads = att.shape[1] // HEAD_DIM
     step = rows // 4
+    half = width // 2
     s, h, odd, core, pair, mate, across = place(devices, cores)
+    near = differing(s, 2)
     head_sum = HeadSum(
         devices, cores, core_got, chip, y_got, own_half, other_half, sum_send, sum_recv
     )
-    load = pltpu.make_async_copy(wd_hbm, wd, store_sem.at[2])
-    load.start()
+    greet(pair, h)
+    greet(near, h)
     greet(s, mate)
     greet(s, across)
-    pl.semaphore_wait(pltpu.get_barrier_semaphore(), 2)
-    for i in range(4):
-        head_sum.to_mate(i, parts_ref.at[0, pl.ds(i * step, step), :]).start()
-    for i in range(4):
-        head_sum.chip_sum(i, parts_ref[1, i * step : (i + 1) * step, :].astype(F32))
-
-    half = width // 2
-    act[...] = act_ref[...].T
-    load.wait()
-
-    def product(i, _):
-        start = lax.rem(i // 2 + 1 + core, 2) * half + lax.rem(i, 2) * (half // 2)
-        lanes = pl.ds(pl.multiple_of(start, half // 2), half // 2)
-        to = pl.ds(pl.multiple_of(lax.rem(i, 2) * (half // 2), half // 2), half // 2)
-        branch_out[i // 2, :, to] = jnp.dot(
-            act[...], wd[:, lanes], preferred_element_type=F32
-        ).astype(BF16)
-        return 0
-
-    lax.fori_loop(0, 4, product, 0)
+    pieces = pieces_of(units, 3 * HEAD_DIM)
+    loads = []
+    for c, (start, size) in enumerate(pieces):
+        at = pl.ds(start, size)
+        loads.append(
+            [
+                pltpu.make_async_copy(src.at[at, :], dst.at[at, :], load_sem.at[3 * c + k])
+                for k, (src, dst) in enumerate(((wg_hbm, wg), (wu_hbm, wu), (wd_hbm, wd)))
+            ]
+        )
+        for copy in loads[-1]:
+            copy.start()
+    first = 3 * len(pieces)
+    later = [
+        pltpu.make_async_copy(src, dst, load_sem.at[first + k])
+        for k, (src, dst) in enumerate(((mid_hbm, mid), (wo_hbm, wo), (att_hbm, att)))
+    ]
+    for copy in later:
+        copy.start()
+    pl.semaphore_wait(pltpu.get_barrier_semaphore(), 4)
+
+    mine, theirs = (pl.ds(pl.multiple_of(c * half, half), half) for c in (core, 1 - core))
+    swaps = []
+
+    def product(tokens, columns):
+        total = jnp.dot(gg[tokens, :], wg[:, columns], preferred_element_type=F32)
+        return total + jnp.dot(gu[tokens, :], wu[:, columns], preferred_element_type=F32)
+
+    for t in range(2):
+        tokens = slice(2 * t * step, 2 * (t + 1) * step)
+        for c, (start, size) in enumerate(pieces):
+            at = slice(start, start + size)
+            if t == 0:
+                for copy in loads[c]:
+                    copy.wait()
+            gate = dot_nt(wg[at, :], two_ref[tokens, :])
+            up = dot_nt(wu[at, :], two_ref[tokens, :])
+            grad = dot_nt(wd[at, :], og_ref[tokens, :])
+            sig = 1.0 / (1.0 + jnp.exp(-gate))
+            silu = gate * sig
+            value = (silu * up).astype(BF16)
+            grad_gate = (grad * up * sig * (1.0 + gate * (1.0 - sig))).astype(BF16)
+            grad_up = (grad * silu).astype(BF16)
+            act_t[at, tokens] = value
+            gg_t[at, tokens] = grad_gate
+            gu_t[at, tokens] = grad_up
+            act[tokens, at] = value.T
+            gg[tokens, at] = grad_gate.T
+            gu[tokens, at] = grad_up.T
+        part = pl.ds(2 * t * step, 2 * step)
+        for k, (src, dst, seq) in enumerate(((gg_t, gg_got, pair), (act_t, act_got, near))):
+            i = 2 * t + k
+            swaps.append(
+                remote(src.at[:, part], dst.at[:, part], far_send.at[i], far_recv.at[i], seq, h)
+            )
+            swaps[-1].start()
+        total = product(tokens, theirs).astype(BF16)
+        for j in range(2):
+            core_send[2 * t + j] = total[j * step : (j + 1) * step, :]
+            head_sum.to_mate(2 * t + j, core_send.at[2 * t + j]).start()
+        total = product(tokens, mine)
+        for j in range(2):
+            head_sum.chip_sum(2 * t + j, total[j * step : (j + 1) * step, :])
+    stores = [
+        pltpu.make_async_copy(src, dst, store_sem.at[k])
+        for k, (src, dst) in enumerate(((act_t, act_out), (gg_t, gg_out), (gu_t, gu_out)))
+    ]
+    for store in stores:
+        store.start()
+
+    for k, columns in enumerate((theirs, mine)):
+        branch_out[k] = jnp.dot(act[...], wd[:, columns], preferred_element_type=F32).astype(BF16)
+    for copy in later:
+        copy.wait()
 
     def finish(i):
         at = slice(i * step, (i + 1) * step)
-        x = mid_ref[at, :]
+        x = mid[at, :]
         root = lax.rsqrt(jnp.mean(x * x, axis=-1, keepdims=True) + EPS)
         grad = head_sum.joined(i)
         unit = x * root
@@ -1071,10 +1093,10 @@
         gm_out[at, :] = total
         low = total.astype(BF16)
         flipped[:, :, at] = low.T.reshape(devices, width // devices, step)
-        do = jnp.dot(low, wo_ref[...], preferred_element_type=F32).astype(BF16).astype(F32)
+        do = jnp.dot(low, wo[...], preferred_element_type=F32).astype(BF16).astype(F32)
         do = jnp.where(valid_ref[at, :] > 0, do, 0.0)
         do_out[at, :] = do.astype(BF16)
-        product = do * att_ref[at, :].astype(F32)
+        product = do * att[at, :].astype(F32)
         for k in range(heads):
             delta = jnp.sum(product[:, k * HEAD_DIM : (k + 1) * HEAD_DIM], axis=1, keepdims=True)
             delta_out[k, at, :] = delta
@@ -1087,60 +1109,78 @@
             finish(i - 1)
     finish(3)
     split = flipped.reshape(devices // 2, 2, width // devices, rows)
-    stores = [
-        pltpu.make_async_copy(split.at[:, odd], keep_out, store_sem.at[0]),
-        pltpu.make_async_copy(split.at[:, 1 - odd], give_out, store_sem.at[1]),
+    stores += [
+        pltpu.make_async_copy(split.at[:, odd], keep_out, store_sem.at[3]),
+        pltpu.make_async_copy(split.at[:, 1 - odd], give_out, store_sem.at[4]),
     ]
-    stores[0].start()
-    stores[1].start()
+    stores[3].start()
+    stores[4].start()
+    for copy in swaps:
+        copy.wait()
     head_sum.all_sent()
-    stores[0].wait()
-    stores[1].wait()
+    for store in stores:
+        store.wait()
 
 
 def sum_scratch(rows, width):
     return [pltpu.VMEM((4, rows // 4, width // 2), BF16)] * 5
 
 
-def norm_two_back(
-    devices, cores, parts, mid, gain, grad, w_out, attended, valid, lse_row, act, w_down
+def middle(
+    devices, cores, two, grad, gain, valid, lse_row, weights, mid, w_out, attended
 ):
     rows, width = mid.shape
+    units = weights[0].shape[0]
     cols = attended.shape[1]
     heads = cols // HEAD_DIM
     depth = width // devices
+    count = len(pieces_of(units, 3 * HEAD_DIM))
     vmem = pl.BlockSpec(memory_space=pltpu.VMEM)
     hbm = pl.BlockSpec(memory_space=pl.ANY)
     dma = pltpu.SemaphoreType.DMA
+
+    def shape(*dims, dtype=BF16):
+        return jax.ShapeDtypeStruct(dims, dtype)
+
     return pl.pallas_call(
-        functools.partial(norm_two_kernel, devices, cores),
-        in_specs=[vmem] * 9 + [hbm],
-        out_specs=[vmem, vmem, hbm, hbm] + [vmem] * 4,
+        functools.partial(middle_kernel, devices, cores),
+        in_specs=[vmem] * 5 + [hbm] * 6,
+        out_specs=[vmem] * 6 + [hbm] * 7,
         out_shape=[
-            jax.ShapeDtypeStruct((2, rows, width // 2), BF16),
-            jax.ShapeDtypeStruct((rows, width), F32),
-            jax.ShapeDtypeStruct((devices // 2, depth, rows), BF16),
-            jax.ShapeDtypeStruct((devices // 2, depth, rows), BF16),
-            jax.ShapeDtypeStruct((1, width), F32),
-            jax.ShapeDtypeStruct((rows, cols), BF16),
-            jax.ShapeDtypeStruct((heads, rows, 1), F32),
-            jax.ShapeDtypeStruct((heads, 2, rows), F32),
-        ],
-        scratch_shapes=sum_scratch(rows, width)
+            shape(2, rows, width // 2),
+            shape(rows, width, dtype=F32),
+            shape(1, width, dtype=F32),
+            shape(rows, cols),
+            shape(heads, rows, 1, dtype=F32),
+            shape(heads, 2, rows, dtype=F32),
+        ]
+        + [shape(units, rows)] * 5
+        + [shape(devices // 2, depth, rows)] * 2,
+        scratch_shapes=[pltpu.VMEM((units, width), BF16)] * 3
+        + [pltpu.VMEM((units, rows), BF16)] * 3
+        + [pltpu.VMEM((rows, units), BF16)] * 3
+        + [
+            pltpu.VMEM((rows, width), F32),
+            pltpu.VMEM((width, cols), BF16),
+            pltpu.VMEM((rows, cols), BF16),
+            pltpu.VMEM((4, rows // 4, width // 2), BF16),
+        ]
+        + sum_scratch(rows, width)
         + [
             pltpu.VMEM((devices, depth, rows), BF16),
-            pltpu.VMEM(w_down.shape, BF16),
-            pltpu.VMEM(act.shape[::-1], BF16),
-            dma((3,)),
+            dma((3 * count + 3,)),
+            dma((5,)),
+            dma((4,)),
+            dma((4,)),
             dma((12,)),
             dma((12,)),
         ],
         compiler_params=pltpu.CompilerParams(
-            collective_id=1, has_side_effects=True, vmem_limit_bytes=52 << 20
+            collective_id=1, has_side_effects=True, vmem_limit_bytes=62 << 20
         ),
-        cost_estimate=cost(4 * rows * width * cols, 60 << 20),
-        name="norm_two_back",
-    )(parts, mid, gain, grad, w_out, attended, valid, lse_row, act, w_down)
+        cost_estimate=cost(12 * rows * width * units, 60 << 20),
+        name="middle",
+    )(two, grad, gain, valid, lse_row, *weights, mid, w_out, attended)
 
 
 def attention_back_kernel(
@@ -1152,6 +1192,7 @@
     gg_got_hbm,
     two_hbm,
     two_got_hbm,
+    gu_hbm,
     parts_ref,
     mid_ref,
     lo_ref,
@@ -1168,6 +1209,7 @@
     gk_out,
     gv_out,
     gate_got,
+    gu_got,
     dx,
     sx,
     dk_acc,
@@ -1183,6 +1225,8 @@
     gate_sem,
     gate_send,
     gate_recv,
+    up_send,
+    up_recv,
     load_sem,
     d_send,
     d_recv,
@@ -1285,6 +1329,18 @@
 
         lax.fori_loop(0, 2 * heads, body, 0)
 
+    ups = [
+        remote(
+            gu_hbm.at[pl.ds(start, size), :],
+            gu_got.at[pl.ds(start, size), :],
+            up_send.at[i],
+            up_recv.at[i],
+            pair,
+            h,
+        )
+        for i, (start, size) in enumerate(pieces_of(gu_hbm.shape[0], 3 * HEAD_DIM))
+    ]
+    ups[0].start()
     gate.loaded()
     gate.make(0)
     gate.half(0, 0).start()
@@ -1293,6 +1349,7 @@
         head_sum.chip_sum(i, parts_ref[1, i * step : (i + 1) * step, :].astype(F32))
     s_chain.second()
     d_chain.second()
+    ups[1].start()
     gate.half(0, 1).start()
     for j in range(1, gate.count):
         gate.make(j)
@@ -1303,6 +1360,8 @@
     keys_back(2)
     s_chain.third()
     d_chain.third()
+    for copy in ups[2:]:
+        copy.start()
     queries_back(heads // 4 + heads // 2, heads - heads // 4 - heads // 2)
     for i in range(4):
         head_sum.total(i)
@@ -1326,10 +1385,12 @@
     s_chain.all_sent()
     head_sum.all_sent()
     gate.finish()
+    for copy in ups:
+        copy.wait()
 
 
 def attention_back(
-    devices, cores, do, stat, gate, branch, mid, low_col, low_row, tables, keys, values, queries, lse, delta
+    devices, cores, do, stat, gate, grad_up, branch, mid, low_col, low_row, tables, keys, values, queries, lse, delta
 ):
     rows, width = mid.shape
     parts, _, cols = keys.shape
@@ -1350,11 +1411,12 @@
     flops = 14 * rows * rows * parts * cols
     return pl.pallas_call(
         functools.partial(attention_back_kernel, devices, cores),
-        in_specs=[hbm] * 6 + [vmem] * 11,
-        out_specs=[vmem] * 5,
+        in_specs=[hbm] * 7 + [vmem] * 11,
+        out_specs=[vmem] * 5 + [hbm],
         out_shape=[jax.ShapeDtypeStruct((rows, width), BF16)]
         + [jax.ShapeDtypeStruct((rows, cols), BF16)] * 3
-        + [jax.ShapeDtypeStruct((count, units, depth), BF16)],
+        + [jax.ShapeDtypeStruct((count, units, depth), BF16)]
+        + [jax.ShapeDtypeStruct((units, rows), BF16)],
         scratch_shapes=[
             pltpu.VMEM((parts, rows, cols), BF16),
             pltpu.VMEM((parts, heads, 2, rows), F32),
@@ -1363,6 +1425,7 @@
         ]
         + sum_scratch(rows, width)
         + give
+        + [dma((len(pieces_of(units, 3 * HEAD_DIM)),))] * 2
         + [dma((2,))]
         + [dma((4,))] * 4
         + [dma((12,))] * 2,
@@ -1371,7 +1434,7 @@
         ),
         cost_estimate=cost(flops, 80 << 20),
         name="attention_back",
-    )(do, stat, *gate, branch, mid, low_col, low_row, *tables, keys, values, queries, lse, delta)
+    )(do, stat, *gate, grad_up, branch, mid, low_col, low_row, *tables, keys, values, queries, lse, delta)
 
 
 class Reduce:
@@ -1432,6 +1495,7 @@
     og_other_hbm,
     gate_got_hbm,
     mid_give_hbm,
+    one_give_hbm,
     wq_hbm,
     wk_hbm,
     wv_hbm,
@@ -1443,9 +1507,7 @@
     gk,
     gv,
     att,
-    att_other,
     one,
-    one_other,
     mid_x,
     gate_out,
     up_out,
@@ -1469,6 +1531,8 @@
     gk_other,
     gv_other,
     mid_other,
+    one_other,
+    att_other,
     slot_att,
     got_att,
     keep_att,
@@ -1595,9 +1659,18 @@
     swaps = [
         remote(src, dst, x_send.at[i], x_recv.at[i], pair, h)
         for i, (src, dst) in enumerate(
-            ((gq, gq_other), (gk, gk_other), (gv, gv_other), (mid_give_hbm, mid_other))
+            ((gq, gq_other), (gk, gk_other), (gv, gv_other), (mid_give_hbm, mid_other), (att, att_other))
         )
     ]
+    share = devices // 4
+    here = pl.ds(core * share, share)
+    one_swap = remote(
+        one_give_hbm.at[here], one_other.at[here], x_send.at[5], x_recv.at[5], pair, h
+    )
+    one_pass = remote(
+        one_other.at[here], one_other.at[here], x_send.at[6], x_recv.at[6], s, mate
+    )
+    one_swap.start()
     for copy in swaps[:3]:
         copy.start()
 
@@ -1609,6 +1682,7 @@
     wait(down_loads)
     down.give()
     swaps[3].start()
+    swaps[4].start()
 
     wait(w_loads)
     mine, theirs = (pl.multiple_of(c * half, half) for c in (core, 1 - core))
@@ -1626,6 +1700,9 @@
         head_sum.to_mate(i, core_send.at[i]).start()
     for i in range(4):
         head_sum.chip_sum(i, product(i, mine))
+    one_swap.wait_recv()
+    one_pass.start()
+    one_pass.wait_recv()
     for k in range(3):
         swaps[k].wait_recv()
         attention[k].give()
@@ -1667,6 +1744,7 @@
     gain_swap(1, near).start()
     down.combine()
     swaps[3].wait_recv()
+    swaps[4].wait_recv()
     attention[3].give()
     attention[2].combine()
     gain_step(1, near)
@@ -1683,7 +1761,8 @@
     up.all_sent(True)
     for k in range(4):
         attention[k].all_sent(True)
-        swaps[k].wait_send()
+    for copy in (*swaps, one_swap, one_pass):
+        copy.wait_send()
     head_sum.all_sent()
 
 
@@ -1720,6 +1799,8 @@
         + [pltpu.VMEM((rows, cols), BF16)] * 3
         + [
             pltpu.VMEM((devices // 2, depth, rows), BF16),
+            pltpu.VMEM((devices // 2, depth, rows), BF16),
+            pltpu.VMEM((rows, cols), BF16),
             pltpu.VMEM((4, 2, depth, cols), BF16),
             pltpu.VMEM((4, 2, depth, cols), BF16),
             pltpu.VMEM((4, 2, depth, cols), BF16),
@@ -1730,7 +1811,7 @@
         + [pltpu.VMEM((4, rows // 4, width // 2), BF16)]
         + sum_scratch(rows, width)
         + [pltpu.VMEM((3, 2, width), F32)]
-        + [dma((32,)), dma((2,)), dma((4,)), dma((4,)), dma((7, 3)), dma((7, 3))]
+        + [dma((32,)), dma((2,)), dma((7,)), dma((7,)), dma((7, 3)), dma((7, 3))]
         + [dma((12,)), dma((12,)), dma((3,)), dma((3,))],
         compiler_params=pltpu.CompilerParams(
             collective_id=3, has_side_effects=True, vmem_limit_bytes=62 << 20
@@ -1768,14 +1849,14 @@
         values,
         queries,
         one_keep,
-        one_got,
+        one_give,
         mid,
         normed_two,
         two_keep,
         two_got,
         out_keep,
         out_give,
-        attended_got,
+        out_got,
         attended,
         lse,
         lse_row,
@@ -1796,49 +1877,44 @@
         (prev_keys, prev_values),
     )
     order = Order()
-    out_keep, out_give = (a.reshape(devices // 2, rows, -1) for a in (out_keep, out_give))
-    out_pair = (out_keep, swap(out_give, "seq", 2))
-    one_pair = (one_keep, one_got)
+    out_keep, out_got = (a.reshape(devices // 2, rows, -1) for a in (out_keep, out_got))
     two_pair = (two_keep, two_got)
-    w_gate, w_up, w_down = w_gate.T, w_up.T, w_down.T
-    act, grad_gate, grad_up = mlp(normed_two, out_grad, w_gate, w_up, w_down)
-    act_got = swap(act, "seq", 2)
-    gate_got = swap(grad_gate, "seq", 1)
-    up_got = swap(grad_up, "seq", 1)
-    norm_parts = back_products(bits, grad_gate, grad_up, w_gate, w_up)
     (
         branch_parts,
         grad_mid,
-        mid_keep,
-        mid_give,
         gain_mlp_part,
         grad_att,
         delta,
         stat,
-    ) = norm_two_back(
+        act,
+        grad_gate,
+        grad_up,
+        act_got,
+        gate_got,
+        mid_keep,
+        mid_give,
+    ) = middle(
         devices,
         cores,
-        norm_parts,
+        normed_two,
+        out_grad,
+        gain_two,
+        valid,
+        lse_row,
+        (w_gate.T, w_up.T, w_down.T),
         mid,
-        gain_two,
-        out_grad,
         w_out,
         attended,
-        valid,
-        lse_row,
-        act,
-        w_down,
     )
+    out_pair = (out_keep, out_got)
     order.ran(delta)
-    gate = WeightGrad(order, two_pair, grad_gate, gate_got, 1, "gate", True)
-    up = WeightGrad(order, two_pair, grad_up, up_got, 1, "up", True)
-    down = WeightGrad(order, out_pair, act, act_got, 2, "down", True)
-    block_out, grad_query_raw, grad_key_raw, grad_value_raw, gate.got = attention_back(
+    block_out, grad_query_raw, grad_key_raw, grad_value_raw, gate_sums, up_got = attention_back(
         devices,
         cores,
         order.after(grad_att),
         stat,
         (grad_gate, gate_got, *two_pair),
+        grad_up,
         branch_parts,
         mid,
         low_col,
@@ -1855,7 +1931,7 @@
             devices,
             cores,
             (grad_gate, gate_got, grad_up, up_got, act, act_got),
-            (*two_pair, *out_pair, gate.got, mid_give),
+            (*two_pair, *out_pair, gate_sums, mid_give, one_give),
             (w_query, w_key, w_value),
             grad_mid,
             tokens,
@@ -1866,8 +1942,7 @@
                 grad_key_raw,
                 grad_value_raw,
                 attended,
-                attended_got,
-                *one_pair,
+                one_keep,
                 mid_keep,
             ),
         )
@@ -1884,6 +1959,12 @@
             down_grad,
         )
     order.ran(grad_query_raw)
+    attended_got = swap(attended, "seq", 1)
+    one_pair = (one_keep, swap(one_give, "seq", 1))
+    gate = WeightGrad(order, two_pair, grad_gate, gate_got, 1, "gate", True)
+    up = WeightGrad(order, two_pair, grad_up, up_got, 1, "up", True)
+    down = WeightGrad(order, out_pair, act, act_got, 2, "down", True)
+    gate.got = gate_sums
     query_got = swap(grad_query_raw, "seq", 1)
     key_got = swap(grad_key_raw, "seq", 1)
     value_got = swap(grad_value_raw, "seq", 1)

time: 452 us -> 426 us (0.942)
  Pallas kernels: 425 us -> 406 us
  starting transfers between devices: 6.18 us -> 0 us
    pallas_call x3 -> x1, Pallas kernels: 65.1 us -> 51.8 us  [middle(): pl.pallas_call(functools.partial(middle_kernel, devices, cores), in_specs...]
    pallas_call x1, Pallas kernels: 122 us -> 109 us  [forward(): pl.pallas_call(functools.partial(forward_kernel, devices, cores), in_spec...]
    ppermute x4 -> x0, starting transfers between devices: 6.18 us -> none  [swap(): lax.ppermute(block, axis, [(i, i ^ bit) for i in range(lax.axis_size(axis...]
  transfers between devices with their start and end apart: 4 -> 0, of which waited for: 0 -> 0; matrix products, arithmetic and copies ran while one was open for 0% -> 0% of each run, Pallas kernels for 26% -> 0%
where the time goes in v5:
time: 426 us; the launch traced here: 420 us
  Pallas kernels  406 us (95%)
  other arithmetic  7.76 us (2%)
  local copies, waits for them, and re-layouts  5.09 us (1%)
    pallas_call x1, Pallas kernels, weight_gradients(): pl.pallas_call(functools.partial(weights_kernel, devices, cores), in_spec...  176 us
    pallas_call x1, Pallas kernels, forward(): pl.pallas_call(functools.partial(forward_kernel, devices, cores), in_spec...  109 us
    pallas_call x1, Pallas kernels, attention_back(): pl.pallas_call(functools.partial(attention_back_kernel, devices, cores),...  68.7 us
    pallas_call x1, Pallas kernels, middle(): pl.pallas_call(functools.partial(middle_kernel, devices, cores), in_specs...  51.8 us

profile of v5, /device:TPU:0, one launch (start us, length us, event | category | flops | bytes accessed | tf_op | source)
XLA Modules:
  0.0 420.0 jit_solution(17873765460735810979)
XLA Ops:
  0.6 109.2 %forward.1 = (bf16[5,512,512]{2,1,0:T(8,128)(2,1)}, bf16[5,512,512]{2,1,0:T(8,128)(2,1)}, bf16[5,512,512]{2,1,0:T(8,128)(2,1)}, bf16[4,256,512]{2,1,0:T(8,128)(2...) custom-call(s32[4]{0:T(128)} %lengths_ref.1, ...), custom_call_target="tpu_custom_call" | custom-call | flops 5368709120 | bytes 41943040 | tf_op jit(solution)/shard_map/forward/pallas_call | solution.py:880
  109.9 51.8 %middle.1 = (bf16[2,512,1024]{2,1,0:T(8,128)(2,1)}, f32[512,2048]{1,0:T(8,128)}, f32[1,2048]{1,0:T(1,128)}, bf16[512,512]{1,0:T(8,128)(2,1)}, f32[4,512,1]{2,1,0...) custom-call(bf16[512,2048]{1,0:T(8,128)(2,1)} %get-tuple-element.59., ...), custom_call_target="tpu_custom_call" | custom-call | flops 17314086912 | bytes 62914560 | tf_op jit(solution)/shard_map/middle/pallas_call | solution.py:1145
  161.7 68.7 %attention_back.1 = (bf16[512,2048]{1,0:T(8,128)(2,1)}, bf16[512,512]{1,0:T(8,128)(2,1)}, bf16[512,512]{1,0:T(8,128)(2,1)}, bf16[512,512]{1,0:T(8,128)(2,1)}, bf...) custom-call(bf16[512,512]{1,0:T(8,128)(2,1)} %get-tuple-element.66.do_hbm, ...), custom_call_target="tpu_custom_call" | custom-call | flops 9395240960 | bytes 83886080 | tf_op jit(solution)/shard_map/attention_back/pallas_call | solution.py:1412
  230.4 176.3 %weight_gradients.1 = (bf16[1376,256]{1,0:T(8,128)(2,1)}, bf16[1376,256]{1,0:T(8,128)(2,1)}, bf16[1376,256]{1,0:T(8,128)(2,1)}, bf16[256,512]{1,0:T(8,128)(2,1)}...) custom-call(bf16[1376,512]{1,0:T(8,128)(2,1)} %get-tuple-element.68., ...), custom_call_target="tpu_custom_call" | custom-call | flops 10737418240 | bytes 62914560 | tf_op jit(solution)/shard_map/weight_gradients/pallas_call | solution.py:1781
  406.7 0.0 copy-start.2
  406.7 3.1 convert_bitcast_fusion
  409.8 0.0 copy-start.6
  409.8 0.0 copy-start.5
  409.8 0.0 copy-start.4
  409.8 0.0 copy-done.2
  409.8 0.0 copy-start.3
  409.8 1.2 convert_bitcast_fusion.2
  411.0 0.0 copy-start
  411.0 0.0 copy-done.6
  411.0 0.9 convert_element_type.15
  411.9 0.0 copy-done.5
  411.9 0.9 convert_element_type.16
  412.7 0.0 copy-done.4
  412.7 0.9 convert_element_type.17
  413.6 0.0 copy-done.3
  413.6 0.9 convert_element_type.18
  414.5 1.4 fusion
  415.9 0.0 copy-done
  415.9 0.0 copy-start.1
  415.9 1.3 copy.27
  417.2 1.0 copy-done.1
  418.2 1.3 copy.28
Async XLA Ops:
  406.7 3.2 copy-start.2
  409.8 1.2 copy-start.6
  409.8 2.1 copy-start.5
  409.8 2.9 copy-start.4
  409.8 3.8 copy-start.3
  411.0 4.8 %copy-start = (bf16[512,2048]{1,0:T(8,128)(2,1)S(1)}, bf16[512,2048]{1,0:T(8,128)(2,1)}, u32[]{:S(2)}) copy-start(bf16[512,2048]{1,0:T(8,128)(2,1)} %get-tuple-element.122) | copy-start | bytes 6291460
  415.9 2.3 copy-start.1

commit v6 on v5

--- a/solution.py
+++ b/solution.py
@@ -529,7 +529,7 @@
     mid_out,
     two_out,
     two_keep_out,
-    two_got_out,
+    two_give_out,
     og_keep_out,
     og_give_out,
     og_got_out,
@@ -561,7 +561,6 @@
     other_half,
     mid,
     two_blocks,
-    two_got,
     og,
     load_sem,
     store_sem,
@@ -760,17 +759,6 @@
     og_stores[1].wait()
     blocks = two_blocks.reshape(devices // 2, 2, rows, depth)
 
-    def to_pair(i):
-        at = pl.ds(i * step, step)
-        return remote(
-            blocks.at[here, 1 - odd, at, :],
-            two_got.at[here, at, :],
-            two_send.at[i],
-            two_recv.at[i],
-            pair,
-            h,
-        )
-
     half = width // 2
     loads[3].wait()
     mine = pl.ds(pl.multiple_of(core * half, half), half)
@@ -794,11 +782,6 @@
         lse = tops[k] + jnp.log2(totals[k])
         lse_out[k] = lse
         row_out[k] = jnp.broadcast_to(lse, (rows, HEAD_DIM)).T[0:1, :]
-    share = devices // 4
-    here = pl.ds(core * share, share)
-    two_pass = remote(
-        two_got.at[here], two_got.at[here], two_send.at[7], two_recv.at[7], s, mate
-    )
     og_here = pl.ds(core * (devices // 8), devices // 8)
     og_swap = remote(
         og_give_out.at[og_here],
@@ -824,7 +807,6 @@
         normed[at, :] = two
         for j in range(devices):
             two_blocks[j, at, :] = two[:, j * depth : (j + 1) * depth]
-        to_pair(i).start()
 
     for i in range(4):
         head_sum.total(i)
@@ -835,6 +817,7 @@
         (mid, mid_out),
         (normed, two_out),
         (blocks.at[:, odd], two_keep_out),
+        (blocks.at[:, 1 - odd], two_give_out),
     ):
         stores.append(pltpu.make_async_copy(src, dst, store_sem.at[2 + len(stores)]))
         stores[-1].start()
@@ -844,17 +827,8 @@
     stores[-1].start()
     og_swap.wait_recv()
     og_pass.start()
-    for i in range(4):
-        to_pair(i).wait_recv()
-    two_pass.start()
-    two_pass.wait_recv()
-    stores.append(pltpu.make_async_copy(two_got, two_got_out, store_sem.at[2 + len(stores)]))
-    stores[-1].start()
     og_swap.wait_send()
     og_pass.wait()
-    two_pass.wait_send()
-    for i in range(4):
-        to_pair(i).wait_send()
     for chain in (*chains, q_chain):
         chain.all_sent()
     head_sum.all_sent()
@@ -916,7 +890,6 @@
         + [
             pltpu.VMEM((rows, width), F32),
             pltpu.VMEM((devices, rows, depth), BF16),
-            pltpu.VMEM((devices // 2, rows, depth), BF16),
             pltpu.VMEM((rows, width), BF16),
             dma((9,)),
             dma((12,)),
@@ -950,6 +923,7 @@
     mid_hbm,
     wo_hbm,
     att_hbm,
+    two_give_hbm,
     branch_out,
     gm_out,
     part_out,
@@ -961,6 +935,7 @@
     gu_out,
     act_got,
     gg_got,
+    two_got,
     keep_out,
     give_out,
     wg,
@@ -1024,6 +999,15 @@
         copy.start()
     pl.semaphore_wait(pltpu.get_barrier_semaphore(), 4)
 
+    share = devices // 4
+    here = pl.ds(core * share, share)
+    two_swap = remote(
+        two_give_hbm.at[here], two_got.at[here], far_send.at[4], far_recv.at[4], pair, h
+    )
+    two_pass = remote(
+        two_got.at[here], two_got.at[here], far_send.at[5], far_recv.at[5], s, mate
+    )
+    two_swap.start()
     mine, theirs = (pl.ds(pl.multiple_of(c * half, half), half) for c in (core, 1 - core))
     swaps = []
 
@@ -1077,6 +1061,8 @@
         branch_out[k] = jnp.dot(act[...], wd[:, columns], preferred_element_type=F32).astype(BF16)
     for copy in later:
         copy.wait()
+    two_swap.wait_recv()
+    two_pass.start()
 
     def finish(i):
         at = slice(i * step, (i + 1) * step)
@@ -1117,6 +1103,8 @@
     stores[4].start()
     for copy in swaps:
         copy.wait()
+    two_swap.wait_send()
+    two_pass.wait()
     head_sum.all_sent()
     for store in stores:
         store.wait()
@@ -1127,7 +1115,7 @@
 
 
 def middle(
-    devices, cores, two, grad, gain, valid, lse_row, weights, mid, w_out, attended
+    devices, cores, two, grad, gain, valid, lse_row, weights, mid, w_out, attended, two_give
 ):
     rows, width = mid.shape
     units = weights[0].shape[0]
@@ -1144,8 +1132,8 @@
 
     return pl.pallas_call(
         functools.partial(middle_kernel, devices, cores),
-        in_specs=[vmem] * 5 + [hbm] * 6,
-        out_specs=[vmem] * 6 + [hbm] * 7,
+        in_specs=[vmem] * 5 + [hbm] * 7,
+        out_specs=[vmem] * 6 + [hbm] * 8,
         out_shape=[
             shape(2, rows, width // 2),
             shape(rows, width, dtype=F32),
@@ -1155,6 +1143,7 @@
             shape(heads, 2, rows, dtype=F32),
         ]
         + [shape(units, rows)] * 5
+        + [shape(devices // 2, rows, depth)]
         + [shape(devices // 2, depth, rows)] * 2,
         scratch_shapes=[pltpu.VMEM((units, width), BF16)] * 3
         + [pltpu.VMEM((units, rows), BF16)] * 3
@@ -1170,8 +1159,8 @@
             pltpu.VMEM((devices, depth, rows), BF16),
             dma((3 * count + 3,)),
             dma((5,)),
-            dma((4,)),
-            dma((4,)),
+            dma((6,)),
+            dma((6,)),
             dma((12,)),
             dma((12,)),
         ],
@@ -1180,7 +1169,7 @@
         ),
         cost_estimate=cost(12 * rows * width * units, 60 << 20),
         name="middle",
-    )(two, grad, gain, valid, lse_row, *weights, mid, w_out, attended)
+    )(two, grad, gain, valid, lse_row, *weights, mid, w_out, attended, two_give)
 
 
 def attention_back_kernel(
@@ -1341,6 +1330,7 @@
         for i, (start, size) in enumerate(pieces_of(gu_hbm.shape[0], 3 * HEAD_DIM))
     ]
     ups[0].start()
+    ups[1].start()
     gate.loaded()
     gate.make(0)
     gate.half(0, 0).start()
@@ -1349,7 +1339,7 @@
         head_sum.chip_sum(i, parts_ref[1, i * step : (i + 1) * step, :].astype(F32))
     s_chain.second()
     d_chain.second()
-    ups[1].start()
+    ups[2].start()
     gate.half(0, 1).start()
     for j in range(1, gate.count):
         gate.make(j)
@@ -1360,7 +1350,7 @@
     keys_back(2)
     s_chain.third()
     d_chain.third()
-    for copy in ups[2:]:
+    for copy in ups[3:]:
         copy.start()
     queries_back(heads // 4 + heads // 2, heads - heads // 4 - heads // 2)
     for i in range(4):
@@ -1659,7 +1649,7 @@
     swaps = [
         remote(src, dst, x_send.at[i], x_recv.at[i], pair, h)
         for i, (src, dst) in enumerate(
-            ((gq, gq_other), (gk, gk_other), (gv, gv_other), (mid_give_hbm, mid_other), (att, att_other))
+            ((gq, gq_other), (gk, gk_other), (gv, gv_other))
         )
     ]
     share = devices // 4
@@ -1669,6 +1659,12 @@
     )
     one_pass = remote(
         one_other.at[here], one_other.at[here], x_send.at[6], x_recv.at[6], s, mate
+    )
+    mid_swap = remote(
+        mid_give_hbm.at[here], mid_other.at[here], x_send.at[3], x_recv.at[3], pair, h
+    )
+    mid_pass = remote(
+        mid_other.at[here], mid_other.at[here], x_send.at[7], x_recv.at[7], s, mate
     )
     one_swap.start()
     for copy in swaps[:3]:
@@ -1681,8 +1677,9 @@
     up.give()
     wait(down_loads)
     down.give()
+    swaps.append(remote(att, att_other, x_send.at[4], x_recv.at[4], pair, h))
+    mid_swap.start()
     swaps[3].start()
-    swaps[4].start()
 
     wait(w_loads)
     mine, theirs = (pl.multiple_of(c * half, half) for c in (core, 1 - core))
@@ -1743,8 +1740,10 @@
     gain_step(0, pair)
     gain_swap(1, near).start()
     down.combine()
+    mid_swap.wait_recv()
+    mid_pass.start()
     swaps[3].wait_recv()
-    swaps[4].wait_recv()
+    mid_pass.wait_recv()
     attention[3].give()
     attention[2].combine()
     gain_step(1, near)
@@ -1761,7 +1760,7 @@
     up.all_sent(True)
     for k in range(4):
         attention[k].all_sent(True)
-    for copy in (*swaps, one_swap, one_pass):
+    for copy in (*swaps, one_swap, one_pass, mid_swap, mid_pass):
         copy.wait_send()
     head_sum.all_sent()
 
@@ -1811,7 +1810,7 @@
         + [pltpu.VMEM((4, rows // 4, width // 2), BF16)]
         + sum_scratch(rows, width)
         + [pltpu.VMEM((3, 2, width), F32)]
-        + [dma((32,)), dma((2,)), dma((7,)), dma((7,)), dma((7, 3)), dma((7, 3))]
+        + [dma((32,)), dma((2,)), dma((8,)), dma((8,)), dma((7, 3)), dma((7, 3))]
         + [dma((12,)), dma((12,)), dma((3,)), dma((3,))],
         compiler_params=pltpu.CompilerParams(
             collective_id=3, has_side_effects=True, vmem_limit_bytes=62 << 20
@@ -1853,7 +1852,7 @@
         mid,
         normed_two,
         two_keep,
-        two_got,
+        two_give,
         out_keep,
         out_give,
         out_got,
@@ -1878,7 +1877,6 @@
     )
     order = Order()
     out_keep, out_got = (a.reshape(devices // 2, rows, -1) for a in (out_keep, out_got))
-    two_pair = (two_keep, two_got)
     (
         branch_parts,
         grad_mid,
@@ -1891,6 +1889,7 @@
         grad_up,
         act_got,
         gate_got,
+        two_got,
         mid_keep,
         mid_give,
     ) = middle(
@@ -1905,8 +1904,10 @@
         mid,
         w_out,
         attended,
+        two_give,
     )
     out_pair = (out_keep, out_got)
+    two_pair = (two_keep, two_got)
     order.ran(delta)
     block_out, grad_query_raw, grad_key_raw, grad_value_raw, gate_sums, up_got = attention_back(
         devices,

time: 426 us -> 416 us (0.977)
  Pallas kernels: 406 us -> 396 us
    pallas_call x1, Pallas kernels: 176 us -> 172 us  [weight_gradients(): pl.pallas_call(functools.partial(weights_kernel, devices, cores), in_spec...]
where the time goes in v6:
time: 416 us; the launch traced here: 410 us
  Pallas kernels  396 us (95%)
  other arithmetic  7.76 us (2%)
  local copies, waits for them, and re-layouts  5.09 us (1%)
    pallas_call x1, Pallas kernels, weight_gradients(): pl.pallas_call(functools.partial(weights_kernel, devices, cores), in_spec...  172 us
    pallas_call x1, Pallas kernels, forward(): pl.pallas_call(functools.partial(forward_kernel, devices, cores), in_spec...  108 us
    pallas_call x1, Pallas kernels, attention_back(): pl.pallas_call(functools.partial(attention_back_kernel, devices, cores),...  65.5 us
    pallas_call x1, Pallas kernels, middle(): pl.pallas_call(functools.partial(middle_kernel, devices, cores), in_specs...  50.7 us

profile of v6, /device:TPU:0, one launch (start us, length us, event | category | flops | bytes accessed | tf_op | source)
XLA Modules:
  0.0 409.9 jit_solution(4433268558864473300)
XLA Ops:
  0.6 108.0 %forward.1 = (bf16[5,512,512]{2,1,0:T(8,128)(2,1)}, bf16[5,512,512]{2,1,0:T(8,128)(2,1)}, bf16[5,512,512]{2,1,0:T(8,128)(2,1)}, bf16[4,256,512]{2,1,0:T(8,128)(2...) custom-call(s32[4]{0:T(128)} %lengths_ref.1, ...), custom_call_target="tpu_custom_call" | custom-call | flops 5368709120 | bytes 41943040 | tf_op jit(solution)/shard_map/forward/pallas_call | solution.py:854
  108.7 50.7 %middle.1 = (bf16[2,512,1024]{2,1,0:T(8,128)(2,1)}, f32[512,2048]{1,0:T(8,128)}, f32[1,2048]{1,0:T(1,128)}, bf16[512,512]{1,0:T(8,128)(2,1)}, f32[4,512,1]{2,1,0...) custom-call(bf16[512,2048]{1,0:T(8,128)(2,1)} %get-tuple-element.60., ...), custom_call_target="tpu_custom_call" | custom-call | flops 17314086912 | bytes 62914560 | tf_op jit(solution)/shard_map/middle/pallas_call | solution.py:1133
  159.4 65.5 %attention_back.1 = (bf16[512,2048]{1,0:T(8,128)(2,1)}, bf16[512,512]{1,0:T(8,128)(2,1)}, bf16[512,512]{1,0:T(8,128)(2,1)}, bf16[512,512]{1,0:T(8,128)(2,1)}, bf...) custom-call(bf16[512,512]{1,0:T(8,128)(2,1)} %get-tuple-element.68.do_hbm, ...), custom_call_target="tpu_custom_call" | custom-call | flops 9395240960 | bytes 83886080 | tf_op jit(solution)/shard_map/attention_back/pallas_call | solution.py:1402
  224.9 171.7 %weight_gradients.1 = (bf16[1376,256]{1,0:T(8,128)(2,1)}, bf16[1376,256]{1,0:T(8,128)(2,1)}, bf16[1376,256]{1,0:T(8,128)(2,1)}, bf16[256,512]{1,0:T(8,128)(2,1)}...) custom-call(bf16[1376,512]{1,0:T(8,128)(2,1)} %get-tuple-element.70., ...), custom_call_target="tpu_custom_call" | custom-call | flops 10737418240 | bytes 62914560 | tf_op jit(solution)/shard_map/weight_gradients/pallas_call | solution.py:1780
  396.6 0.0 copy-start.2
  396.6 3.1 convert_bitcast_fusion
  399.7 0.0 copy-start.6
  399.7 0.0 copy-start.5
  399.7 0.0 copy-start.4
  399.7 0.0 copy-done.2
  399.7 0.0 copy-start.3
  399.8 1.2 convert_bitcast_fusion.2
  400.9 0.0 copy-start
  401.0 0.0 copy-done.6
  401.0 0.9 convert_element_type.15
  401.8 0.0 copy-done.5
  401.8 0.9 convert_element_type.16
  402.7 0.0 copy-done.4
  402.7 0.9 convert_element_type.17
  403.5 0.0 copy-done.3
  403.5 0.9 convert_element_type.18
  404.4 1.4 fusion
  405.8 0.0 copy-done
  405.8 0.0 copy-start.1
  405.8 1.3 copy.27
  407.1 1.0 copy-done.1
  408.1 1.3 copy.28
Async XLA Ops:
  396.6 3.2 copy-start.2
  399.7 1.2 copy-start.6
  399.7 2.1 copy-start.5
  399.7 2.9 copy-start.4
  399.7 3.8 copy-start.3
  400.9 4.8 %copy-start = (bf16[512,2048]{1,0:T(8,128)(2,1)S(1)}, bf16[512,2048]{1,0:T(8,128)(2,1)}, u32[]{:S(2)}) copy-start(bf16[512,2048]{1,0:T(8,128)(2,1)} %get-tuple-element.124) | copy-start | bytes 6291460
  405.8 2.3 copy-start.1

commit v7 on v6

--- a/solution.py
+++ b/solution.py
@@ -1182,15 +1182,15 @@
     two_hbm,
     two_got_hbm,
     gu_hbm,
-    parts_ref,
-    mid_ref,
+    parts_hbm,
+    mid_hbm,
+    kx_hbm,
+    vx_hbm,
+    qx_hbm,
     lo_ref,
     lo_row_ref,
     cos_ref,
     sin_ref,
-    kx,
-    vx,
-    qx,
     lse_ref,
     delta_ref,
     block_out,
@@ -1199,6 +1199,11 @@
     gv_out,
     gate_got,
     gu_got,
+    kx,
+    vx,
+    qx,
+    mid_ref,
+    parts_ref,
     dx,
     sx,
     dk_acc,
@@ -1248,9 +1253,17 @@
         pltpu.make_async_copy(do_hbm, dx.at[0], load_sem.at[0]),
         pltpu.make_async_copy(stat_hbm, sx.at[0], load_sem.at[1]),
     ]
+    loads += [
+        pltpu.make_async_copy(src, dst, load_sem.at[2 + i])
+        for i, (src, dst) in enumerate(
+            ((qx_hbm, qx), (kx_hbm, kx), (vx_hbm, vx), (parts_hbm, parts_ref), (mid_hbm, mid_ref))
+        )
+    ]
     loads[0].start()
     loads[1].start()
     gate.load()
+    for copy in loads[2:]:
+        copy.start()
 
     @pl.when(s >= devices - 2)
     def _():
@@ -1264,7 +1277,7 @@
     d_chain.first()
     s_chain.first()
     for i in range(4):
-        head_sum.to_mate(i, parts_ref.at[0, pl.ds(i * step, step), :]).start()
+        head_sum.to_mate(i, parts_hbm.at[0, pl.ds(i * step, step), :]).start()
 
     def queries_back(start, count):
         def body(i, _):
@@ -1334,6 +1347,8 @@
     gate.loaded()
     gate.make(0)
     gate.half(0, 0).start()
+    for copy in loads[2:6]:
+        copy.wait()
     queries_back(0, heads // 4)
     for i in range(4):
         head_sum.chip_sum(i, parts_ref[1, i * step : (i + 1) * step, :].astype(F32))
@@ -1361,6 +1376,8 @@
     keys_back(4)
     for i in range(4):
         at = slice(i * step, (i + 1) * step)
+        if i == 0:
+            loads[6].wait()
         block_out[at, :] = (mid_ref[at, :] + head_sum.joined(i)).astype(BF16)
     s_chain.arrived(3)
     d_chain.arrived(3)
@@ -1401,13 +1418,16 @@
     flops = 14 * rows * rows * parts * cols
     return pl.pallas_call(
         functools.partial(attention_back_kernel, devices, cores),
-        in_specs=[hbm] * 7 + [vmem] * 11,
+        in_specs=[hbm] * 12 + [vmem] * 6,
         out_specs=[vmem] * 5 + [hbm],
         out_shape=[jax.ShapeDtypeStruct((rows, width), BF16)]
         + [jax.ShapeDtypeStruct((rows, cols), BF16)] * 3
         + [jax.ShapeDtypeStruct((count, units, depth), BF16)]
         + [jax.ShapeDtypeStruct((units, rows), BF16)],
-        scratch_shapes=[
+        scratch_shapes=[pltpu.VMEM((parts, rows, cols), BF16)] * 3
+        + [
+            pltpu.VMEM((rows, width), F32),
+            pltpu.VMEM((2, rows, width // 2), BF16),
             pltpu.VMEM((parts, rows, cols), BF16),
             pltpu.VMEM((parts, heads, 2, rows), F32),
             pltpu.VMEM((rows, cols), F32),
@@ -1416,7 +1436,7 @@
         + sum_scratch(rows, width)
         + give
         + [dma((len(pieces_of(units, 3 * HEAD_DIM)),))] * 2
-        + [dma((2,))]
+        + [dma((7,))]
         + [dma((4,))] * 4
         + [dma((12,))] * 2,
         compiler_params=pltpu.CompilerParams(
@@ -1424,7 +1444,22 @@
         ),
         cost_estimate=cost(flops, 80 << 20),
         name="attention_back",
-    )(do, stat, *gate, grad_up, branch, mid, low_col, low_row, *tables, keys, values, queries, lse, delta)
+    )(
+        do,
+        stat,
+        *gate,
+        grad_up,
+        branch,
+        mid,
+        keys,
+        values,
+        queries,
+        low_col,
+        low_row,
+        *tables,
+        lse,
+        delta,
+    )
 
 
 class Reduce:

time: 416 us -> 411 us (0.988)
  Pallas kernels: 396 us -> 391 us
    pallas_call x1, Pallas kernels: 65.5 us -> 60.6 us  [attention_back(): pl.pallas_call(functools.partial(attention_back_kernel, devices, cores),...]
where the time goes in v7:
time: 411 us; the launch traced here: 405 us
  Pallas kernels  391 us (95%)
  other arithmetic  7.76 us (2%)
  local copies, waits for them, and re-layouts  5.09 us (1%)
    pallas_call x1, Pallas kernels, weight_gradients(): pl.pallas_call(functools.partial(weights_kernel, devices, cores), in_spec...  171 us
    pallas_call x1, Pallas kernels, forward(): pl.pallas_call(functools.partial(forward_kernel, devices, cores), in_spec...  108 us
    pallas_call x1, Pallas kernels, attention_back(): pl.pallas_call(functools.partial(attention_back_kernel, devices, cores),...  60.6 us
    pallas_call x1, Pallas kernels, middle(): pl.pallas_call(functools.partial(middle_kernel, devices, cores), in_specs...  50.7 us

profile of v7, /device:TPU:0, one launch (start us, length us, event | category | flops | bytes accessed | tf_op | source)
XLA Modules:
  0.0 404.7 jit_solution(16027746417187039043)
XLA Ops:
  0.6 108.0 %forward.1 = (bf16[5,512,512]{2,1,0:T(8,128)(2,1)}, bf16[5,512,512]{2,1,0:T(8,128)(2,1)}, bf16[5,512,512]{2,1,0:T(8,128)(2,1)}, bf16[4,256,512]{2,1,0:T(8,128)(2...) custom-call(s32[4]{0:T(128)} %lengths_ref.1, ...), custom_call_target="tpu_custom_call" | custom-call | flops 5368709120 | bytes 41943040 | tf_op jit(solution)/shard_map/forward/pallas_call | solution.py:854
  108.7 50.7 %middle.1 = (bf16[2,512,1024]{2,1,0:T(8,128)(2,1)}, f32[512,2048]{1,0:T(8,128)}, f32[1,2048]{1,0:T(1,128)}, bf16[512,512]{1,0:T(8,128)(2,1)}, f32[4,512,1]{2,1,0...) custom-call(bf16[512,2048]{1,0:T(8,128)(2,1)} %get-tuple-element.60., ...), custom_call_target="tpu_custom_call" | custom-call | flops 17314086912 | bytes 62914560 | tf_op jit(solution)/shard_map/middle/pallas_call | solution.py:1133
  159.4 60.6 %attention_back.1 = (bf16[512,2048]{1,0:T(8,128)(2,1)}, bf16[512,512]{1,0:T(8,128)(2,1)}, bf16[512,512]{1,0:T(8,128)(2,1)}, bf16[512,512]{1,0:T(8,128)(2,1)}, bf...) custom-call(bf16[512,512]{1,0:T(8,128)(2,1)} %get-tuple-element.68.do_hbm, ...), custom_call_target="tpu_custom_call" | custom-call | flops 9395240960 | bytes 83886080 | tf_op jit(solution)/shard_map/attention_back/pallas_call | solution.py:1419
  220.0 171.4 %weight_gradients.1 = (bf16[1376,256]{1,0:T(8,128)(2,1)}, bf16[1376,256]{1,0:T(8,128)(2,1)}, bf16[1376,256]{1,0:T(8,128)(2,1)}, bf16[256,512]{1,0:T(8,128)(2,1)}...) custom-call(bf16[1376,512]{1,0:T(8,128)(2,1)} %get-tuple-element.70., ...), custom_call_target="tpu_custom_call" | custom-call | flops 10737418240 | bytes 62914560 | tf_op jit(solution)/shard_map/weight_gradients/pallas_call | solution.py:1815
  391.4 0.0 copy-start.2
  391.4 3.1 convert_bitcast_fusion
  394.6 0.0 copy-start.6
  394.6 0.0 copy-start.5
  394.6 0.0 copy-start.4
  394.6 0.0 copy-done.2
  394.6 0.0 copy-start.3
  394.6 1.2 convert_bitcast_fusion.2
  395.8 0.0 copy-start
  395.8 0.0 copy-done.6
  395.8 0.9 convert_element_type.15
  396.6 0.0 copy-done.5
  396.6 0.9 convert_element_type.16
  397.5 0.0 copy-done.4
  397.5 0.9 convert_element_type.17
  398.4 0.0 copy-done.3
  398.4 0.9 convert_element_type.18
  399.2 1.4 fusion
  400.6 0.0 copy-done
  400.6 0.0 copy-start.1
  400.6 1.3 copy.27
  401.9 1.0 copy-done.1
  403.0 1.3 copy.28
Async XLA Ops:
  391.4 3.2 copy-start.2
  394.6 1.2 copy-start.6
  394.6 2.1 copy-start.5
  394.6 2.9 copy-start.4
  394.6 3.8 copy-start.3
  395.8 4.8 %copy-start = (bf16[512,2048]{1,0:T(8,128)(2,1)S(1)}, bf16[512,2048]{1,0:T(8,128)(2,1)}, u32[]{:S(2)}) copy-start(bf16[512,2048]{1,0:T(8,128)(2,1)} %get-tuple-element.124) | copy-start | bytes 6291460
  400.6 2.3 copy-start.1
